TPU v7x, 32 devices: a whole 2x2x4 slice. The times are simulated.
32 devices in a mesh: grp: 2 (over y), tile: 8 (over z, x), gene: 2 (over core).
Axes of the slice: x: 2, y: 2, z: 4, core: 2. Of those that a mesh axis runs over, the one named last changes fastest.
Arguments:
- counts: int32 [4096, 8192], P(('grp', 'tile'), 'gene'), parts along dimension 0, may hold values from 0 to 86, as said below
- cell_factor: float32 [32, 4096], P(None, ('grp', 'tile')), parts along dimension 1, may hold values from 0.05 to 1
- gene_factor: bfloat16 [32, 16384], P(None, ('grp', 'gene')), parts along dimension 1, may hold values from 0.049804688 to 1
- tissue: int32 [4096], P(('grp', 'tile')), parts along dimension 0, may hold values from 0 to 1, as said below
- neighbours: int32 [8, 4096], P(None, ('grp', 'tile')), parts along dimension 1, may hold values from 0 to 2047, as said below
Outputs:
- new_cells: float32 [32, 4096], P(None, ('grp', 'tile')), parts along dimension 1
- new_genes: bfloat16 [32, 16384], P(None, ('grp', 'gene')), parts along dimension 1
There are 2 independent parts, one for each index of `grp`. A program takes and returns all parts, laid end to end along the dimension named above; each array names one. Nothing has to cross between parts.
Inputs may be any that keep to these rules, and one draw needn't show every extreme that they name: `counts`: counts of each cell and gene. Share of tissue differs among tiles. `neighbours`: every neighbour index lies within 32 positions of its cell in cell order, and that distance is reached.
All inputs are finite; a program needn't handle non-finite values.
Results may differ from a plain program's by a relative error of at most 0.00165.
Values may be sent and summed in bfloat16 or wider, within the bound.
No kernel may reach another device: no remote copies, remote signals or barrier semaphores. Data moves between devices by JAX's collectives and lax.ppermute only.
A program may use at most 64 MiB of HBM per device.

v0:
```python
import jax
import jax.numpy as jnp
from jax import lax
from jax.sharding import PartitionSpec as P

RANK = 32
BORDER = 32
PASSES = 2


smooth_weight = 0.5


def extended(array, sides, width):
    for axis, dim in sides:
        count, length = (lax.axis_size(axis), array.shape[dim])
        up = [(i, (i + 1) % count) for i in range(count - 1)]
        down = [(j, i) for i, j in up]
        last = lax.slice_in_dim(array, length - width, length, axis=dim)
        first = lax.slice_in_dim(array, 0, width, axis=dim)
        before = lax.ppermute(last, axis, up)
        after = lax.ppermute(first, axis, down)
        array = jnp.concatenate([before, array, after], axis=dim)
    return array


def on_device(counts, cell_factor, gene_factor, tissue, neighbours):
    hfull = gene_factor.astype(jnp.float32)
    xfull = counts.astype(jnp.float32)
    maskf = tissue.astype(jnp.float32)
    mask_row = maskf[None]
    width = cell_factor.shape[1]
    count = neighbours.shape[0]
    anchor = lax.axis_index("tile") * width
    local = (neighbours - anchor + BORDER).reshape(-1)
    gsum_local = jnp.sum(hfull, axis=1)
    inside = tissue[None] > 0
    cells = cell_factor
    for step in range(PASSES):
        product = lax.dot_general(
            cells, hfull, (((0,), (0,)), ((), ())), precision=lax.Precision.HIGHEST
        )
        ratio = xfull / product
        numer_part = lax.dot_general(
            hfull, ratio, (((1,), (1,)), ((), ())), precision=lax.Precision.HIGHEST
        )
        numer, gsum = lax.psum((numer_part, gsum_local), "gene")
        updated = jnp.where(inside, cells * numer / gsum[:, None], cells)
        padded, mask_padded = (
            extended(updated.astype(jnp.bfloat16), (("tile", 1),), BORDER).astype(updated.dtype),
            extended(mask_row.astype(jnp.bfloat16), (("tile", 1),), BORDER).astype(mask_row.dtype),
        )
        near_mask = jnp.take(mask_padded[0], local).reshape(count, width)
        near_count = jnp.maximum(jnp.sum(near_mask, axis=0), 1.0)
        gathered = jnp.take(padded, local, axis=1).reshape(RANK, count, width)
        near = jnp.sum(gathered * near_mask[None], axis=1) / near_count
        cells = jnp.where(inside, (1.0 - smooth_weight) * updated + smooth_weight * near, updated)
    product = lax.dot_general(
        cells, hfull, (((0,), (0,)), ((), ())), precision=lax.Precision.HIGHEST
    )
    ratio = maskf[:, None] * xfull / product
    hnum_part = jnp.dot(cells, ratio, precision=lax.Precision.HIGHEST)
    hden_part = jnp.sum(cells * maskf[None], axis=1)
    hnum, hden = lax.psum((hnum_part, hden_part), "tile")
    new_genes = (hfull * hnum / hden[:, None]).astype(jnp.bfloat16)
    return (cells, new_genes)


def solution(mesh):
    return jax.shard_map(
        on_device,
        mesh=mesh,
        in_specs=(
            P(("grp", "tile"), "gene"),
            P(None, ("grp", "tile")),
            P(None, ("grp", "gene")),
            P(("grp", "tile")),
            P(None, ("grp", "tile")),
        ),
        out_specs=(P(None, ("grp", "tile")), P(None, ("grp", "gene"))),
        check_vma=False,
    )
```

profile of v0, /device:TPU:0, one launch (start us, length us, event | category | flops | bytes accessed | tf_op | source)
XLA Modules:
  0.0 170.4 jit_solution(17767506239490851735)
XLA Ops:
  7.2 0.0 all-reduce.3.cloned.1.call-start
  7.2 0.7 convert_convert_fusion
  7.9 0.1 fusion.7
  8.0 4.8 %collective-permute-start.2 = (bf16[1,32]{1,0:T(2,128)(2,1)S(1)}, bf16[1,32]{1,0:T(2,128)(2,1)S(1)}, u32[]{:S(2)}, u32[]{:S(2)}) collective-permute-start(bf16[1,32]{1,0:T(2,128)(2,1)S(1)} %get-tuple-element.18), channel_id=1, source_target_pairs={{0,2},{2,4},{4,6},{6,8},{8,10},{10,12},{12,14},{1,3},{3,5},{5,7},{... | collective-permute-start | bytes 200 | tf_op jit(solution)/shard_map/ppermute | solution.py:21
  12.8 1.3 collective-permute-start.3
  14.1 0.7 broadcast_compare_fusion
  14.8 1.1 convert_reduce_fusion
  15.9 0.0 copy-start
  15.9 4.3 %convolution_divide_fusion.2 = f32[256,4096]{1,0:T(8,128)S(1)} fusion(f32[32,256]{1,0:T(8,128)} %param.10, bf16[32,4096]{1,0:T(8,128)(2,1)} %param.11, s32[256,4096]{1,0:T(8,128)} %param.9), kind=kOutput, calls=%fused_computation.5 | convolution fusion | flops 404750336 | bytes 8683520 | tf_op jit(solution)/shard_map/dot_general | solution.py:40
  20.3 0.0 copy-done
  20.3 0.0 copy-start.2
  20.3 0.0 copy-start.3
  20.3 2.2 %convolution_bitcast_fusion.1 = f32[32,256]{1,0:T(8,128)S(1)} fusion(f32[256,4096]{1,0:T(8,128)S(1)} %convolution_divide_fusion.2, bf16[32,4096]{1,0:T(8,128)(2,1)S(1)} %copy-done), kind=kOutput, calls=%fused_computation.7 | convolution fusion | flops 402653184 | bytes 4489216 | tf_op jit(solution)/shard_map/dot_general | solution.py:44
  22.5 3.5 %all-reduce = (f32[32,256]{1,0:T(8,128)S(1)}, f32[32]{0:T(128)S(1)}) all-reduce(f32[32,256]{1,0:T(8,128)S(1)} %convolution_bitcast_fusion.1, f32[32]{0:T(128)S(1)} %convert_reduce_fusion), channel_id=1, replica_groups=mesh['grp'=2,'tile'=8,'gene'=2] {'gene'}, use_global_device_ids=true, to_apply=%region_0.0 | all-reduce | flops 8224 | bytes 65792 | tf_op jit(solution)/shard_map/psum | solution.py:47
  26.0 0.0 copy-done.2
  26.0 0.1 fusion.4
  26.1 0.1 fusion.6
  26.1 4.5 %collective-permute-start = (bf16[32,32]{1,0:T(8,128)(2,1)S(1)}, bf16[32,32]{1,0:T(8,128)(2,1)S(1)}, u32[]{:S(2)}, u32[]{:S(2)}) collective-permute-start(bf16[32,32]{1,0:T(8,128)(2,1)S(1)} %get-tuple-element.16), channel_id=1, source_target_pairs={{0,2},{2,4},{4,6},{6,8},{8,10},{10,12},{12,14},{1,3},{3,5},{5,7},{... | collective-permute-start | bytes 6152 | tf_op jit(solution)/shard_map/ppermute | solution.py:21
  30.7 1.3 collective-permute-start.1
  32.0 0.0 copy-done.3
  32.0 0.0 collective-permute-done.2
  32.0 0.0 collective-permute-done.3
  32.1 0.1 maximum_convert_fusion.2
  32.1 13.2 %gather_fusion.1 = f32[2048]{0:T(1024)S(1)} fusion(f32[320]{0:T(512)S(1)} %maximum_convert_fusion.2, s32[2048]{0:T(1024)S(1)} %fusion.2), kind=kCustom, calls=%fused_computation.1.clone | custom fusion | bytes 24576 | tf_op jit(solution)/shard_map/jit(_take)/gather | solution.py:53
  45.4 0.0 collective-permute-done
  45.4 0.0 collective-permute-done.1
  45.4 0.1 maximum_convert_fusion
  45.5 0.1 copy.11
  45.6 5.5 %gather_fusion = f32[2048,32]{1,0:T(8,128)S(1)} fusion(f32[32,320]{0,1:T(8,128)S(1)} %copy.11, s32[2048]{0:T(1024)S(1)} %fusion.2), kind=kCustom, calls=%fused_computation.clone | custom fusion | bytes 532480 | tf_op jit(solution)/shard_map/jit(_take)/gather | solution.py:55
  51.1 0.3 broadcast_select_fusion.1
  51.5 0.3 multiply_reduce_fusion.1
  51.8 0.1 copy.12
  51.9 4.2 %convolution_divide_fusion.1 = f32[256,4096]{1,0:T(8,128)S(1)} fusion(bf16[32,4096]{1,0:T(8,128)(2,1)S(1)} %copy-done, s32[256,4096]{1,0:T(8,128)} %param.9, f32[32,256]{1,0:T(8,128)S(1)} %get-tuple-element.13, f32[32,256]{1,0:T(8,128)S(1)} %copy.12, f32[256]{0:T(256)S(1)} %broadcast_maximum_fusion, pred[256]{0:T(512)(128)(4,1)S(1)} %broadcast_compare_fusion), kind=kOutput, calls=%fused_computation.4 | convolution fusion | flops 404783104 | bytes 8717568 | tf_op jit(solution)/shard_map/dot_general | solution.py:40
  56.1 2.2 %convolution_bitcast_fusion = f32[32,256]{1,0:T(8,128)S(1)} fusion(f32[256,4096]{1,0:T(8,128)S(1)} %convolution_divide_fusion.1, bf16[32,4096]{1,0:T(8,128)(2,1)S(1)} %copy-done), kind=kOutput, calls=%fused_computation.6 | convolution fusion | flops 402653184 | bytes 4489216 | tf_op jit(solution)/shard_map/dot_general | solution.py:44
  58.3 3.4 %psum.40 = f32[32,256]{1,0:T(8,128)S(1)} all-reduce(f32[32,256]{1,0:T(8,128)S(1)} %convolution_bitcast_fusion), channel_id=1, replica_groups=mesh['grp'=2,'tile'=8,'gene'=2] {'gene'}, use_global_device_ids=true, to_apply=%region_5.8 | all-reduce | flops 8192 | bytes 65536 | tf_op jit(solution)/shard_map/psum | solution.py:47
  61.7 0.1 fusion.3
  61.8 0.1 fusion.5
  61.9 5.0 %collective-permute-start.4 = (bf16[32,32]{1,0:T(8,128)(2,1)S(1)}, bf16[32,32]{1,0:T(8,128)(2,1)S(1)}, u32[]{:S(2)}, u32[]{:S(2)}) collective-permute-start(bf16[32,32]{1,0:T(8,128)(2,1)S(1)} %get-tuple-element.14), channel_id=1, source_target_pairs={{0,2},{2,4},{4,6},{6,8},{8,10},{10,12},{12,14},{1,3},{3,5},{5,7},{... | collective-permute-start | bytes 6152 | tf_op jit(solution)/shard_map/ppermute | solution.py:21
  66.9 1.5 collective-permute-start.5
  68.4 0.0 collective-permute-done.4
  68.4 5.0 %collective-permute-done.5 = bf16[32,32]{1,0:T(8,128)(2,1)S(1)} collective-permute-done((bf16[32,32]{1,0:T(8,128)(2,1)S(1)}, bf16[32,32]{1,0:T(8,128)(2,1)S(1)}, u32[]{:S(2)}, u32[]{:S(2)}) %collective-permute-start.5) | collective-permute-done | bytes 2080 | tf_op jit(solution)/shard_map/ppermute | solution.py:22
  73.3 0.1 maximum_convert_fusion.1
  73.4 0.1 copy.13
  73.5 5.5 %gather_fusion.2 = f32[2048,32]{1,0:T(8,128)S(1)} fusion(f32[32,320]{0,1:T(8,128)S(1)} %copy.13, s32[2048]{0:T(1024)S(1)} %fusion.2), kind=kCustom, calls=%fused_computation.2.clone | custom fusion | bytes 532480 | tf_op jit(solution)/shard_map/jit(_take)/gather | solution.py:55
  79.0 0.3 broadcast_select_fusion
  79.3 0.3 multiply_reduce_fusion
  79.7 0.1 copy.14
  79.8 0.1 multiply_reduce_fusion.2
  79.9 0.0 copy-start.1
  79.9 4.4 %convolution_divide_fusion = f32[256,4096]{1,0:T(8,128)S(1)} fusion(f32[32,256]{1,0:T(8,128)S(1)} %get-tuple-element.7, bf16[32,4096]{1,0:T(8,128)(2,1)S(1)} %copy-done, s32[256,4096]{1,0:T(8,128)} %param.9, f32[256]{0:T(256)S(1)} %get-tuple-element.21), kind=kOutput, calls=%fused_computation.3 | convolution fusion | flops 405798912 | bytes 8684544 | tf_op jit(solution)/shard_map/dot_general | solution.py:58
  84.3 0.0 copy-done.1
  84.3 3.3 %fusion.8 = f32[32,4096]{1,0:T(8,128)} fusion(f32[32,256]{1,0:T(8,128)S(1)} %get-tuple-element.7, f32[256,4096]{1,0:T(8,128)S(1)} %convolution_divide_fusion), kind=kOutput, calls=%fused_computation.37 | convolution fusion | flops 402653184 | bytes 4751360 | tf_op jit(solution)/shard_map/dot_general | solution.py:62
  87.6 0.0 all-reduce.3.cloned.1.call-update
  87.6 20.3 %psum.42 = f32[32]{0:T(128)S(1)} all-reduce(f32[32]{0:T(128)S(1)} %get-tuple-element.6), channel_id=1, replica_groups=mesh['grp'=2,'tile'=8,'gene'=2] {'tile'}, use_global_device_ids=true, to_apply=%region_9.12 | all-reduce | flops 32 | bytes 256 | tf_op jit(solution)/shard_map/psum | solution.py:64
  107.9 53.9 %all-reduce.3.cloned.1.call-done = f32[32,4096]{1,0:T(8,128)} async-done(((f32[32,4096]{1,0:T(8,128)}), f32[32,4096]{1,0:T(8,128)}) %all-reduce.3.cloned.1.call-update) | async-done | bytes 524304 | tf_op jit(solution)/shard_map/psum | solution.py:64
  161.8 1.8 %fusion.1 = bf16[32,4096]{1,0:T(8,128)(2,1)} fusion(f32[32,4096]{1,0:T(8,128)} %all-reduce.3.cloned.1.call-done, bf16[32,4096]{1,0:T(8,128)(2,1)S(1)} %copy-done, f32[32]{0:T(128)S(1)} %psum.42), kind=kLoop, calls=%fused_computation.13 | loop fusion | flops 524288 | bytes 1048704 | tf_op jit(solution)/shard_map/convert_element_type | solution.py:65
  (8 shorter events, 0.1 us)
Async XLA Ops:
  7.2 154.6 %all-reduce.3.cloned.1.call-start = ((), (), s32[]{:S(2)}) async-start(), calls=%async_computation | async-start | bytes 1048576 | tf_op jit(solution)/shard_map/psum | solution.py:64
  8.0 24.1 %collective-permute-start.2 = (bf16[1,32]{1,0:T(2,128)(2,1)S(1)}, bf16[1,32]{1,0:T(2,128)(2,1)S(1)}, u32[]{:S(2)}, u32[]{:S(2)}) collective-permute-start(bf16[1,32]{1,0:T(2,128)(2,1)S(1)} %get-tuple-element.18), channel_id=1, source_target_pairs={{0,2},{2,4},{4,6},{6,8},{8,10},{10,12},{12,14},{1,3},{3,5},{5,7},{... | collective-permute-start | bytes 200 | tf_op jit(solution)/shard_map/ppermute | solution.py:21
  12.8 19.2 %collective-permute-start.3 = (bf16[1,32]{1,0:T(2,128)(2,1)S(1)}, bf16[1,32]{1,0:T(2,128)(2,1)S(1)}, u32[]{:S(2)}, u32[]{:S(2)}) collective-permute-start(bf16[1,32]{1,0:T(2,128)(2,1)S(1)} %get-tuple-element.19), channel_id=1, source_target_pairs={{2,0},{4,2},{6,4},{8,6},{10,8},{12,10},{14,12},{3,1},{5,3},{7,5},{... | collective-permute-start | bytes 200 | tf_op jit(solution)/shard_map/ppermute | solution.py:22
  15.9 4.4 %copy-start = (bf16[32,4096]{1,0:T(8,128)(2,1)S(1)}, bf16[32,4096]{1,0:T(8,128)(2,1)}, u32[]{:S(2)}) copy-start(bf16[32,4096]{1,0:T(8,128)(2,1)} %param.11) | copy-start | bytes 786436
  20.3 5.7 %copy-start.2 = (f32[32,256]{1,0:T(8,128)S(1)}, f32[32,256]{1,0:T(8,128)}, u32[]{:S(2)}) copy-start(f32[32,256]{1,0:T(8,128)} %param.10) | copy-start | bytes 98308
  20.3 11.7 %copy-start.3 = (s32[8,256]{1,0:T(8,128)S(1)}, s32[8,256]{1,0:T(8,128)}, u32[]{:S(2)}) copy-start(s32[8,256]{1,0:T(8,128)} %param.13) | copy-start | bytes 24580
  26.1 19.3 %collective-permute-start = (bf16[32,32]{1,0:T(8,128)(2,1)S(1)}, bf16[32,32]{1,0:T(8,128)(2,1)S(1)}, u32[]{:S(2)}, u32[]{:S(2)}) collective-permute-start(bf16[32,32]{1,0:T(8,128)(2,1)S(1)} %get-tuple-element.16), channel_id=1, source_target_pairs={{0,2},{2,4},{4,6},{6,8},{8,10},{10,12},{12,14},{1,3},{3,5},{5,7},{... | collective-permute-start | bytes 6152 | tf_op jit(solution)/shard_map/ppermute | solution.py:21
  30.7 14.7 %collective-permute-start.1 = (bf16[32,32]{1,0:T(8,128)(2,1)S(1)}, bf16[32,32]{1,0:T(8,128)(2,1)S(1)}, u32[]{:S(2)}, u32[]{:S(2)}) collective-permute-start(bf16[32,32]{1,0:T(8,128)(2,1)S(1)} %get-tuple-element.17), channel_id=1, source_target_pairs={{2,0},{4,2},{6,4},{8,6},{10,8},{12,10},{14,12},{3,1},{5,3},{7,5},{... | collective-permute-start | bytes 6152 | tf_op jit(solution)/shard_map/ppermute | solution.py:22
  61.9 6.5 %collective-permute-start.4 = (bf16[32,32]{1,0:T(8,128)(2,1)S(1)}, bf16[32,32]{1,0:T(8,128)(2,1)S(1)}, u32[]{:S(2)}, u32[]{:S(2)}) collective-permute-start(bf16[32,32]{1,0:T(8,128)(2,1)S(1)} %get-tuple-element.14), channel_id=1, source_target_pairs={{0,2},{2,4},{4,6},{6,8},{8,10},{10,12},{12,14},{1,3},{3,5},{5,7},{... | collective-permute-start | bytes 6152 | tf_op jit(solution)/shard_map/ppermute | solution.py:21
  66.9 6.4 %collective-permute-start.5 = (bf16[32,32]{1,0:T(8,128)(2,1)S(1)}, bf16[32,32]{1,0:T(8,128)(2,1)S(1)}, u32[]{:S(2)}, u32[]{:S(2)}) collective-permute-start(bf16[32,32]{1,0:T(8,128)(2,1)S(1)} %get-tuple-element.15), channel_id=1, source_target_pairs={{2,0},{4,2},{6,4},{8,6},{10,8},{12,10},{14,12},{3,1},{5,3},{7,5},{... | collective-permute-start | bytes 6152 | tf_op jit(solution)/shard_map/ppermute | solution.py:22
  79.9 4.4 %copy-start.1 = (f32[32,256]{1,0:T(8,128)}, f32[32,256]{1,0:T(8,128)S(1)}, u32[]{:S(2)}) copy-start(f32[32,256]{1,0:T(8,128)S(1)} %get-tuple-element.7) | copy-start | bytes 98308
Sparse Core Ops, SparseCore 0:
  87.7 73.9 all-reduce.2
where the time goes:
time: 171 us; the launch traced here: 170 us
  waiting for transfers between devices  58.9 us (34%)
  blocking collectives  27.1 us (16%)
  local copies, waits for them, and re-layouts  24.8 us (15%)
  matrix products  20.6 us (12%)
  starting transfers between devices  18.4 us (11%)
  between operations  14.4 us (8%)
  other arithmetic  6.23 us (4%)
    psum x1, waiting for transfers between devices, on_device(): hnum, hden = lax.psum((hnum_part, hden_part), 'tile')  53.9 us
    psum x1, blocking collectives, on_device(): hnum, hden = lax.psum((hnum_part, hden_part), 'tile')  20.3 us
    ppermute x3, starting transfers between devices, extended(): before = lax.ppermute(last, axis, up)  14.4 us
    gather x1, local copies, waits for them, and re-layouts, on_device(): near_mask = jnp.take(mask_padded[0], local).reshape(count, width)  13.2 us
    dot_general x3, matrix products, on_device(): lax.dot_general(cells, hfull, (((0,), (0,)), ((), ())), precision=lax.Pre...  12.9 us
    gather x2, local copies, waits for them, and re-layouts, on_device(): gathered = jnp.take(padded, local, axis=1).reshape(RANK, count, width)  11 us
    psum x2, blocking collectives, on_device(): numer, gsum = lax.psum((numer_part, gsum_local), 'gene')  6.86 us
    ppermute x3, waiting for transfers between devices, extended(): after = lax.ppermute(first, axis, down)  4.96 us
  transfers between devices with their start and end apart: 7, of which 2 were waited for; matrix products, arithmetic and copies ran while one was open for 13% of the time, Pallas kernels for 0%

commit v1 on v0

v1 whole, which is shorter than its diff:
```python
import functools

import jax
import jax.numpy as jnp
from jax import lax
from jax.experimental import pallas as pl
from jax.experimental.pallas import tpu as pltpu
from jax.sharding import PartitionSpec as P

BORDER = 32
LANES = 128
FLAG_ROWS = 8
smooth_weight = 0.5
VMEM_BYTES = 24 * 1024 * 1024


def split(values):
    high = values.astype(jnp.bfloat16)
    low = (values - high.astype(jnp.float32)).astype(jnp.bfloat16)
    return high, low


def chunk_of(genes):
    for size in (512, 256, 128):
        if genes % size == 0:
            return size
    return genes


def factor_columns(cells):
    return jnp.concatenate(split(cells.T), axis=1)


def numerator(columns, gene_ref, counts_at, part_ref):
    rank, genes = gene_ref.shape
    size = chunk_of(genes)
    total = jnp.zeros((rank, columns.shape[0]), jnp.float32)
    for start in range(0, genes, size):
        hf = gene_ref[:, start : start + size]
        product = jnp.dot(
            columns, jnp.concatenate([hf, hf], axis=0), preferred_element_type=jnp.float32
        )
        ratio = counts_at(start, size) * pl.reciprocal(product, approx=True)
        total += lax.dot_general(
            hf,
            ratio.astype(jnp.bfloat16),
            (((1,), (1,)), ((), ())),
            preferred_element_type=jnp.float32,
        )
    part_ref[:, : columns.shape[0]] = total


def first_kernel(
    tiles, place_ref, counts_ref, cells_ref, gene_ref, neigh_ref,
    part_ref, kept_ref, pick_ref, landed, sems,
):
    rank, genes = gene_ref.shape
    width = cells_ref.shape[1]
    size = chunk_of(genes)
    copies = [
        pltpu.make_async_copy(
            counts_ref.at[:, pl.ds(at, size)], landed.at[:, pl.ds(at, size)], sems.at[i]
        )
        for i, at in enumerate(range(0, genes, size))
    ]
    for copy in copies:
        copy.start()
    here = place_ref[0]
    neigh = neigh_ref[...] - here * width
    for at in range(0, width, LANES):
        where = at + lax.broadcasted_iota(jnp.int32, (LANES, width), 0)
        found = jnp.zeros((LANES, width), jnp.float32)
        for j in range(neigh.shape[0]):
            found += (neigh[j : j + 1] == where).astype(jnp.float32)
        pick_ref[at : at + LANES] = found.astype(jnp.bfloat16)
    row = lax.broadcasted_iota(jnp.int32, (LANES, width), 0)
    slot = row % (2 * BORDER)
    beside = jnp.where(row < 2 * BORDER, place_ref[1], place_ref[2])
    where = (beside - here) * width + slot + jnp.where(slot < BORDER, 0, width - 2 * BORDER)
    found = jnp.zeros((LANES, width), jnp.float32)
    for j in range(neigh.shape[0]):
        found += (neigh[j : j + 1] == where).astype(jnp.float32)
    pick_ref[width:] = jnp.where(beside < 0, 0.0, found).astype(jnp.bfloat16)

    gsum = jnp.sum(gene_ref[...].astype(jnp.float32), axis=1, keepdims=True)
    part_ref[:, width:] = jnp.broadcast_to(gsum, (rank, LANES))

    def counts_at(start, size):
        copies[start // size].wait()
        values = landed[:, start : start + size].astype(jnp.float32)
        kept_ref[:, start : start + size] = values.astype(jnp.bfloat16)
        return values

    numerator(factor_columns(cells_ref[...]), gene_ref, counts_at, part_ref)


def update_kernel(part_ref, other_ref, cells_ref, tissue_ref, updated_ref, edges_ref):
    rank, width = cells_ref.shape
    flags = tissue_ref[...] > 0
    numer = part_ref[:, :width] + other_ref[:, :width]
    gsum = part_ref[:, width:] + other_ref[:, width:]
    cells = cells_ref[...]
    updated = jnp.where(flags, cells * numer / gsum[:, :1], cells)
    updated_ref[...] = updated
    masked = jnp.where(flags, updated, 0.0)
    row = jnp.broadcast_to(flags.astype(jnp.float32), (FLAG_ROWS, width))
    both = jnp.concatenate([masked, row], axis=0)
    edges_ref[:, :BORDER] = both[:, :BORDER]
    edges_ref[:, BORDER : 2 * BORDER] = both[:, width - BORDER :]
    edges_ref[:, 2 * BORDER :] = jnp.zeros_like(edges_ref[:, 2 * BORDER :])


def smoothed(updated_ref, tissue_ref, first_ref, second_ref, pick_ref):
    rank, width = updated_ref.shape
    updated = updated_ref[...]
    flags = tissue_ref[...] > 0
    masked = jnp.where(flags, updated, 0.0)
    row = jnp.broadcast_to(flags.astype(jnp.float32), (FLAG_ROWS, width))
    own = jnp.concatenate([masked, row], axis=0)
    sides = jnp.concatenate(
        [first_ref[:, : 2 * BORDER], second_ref[:, : 2 * BORDER]], axis=1
    )
    near = jnp.zeros((rank + FLAG_ROWS, width), jnp.float32)
    for values, pick in ((own, pick_ref[:width]), (sides, pick_ref[width:])):
        for part in split(values):
            near += jnp.dot(part, pick, preferred_element_type=jnp.float32)
    mean = near[:rank] / jnp.maximum(near[rank : rank + 1], 1.0)
    return jnp.where(
        flags, (1.0 - smooth_weight) * updated + smooth_weight * mean, updated
    ), flags


def next_kernel(
    updated_ref, tissue_ref, first_ref, second_ref, pick_ref, kept_ref, gene_ref,
    cells_ref, part_ref,
):
    cells, flags = smoothed(updated_ref, tissue_ref, first_ref, second_ref, pick_ref)
    cells_ref[...] = cells

    def counts_at(start, size):
        return kept_ref[:, start : start + size].astype(jnp.float32)

    numerator(factor_columns(cells), gene_ref, counts_at, part_ref)


def last_kernel(
    updated_ref, tissue_ref, first_ref, second_ref, pick_ref, kept_ref, gene_ref,
    cells_ref, hnum_ref, hden_ref,
):
    rank, genes = gene_ref.shape
    size = chunk_of(genes)
    cells, flags = smoothed(updated_ref, tissue_ref, first_ref, second_ref, pick_ref)
    cells_ref[...] = cells
    masked = jnp.where(flags, cells, 0.0)
    hden_ref[...] = jnp.broadcast_to(jnp.sum(masked, axis=1, keepdims=True), hden_ref.shape)
    columns = factor_columns(cells)
    high, low = split(masked)
    rows = jnp.concatenate([high, low], axis=0)
    for start in range(0, genes, size):
        hf = gene_ref[:, start : start + size]
        product = jnp.dot(
            columns, jnp.concatenate([hf, hf], axis=0), preferred_element_type=jnp.float32
        )
        counts = kept_ref[:, start : start + size].astype(jnp.float32)
        ratio = (counts * pl.reciprocal(product, approx=True)).astype(jnp.bfloat16)
        both = jnp.dot(rows, ratio, preferred_element_type=jnp.float32)
        hnum_ref[:, start : start + size] = both[:rank] + both[rank:]


def call(kernel, outs, scratch=(), specs=None, limit=VMEM_BYTES):
    whole = pl.BlockSpec(memory_space=pltpu.VMEM)
    return lambda *args: pl.pallas_call(
        kernel,
        out_shape=outs,
        in_specs=specs or [whole] * len(args),
        out_specs=jax.tree.map(lambda _: whole, outs),
        scratch_shapes=list(scratch),
        compiler_params=pltpu.CompilerParams(vmem_limit_bytes=limit),
    )(*args)


def beside(tiles, genes, offset):
    pairs = []
    paired = set()
    for low in range(offset, tiles - 1, 2):
        paired |= {low, low + 1}
        for gene in range(genes):
            pairs.append((low * genes + gene, (low + 1) * genes + gene))
            pairs.append(((low + 1) * genes + gene, low * genes + gene))
    for tile in range(tiles):
        if tile not in paired:
            for gene in range(genes):
                pairs.append((tile * genes + gene, tile * genes + (gene + 1) % genes))
    return pairs


def on_device(counts, cell_factor, gene_factor, tissue, neighbours):
    rank, width = cell_factor.shape
    genes = gene_factor.shape[1]
    tiles, halves = lax.axis_size("tile"), lax.axis_size("gene")
    tile = lax.axis_index("tile")
    flag_row = tissue[None]
    shape = jax.ShapeDtypeStruct

    def partner(offset):
        other = jnp.where((tile - offset) % 2 == 0, tile + 1, tile - 1)
        return jnp.where((other >= 0) & (other < tiles), other, -1)

    place = jnp.stack([tile, partner(0), partner(1)]).astype(jnp.int32)
    factor = shape((rank, width), jnp.float32)
    part_shape = shape((rank, width + LANES), jnp.float32)
    whole = pl.BlockSpec(memory_space=pltpu.VMEM)
    chunks = genes // chunk_of(genes)
    part, kept, pick = call(
        functools.partial(first_kernel, tiles),
        (
            part_shape,
            shape((counts.shape[0], genes), jnp.bfloat16),
            shape((width + LANES, width), jnp.bfloat16),
        ),
        scratch=[pltpu.VMEM(counts.shape, jnp.int32), pltpu.SemaphoreType.DMA((chunks,))],
        specs=[pl.BlockSpec(memory_space=pltpu.SMEM), pl.BlockSpec(memory_space=pl.ANY)]
        + [whole] * 3,
    )(place, counts, cell_factor, gene_factor, neighbours)
    gsum_part = part[:, width:]
    cells = cell_factor

    def update(part, cells):
        if halves == 2:
            other = lax.ppermute(part, "gene", [(0, 1), (1, 0)])
        else:
            other = lax.psum(part, "gene") - part
        updated, edges = call(
            update_kernel, (factor, shape((rank + FLAG_ROWS, LANES), jnp.float32))
        )(part, other, cells, flag_row)
        sides = [
            lax.ppermute(edges, ("tile", "gene"), beside(tiles, halves, offset))
            for offset in (0, 1)
        ]
        return updated, flag_row, *sides, pick, kept, gene_factor

    cells, numer = call(next_kernel, (factor, factor))(*update(part, cells))
    part = jnp.concatenate([numer, gsum_part], axis=1)
    cells, hnum, hden = call(
        last_kernel,
        (factor, shape((rank, genes), jnp.float32), shape((rank, LANES), jnp.float32)),
    )(*update(part, cells))

    share = genes // tiles
    sent = jnp.concatenate(
        [
            hnum.reshape(rank, tiles, share).transpose(1, 0, 2),
            jnp.broadcast_to(hden[None, :, :1], (tiles, rank, 1)),
        ],
        axis=2,
    )
    got = jnp.sum(lax.all_to_all(sent, "tile", 0, 0), axis=0)
    mine = lax.dynamic_slice_in_dim(gene_factor, tile * share, share, 1).astype(jnp.float32)
    fresh = (mine * got[:, :share] / got[:, share:]).astype(jnp.bfloat16)
    every = lax.all_to_all(jnp.broadcast_to(fresh[None], (tiles, rank, share)), "tile", 0, 0)
    return cells, every.transpose(1, 0, 2).reshape(rank, genes)


def solution(mesh):
    return jax.shard_map(
        on_device,
        mesh=mesh,
        in_specs=(
            P(("grp", "tile"), "gene"),
            P(None, ("grp", "tile")),
            P(None, ("grp", "gene")),
            P(("grp", "tile")),
            P(None, ("grp", "tile")),
        ),
        out_specs=(P(None, ("grp", "tile")), P(None, ("grp", "gene"))),
        check_vma=False,
    )
```

time: 171 us -> 65.8 us (0.38)
  waiting for transfers between devices: 58.9 us -> 22.1 us
  matrix products: 20.6 us -> 0 us
  local copies, waits for them, and re-layouts: 24.8 us -> 5.69 us
  blocking collectives: 27.1 us -> 12.1 us
  between operations: 14.4 us -> 0.75 us
  Pallas kernels: 0 us -> 8.91 us
  starting transfers between devices: 18.4 us -> 13.8 us
  other arithmetic: 6.23 us -> 1.87 us
    psum x1 -> x0, waiting for transfers between devices: 53.9 us -> none  [on_device(): hnum, hden = lax.psum((hnum_part, hden_part), 'tile')]
    psum x3 -> x0, blocking collectives: 27.1 us -> none  [the longest x1 20.3 us: on_device(): hnum, hden = lax.psum((hnum_part, hden_part), 'tile')]
    gather x3 -> x0, local copies, waits for them, and re-layouts: 24.2 us -> none  [the longest x1 13.2 us: on_device(): near_mask = jnp.take(mask_padded[0], local).reshape(count, width)]
    dot_general x6 -> x0, matrix products: 20.6 us -> none  [the longest x3 12.9 us: on_device(): lax.dot_general(cells, hfull, (((0,), (0,)), ((), ())), precision=lax.Pre...]
    all_to_all x0 -> x1, waiting for transfers between devices: none -> 16.5 us  [on_device(): got = jnp.sum(lax.all_to_all(sent, 'tile', 0, 0), axis=0)]
    all_to_all x0 -> x1, blocking collectives: none -> 12.1 us  [on_device(): lax.all_to_all(jnp.broadcast_to(fresh[None], (tiles, rank, share)), 'tile...]
    ppermute x6, starting transfers between devices: 18.4 us -> 8.39 us  [the longest x4 7.8 us: update(): lax.ppermute(edges, ('tile', 'gene'), beside(tiles, halves, offset))]
    pallas_call x0 -> x5, Pallas kernels: none -> 8.91 us  [call(): pl.pallas_call(kernel, out_shape=outs, in_specs=specs or [whole] * len(ar...]
  transfers between devices with their start and end apart: 7 -> 7, of which waited for: 2 -> 5; matrix products, arithmetic and copies ran while one was open for 13% -> 0% of each run, Pallas kernels for 0% -> 0%
where the time goes in v1:
time: 65.8 us; the launch traced here: 65.3 us
  waiting for transfers between devices  22.1 us (34%)
  starting transfers between devices  13.8 us (21%)
  blocking collectives  12.1 us (18%)
  Pallas kernels  8.91 us (14%)
  local copies, waits for them, and re-layouts  5.69 us (9%)
  other arithmetic  1.87 us (3%)
  between operations  0.75 us (1%)
    all_to_all x1, waiting for transfers between devices, on_device(): got = jnp.sum(lax.all_to_all(sent, 'tile', 0, 0), axis=0)  16.5 us
    all_to_all x1, blocking collectives, on_device(): lax.all_to_all(jnp.broadcast_to(fresh[None], (tiles, rank, share)), 'tile...  12.1 us
    pallas_call x5, Pallas kernels, call(): pl.pallas_call(kernel, out_shape=outs, in_specs=specs or [whole] * len(ar...  8.91 us
    ppermute x4, starting transfers between devices, update(): lax.ppermute(edges, ('tile', 'gene'), beside(tiles, halves, offset))  7.8 us
    all_to_all x1, starting transfers between devices, on_device(): got = jnp.sum(lax.all_to_all(sent, 'tile', 0, 0), axis=0)  5.41 us
    unnamed x10, local copies, waits for them, and re-layouts  4.6 us
    ppermute x4, waiting for transfers between devices, update(): lax.ppermute(edges, ('tile', 'gene'), beside(tiles, halves, offset))  3.51 us
    ppermute x2, waiting for transfers between devices, update(): other = lax.ppermute(part, 'gene', [(0, 1), (1, 0)])  2.1 us
  transfers between devices with their start and end apart: 7, of which 5 were waited for; matrix products, arithmetic and copies ran while one was open for 0% of the time, Pallas kernels for 0%

profile of v1, /device:TPU:0, one launch (start us, length us, event | category | flops | bytes accessed | tf_op | source)
XLA Modules:
  0.0 65.3 jit_solution(6923491272261239520)
XLA Ops:
  0.6 0.0 copy-start.3
  0.7 0.1 pad_add_fusion.place_ref
  0.8 0.0 copy-start
  0.8 2.2 %copy-done = s32[256,4096]{1,0:T(8,128)S(1)} copy-done((s32[256,4096]{1,0:T(8,128)S(1)}, s32[256,4096]{1,0:T(8,128)}, u32[]{:S(2)}) %copy-start) | copy-done | bytes 4194328
  3.0 0.0 copy-start.1
  3.0 0.9 %copy-done.1 = bf16[32,4096]{1,0:T(8,128)(2,1)S(1)} copy-done((bf16[32,4096]{1,0:T(8,128)(2,1)S(1)}, bf16[32,4096]{1,0:T(8,128)(2,1)}, u32[]{:S(2)}) %copy-start.1) | copy-done | bytes 262168
  3.9 0.0 copy-start.2
  3.9 0.8 %copy-done.2 = f32[32,256]{1,0:T(8,128)S(1)} copy-done((f32[32,256]{1,0:T(8,128)S(1)}, f32[32,256]{1,0:T(8,128)}, u32[]{:S(2)}) %copy-start.2) | copy-done | bytes 32792
  4.7 0.0 copy-start.4
  4.7 0.7 %copy-done.4 = s32[8,256]{1,0:T(8,128)S(1)} copy-done((s32[8,256]{1,0:T(8,128)S(1)}, s32[8,256]{1,0:T(8,128)}, u32[]{:S(2)}) %copy-start.4) | copy-done | bytes 8216
  5.4 4.0 %shard_map.68 = (f32[32,384]{1,0:T(8,128)S(1)}, bf16[256,4096]{1,0:T(8,128)(2,1)S(1)}, bf16[384,256]{1,0:T(8,128)(2,1)S(1)}) custom-call(s32[3]{0:T(128)S(1)} %pad_add_fusion.place_ref, s32[256,4096]{1,0:T(8,128)S(1)} %copy-done, f32[32,256]{1,0:T(8,128)S(1)} %copy-done.2, bf16[32,4096]{1,0:T(8,128)(2,1)S(1)} %copy-done.1, s32[8,256]{1,0:T(8,128)S(1)} %copy-done.4), custom_call_target="tpu_custom_call" | custom-call | tf_op jit(solution)/shard_map/pallas_call | solution.py:172
  9.4 0.5 collective-permute-start
  9.9 0.9 %collective-permute-done.other_ref = f32[32,384]{1,0:T(8,128)S(1)} collective-permute-done((f32[32,384]{1,0:T(8,128)S(1)}, f32[32,384]{1,0:T(8,128)S(1)}, u32[]{:S(2)}, u32[]{:S(2)}) %collective-permute-start) | collective-permute-done | bytes 49184 | tf_op jit(solution)/shard_map/ppermute | solution.py:230
  10.8 0.0 copy-done.3
  10.8 0.1 shard_map.69
  10.9 0.4 collective-permute-start.2
  11.3 4.0 %collective-permute-start.1 = (f32[40,128]{1,0:T(8,128)S(1)}, f32[40,128]{1,0:T(8,128)S(1)}, u32[]{:S(2)}, u32[]{:S(2)}) collective-permute-start(f32[40,128]{1,0:T(8,128)S(1)} %get-tuple-element.16), channel_id=1, source_target_pairs={{0,2},{2,0},{1,3},{3,1},{4,6},{6,4},{5,7},{7,5},{8,10},{10,8},{9,1... | collective-permute-start | bytes 61448 | tf_op jit(solution)/shard_map/ppermute | solution.py:237
  15.3 0.0 collective-permute-done.2.second_ref
  15.3 1.8 %collective-permute-done.1.first_ref = f32[40,128]{1,0:T(8,128)S(1)} collective-permute-done((f32[40,128]{1,0:T(8,128)S(1)}, f32[40,128]{1,0:T(8,128)S(1)}, u32[]{:S(2)}, u32[]{:S(2)}) %collective-permute-start.1) | collective-permute-done | bytes 20512 | tf_op jit(solution)/shard_map/ppermute | solution.py:237
  17.1 2.3 %shard_map.70 = (f32[32,256]{1,0:T(8,128)S(1)}, f32[32,256]{1,0:T(8,128)S(1)}) custom-call(f32[32,256]{1,0:T(8,128)S(1)} %get-tuple-element.15.updated_ref, s32[1,256]{1,0:T(1,128)S(1)} %bitcast.16, f32[40,128]{1,0:T(8,128)S(1)} %collective-permute-done.1.first_ref, f32[40,128]{1,0:T(8,128)S(1)} %collective-permute-done.2.second_ref, ...), custom_call_target="tpu_custom_call" | custom-call | tf_op jit(solution)/shard_map/pallas_call | solution.py:172
  19.4 0.1 collective-permute-start.3
  19.5 1.2 %collective-permute-done.3.other_ref = f32[32,384]{1,0:T(8,128)S(1)} collective-permute-done((f32[32,384]{1,0:T(8,128)S(1)}, f32[32,384]{1,0:T(8,128)S(1)}, u32[]{:S(2)}, u32[]{:S(2)}) %collective-permute-start.3) | collective-permute-done | bytes 49184 | tf_op jit(solution)/shard_map/ppermute | solution.py:230
  20.7 0.1 shard_map.71
  20.8 0.2 collective-permute-start.5
  21.0 3.2 %collective-permute-start.4 = (f32[40,128]{1,0:T(8,128)S(1)}, f32[40,128]{1,0:T(8,128)S(1)}, u32[]{:S(2)}, u32[]{:S(2)}) collective-permute-start(f32[40,128]{1,0:T(8,128)S(1)} %get-tuple-element.22), channel_id=1, source_target_pairs={{0,2},{2,0},{1,3},{3,1},{4,6},{6,4},{5,7},{7,5},{8,10},{10,8},{9,1... | collective-permute-start | bytes 61448 | tf_op jit(solution)/shard_map/ppermute | solution.py:237
  24.3 0.0 collective-permute-done.5.second_ref
  24.3 1.8 %collective-permute-done.4.first_ref = f32[40,128]{1,0:T(8,128)S(1)} collective-permute-done((f32[40,128]{1,0:T(8,128)S(1)}, f32[40,128]{1,0:T(8,128)S(1)}, u32[]{:S(2)}, u32[]{:S(2)}) %collective-permute-start.4) | collective-permute-done | bytes 20512 | tf_op jit(solution)/shard_map/ppermute | solution.py:237
  26.0 2.3 %shard_map.72 = (f32[32,256]{1,0:T(8,128)}, f32[32,4096]{1,0:T(8,128)S(1)}, f32[32,128]{1,0:T(8,128)S(1)}) custom-call(f32[32,256]{1,0:T(8,128)S(1)} %get-tuple-element.21.updated_ref, s32[1,256]{1,0:T(1,128)S(1)} %bitcast.18, f32[40,128]{1,0:T(8,128)S(1)} %collective-permute-done.4.first_ref, f32[40,128]{1,0:T(8,128)S(1)} %collective-permute-done.5.second_ref, ...), custom_call_target="tpu_custom_call" | custom-call | tf_op jit(solution)/shard_map/pallas_call | solution.py:172
  28.4 0.1 slice_reduce_fusion.1
  28.5 0.1 broadcast_in_dim.19
  28.6 0.9 %pad_maximum_fusion = f32[8,32,513]{2,1,0:T(8,128)} fusion(f32[8,32,1]{2,1,0:T(8,128)S(1)} %broadcast_in_dim.19, f32[8,32,512]{2,1,0:T(8,128)S(1)} %bitcast.19), kind=kLoop, calls=%fused_computation | loop fusion | flops 131328 | bytes 1050624 | tf_op jit(solution)/shard_map/concatenate | solution.py:250
  29.5 5.4 %all-to-all-start = ((f32[8,32,513]{2,1,0:T(8,128)}), f32[8,32,513]{2,1,0:T(8,128)S(1)}, u32[]{:S(2)}, u32[]{:S(2)}) async-start(f32[8,32,513]{2,1,0:T(8,128)} %pad_maximum_fusion), calls=%async_computation | async-start | bytes 1310720 | tf_op jit(solution)/shard_map/all_to_all | solution.py:257
  34.9 16.5 %all-to-all-done = f32[8,32,513]{2,1,0:T(8,128)S(1)} async-done(((f32[8,32,513]{2,1,0:T(8,128)}), f32[8,32,513]{2,1,0:T(8,128)S(1)}, u32[]{:S(2)}, u32[]{:S(2)}) %all-to-all-start) | async-done | bytes 525344 | tf_op jit(solution)/shard_map/all_to_all | solution.py:257
  51.4 0.1 slice_reduce_fusion
  51.6 0.8 %fusion.1 = bf16[32,512]{1,0:T(8,128)(2,1)S(1)} fusion(f32[32,513]{1,0:T(8,128)S(1)} %reduce_sum.9, f32[32]{0:T(128)S(1)} %slice_reduce_fusion, bf16[32,4096]{1,0:T(8,128)(2,1)} %gene_ref.5, s32[]{:T(128)S(6)} %select_n.33), kind=kLoop, calls=%fused_computation.4 | loop fusion | flops 65536 | bytes 131204 | tf_op jit(solution)/shard_map/convert_element_type | solution.py:259
  52.4 12.1 %all_to_all.10 = bf16[8,32,512]{2,1,0:T(8,128)(2,1)S(1)} all-to-all(bf16[8,32,512]{2,1,0:T(8,128)(2,1)S(1)} %broadcast_in_dim.20), channel_id=1, replica_groups=mesh['grp'=2,'tile'=8,'gene'=2] {'tile'}, dimensions={0} | all-to-all | bytes 524288 | tf_op jit(solution)/shard_map/all_to_all | solution.py:260
  64.6 0.7 %copy.11 = bf16[8,4,8,512]{3,2,0,1:T(8,128)(2,1)} copy(bf16[8,4,8,512]{3,2,1,0:T(8,128)(2,1)S(1)} %bitcast.20) | data formatting | bytes 524288 | tf_op jit(solution)/shard_map/reshape | solution.py:261
  (5 shorter events, 0.1 us)
Async XLA Ops:
  0.6 10.1 %copy-start.3 = (s32[256]{0:T(256)S(1)}, s32[256]{0:T(256)}, u32[]{:S(2)}) copy-start(s32[256]{0:T(256)} %param.8) | copy-start | bytes 3076
  0.8 2.2 %copy-start = (s32[256,4096]{1,0:T(8,128)S(1)}, s32[256,4096]{1,0:T(8,128)}, u32[]{:S(2)}) copy-start(s32[256,4096]{1,0:T(8,128)} %counts_ref.1) | copy-start | bytes 12582916
  3.0 0.9 %copy-start.1 = (bf16[32,4096]{1,0:T(8,128)(2,1)S(1)}, bf16[32,4096]{1,0:T(8,128)(2,1)}, u32[]{:S(2)}) copy-start(bf16[32,4096]{1,0:T(8,128)(2,1)} %gene_ref.5) | copy-start | bytes 786436
  3.9 0.8 %copy-start.2 = (f32[32,256]{1,0:T(8,128)S(1)}, f32[32,256]{1,0:T(8,128)}, u32[]{:S(2)}) copy-start(f32[32,256]{1,0:T(8,128)} %cells_ref.3) | copy-start | bytes 98308
  4.7 0.7 %copy-start.4 = (s32[8,256]{1,0:T(8,128)S(1)}, s32[8,256]{1,0:T(8,128)}, u32[]{:S(2)}) copy-start(s32[8,256]{1,0:T(8,128)} %neigh_ref.1) | copy-start | bytes 24580
  9.4 1.4 %collective-permute-start = (f32[32,384]{1,0:T(8,128)S(1)}, f32[32,384]{1,0:T(8,128)S(1)}, u32[]{:S(2)}, u32[]{:S(2)}) collective-permute-start(f32[32,384]{1,0:T(8,128)S(1)} %get-tuple-element.14.part_ref), channel_id=1, source_target_pairs={{0,1},{1,0},{2,3},{3,2},{4,5},{5,4},{6,7},{7,6},{8,9},{9,8},{10,11... | collective-permute-start | bytes 147464 | tf_op jit(solution)/shard_map/ppermute | solution.py:230
  10.9 4.4 %collective-permute-start.2 = (f32[40,128]{1,0:T(8,128)S(1)}, f32[40,128]{1,0:T(8,128)S(1)}, u32[]{:S(2)}, u32[]{:S(2)}) collective-permute-start(f32[40,128]{1,0:T(8,128)S(1)} %get-tuple-element.16), channel_id=1, source_target_pairs={{2,4},{4,2},{3,5},{5,3},{6,8},{8,6},{7,9},{9,7},{10,12},{12,10},{1... | collective-permute-start | bytes 61448 | tf_op jit(solution)/shard_map/ppermute | solution.py:237
  11.3 5.8 %collective-permute-start.1 = (f32[40,128]{1,0:T(8,128)S(1)}, f32[40,128]{1,0:T(8,128)S(1)}, u32[]{:S(2)}, u32[]{:S(2)}) collective-permute-start(f32[40,128]{1,0:T(8,128)S(1)} %get-tuple-element.16), channel_id=1, source_target_pairs={{0,2},{2,0},{1,3},{3,1},{4,6},{6,4},{5,7},{7,5},{8,10},{10,8},{9,1... | collective-permute-start | bytes 61448 | tf_op jit(solution)/shard_map/ppermute | solution.py:237
  19.4 1.3 %collective-permute-start.3 = (f32[32,384]{1,0:T(8,128)S(1)}, f32[32,384]{1,0:T(8,128)S(1)}, u32[]{:S(2)}, u32[]{:S(2)}) collective-permute-start(f32[32,384]{1,0:T(8,128)S(1)} %pad_maximum_fusion.1.part_ref), channel_id=1, source_target_pairs={{0,1},{1,0},{2,3},{3,2},{4,5},{5,4},{6,7},{7,6},{8,9},{9,8},{10,11... | collective-permute-start | bytes 147464 | tf_op jit(solution)/shard_map/ppermute | solution.py:230
  20.8 3.4 %collective-permute-start.5 = (f32[40,128]{1,0:T(8,128)S(1)}, f32[40,128]{1,0:T(8,128)S(1)}, u32[]{:S(2)}, u32[]{:S(2)}) collective-permute-start(f32[40,128]{1,0:T(8,128)S(1)} %get-tuple-element.22), channel_id=1, source_target_pairs={{2,4},{4,2},{3,5},{5,3},{6,8},{8,6},{7,9},{9,7},{10,12},{12,10},{1... | collective-permute-start | bytes 61448 | tf_op jit(solution)/shard_map/ppermute | solution.py:237
  21.0 5.0 %collective-permute-start.4 = (f32[40,128]{1,0:T(8,128)S(1)}, f32[40,128]{1,0:T(8,128)S(1)}, u32[]{:S(2)}, u32[]{:S(2)}) collective-permute-start(f32[40,128]{1,0:T(8,128)S(1)} %get-tuple-element.22), channel_id=1, source_target_pairs={{0,2},{2,0},{1,3},{3,1},{4,6},{6,4},{5,7},{7,5},{8,10},{10,8},{9,1... | collective-permute-start | bytes 61448 | tf_op jit(solution)/shard_map/ppermute | solution.py:237
  29.5 21.9 %all-to-all-start = ((f32[8,32,513]{2,1,0:T(8,128)}), f32[8,32,513]{2,1,0:T(8,128)S(1)}, u32[]{:S(2)}, u32[]{:S(2)}) async-start(f32[8,32,513]{2,1,0:T(8,128)} %pad_maximum_fusion), calls=%async_computation | async-start | bytes 1310720 | tf_op jit(solution)/shard_map/all_to_all | solution.py:257

commit v2 on v1

--- a/solution.py
+++ b/solution.py
@@ -1,5 +1,3 @@
-import functools
-
 import jax
 import jax.numpy as jnp
 from jax import lax
@@ -10,6 +8,8 @@
 BORDER = 32
 LANES = 128
 FLAG_ROWS = 8
+STAT_ROWS = 16
+FULL = 32767.0
 smooth_weight = 0.5
 VMEM_BYTES = 24 * 1024 * 1024
 
@@ -50,22 +50,36 @@
     part_ref[:, : columns.shape[0]] = total
 
 
+def partner(tile, tiles, offset):
+    other = jnp.where((tile + offset) % 2 == 0, tile + 1, tile - 1)
+    return jnp.where((other >= 0) & (other < tiles), other, -1)
+
+
 def first_kernel(
-    tiles, place_ref, counts_ref, cells_ref, gene_ref, neigh_ref,
-    part_ref, kept_ref, pick_ref, landed, sems,
+    counts_ref, cells_in, gene_in, neigh_in,
+    part_ref, kept_ref, pick_ref, cells_ref, gene_ref, neigh_ref, landed, sems, small_sems,
 ):
     rank, genes = gene_ref.shape
     width = cells_ref.shape[1]
     size = chunk_of(genes)
+    small = [
+        pltpu.make_async_copy(source, target, small_sems.at[i])
+        for i, (source, target) in enumerate(
+            ((neigh_in, neigh_ref), (cells_in, cells_ref), (gene_in, gene_ref))
+        )
+    ]
     copies = [
         pltpu.make_async_copy(
             counts_ref.at[:, pl.ds(at, size)], landed.at[:, pl.ds(at, size)], sems.at[i]
         )
         for i, at in enumerate(range(0, genes, size))
     ]
-    for copy in copies:
+    for copy in small + copies:
         copy.start()
-    here = place_ref[0]
+    tiles = lax.axis_size("tile")
+    here = lax.axis_index("tile")
+    sides = [partner(here, tiles, offset) for offset in (0, 1)]
+    small[0].wait()
     neigh = neigh_ref[...] - here * width
     for at in range(0, width, LANES):
         where = at + lax.broadcasted_iota(jnp.int32, (LANES, width), 0)
@@ -75,13 +89,15 @@
         pick_ref[at : at + LANES] = found.astype(jnp.bfloat16)
     row = lax.broadcasted_iota(jnp.int32, (LANES, width), 0)
     slot = row % (2 * BORDER)
-    beside = jnp.where(row < 2 * BORDER, place_ref[1], place_ref[2])
+    beside = jnp.where(row < 2 * BORDER, sides[0], sides[1])
     where = (beside - here) * width + slot + jnp.where(slot < BORDER, 0, width - 2 * BORDER)
     found = jnp.zeros((LANES, width), jnp.float32)
     for j in range(neigh.shape[0]):
         found += (neigh[j : j + 1] == where).astype(jnp.float32)
     pick_ref[width:] = jnp.where(beside < 0, 0.0, found).astype(jnp.bfloat16)
 
+    small[1].wait()
+    small[2].wait()
     gsum = jnp.sum(gene_ref[...].astype(jnp.float32), axis=1, keepdims=True)
     part_ref[:, width:] = jnp.broadcast_to(gsum, (rank, LANES))
 
@@ -143,6 +159,18 @@
     numerator(factor_columns(cells), gene_ref, counts_at, part_ref)
 
 
+def gene_totals(columns, rows, kept_ref, gene_ref, start, size):
+    rank = gene_ref.shape[0]
+    hf = gene_ref[:, start : start + size]
+    product = jnp.dot(
+        columns, jnp.concatenate([hf, hf], axis=0), preferred_element_type=jnp.float32
+    )
+    counts = kept_ref[:, start : start + size].astype(jnp.float32)
+    ratio = (counts * pl.reciprocal(product, approx=True)).astype(jnp.bfloat16)
+    both = jnp.dot(rows, ratio, preferred_element_type=jnp.float32)
+    return both[:rank] + both[rank:]
+
+
 def last_kernel(
     updated_ref, tissue_ref, first_ref, second_ref, pick_ref, kept_ref, gene_ref,
     cells_ref, hnum_ref, hden_ref,
@@ -154,17 +182,101 @@
     masked = jnp.where(flags, cells, 0.0)
     hden_ref[...] = jnp.broadcast_to(jnp.sum(masked, axis=1, keepdims=True), hden_ref.shape)
     columns = factor_columns(cells)
-    high, low = split(masked)
-    rows = jnp.concatenate([high, low], axis=0)
+    rows = jnp.concatenate(split(masked), axis=0)
     for start in range(0, genes, size):
-        hf = gene_ref[:, start : start + size]
-        product = jnp.dot(
-            columns, jnp.concatenate([hf, hf], axis=0), preferred_element_type=jnp.float32
-        )
-        counts = kept_ref[:, start : start + size].astype(jnp.float32)
-        ratio = (counts * pl.reciprocal(product, approx=True)).astype(jnp.bfloat16)
-        both = jnp.dot(rows, ratio, preferred_element_type=jnp.float32)
-        hnum_ref[:, start : start + size] = both[:rank] + both[rank:]
+        hnum_ref[:, start : start + size] = gene_totals(
+            columns, rows, kept_ref, gene_ref, start, size
+        )
+
+
+def exponent(values):
+    return jnp.ceil(jnp.log2(jnp.maximum(values, 1e-30)))
+
+
+def whole_part(values):
+    return (values + 0.5).astype(jnp.int32)
+
+
+def coded_kernel(
+    updated_ref, tissue_ref, first_ref, second_ref, pick_ref, kept_ref, gene_ref,
+    cells_ref, sent_ref,
+):
+    rank, genes = gene_ref.shape
+    tiles = sent_ref.shape[0]
+    share = genes // tiles
+    runs = share // LANES
+    cells, flags = smoothed(updated_ref, tissue_ref, first_ref, second_ref, pick_ref)
+    cells_ref[...] = cells
+    masked = jnp.where(flags, cells, 0.0)
+    columns = factor_columns(cells)
+    rows = jnp.concatenate(split(masked), axis=0)
+    hden = jnp.sum(masked, axis=1, keepdims=True)
+    power = exponent(hden)
+    scaled = hden * jnp.exp2(-power) * FULL
+    high = jnp.floor(scaled)
+    low = jnp.floor((scaled - high) * FULL)
+    lane = lax.broadcasted_iota(jnp.int32, (rank, LANES), 1)
+    stats = jnp.zeros((rank, LANES), jnp.float32)
+    for at, value in enumerate((power, high, low)):
+        stats = jnp.where(lane == tiles + at, value, stats)
+    for tile in range(tiles):
+        totals = gene_totals(columns, rows, kept_ref, gene_ref, tile * share, share)
+        power = exponent(jnp.max(totals, axis=1, keepdims=True))
+        stats = jnp.where(lane == tile, power, stats)
+        coded = whole_part(totals * (jnp.exp2(-power) * FULL)).astype(jnp.int16)
+        for run in range(runs):
+            sent_ref[tile, run * rank : (run + 1) * rank] = coded[
+                :, run * LANES : (run + 1) * LANES
+            ]
+    turned = jnp.concatenate([stats, jnp.zeros((LANES - rank, LANES), jnp.float32)], axis=0).T
+    turned = turned[:STAT_ROWS].astype(jnp.int32).astype(jnp.int16)
+    for tile in range(tiles):
+        sent_ref[tile, runs * rank :] = turned
+
+
+def fresh_kernel(got_ref, gene_ref, fresh_ref):
+    tiles, _, share = fresh_ref.shape
+    rank = gene_ref.shape[0]
+    runs = share // LANES
+    here = lax.axis_index("tile")
+
+    def number(coded):
+        return coded.astype(jnp.int32).astype(jnp.float32)
+
+    stats = [number(got_ref[tile, runs * rank :]) for tile in range(tiles)]
+    lane = lax.broadcasted_iota(jnp.int32, (rank, LANES), 1)
+    scales = []
+    hden = jnp.zeros((rank, 1), jnp.float32)
+    group = LANES // STAT_ROWS
+    for first in range(0, tiles, group):
+        block = stats[first : first + group]
+        short = LANES - len(block) * STAT_ROWS
+        if short:
+            block = block + [jnp.zeros((short, LANES), jnp.float32)]
+        turned = jnp.concatenate(block, axis=0).T[:rank]
+        for tile in range(first, min(first + group, tiles)):
+            at = (tile - first) * STAT_ROWS
+            power = jnp.sum(jnp.where(lane == at + here, turned, 0.0), axis=1, keepdims=True)
+            scales.append(jnp.exp2(power) / FULL)
+            at += tiles
+            hden += (turned[:, at + 1 : at + 2] + turned[:, at + 2 : at + 3] / FULL) * (
+                jnp.exp2(turned[:, at : at + 1]) / FULL
+            )
+    for run in range(runs):
+        total = jnp.zeros((rank, LANES), jnp.float32)
+        for tile in range(tiles):
+            total += number(got_ref[tile, run * rank : (run + 1) * rank]) * scales[tile]
+        place = pl.multiple_of(here * share + run * LANES, LANES)
+        hf = gene_ref[:, pl.ds(place, LANES)].astype(jnp.float32)
+        fresh = (hf * total / hden).astype(jnp.bfloat16)
+        for tile in range(tiles):
+            fresh_ref[tile, :, run * LANES : (run + 1) * LANES] = fresh
+
+
+def spread_kernel(every_ref, out_ref):
+    tiles, _, share = every_ref.shape
+    for tile in range(tiles):
+        out_ref[:, tile * share : (tile + 1) * share] = every_ref[tile]
 
 
 def call(kernel, outs, scratch=(), specs=None, limit=VMEM_BYTES):
@@ -201,27 +313,25 @@
     tile = lax.axis_index("tile")
     flag_row = tissue[None]
     shape = jax.ShapeDtypeStruct
-
-    def partner(offset):
-        other = jnp.where((tile - offset) % 2 == 0, tile + 1, tile - 1)
-        return jnp.where((other >= 0) & (other < tiles), other, -1)
-
-    place = jnp.stack([tile, partner(0), partner(1)]).astype(jnp.int32)
     factor = shape((rank, width), jnp.float32)
-    part_shape = shape((rank, width + LANES), jnp.float32)
-    whole = pl.BlockSpec(memory_space=pltpu.VMEM)
     chunks = genes // chunk_of(genes)
     part, kept, pick = call(
-        functools.partial(first_kernel, tiles),
+        first_kernel,
         (
-            part_shape,
+            shape((rank, width + LANES), jnp.float32),
             shape((counts.shape[0], genes), jnp.bfloat16),
             shape((width + LANES, width), jnp.bfloat16),
         ),
-        scratch=[pltpu.VMEM(counts.shape, jnp.int32), pltpu.SemaphoreType.DMA((chunks,))],
-        specs=[pl.BlockSpec(memory_space=pltpu.SMEM), pl.BlockSpec(memory_space=pl.ANY)]
-        + [whole] * 3,
-    )(place, counts, cell_factor, gene_factor, neighbours)
+        scratch=[
+            pltpu.VMEM(cell_factor.shape, cell_factor.dtype),
+            pltpu.VMEM(gene_factor.shape, gene_factor.dtype),
+            pltpu.VMEM(neighbours.shape, neighbours.dtype),
+            pltpu.VMEM(counts.shape, counts.dtype),
+            pltpu.SemaphoreType.DMA((chunks,)),
+            pltpu.SemaphoreType.DMA((3,)),
+        ],
+        specs=[pl.BlockSpec(memory_space=pltpu.HBM)] * 4,
+    )(counts, cell_factor, gene_factor, neighbours)
     gsum_part = part[:, width:]
     cells = cell_factor
 
@@ -241,12 +351,22 @@
 
     cells, numer = call(next_kernel, (factor, factor))(*update(part, cells))
     part = jnp.concatenate([numer, gsum_part], axis=1)
+    share = genes // tiles
+    last = update(part, cells)
+    if share % LANES == 0 and tiles + 3 <= STAT_ROWS:
+        cells, sent = call(
+            coded_kernel,
+            (factor, shape((tiles, share // LANES * rank + STAT_ROWS, LANES), jnp.int16)),
+        )(*last)
+        got = lax.all_to_all(sent, "tile", 0, 0)
+        fresh = call(fresh_kernel, shape((tiles, rank, share), jnp.bfloat16))(got, gene_factor)
+        every = lax.all_to_all(fresh, "tile", 0, 0)
+        return cells, call(spread_kernel, shape((rank, genes), jnp.bfloat16))(every)
+
     cells, hnum, hden = call(
         last_kernel,
         (factor, shape((rank, genes), jnp.float32), shape((rank, LANES), jnp.float32)),
-    )(*update(part, cells))
-
-    share = genes // tiles
+    )(*last)
     sent = jnp.concatenate(
         [
             hnum.reshape(rank, tiles, share).transpose(1, 0, 2),

time: 65.8 us -> 55.3 us (0.84)
  waiting for transfers between devices: 22.1 us -> 5.61 us
  blocking collectives: 12.1 us -> 25.9 us
  starting transfers between devices: 13.8 us -> 8.39 us
  other arithmetic: 1.87 us -> 0.01 us
  local copies, waits for them, and re-layouts: 5.69 us -> 4.59 us
  Pallas kernels: 8.91 us -> 9.69 us
    all_to_all x1 -> x0, waiting for transfers between devices: 16.5 us -> none  [on_device(): got = jnp.sum(lax.all_to_all(sent, 'tile', 0, 0), axis=0)]
    all_to_all x1 -> x2, blocking collectives: 12.1 us -> 25.9 us  [the longest x1 14.7 us: on_device(): got = lax.all_to_all(sent, 'tile', 0, 0)]
    all_to_all x1 -> x0, starting transfers between devices: 5.41 us -> none  [on_device(): got = jnp.sum(lax.all_to_all(sent, 'tile', 0, 0), axis=0)]
    concatenate x1 -> x0, other arithmetic: 0.9 us -> none  [on_device(): jnp.concatenate([hnum.reshape(rank, tiles, share).transpose(1, 0, 2), jnp...]
    convert_element_type x1 -> x0, other arithmetic: 0.84 us -> none  [on_device(): fresh = (mine * got[:, :share] / got[:, share:]).astype(jnp.bfloat16)]
    pallas_call x5 -> x7, Pallas kernels: 8.91 us -> 9.69 us  [call(): pl.pallas_call(kernel, out_shape=outs, in_specs=specs or [whole] * len(ar...]
    reshape x2 -> x0, local copies, waits for them, and re-layouts: 0.77 us -> none  [the longest x1 0.72 us: on_device(): return (cells, every.transpose(1, 0, 2).reshape(rank, genes))]
  transfers between devices with their start and end apart: 7 -> 6, of which waited for: 5 -> 4; matrix products, arithmetic and copies ran while one was open for 0% -> 0% of each run, Pallas kernels for 0% -> 0%
where the time goes in v2:
time: 55.3 us; the launch traced here: 54.9 us
  blocking collectives  25.9 us (47%)
  Pallas kernels  9.69 us (18%)
  starting transfers between devices  8.39 us (15%)
  waiting for transfers between devices  5.61 us (10%)
  local copies, waits for them, and re-layouts  4.59 us (8%)
  between operations  0.68 us (1%)
    all_to_all x1, blocking collectives, on_device(): got = lax.all_to_all(sent, 'tile', 0, 0)  14.7 us
    all_to_all x1, blocking collectives, on_device(): every = lax.all_to_all(fresh, 'tile', 0, 0)  11.2 us
    pallas_call x7, Pallas kernels, call(): pl.pallas_call(kernel, out_shape=outs, in_specs=specs or [whole] * len(ar...  9.69 us
    ppermute x4, starting transfers between devices, update(): lax.ppermute(edges, ('tile', 'gene'), beside(tiles, halves, offset))  7.8 us
    unnamed x10, local copies, waits for them, and re-layouts  4.59 us
    ppermute x4, waiting for transfers between devices, update(): lax.ppermute(edges, ('tile', 'gene'), beside(tiles, halves, offset))  3.51 us
    ppermute x2, waiting for transfers between devices, update(): other = lax.ppermute(part, 'gene', [(0, 1), (1, 0)])  2.1 us
  transfers between devices with their start and end apart: 6, of which 4 were waited for; matrix products, arithmetic and copies ran while one was open for 0% of the time, Pallas kernels for 0%

profile of v2, /device:TPU:0, one launch (start us, length us, event | category | flops | bytes accessed | tf_op | source)
XLA Modules:
  0.0 54.9 jit_solution(10485261724116608384)
XLA Ops:
  0.6 0.0 copy-start
  0.6 0.9 %copy-done = bf16[32,4096]{1,0:T(8,128)(2,1)S(1)} copy-done((bf16[32,4096]{1,0:T(8,128)(2,1)S(1)}, bf16[32,4096]{1,0:T(8,128)(2,1)}, u32[]{:S(2)}) %copy-start) | copy-done | bytes 262168
  1.6 0.0 copy-start.1
  1.6 2.2 %copy-done.1 = s32[256,4096]{1,0:T(8,128)S(1)} copy-done((s32[256,4096]{1,0:T(8,128)S(1)}, s32[256,4096]{1,0:T(8,128)}, u32[]{:S(2)}) %copy-start.1) | copy-done | bytes 4194328
  3.8 0.0 copy-start.2
  3.8 0.8 %copy-done.2 = f32[32,256]{1,0:T(8,128)S(1)} copy-done((f32[32,256]{1,0:T(8,128)S(1)}, f32[32,256]{1,0:T(8,128)}, u32[]{:S(2)}) %copy-start.2) | copy-done | bytes 32792
  4.5 0.0 copy-start.4
  4.5 0.7 %copy-done.4 = s32[8,256]{1,0:T(8,128)S(1)} copy-done((s32[8,256]{1,0:T(8,128)S(1)}, s32[8,256]{1,0:T(8,128)}, u32[]{:S(2)}) %copy-start.4) | copy-done | bytes 8216
  5.2 0.0 copy-start.3
  5.2 3.4 %shard_map.68 = (f32[32,384]{1,0:T(8,128)S(1)}, bf16[256,4096]{1,0:T(8,128)(2,1)S(1)}, bf16[384,256]{1,0:T(8,128)(2,1)S(1)}) custom-call(s32[256,4096]{1,0:T(8,128)S(1)} %copy-done.1, f32[32,256]{1,0:T(8,128)S(1)} %copy-done.2, bf16[32,4096]{1,0:T(8,128)(2,1)S(1)} %copy-done, s32[8,256]{1,0:T(8,128)S(1)} %copy-done.4), custom_call_target="tpu_custom_call" | custom-call | tf_op jit(solution)/shard_map/pallas_call | solution.py:284
  8.7 0.5 collective-permute-start
  9.2 0.9 %collective-permute-done.other_ref = f32[32,384]{1,0:T(8,128)S(1)} collective-permute-done((f32[32,384]{1,0:T(8,128)S(1)}, f32[32,384]{1,0:T(8,128)S(1)}, u32[]{:S(2)}, u32[]{:S(2)}) %collective-permute-start) | collective-permute-done | bytes 49184 | tf_op jit(solution)/shard_map/ppermute | solution.py:340
  10.1 0.0 copy-done.3
  10.1 0.1 shard_map.69
  10.2 0.4 collective-permute-start.2
  10.6 4.0 %collective-permute-start.1 = (f32[40,128]{1,0:T(8,128)S(1)}, f32[40,128]{1,0:T(8,128)S(1)}, u32[]{:S(2)}, u32[]{:S(2)}) collective-permute-start(f32[40,128]{1,0:T(8,128)S(1)} %get-tuple-element.15), channel_id=1, source_target_pairs={{0,2},{2,0},{1,3},{3,1},{4,6},{6,4},{5,7},{7,5},{8,10},{10,8},{9,1... | collective-permute-start | bytes 61448 | tf_op jit(solution)/shard_map/ppermute | solution.py:347
  14.6 0.0 collective-permute-done.2.second_ref
  14.6 1.8 %collective-permute-done.1.first_ref = f32[40,128]{1,0:T(8,128)S(1)} collective-permute-done((f32[40,128]{1,0:T(8,128)S(1)}, f32[40,128]{1,0:T(8,128)S(1)}, u32[]{:S(2)}, u32[]{:S(2)}) %collective-permute-start.1) | collective-permute-done | bytes 20512 | tf_op jit(solution)/shard_map/ppermute | solution.py:347
  16.4 2.3 %shard_map.70 = (f32[32,256]{1,0:T(8,128)S(1)}, f32[32,256]{1,0:T(8,128)S(1)}) custom-call(f32[32,256]{1,0:T(8,128)S(1)} %get-tuple-element.14.updated_ref, s32[1,256]{1,0:T(1,128)S(1)} %bitcast.2, f32[40,128]{1,0:T(8,128)S(1)} %collective-permute-done.1.first_ref, f32[40,128]{1,0:T(8,128)S(1)} %collective-permute-done.2.second_ref, ...), custom_call_target="tpu_custom_call" | custom-call | tf_op jit(solution)/shard_map/pallas_call | solution.py:284
  18.7 0.1 collective-permute-start.3
  18.8 1.2 %collective-permute-done.3.other_ref = f32[32,384]{1,0:T(8,128)S(1)} collective-permute-done((f32[32,384]{1,0:T(8,128)S(1)}, f32[32,384]{1,0:T(8,128)S(1)}, u32[]{:S(2)}, u32[]{:S(2)}) %collective-permute-start.3) | collective-permute-done | bytes 49184 | tf_op jit(solution)/shard_map/ppermute | solution.py:340
  20.0 0.1 shard_map.71
  20.1 0.2 collective-permute-start.5
  20.3 3.2 %collective-permute-start.4 = (f32[40,128]{1,0:T(8,128)S(1)}, f32[40,128]{1,0:T(8,128)S(1)}, u32[]{:S(2)}, u32[]{:S(2)}) collective-permute-start(f32[40,128]{1,0:T(8,128)S(1)} %get-tuple-element.21), channel_id=1, source_target_pairs={{0,2},{2,0},{1,3},{3,1},{4,6},{6,4},{5,7},{7,5},{8,10},{10,8},{9,1... | collective-permute-start | bytes 61448 | tf_op jit(solution)/shard_map/ppermute | solution.py:347
  23.5 0.0 collective-permute-done.5.second_ref
  23.5 1.8 %collective-permute-done.4.first_ref = f32[40,128]{1,0:T(8,128)S(1)} collective-permute-done((f32[40,128]{1,0:T(8,128)S(1)}, f32[40,128]{1,0:T(8,128)S(1)}, u32[]{:S(2)}, u32[]{:S(2)}) %collective-permute-start.4) | collective-permute-done | bytes 20512 | tf_op jit(solution)/shard_map/ppermute | solution.py:347
  25.3 2.5 %shard_map.72 = (f32[32,256]{1,0:T(8,128)}, s16[8,144,128]{2,1,0:T(8,128)(2,1)S(1)}) custom-call(f32[32,256]{1,0:T(8,128)S(1)} %get-tuple-element.20.updated_ref, s32[1,256]{1,0:T(1,128)S(1)} %bitcast.4, f32[40,128]{1,0:T(8,128)S(1)} %collective-permute-done.4.first_ref, f32[40,128]{1,0:T(8,128)S(1)} %collective-permute-done.5.second_ref, ...), custom_call_target="tpu_custom_call" | custom-call | tf_op jit(solution)/shard_map/pallas_call | solution.py:284
  27.8 14.7 %all_to_all.10.got_ref = s16[8,144,128]{2,1,0:T(8,128)(2,1)S(1)} all-to-all(s16[8,144,128]{2,1,0:T(8,128)(2,1)S(1)} %get-tuple-element.23), channel_id=1, replica_groups=mesh['grp'=2,'tile'=8,'gene'=2] {'tile'}, dimensions={0} | all-to-all | bytes 589824 | tf_op jit(solution)/shard_map/all_to_all | solution.py:361
  42.5 0.5 shard_map.73
  43.0 11.2 %all_to_all.11.every_ref = bf16[8,32,512]{2,1,0:T(8,128)(2,1)S(1)} all-to-all(bf16[8,32,512]{2,1,0:T(8,128)(2,1)S(1)} %shard_map.73), channel_id=1, replica_groups=mesh['grp'=2,'tile'=8,'gene'=2] {'tile'}, dimensions={0} | all-to-all | bytes 524288 | tf_op jit(solution)/shard_map/all_to_all | solution.py:363
  54.2 0.7 %shard_map.74 = bf16[32,4096]{1,0:T(8,128)(2,1)} custom-call(bf16[8,32,512]{2,1,0:T(8,128)(2,1)S(1)} %all_to_all.11.every_ref), custom_call_target="tpu_custom_call" | custom-call | tf_op jit(solution)/shard_map/pallas_call | solution.py:284
  (2 shorter events, 0.0 us)
Async XLA Ops:
  0.6 1.0 %copy-start = (bf16[32,4096]{1,0:T(8,128)(2,1)S(1)}, bf16[32,4096]{1,0:T(8,128)(2,1)}, u32[]{:S(2)}) copy-start(bf16[32,4096]{1,0:T(8,128)(2,1)} %gene_ref.5) | copy-start | bytes 786436
  1.6 2.2 %copy-start.1 = (s32[256,4096]{1,0:T(8,128)S(1)}, s32[256,4096]{1,0:T(8,128)}, u32[]{:S(2)}) copy-start(s32[256,4096]{1,0:T(8,128)} %counts_ref.1) | copy-start | bytes 12582916
  3.8 0.8 %copy-start.2 = (f32[32,256]{1,0:T(8,128)S(1)}, f32[32,256]{1,0:T(8,128)}, u32[]{:S(2)}) copy-start(f32[32,256]{1,0:T(8,128)} %cells_ref.1) | copy-start | bytes 98308
  4.5 0.7 %copy-start.4 = (s32[8,256]{1,0:T(8,128)S(1)}, s32[8,256]{1,0:T(8,128)}, u32[]{:S(2)}) copy-start(s32[8,256]{1,0:T(8,128)} %neigh_in.1) | copy-start | bytes 24580
  5.2 4.8 %copy-start.3 = (s32[256]{0:T(256)S(1)}, s32[256]{0:T(256)}, u32[]{:S(2)}) copy-start(s32[256]{0:T(256)} %param.8) | copy-start | bytes 3076
  8.7 1.4 %collective-permute-start = (f32[32,384]{1,0:T(8,128)S(1)}, f32[32,384]{1,0:T(8,128)S(1)}, u32[]{:S(2)}, u32[]{:S(2)}) collective-permute-start(f32[32,384]{1,0:T(8,128)S(1)} %get-tuple-element.13.part_ref), channel_id=1, source_target_pairs={{0,1},{1,0},{2,3},{3,2},{4,5},{5,4},{6,7},{7,6},{8,9},{9,8},{10,11... | collective-permute-start | bytes 147464 | tf_op jit(solution)/shard_map/ppermute | solution.py:340
  10.2 4.4 %collective-permute-start.2 = (f32[40,128]{1,0:T(8,128)S(1)}, f32[40,128]{1,0:T(8,128)S(1)}, u32[]{:S(2)}, u32[]{:S(2)}) collective-permute-start(f32[40,128]{1,0:T(8,128)S(1)} %get-tuple-element.15), channel_id=1, source_target_pairs={{2,4},{4,2},{3,5},{5,3},{6,8},{8,6},{7,9},{9,7},{10,12},{12,10},{1... | collective-permute-start | bytes 61448 | tf_op jit(solution)/shard_map/ppermute | solution.py:347
  10.6 5.8 %collective-permute-start.1 = (f32[40,128]{1,0:T(8,128)S(1)}, f32[40,128]{1,0:T(8,128)S(1)}, u32[]{:S(2)}, u32[]{:S(2)}) collective-permute-start(f32[40,128]{1,0:T(8,128)S(1)} %get-tuple-element.15), channel_id=1, source_target_pairs={{0,2},{2,0},{1,3},{3,1},{4,6},{6,4},{5,7},{7,5},{8,10},{10,8},{9,1... | collective-permute-start | bytes 61448 | tf_op jit(solution)/shard_map/ppermute | solution.py:347
  18.7 1.3 %collective-permute-start.3 = (f32[32,384]{1,0:T(8,128)S(1)}, f32[32,384]{1,0:T(8,128)S(1)}, u32[]{:S(2)}, u32[]{:S(2)}) collective-permute-start(f32[32,384]{1,0:T(8,128)S(1)} %pad_maximum_fusion.part_ref), channel_id=1, source_target_pairs={{0,1},{1,0},{2,3},{3,2},{4,5},{5,4},{6,7},{7,6},{8,9},{9,8},{10,11... | collective-permute-start | bytes 147464 | tf_op jit(solution)/shard_map/ppermute | solution.py:340
  20.1 3.4 %collective-permute-start.5 = (f32[40,128]{1,0:T(8,128)S(1)}, f32[40,128]{1,0:T(8,128)S(1)}, u32[]{:S(2)}, u32[]{:S(2)}) collective-permute-start(f32[40,128]{1,0:T(8,128)S(1)} %get-tuple-element.21), channel_id=1, source_target_pairs={{2,4},{4,2},{3,5},{5,3},{6,8},{8,6},{7,9},{9,7},{10,12},{12,10},{1... | collective-permute-start | bytes 61448 | tf_op jit(solution)/shard_map/ppermute | solution.py:347
  20.3 5.0 %collective-permute-start.4 = (f32[40,128]{1,0:T(8,128)S(1)}, f32[40,128]{1,0:T(8,128)S(1)}, u32[]{:S(2)}, u32[]{:S(2)}) collective-permute-start(f32[40,128]{1,0:T(8,128)S(1)} %get-tuple-element.21), channel_id=1, source_target_pairs={{0,2},{2,0},{1,3},{3,1},{4,6},{6,4},{5,7},{7,5},{8,10},{10,8},{9,1... | collective-permute-start | bytes 61448 | tf_op jit(solution)/shard_map/ppermute | solution.py:347

commit v3 on v2

--- a/solution.py
+++ b/solution.py
@@ -12,6 +12,7 @@
 FULL = 32767.0
 smooth_weight = 0.5
 VMEM_BYTES = 24 * 1024 * 1024
+FIRST_VMEM_BYTES = 49 * 1024 * 1024
 
 
 def split(values):
@@ -55,49 +56,41 @@
     return jnp.where((other >= 0) & (other < tiles), other, -1)
 
 
-def first_kernel(
-    counts_ref, cells_in, gene_in, neigh_in,
-    part_ref, kept_ref, pick_ref, cells_ref, gene_ref, neigh_ref, landed, sems, small_sems,
-):
+def pick_kernel(neigh_ref, pick_ref):
+    width = neigh_ref.shape[1]
+    tiles = lax.axis_size("tile")
+    here = lax.axis_index("tile")
+    neigh = neigh_ref[...] - here * width
+
+    def found(where):
+        total = jnp.zeros((LANES, width), jnp.float32)
+        for j in range(neigh.shape[0]):
+            total += (neigh[j : j + 1] == where).astype(jnp.float32)
+        return total
+
+    row = lax.broadcasted_iota(jnp.int32, (LANES, width), 0)
+    for at in range(0, width, LANES):
+        pick_ref[at : at + LANES] = found(at + row).astype(jnp.bfloat16)
+    slot = row % (2 * BORDER)
+    beside = jnp.where(
+        row < 2 * BORDER, partner(here, tiles, 0), partner(here, tiles, 1)
+    )
+    where = (beside - here) * width + slot + jnp.where(slot < BORDER, 0, width - 2 * BORDER)
+    pick_ref[width:] = jnp.where(beside < 0, 0.0, found(where)).astype(jnp.bfloat16)
+
+
+def first_kernel(counts_ref, cells_ref, gene_ref, part_ref, kept_ref, landed, sems):
     rank, genes = gene_ref.shape
     width = cells_ref.shape[1]
     size = chunk_of(genes)
-    small = [
-        pltpu.make_async_copy(source, target, small_sems.at[i])
-        for i, (source, target) in enumerate(
-            ((neigh_in, neigh_ref), (cells_in, cells_ref), (gene_in, gene_ref))
-        )
-    ]
     copies = [
         pltpu.make_async_copy(
             counts_ref.at[:, pl.ds(at, size)], landed.at[:, pl.ds(at, size)], sems.at[i]
         )
         for i, at in enumerate(range(0, genes, size))
     ]
-    for copy in small + copies:
+    for copy in copies:
         copy.start()
-    tiles = lax.axis_size("tile")
-    here = lax.axis_index("tile")
-    sides = [partner(here, tiles, offset) for offset in (0, 1)]
-    small[0].wait()
-    neigh = neigh_ref[...] - here * width
-    for at in range(0, width, LANES):
-        where = at + lax.broadcasted_iota(jnp.int32, (LANES, width), 0)
-        found = jnp.zeros((LANES, width), jnp.float32)
-        for j in range(neigh.shape[0]):
-            found += (neigh[j : j + 1] == where).astype(jnp.float32)
-        pick_ref[at : at + LANES] = found.astype(jnp.bfloat16)
-    row = lax.broadcasted_iota(jnp.int32, (LANES, width), 0)
-    slot = row % (2 * BORDER)
-    beside = jnp.where(row < 2 * BORDER, sides[0], sides[1])
-    where = (beside - here) * width + slot + jnp.where(slot < BORDER, 0, width - 2 * BORDER)
-    found = jnp.zeros((LANES, width), jnp.float32)
-    for j in range(neigh.shape[0]):
-        found += (neigh[j : j + 1] == where).astype(jnp.float32)
-    pick_ref[width:] = jnp.where(beside < 0, 0.0, found).astype(jnp.bfloat16)
-
-    small[1].wait()
-    small[2].wait()
     gsum = jnp.sum(gene_ref[...].astype(jnp.float32), axis=1, keepdims=True)
     part_ref[:, width:] = jnp.broadcast_to(gsum, (rank, LANES))
 
@@ -315,23 +308,21 @@
     shape = jax.ShapeDtypeStruct
     factor = shape((rank, width), jnp.float32)
     chunks = genes // chunk_of(genes)
-    part, kept, pick = call(
+    pick = call(pick_kernel, shape((width + LANES, width), jnp.bfloat16))(neighbours)
+    part, kept = call(
         first_kernel,
         (
             shape((rank, width + LANES), jnp.float32),
             shape((counts.shape[0], genes), jnp.bfloat16),
-            shape((width + LANES, width), jnp.bfloat16),
         ),
         scratch=[
-            pltpu.VMEM(cell_factor.shape, cell_factor.dtype),
-            pltpu.VMEM(gene_factor.shape, gene_factor.dtype),
-            pltpu.VMEM(neighbours.shape, neighbours.dtype),
             pltpu.VMEM(counts.shape, counts.dtype),
             pltpu.SemaphoreType.DMA((chunks,)),
-            pltpu.SemaphoreType.DMA((3,)),
         ],
-        specs=[pl.BlockSpec(memory_space=pltpu.HBM)] * 4,
-    )(counts, cell_factor, gene_factor, neighbours)
+        specs=[pl.BlockSpec(memory_space=pl.ANY)]
+        + [pl.BlockSpec(memory_space=pltpu.VMEM)] * 2,
+        limit=FIRST_VMEM_BYTES,
+    )(counts, cell_factor, gene_factor)
     gsum_part = part[:, width:]
     cells = cell_factor
 

time: 55.3 us -> 52.2 us (0.944)
  local copies, waits for them, and re-layouts: 4.59 us -> 1.71 us
    unnamed x10 -> x8, local copies, waits for them, and re-layouts: 4.59 us -> 1.71 us
    pallas_call x7 -> x8, Pallas kernels: 9.69 us -> 9.92 us  [call(): pl.pallas_call(kernel, out_shape=outs, in_specs=specs or [whole] * len(ar...]
  transfers between devices with their start and end apart: 6 -> 6, of which waited for: 4 -> 4; matrix products, arithmetic and copies ran while one was open for 0% -> 0% of each run, Pallas kernels for 0% -> 1%
where the time goes in v3:
time: 52.2 us; the launch traced here: 51.9 us
  blocking collectives  25.9 us (50%)
  Pallas kernels  9.92 us (19%)
  starting transfers between devices  8.38 us (16%)
  waiting for transfers between devices  5.27 us (10%)
  local copies, waits for them, and re-layouts  1.71 us (3%)
  between operations  0.7 us (1%)
    all_to_all x1, blocking collectives, on_device(): got = lax.all_to_all(sent, 'tile', 0, 0)  14.7 us
    all_to_all x1, blocking collectives, on_device(): every = lax.all_to_all(fresh, 'tile', 0, 0)  11.2 us
    pallas_call x8, Pallas kernels, call(): pl.pallas_call(kernel, out_shape=outs, in_specs=specs or [whole] * len(ar...  9.92 us
    ppermute x4, starting transfers between devices, update(): lax.ppermute(edges, ('tile', 'gene'), beside(tiles, halves, offset))  7.8 us
    ppermute x4, waiting for transfers between devices, update(): lax.ppermute(edges, ('tile', 'gene'), beside(tiles, halves, offset))  3.17 us
    ppermute x2, waiting for transfers between devices, update(): other = lax.ppermute(part, 'gene', [(0, 1), (1, 0)])  2.1 us
    unnamed x8, local copies, waits for them, and re-layouts  1.71 us
  transfers between devices with their start and end apart: 6, of which 4 were waited for; matrix products, arithmetic and copies ran while one was open for 0% of the time, Pallas kernels for 1%

profile of v3, /device:TPU:0, one launch (start us, length us, event | category | flops | bytes accessed | tf_op | source)
XLA Modules:
  0.0 51.9 jit_solution(8725801074543041646)
XLA Ops:
  0.6 0.0 copy-start
  0.6 0.9 %copy-done = bf16[32,4096]{1,0:T(8,128)(2,1)S(1)} copy-done((bf16[32,4096]{1,0:T(8,128)(2,1)S(1)}, bf16[32,4096]{1,0:T(8,128)(2,1)}, u32[]{:S(2)}) %copy-start) | copy-done | bytes 262168
  1.6 0.0 copy-start.1
  1.6 0.8 %copy-done.1 = f32[32,256]{1,0:T(8,128)S(1)} copy-done((f32[32,256]{1,0:T(8,128)S(1)}, f32[32,256]{1,0:T(8,128)}, u32[]{:S(2)}) %copy-start.1) | copy-done | bytes 32792
  2.3 0.0 copy-start.2
  2.3 0.0 copy-start.3
  2.3 3.3 %shard_map.68 = (f32[32,384]{1,0:T(8,128)S(1)}, bf16[256,4096]{1,0:T(8,128)(2,1)S(1)}) custom-call(s32[256,4096]{1,0:T(8,128)} %counts_ref.1, f32[32,256]{1,0:T(8,128)S(1)} %copy-done.1, bf16[32,4096]{1,0:T(8,128)(2,1)S(1)} %copy-done), custom_call_target="tpu_custom_call" | custom-call | tf_op jit(solution)/shard_map/pallas_call | solution.py:277
  5.7 0.5 collective-permute-start
  6.2 0.9 %collective-permute-done.other_ref = f32[32,384]{1,0:T(8,128)S(1)} collective-permute-done((f32[32,384]{1,0:T(8,128)S(1)}, f32[32,384]{1,0:T(8,128)S(1)}, u32[]{:S(2)}, u32[]{:S(2)}) %collective-permute-start) | collective-permute-done | bytes 49184 | tf_op jit(solution)/shard_map/ppermute | solution.py:331
  7.1 0.0 copy-done.2
  7.1 0.1 shard_map.69
  7.2 0.4 collective-permute-start.2
  7.6 4.0 %collective-permute-start.1 = (f32[40,128]{1,0:T(8,128)S(1)}, f32[40,128]{1,0:T(8,128)S(1)}, u32[]{:S(2)}, u32[]{:S(2)}) collective-permute-start(f32[40,128]{1,0:T(8,128)S(1)} %get-tuple-element.14), channel_id=1, source_target_pairs={{0,2},{2,0},{1,3},{3,1},{4,6},{6,4},{5,7},{7,5},{8,10},{10,8},{9,1... | collective-permute-start | bytes 61448 | tf_op jit(solution)/shard_map/ppermute | solution.py:338
  11.6 0.0 copy-done.3
  11.6 0.3 shard_map.70.pick_ref
  12.0 0.0 collective-permute-done.2.second_ref
  12.0 1.4 %collective-permute-done.1.first_ref = f32[40,128]{1,0:T(8,128)S(1)} collective-permute-done((f32[40,128]{1,0:T(8,128)S(1)}, f32[40,128]{1,0:T(8,128)S(1)}, u32[]{:S(2)}, u32[]{:S(2)}) %collective-permute-start.1) | collective-permute-done | bytes 20512 | tf_op jit(solution)/shard_map/ppermute | solution.py:338
  13.4 2.3 %shard_map.71 = (f32[32,256]{1,0:T(8,128)S(1)}, f32[32,256]{1,0:T(8,128)S(1)}) custom-call(f32[32,256]{1,0:T(8,128)S(1)} %get-tuple-element.13.updated_ref, s32[1,256]{1,0:T(1,128)S(1)} %bitcast.2, f32[40,128]{1,0:T(8,128)S(1)} %collective-permute-done.1.first_ref, f32[40,128]{1,0:T(8,128)S(1)} %collective-permute-done.2.second_ref, ...), custom_call_target="tpu_custom_call" | custom-call | tf_op jit(solution)/shard_map/pallas_call | solution.py:277
  15.7 0.1 collective-permute-start.3
  15.8 1.2 %collective-permute-done.3.other_ref = f32[32,384]{1,0:T(8,128)S(1)} collective-permute-done((f32[32,384]{1,0:T(8,128)S(1)}, f32[32,384]{1,0:T(8,128)S(1)}, u32[]{:S(2)}, u32[]{:S(2)}) %collective-permute-start.3) | collective-permute-done | bytes 49184 | tf_op jit(solution)/shard_map/ppermute | solution.py:331
  17.0 0.1 shard_map.72
  17.1 0.2 collective-permute-start.5
  17.3 3.2 %collective-permute-start.4 = (f32[40,128]{1,0:T(8,128)S(1)}, f32[40,128]{1,0:T(8,128)S(1)}, u32[]{:S(2)}, u32[]{:S(2)}) collective-permute-start(f32[40,128]{1,0:T(8,128)S(1)} %get-tuple-element.19), channel_id=1, source_target_pairs={{0,2},{2,0},{1,3},{3,1},{4,6},{6,4},{5,7},{7,5},{8,10},{10,8},{9,1... | collective-permute-start | bytes 61448 | tf_op jit(solution)/shard_map/ppermute | solution.py:338
  20.6 0.0 collective-permute-done.5.second_ref
  20.6 1.8 %collective-permute-done.4.first_ref = f32[40,128]{1,0:T(8,128)S(1)} collective-permute-done((f32[40,128]{1,0:T(8,128)S(1)}, f32[40,128]{1,0:T(8,128)S(1)}, u32[]{:S(2)}, u32[]{:S(2)}) %collective-permute-start.4) | collective-permute-done | bytes 20512 | tf_op jit(solution)/shard_map/ppermute | solution.py:338
  22.3 2.5 %shard_map.73 = (f32[32,256]{1,0:T(8,128)}, s16[8,144,128]{2,1,0:T(8,128)(2,1)S(1)}) custom-call(f32[32,256]{1,0:T(8,128)S(1)} %get-tuple-element.18.updated_ref, s32[1,256]{1,0:T(1,128)S(1)} %bitcast.4, f32[40,128]{1,0:T(8,128)S(1)} %collective-permute-done.4.first_ref, f32[40,128]{1,0:T(8,128)S(1)} %collective-permute-done.5.second_ref, ...), custom_call_target="tpu_custom_call" | custom-call | tf_op jit(solution)/shard_map/pallas_call | solution.py:277
  24.8 14.7 %all_to_all.10.got_ref = s16[8,144,128]{2,1,0:T(8,128)(2,1)S(1)} all-to-all(s16[8,144,128]{2,1,0:T(8,128)(2,1)S(1)} %get-tuple-element.21), channel_id=1, replica_groups=mesh['grp'=2,'tile'=8,'gene'=2] {'tile'}, dimensions={0} | all-to-all | bytes 589824 | tf_op jit(solution)/shard_map/all_to_all | solution.py:352
  39.5 0.5 shard_map.74
  40.0 11.2 %all_to_all.11.every_ref = bf16[8,32,512]{2,1,0:T(8,128)(2,1)S(1)} all-to-all(bf16[8,32,512]{2,1,0:T(8,128)(2,1)S(1)} %shard_map.74), channel_id=1, replica_groups=mesh['grp'=2,'tile'=8,'gene'=2] {'tile'}, dimensions={0} | all-to-all | bytes 524288 | tf_op jit(solution)/shard_map/all_to_all | solution.py:354
  51.2 0.7 %shard_map.75 = bf16[32,4096]{1,0:T(8,128)(2,1)} custom-call(bf16[8,32,512]{2,1,0:T(8,128)(2,1)S(1)} %all_to_all.11.every_ref), custom_call_target="tpu_custom_call" | custom-call | tf_op jit(solution)/shard_map/pallas_call | solution.py:277
  (2 shorter events, 0.0 us)
Async XLA Ops:
  0.6 1.0 %copy-start = (bf16[32,4096]{1,0:T(8,128)(2,1)S(1)}, bf16[32,4096]{1,0:T(8,128)(2,1)}, u32[]{:S(2)}) copy-start(bf16[32,4096]{1,0:T(8,128)(2,1)} %gene_ref.7) | copy-start | bytes 786436
  1.6 0.8 %copy-start.1 = (f32[32,256]{1,0:T(8,128)S(1)}, f32[32,256]{1,0:T(8,128)}, u32[]{:S(2)}) copy-start(f32[32,256]{1,0:T(8,128)} %cells_ref.3) | copy-start | bytes 98308
  2.3 4.7 %copy-start.2 = (s32[256]{0:T(256)S(1)}, s32[256]{0:T(256)}, u32[]{:S(2)}) copy-start(s32[256]{0:T(256)} %param.8) | copy-start | bytes 3076
  2.3 9.3 %copy-start.3 = (s32[8,256]{1,0:T(8,128)S(1)}, s32[8,256]{1,0:T(8,128)}, u32[]{:S(2)}) copy-start(s32[8,256]{1,0:T(8,128)} %neigh_ref.1) | copy-start | bytes 24580
  5.7 1.4 %collective-permute-start = (f32[32,384]{1,0:T(8,128)S(1)}, f32[32,384]{1,0:T(8,128)S(1)}, u32[]{:S(2)}, u32[]{:S(2)}) collective-permute-start(f32[32,384]{1,0:T(8,128)S(1)} %get-tuple-element.12.part_ref), channel_id=1, source_target_pairs={{0,1},{1,0},{2,3},{3,2},{4,5},{5,4},{6,7},{7,6},{8,9},{9,8},{10,11... | collective-permute-start | bytes 147464 | tf_op jit(solution)/shard_map/ppermute | solution.py:331
  7.2 4.7 %collective-permute-start.2 = (f32[40,128]{1,0:T(8,128)S(1)}, f32[40,128]{1,0:T(8,128)S(1)}, u32[]{:S(2)}, u32[]{:S(2)}) collective-permute-start(f32[40,128]{1,0:T(8,128)S(1)} %get-tuple-element.14), channel_id=1, source_target_pairs={{2,4},{4,2},{3,5},{5,3},{6,8},{8,6},{7,9},{9,7},{10,12},{12,10},{1... | collective-permute-start | bytes 61448 | tf_op jit(solution)/shard_map/ppermute | solution.py:338
  7.6 5.8 %collective-permute-start.1 = (f32[40,128]{1,0:T(8,128)S(1)}, f32[40,128]{1,0:T(8,128)S(1)}, u32[]{:S(2)}, u32[]{:S(2)}) collective-permute-start(f32[40,128]{1,0:T(8,128)S(1)} %get-tuple-element.14), channel_id=1, source_target_pairs={{0,2},{2,0},{1,3},{3,1},{4,6},{6,4},{5,7},{7,5},{8,10},{10,8},{9,1... | collective-permute-start | bytes 61448 | tf_op jit(solution)/shard_map/ppermute | solution.py:338
  15.7 1.3 %collective-permute-start.3 = (f32[32,384]{1,0:T(8,128)S(1)}, f32[32,384]{1,0:T(8,128)S(1)}, u32[]{:S(2)}, u32[]{:S(2)}) collective-permute-start(f32[32,384]{1,0:T(8,128)S(1)} %pad_maximum_fusion.part_ref), channel_id=1, source_target_pairs={{0,1},{1,0},{2,3},{3,2},{4,5},{5,4},{6,7},{7,6},{8,9},{9,8},{10,11... | collective-permute-start | bytes 147464 | tf_op jit(solution)/shard_map/ppermute | solution.py:331
  17.1 3.4 %collective-permute-start.5 = (f32[40,128]{1,0:T(8,128)S(1)}, f32[40,128]{1,0:T(8,128)S(1)}, u32[]{:S(2)}, u32[]{:S(2)}) collective-permute-start(f32[40,128]{1,0:T(8,128)S(1)} %get-tuple-element.19), channel_id=1, source_target_pairs={{2,4},{4,2},{3,5},{5,3},{6,8},{8,6},{7,9},{9,7},{10,12},{12,10},{1... | collective-permute-start | bytes 61448 | tf_op jit(solution)/shard_map/ppermute | solution.py:338
  17.3 5.0 %collective-permute-start.4 = (f32[40,128]{1,0:T(8,128)S(1)}, f32[40,128]{1,0:T(8,128)S(1)}, u32[]{:S(2)}, u32[]{:S(2)}) collective-permute-start(f32[40,128]{1,0:T(8,128)S(1)} %get-tuple-element.19), channel_id=1, source_target_pairs={{0,2},{2,0},{1,3},{3,1},{4,6},{6,4},{5,7},{7,5},{8,10},{10,8},{9,1... | collective-permute-start | bytes 61448 | tf_op jit(solution)/shard_map/ppermute | solution.py:338

commit v4 on v0

v4 whole, which is shorter than its diff:
```python
import jax
import jax.numpy as jnp
from jax import lax
from jax.experimental import pallas as pl
from jax.experimental.pallas import tpu as pltpu
from jax.sharding import PartitionSpec as P

BORDER = 32
LANES = 128
ROWS = 8
STAT_ROWS = 16
FULL = 32767.0
smooth_weight = 0.5
VMEM_BYTES = 24 * 1024 * 1024
HEAD_VMEM_BYTES = 53 * 1024 * 1024
FIRST_VMEM_BYTES = 50 * 1024 * 1024
COPY_COLUMNS = 512


def split(values):
    high = values.astype(jnp.bfloat16)
    low = (values - high.astype(jnp.float32)).astype(jnp.bfloat16)
    return high, low


def piece(total, wanted):
    for size in (1024, 512, 256, 128):
        if size <= wanted and total % size == 0:
            return size
    return total


def ratio_of(counts, gene_rows, factor_rows):
    product = jnp.dot(gene_rows, factor_rows, preferred_element_type=jnp.float32)
    return (counts.astype(jnp.float32) * pl.reciprocal(product, approx=True)).astype(
        jnp.bfloat16
    )


def partner(tile, tiles, offset):
    other = jnp.where((tile + offset) % 2 == 0, tile + 1, tile - 1)
    return jnp.where((other >= 0) & (other < tiles), other, -1)


def pick_kernel(neigh_ref, pick_ref):
    width = neigh_ref.shape[1]
    tiles = lax.axis_size("tile")
    here = lax.axis_index("tile")
    neigh = neigh_ref[...] - here * width

    def found(where):
        total = jnp.zeros((LANES, width), jnp.float32)
        for j in range(neigh.shape[0]):
            total += (neigh[j : j + 1] == where).astype(jnp.float32)
        return total

    row = lax.broadcasted_iota(jnp.int32, (LANES, width), 0)
    for at in range(0, width, LANES):
        pick_ref[at : at + LANES] = found(at + row).astype(jnp.bfloat16)
    slot = row % (2 * BORDER)
    beside = jnp.where(
        row < 2 * BORDER, partner(here, tiles, 0), partner(here, tiles, 1)
    )
    where = (beside - here) * width + slot + jnp.where(slot < BORDER, 0, width - 2 * BORDER)
    pick_ref[width:] = jnp.where(beside < 0, 0.0, found(where)).astype(jnp.bfloat16)


def start_copies(counts_ref, landed, sems, first):
    copies = []
    for i in range(landed.shape[1] // COPY_COLUMNS):
        at = i * COPY_COLUMNS
        copies.append(
            pltpu.make_async_copy(
                counts_ref.at[:, pl.ds(first + at, COPY_COLUMNS)],
                landed.at[:, pl.ds(at, COPY_COLUMNS)],
                sems.at[i],
            )
        )
    for copy in copies:
        copy.start()
    return copies


def turned(landed, at):
    return landed[:, at : at + COPY_COLUMNS].astype(jnp.float32).T.astype(jnp.bfloat16)


def head_kernel(counts_ref, kept_ref, landed, sems):
    for i, copy in enumerate(start_copies(counts_ref, landed, sems, 0)):
        copy.wait()
        at = i * COPY_COLUMNS
        kept_ref[at : at + COPY_COLUMNS] = turned(landed, at)


def first_kernel(
    counts_ref, head_ref, cells_ref, gene_ref, part_ref, tail_ref, rows_ref, landed, sems
):
    rank, genes = gene_ref.shape
    width = cells_ref.shape[1]
    done = head_ref.shape[0]
    copies = start_copies(counts_ref, landed, sems, done)
    factor_rows = jnp.concatenate(split(cells_ref[...]), axis=0)
    gsum = jnp.zeros((rank, 1), jnp.float32)
    total = jnp.zeros((rank, width), jnp.float32)
    for at in range(0, genes, COPY_COLUMNS):
        hf = gene_ref[:, at : at + COPY_COLUMNS]
        wide = hf.astype(jnp.float32)
        gsum += jnp.sum(wide, axis=1, keepdims=True)
        rows = jnp.concatenate([wide, wide], axis=0).T.astype(jnp.bfloat16)
        rows_ref[at : at + COPY_COLUMNS] = rows
        if at < done:
            counts = head_ref[at : at + COPY_COLUMNS]
        else:
            copies[(at - done) // COPY_COLUMNS].wait()
            counts = turned(landed, at - done)
            tail_ref[at - done : at - done + COPY_COLUMNS] = counts
        ratio = ratio_of(counts, rows, factor_rows)
        total += jnp.dot(hf, ratio, preferred_element_type=jnp.float32)
    part_ref[:, :width] = total
    part_ref[:, width:] = jnp.broadcast_to(gsum, (rank, LANES))


def masked_rows(values, flags):
    flag_rows = jnp.broadcast_to(flags.astype(jnp.float32), (ROWS, flags.shape[1]))
    return jnp.concatenate([jnp.where(flags, values, 0.0), flag_rows], axis=0)


def update_kernel(numer_ref, other_ref, gsum_ref, cells_ref, tissue_ref, updated_ref, edges_ref):
    width = cells_ref.shape[1]
    flags = tissue_ref[...] > 0
    numer = numer_ref[...] + other_ref[...]
    cells = cells_ref[...]
    updated = jnp.where(flags, cells * numer / gsum_ref[:, :1], cells)
    updated_ref[...] = updated
    both = masked_rows(updated, flags)
    edges_ref[:, :BORDER] = both[:, :BORDER]
    edges_ref[:, BORDER : 2 * BORDER] = both[:, width - BORDER :]
    edges_ref[:, 2 * BORDER :] = jnp.zeros_like(edges_ref[:, 2 * BORDER :])


def first_update_kernel(
    part_ref, other_ref, cells_ref, tissue_ref, updated_ref, edges_ref, gsum_ref
):
    width = cells_ref.shape[1]
    gsum_ref[...] = part_ref[:, width:] + other_ref[:, width:]
    update_kernel(
        part_ref.at[:, :width], other_ref.at[:, :width], gsum_ref,
        cells_ref, tissue_ref, updated_ref, edges_ref,
    )


def smoothed(updated_ref, tissue_ref, first_ref, second_ref, pick_ref):
    rank, width = updated_ref.shape
    updated = updated_ref[...]
    flags = tissue_ref[...] > 0
    own = masked_rows(updated, flags)
    sides = jnp.concatenate(
        [first_ref[:, : 2 * BORDER], second_ref[:, : 2 * BORDER]], axis=1
    )
    near = jnp.zeros(own.shape, jnp.float32)
    for values, pick in ((own, pick_ref[:width]), (sides, pick_ref[width:])):
        for part in split(values):
            near += jnp.dot(part, pick, preferred_element_type=jnp.float32)
    mean = near[:rank] / jnp.maximum(near[rank : rank + 1], 1.0)
    cells = jnp.where(
        flags, (1.0 - smooth_weight) * updated + smooth_weight * mean, updated
    )
    return cells, flags


def runs_of(head_ref, tail_ref, wanted):
    start = 0
    for ref in (head_ref, tail_ref):
        size = piece(ref.shape[0], wanted)
        for at in range(0, ref.shape[0], size):
            yield start + at, ref[at : at + size]
        start += ref.shape[0]


def next_kernel(
    updated_ref, tissue_ref, first_ref, second_ref, pick_ref, head_ref, tail_ref,
    gene_ref, rows_ref, cells_ref, numer_ref,
):
    cells, _ = smoothed(updated_ref, tissue_ref, first_ref, second_ref, pick_ref)
    cells_ref[...] = cells
    factor_rows = jnp.concatenate(split(cells), axis=0)
    total = jnp.zeros(cells.shape, jnp.float32)
    for at, counts in runs_of(head_ref, tail_ref, 1024):
        end = at + counts.shape[0]
        ratio = ratio_of(counts, rows_ref[at:end], factor_rows)
        total += jnp.dot(gene_ref[:, at:end], ratio, preferred_element_type=jnp.float32)
    numer_ref[...] = total


def exponent(values):
    return jnp.ceil(jnp.log2(jnp.maximum(values, 1e-30)))


def coded_kernel(
    updated_ref, tissue_ref, first_ref, second_ref, pick_ref, head_ref, tail_ref,
    rows_ref, cells_ref, sent_ref, totals_ref,
):
    rank, genes = totals_ref.shape
    tiles = sent_ref.shape[0]
    groups = rank // ROWS
    columns = genes * groups // tiles
    cells, flags = smoothed(updated_ref, tissue_ref, first_ref, second_ref, pick_ref)
    cells_ref[...] = cells
    masked = jnp.where(flags, cells, 0.0)
    factor_rows = jnp.concatenate(split(cells), axis=0)
    masked_parts = jnp.concatenate(split(masked), axis=0)
    hden = jnp.sum(masked, axis=1, keepdims=True)
    power = exponent(hden)
    scaled = hden * jnp.exp2(-power) * FULL
    high = jnp.floor(scaled)
    lane = lax.broadcasted_iota(jnp.int32, (rank, LANES), 1)
    stats = jnp.zeros((rank, LANES), jnp.float32)
    for at, value in enumerate((power, high, jnp.floor((scaled - high) * FULL))):
        stats = jnp.where(lane == at + 1, value, stats)
    for at, counts in runs_of(head_ref, tail_ref, 512):
        end = at + counts.shape[0]
        ratio = ratio_of(counts, rows_ref[at:end], factor_rows)
        both = lax.dot_general(
            masked_parts, ratio, (((1,), (1,)), ((), ())), preferred_element_type=jnp.float32
        )
        totals_ref[:, at:end] = both[:rank] + both[rank:]
    blank = jnp.zeros((ROWS, LANES), jnp.int32)
    for column in range(genes // columns):
        totals = totals_ref[:, column * columns : (column + 1) * columns]
        power = exponent(jnp.max(totals, axis=1, keepdims=True))
        coded = (totals * (jnp.exp2(-power) * FULL) + 0.5).astype(jnp.int32)
        marks = jnp.where(lane == 0, power, stats).astype(jnp.int32)
        for group in range(groups):
            tile = group * (genes // columns) + column
            ranks = slice(group * ROWS, (group + 1) * ROWS)
            blocks = [coded[ranks, at : at + LANES] for at in range(0, columns, LANES)]
            blocks += [blank] * (len(blocks) % 2) + [marks[ranks], blank]
            for i in range(0, len(blocks), 2):
                sent_ref[tile, i * ROWS : (i + 2) * ROWS] = jnp.concatenate(
                    blocks[i : i + 2], axis=0
                ).astype(jnp.int16)


def fresh_kernel(got_ref, gene_ref, fresh_ref):
    tiles, height, _ = got_ref.shape
    columns = fresh_ref.shape[2]
    groups = gene_ref.shape[0] // ROWS
    here = lax.axis_index("tile")
    across = tiles // groups

    def number(coded):
        return coded.astype(jnp.int32).astype(jnp.float32)

    def twice(values):
        return jnp.concatenate([values, values], axis=0)

    hden = jnp.zeros((ROWS, 1), jnp.float32)
    scales = []
    for tile in range(tiles):
        marks = number(got_ref[tile, height - STAT_ROWS :])[:ROWS]
        scales.append(twice(jnp.exp2(marks[:, :1]) / FULL))
        hden += (marks[:, 2:3] + marks[:, 3:4] / FULL) * (jnp.exp2(marks[:, 1:2]) / FULL)
    totals = []
    for at in range(0, height - STAT_ROWS, 2 * ROWS):
        total = jnp.zeros((2 * ROWS, LANES), jnp.float32)
        for tile in range(tiles):
            total += number(got_ref[tile, at : at + 2 * ROWS]) * scales[tile]
        totals += [total[:ROWS], total[ROWS:]]
    hnum = jnp.concatenate(totals[: columns // LANES], axis=1)
    place = pl.multiple_of(lax.rem(here, across) * columns, LANES)
    every = gene_ref[:, pl.ds(place, columns)].astype(jnp.float32)
    hf = every[:ROWS]
    for group in range(1, groups):
        hf = jnp.where(here // across == group, every[group * ROWS : (group + 1) * ROWS], hf)
    fresh = (hf * hnum / hden).astype(jnp.bfloat16)
    for tile in range(tiles):
        fresh_ref[tile] = fresh


def call(kernel, outs, scratch=(), specs=None, limit=VMEM_BYTES):
    whole = pl.BlockSpec(memory_space=pltpu.VMEM)
    return lambda *args: pl.pallas_call(
        kernel,
        out_shape=outs,
        in_specs=specs or [whole] * len(args),
        out_specs=jax.tree.map(lambda _: whole, outs),
        scratch_shapes=list(scratch),
        compiler_params=pltpu.CompilerParams(vmem_limit_bytes=limit),
    )(*args)


def beside(tiles, halves, offset):
    pairs = []
    paired = set()
    for low in range(offset, tiles - 1, 2):
        paired |= {low, low + 1}
        for gene in range(halves):
            pairs.append((low * halves + gene, (low + 1) * halves + gene))
            pairs.append(((low + 1) * halves + gene, low * halves + gene))
    for tile in range(tiles):
        if tile not in paired:
            for gene in range(halves):
                pairs.append((tile * halves + gene, tile * halves + (gene + 1) % halves))
    return pairs


def on_device(counts, cell_factor, gene_factor, tissue, neighbours):
    rank, width = cell_factor.shape
    genes = gene_factor.shape[1]
    tiles, halves = lax.axis_size("tile"), lax.axis_size("gene")
    flag_row = tissue[None]
    shape = jax.ShapeDtypeStruct
    factor = shape((rank, width), jnp.float32)
    edge = shape((rank + ROWS, LANES), jnp.float32)
    gene_rows = shape((genes, 2 * rank), jnp.bfloat16)
    far = pl.BlockSpec(memory_space=pl.ANY)
    near = pl.BlockSpec(memory_space=pltpu.VMEM)

    def landing(columns):
        return [
            pltpu.VMEM((width, columns), counts.dtype),
            pltpu.SemaphoreType.DMA((columns // COPY_COLUMNS,)),
        ]

    head = genes // 4
    kept_head = call(
        head_kernel, shape((head, width), jnp.bfloat16), landing(head), [far],
        HEAD_VMEM_BYTES,
    )(counts)
    part, kept_tail, rows = call(
        first_kernel,
        (
            shape((rank, width + LANES), jnp.float32),
            shape((genes - head, width), jnp.bfloat16),
            gene_rows,
        ),
        landing(genes - head),
        [far] + [near] * 3,
        FIRST_VMEM_BYTES,
    )(counts, kept_head, cell_factor, gene_factor)
    pick = call(pick_kernel, shape((width + LANES, width), jnp.bfloat16))(neighbours)

    def swapped(part):
        if halves == 2:
            return lax.ppermute(part, "gene", [(0, 1), (1, 0)])
        return lax.psum(part, "gene") - part

    def around(updated, edges):
        sides = [
            lax.ppermute(edges, ("tile", "gene"), beside(tiles, halves, offset))
            for offset in (0, 1)
        ]
        return updated, flag_row, *sides, pick, kept_head, kept_tail

    updated, edges, gsum = call(
        first_update_kernel, (factor, edge, shape((rank, LANES), jnp.float32))
    )(part, swapped(part), cell_factor, flag_row)
    cells, numer = call(next_kernel, (factor, factor))(
        *around(updated, edges), gene_factor, rows
    )
    updated, edges = call(update_kernel, (factor, edge))(
        numer, swapped(numer), gsum, cells, flag_row
    )
    across = tiles * ROWS // rank
    columns = genes // across
    blocks = columns // LANES
    height = (blocks + blocks % 2) * ROWS + STAT_ROWS
    cells, sent = call(
        coded_kernel,
        (factor, shape((tiles, height, LANES), jnp.int16)),
        [pltpu.VMEM((rank, genes), jnp.float32)],
    )(*around(updated, edges), rows)
    got = lax.all_to_all(sent, "tile", 0, 0)
    fresh = call(fresh_kernel, shape((tiles, ROWS, columns), jnp.bfloat16))(got, gene_factor)
    every = lax.all_to_all(fresh, "tile", 0, 0)
    every = every.reshape(rank // ROWS, across, ROWS, columns)
    return cells, every.transpose(0, 2, 1, 3).reshape(rank, genes)


def solution(mesh):
    return jax.shard_map(
        on_device,
        mesh=mesh,
        in_specs=(
            P(("grp", "tile"), "gene"),
            P(None, ("grp", "tile")),
            P(None, ("grp", "gene")),
            P(("grp", "tile")),
            P(None, ("grp", "tile")),
        ),
        out_specs=(P(None, ("grp", "tile")), P(None, ("grp", "gene"))),
        check_vma=False,
    )
```

time: 171 us -> 50.1 us (0.29)
  waiting for transfers between devices: 58.9 us -> 5.28 us
  local copies, waits for them, and re-layouts: 24.8 us -> 0.72 us
  matrix products: 20.6 us -> 0 us
  between operations: 14.4 us -> 0.72 us
  starting transfers between devices: 18.4 us -> 8.32 us
  Pallas kernels: 0 us -> 8.9 us
  other arithmetic: 6.23 us -> 0 us
    psum x1 -> x0, waiting for transfers between devices: 53.9 us -> none  [on_device(): hnum, hden = lax.psum((hnum_part, hden_part), 'tile')]
    psum x3 -> x0, blocking collectives: 27.1 us -> none  [the longest x1 20.3 us: on_device(): hnum, hden = lax.psum((hnum_part, hden_part), 'tile')]
    all_to_all x0 -> x2, blocking collectives: none -> 25.9 us  [the longest x1 14.7 us: on_device(): got = lax.all_to_all(sent, 'tile', 0, 0)]
    gather x3 -> x0, local copies, waits for them, and re-layouts: 24.2 us -> none  [the longest x1 13.2 us: on_device(): near_mask = jnp.take(mask_padded[0], local).reshape(count, width)]
    dot_general x6 -> x0, matrix products: 20.6 us -> none  [the longest x3 12.9 us: on_device(): lax.dot_general(cells, hfull, (((0,), (0,)), ((), ())), precision=lax.Pre...]
    ppermute x6, starting transfers between devices: 18.4 us -> 8.32 us  [the longest x4 7.8 us: around(): lax.ppermute(edges, ('tile', 'gene'), beside(tiles, halves, offset))]
    pallas_call x0 -> x8, Pallas kernels: none -> 8.9 us  [call(): pl.pallas_call(kernel, out_shape=outs, in_specs=specs or [whole] * len(ar...]
    convert_element_type x7 -> x0, other arithmetic: 2.93 us -> none  [the longest x1 1.85 us: on_device(): new_genes = (hfull * hnum / hden[:, None]).astype(jnp.bfloat16)]
  transfers between devices with their start and end apart: 7 -> 6, of which waited for: 2 -> 4; matrix products, arithmetic and copies ran while one was open for 13% -> 0% of each run, Pallas kernels for 0% -> 1%
where the time goes in v4:
time: 50.1 us; the launch traced here: 49.9 us
  blocking collectives  25.9 us (52%)
  Pallas kernels  8.9 us (18%)
  starting transfers between devices  8.32 us (17%)
  waiting for transfers between devices  5.28 us (11%)
  local copies, waits for them, and re-layouts  0.72 us (1%)
  between operations  0.72 us (1%)
    all_to_all x1, blocking collectives, on_device(): got = lax.all_to_all(sent, 'tile', 0, 0)  14.7 us
    all_to_all x1, blocking collectives, on_device(): every = lax.all_to_all(fresh, 'tile', 0, 0)  11.2 us
    pallas_call x8, Pallas kernels, call(): pl.pallas_call(kernel, out_shape=outs, in_specs=specs or [whole] * len(ar...  8.9 us
    ppermute x4, starting transfers between devices, around(): lax.ppermute(edges, ('tile', 'gene'), beside(tiles, halves, offset))  7.8 us
    ppermute x4, waiting for transfers between devices, around(): lax.ppermute(edges, ('tile', 'gene'), beside(tiles, halves, offset))  3.18 us
    ppermute x2, waiting for transfers between devices, swapped(): return lax.ppermute(part, 'gene', [(0, 1), (1, 0)])  2.1 us
  transfers between devices with their start and end apart: 6, of which 4 were waited for; matrix products, arithmetic and copies ran while one was open for 0% of the time, Pallas kernels for 1%

profile of v4, /device:TPU:0, one launch (start us, length us, event | category | flops | bytes accessed | tf_op | source)
XLA Modules:
  0.0 49.9 jit_solution(858835113910583199)
XLA Ops:
  0.6 0.0 copy-start
  0.6 0.0 copy-start.1
  0.7 0.0 copy-start.2
  0.7 0.0 copy-start.3
  0.7 1.4 %shard_map.68.head_ref = bf16[1024,256]{1,0:T(8,128)(2,1)S(1)} custom-call(s32[256,4096]{1,0:T(8,128)} %counts_ref.3), custom_call_target="tpu_custom_call" | custom-call | tf_op jit(solution)/shard_map/pallas_call | solution.py:282
  2.1 0.0 copy-done
  2.1 0.0 copy-done.1
  2.1 2.8 %shard_map.69 = (f32[32,384]{1,0:T(8,128)S(1)}, bf16[3072,256]{1,0:T(8,128)(2,1)S(1)}, bf16[4096,64]{1,0:T(8,128)(2,1)S(1)}) custom-call(s32[256,4096]{1,0:T(8,128)} %counts_ref.3, bf16[1024,256]{1,0:T(8,128)(2,1)S(1)} %shard_map.68.head_ref, f32[32,256]{1,0:T(8,128)S(1)} %copy-done.1, bf16[32,4096]{1,0:T(8,128)(2,1)S(1)} %copy-done), custom_call_target="tpu_custom_call" | custom-call | tf_op jit(solution)/shard_map/pallas_call | solution.py:282
  4.9 0.5 %collective-permute-start = (f32[32,384]{1,0:T(8,128)S(1)}, f32[32,384]{1,0:T(8,128)S(1)}, u32[]{:S(2)}, u32[]{:S(2)}) collective-permute-start(f32[32,384]{1,0:T(8,128)S(1)} %get-tuple-element.14.part_ref), channel_id=1, source_target_pairs={{0,1},{1,0},{2,3},{3,2},{4,5},{5,4},{6,7},{7,6},{8,9},{9,8},{10,11... | collective-permute-start | bytes 147464 | tf_op jit(solution)/shard_map/ppermute | solution.py:345
  5.5 0.9 %collective-permute-done.other_ref = f32[32,384]{1,0:T(8,128)S(1)} collective-permute-done((f32[32,384]{1,0:T(8,128)S(1)}, f32[32,384]{1,0:T(8,128)S(1)}, u32[]{:S(2)}, u32[]{:S(2)}) %collective-permute-start) | collective-permute-done | bytes 49184 | tf_op jit(solution)/shard_map/ppermute | solution.py:345
  6.3 0.0 copy-done.2
  6.3 0.1 shard_map.70
  6.5 0.4 collective-permute-start.2
  6.8 4.0 %collective-permute-start.1 = (f32[40,128]{1,0:T(8,128)S(1)}, f32[40,128]{1,0:T(8,128)S(1)}, u32[]{:S(2)}, u32[]{:S(2)}) collective-permute-start(f32[40,128]{1,0:T(8,128)S(1)} %get-tuple-element.16), channel_id=1, source_target_pairs={{0,2},{2,0},{1,3},{3,1},{4,6},{6,4},{5,7},{7,5},{8,10},{10,8},{9,1... | collective-permute-start | bytes 61448 | tf_op jit(solution)/shard_map/ppermute | solution.py:350
  10.9 0.0 copy-done.3
  10.9 0.3 shard_map.71.pick_ref
  11.2 0.0 collective-permute-done.2.second_ref
  11.2 1.4 %collective-permute-done.1.first_ref = f32[40,128]{1,0:T(8,128)S(1)} collective-permute-done((f32[40,128]{1,0:T(8,128)S(1)}, f32[40,128]{1,0:T(8,128)S(1)}, u32[]{:S(2)}, u32[]{:S(2)}) %collective-permute-start.1) | collective-permute-done | bytes 20512 | tf_op jit(solution)/shard_map/ppermute | solution.py:350
  12.6 1.2 %shard_map.72 = (f32[32,256]{1,0:T(8,128)S(1)}, f32[32,256]{1,0:T(8,128)S(1)}) custom-call(f32[32,256]{1,0:T(8,128)S(1)} %get-tuple-element.15.updated_ref, s32[1,256]{1,0:T(1,128)S(1)} %bitcast.7, f32[40,128]{1,0:T(8,128)S(1)} %collective-permute-done.1.first_ref, f32[40,128]{1,0:T(8,128)S(1)} %collective-permute-done.2.second_ref, ...), custom_call_target="tpu_custom_call" | custom-call | tf_op jit(solution)/shard_map/pallas_call | solution.py:282
  13.9 0.0 collective-permute-start.3
  13.9 1.2 %collective-permute-done.3.other_ref = f32[32,256]{1,0:T(8,128)S(1)} collective-permute-done((f32[32,256]{1,0:T(8,128)S(1)}, f32[32,256]{1,0:T(8,128)S(1)}, u32[]{:S(2)}, u32[]{:S(2)}) %collective-permute-start.3) | collective-permute-done | bytes 32800 | tf_op jit(solution)/shard_map/ppermute | solution.py:345
  15.1 0.1 shard_map.73
  15.3 0.2 collective-permute-start.5
  15.4 3.2 %collective-permute-start.4 = (f32[40,128]{1,0:T(8,128)S(1)}, f32[40,128]{1,0:T(8,128)S(1)}, u32[]{:S(2)}, u32[]{:S(2)}) collective-permute-start(f32[40,128]{1,0:T(8,128)S(1)} %get-tuple-element.23), channel_id=1, source_target_pairs={{0,2},{2,0},{1,3},{3,1},{4,6},{6,4},{5,7},{7,5},{8,10},{10,8},{9,1... | collective-permute-start | bytes 61448 | tf_op jit(solution)/shard_map/ppermute | solution.py:350
  18.7 0.0 collective-permute-done.5.second_ref
  18.7 1.8 %collective-permute-done.4.first_ref = f32[40,128]{1,0:T(8,128)S(1)} collective-permute-done((f32[40,128]{1,0:T(8,128)S(1)}, f32[40,128]{1,0:T(8,128)S(1)}, u32[]{:S(2)}, u32[]{:S(2)}) %collective-permute-start.4) | collective-permute-done | bytes 20512 | tf_op jit(solution)/shard_map/ppermute | solution.py:350
  20.4 2.6 %shard_map.74 = (f32[32,256]{1,0:T(8,128)}, s16[8,144,128]{2,1,0:T(8,128)(2,1)S(1)}) custom-call(f32[32,256]{1,0:T(8,128)S(1)} %get-tuple-element.22.updated_ref, s32[1,256]{1,0:T(1,128)S(1)} %bitcast.9, f32[40,128]{1,0:T(8,128)S(1)} %collective-permute-done.4.first_ref, f32[40,128]{1,0:T(8,128)S(1)} %collective-permute-done.5.second_ref, ...), custom_call_target="tpu_custom_call" | custom-call | tf_op jit(solution)/shard_map/pallas_call | solution.py:282
  23.0 14.7 %all_to_all.10.got_ref = s16[8,144,128]{2,1,0:T(8,128)(2,1)S(1)} all-to-all(s16[8,144,128]{2,1,0:T(8,128)(2,1)S(1)} %get-tuple-element.25), channel_id=1, replica_groups=mesh['grp'=2,'tile'=8,'gene'=2] {'tile'}, dimensions={0} | all-to-all | bytes 589824 | tf_op jit(solution)/shard_map/all_to_all | solution.py:373
  37.8 0.2 shard_map.75
  38.0 11.2 %all_to_all.11 = bf16[8,8,2048]{2,1,0:T(8,128)(2,1)S(1)} all-to-all(bf16[8,8,2048]{2,1,0:T(8,128)(2,1)S(1)} %shard_map.75), channel_id=1, replica_groups=mesh['grp'=2,'tile'=8,'gene'=2] {'tile'}, dimensions={0} | all-to-all | bytes 524288 | tf_op jit(solution)/shard_map/all_to_all | solution.py:375
  49.2 0.7 %copy.8 = bf16[32,4096]{1,0:T(8,128)(2,1)} copy(bf16[32,4096]{1,0:T(8,128)(2,1)S(1)} %bitcast.10) | data formatting | bytes 524288
Async XLA Ops:
  0.6 1.4 %copy-start = (bf16[32,4096]{1,0:T(8,128)(2,1)S(1)}, bf16[32,4096]{1,0:T(8,128)(2,1)}, u32[]{:S(2)}) copy-start(bf16[32,4096]{1,0:T(8,128)(2,1)} %gene_ref.5) | copy-start | bytes 786436
  0.6 1.4 %copy-start.1 = (f32[32,256]{1,0:T(8,128)S(1)}, f32[32,256]{1,0:T(8,128)}, u32[]{:S(2)}) copy-start(f32[32,256]{1,0:T(8,128)} %cells_ref.3) | copy-start | bytes 98308
  0.7 5.7 %copy-start.2 = (s32[256]{0:T(256)S(1)}, s32[256]{0:T(256)}, u32[]{:S(2)}) copy-start(s32[256]{0:T(256)} %param.8) | copy-start | bytes 3076
  0.7 10.2 %copy-start.3 = (s32[8,256]{1,0:T(8,128)S(1)}, s32[8,256]{1,0:T(8,128)}, u32[]{:S(2)}) copy-start(s32[8,256]{1,0:T(8,128)} %neigh_ref.1) | copy-start | bytes 24580
  4.9 1.4 %collective-permute-start = (f32[32,384]{1,0:T(8,128)S(1)}, f32[32,384]{1,0:T(8,128)S(1)}, u32[]{:S(2)}, u32[]{:S(2)}) collective-permute-start(f32[32,384]{1,0:T(8,128)S(1)} %get-tuple-element.14.part_ref), channel_id=1, source_target_pairs={{0,1},{1,0},{2,3},{3,2},{4,5},{5,4},{6,7},{7,6},{8,9},{9,8},{10,11... | collective-permute-start | bytes 147464 | tf_op jit(solution)/shard_map/ppermute | solution.py:345
  6.5 4.7 %collective-permute-start.2 = (f32[40,128]{1,0:T(8,128)S(1)}, f32[40,128]{1,0:T(8,128)S(1)}, u32[]{:S(2)}, u32[]{:S(2)}) collective-permute-start(f32[40,128]{1,0:T(8,128)S(1)} %get-tuple-element.16), channel_id=1, source_target_pairs={{2,4},{4,2},{3,5},{5,3},{6,8},{8,6},{7,9},{9,7},{10,12},{12,10},{1... | collective-permute-start | bytes 61448 | tf_op jit(solution)/shard_map/ppermute | solution.py:350
  6.8 5.8 %collective-permute-start.1 = (f32[40,128]{1,0:T(8,128)S(1)}, f32[40,128]{1,0:T(8,128)S(1)}, u32[]{:S(2)}, u32[]{:S(2)}) collective-permute-start(f32[40,128]{1,0:T(8,128)S(1)} %get-tuple-element.16), channel_id=1, source_target_pairs={{0,2},{2,0},{1,3},{3,1},{4,6},{6,4},{5,7},{7,5},{8,10},{10,8},{9,1... | collective-permute-start | bytes 61448 | tf_op jit(solution)/shard_map/ppermute | solution.py:350
  13.9 1.2 %collective-permute-start.3 = (f32[32,256]{1,0:T(8,128)S(1)}, f32[32,256]{1,0:T(8,128)S(1)}, u32[]{:S(2)}, u32[]{:S(2)}) collective-permute-start(f32[32,256]{1,0:T(8,128)S(1)} %get-tuple-element.19.numer_ref), channel_id=1, source_target_pairs={{0,1},{1,0},{2,3},{3,2},{4,5},{5,4},{6,7},{7,6},{8,9},{9,8},{10,11... | collective-permute-start | bytes 98312 | tf_op jit(solution)/shard_map/ppermute | solution.py:345
  15.3 3.4 %collective-permute-start.5 = (f32[40,128]{1,0:T(8,128)S(1)}, f32[40,128]{1,0:T(8,128)S(1)}, u32[]{:S(2)}, u32[]{:S(2)}) collective-permute-start(f32[40,128]{1,0:T(8,128)S(1)} %get-tuple-element.23), channel_id=1, source_target_pairs={{2,4},{4,2},{3,5},{5,3},{6,8},{8,6},{7,9},{9,7},{10,12},{12,10},{1... | collective-permute-start | bytes 61448 | tf_op jit(solution)/shard_map/ppermute | solution.py:350
  15.4 5.0 %collective-permute-start.4 = (f32[40,128]{1,0:T(8,128)S(1)}, f32[40,128]{1,0:T(8,128)S(1)}, u32[]{:S(2)}, u32[]{:S(2)}) collective-permute-start(f32[40,128]{1,0:T(8,128)S(1)} %get-tuple-element.23), channel_id=1, source_target_pairs={{0,2},{2,0},{1,3},{3,1},{4,6},{6,4},{5,7},{7,5},{8,10},{10,8},{9,1... | collective-permute-start | bytes 61448 | tf_op jit(solution)/shard_map/ppermute | solution.py:350

commit v5 on v4

--- a/solution.py
+++ b/solution.py
@@ -12,8 +12,7 @@
 FULL = 32767.0
 smooth_weight = 0.5
 VMEM_BYTES = 24 * 1024 * 1024
-HEAD_VMEM_BYTES = 53 * 1024 * 1024
-FIRST_VMEM_BYTES = 50 * 1024 * 1024
+COUNTS_VMEM_BYTES = 51 * 1024 * 1024
 COPY_COLUMNS = 512
 
 
@@ -65,13 +64,13 @@
     pick_ref[width:] = jnp.where(beside < 0, 0.0, found(where)).astype(jnp.bfloat16)
 
 
-def start_copies(counts_ref, landed, sems, first):
+def start_copies(counts_ref, landed, sems):
     copies = []
     for i in range(landed.shape[1] // COPY_COLUMNS):
         at = i * COPY_COLUMNS
         copies.append(
             pltpu.make_async_copy(
-                counts_ref.at[:, pl.ds(first + at, COPY_COLUMNS)],
+                counts_ref.at[:, pl.ds(at, COPY_COLUMNS)],
                 landed.at[:, pl.ds(at, COPY_COLUMNS)],
                 sems.at[i],
             )
@@ -85,35 +84,33 @@
     return landed[:, at : at + COPY_COLUMNS].astype(jnp.float32).T.astype(jnp.bfloat16)
 
 
-def head_kernel(counts_ref, kept_ref, landed, sems):
-    for i, copy in enumerate(start_copies(counts_ref, landed, sems, 0)):
+def turn_kernel(counts_ref, kept_ref, landed, sems):
+    for i, copy in enumerate(start_copies(counts_ref, landed, sems)):
         copy.wait()
         at = i * COPY_COLUMNS
         kept_ref[at : at + COPY_COLUMNS] = turned(landed, at)
 
 
-def first_kernel(
-    counts_ref, head_ref, cells_ref, gene_ref, part_ref, tail_ref, rows_ref, landed, sems
-):
+def runs_of(kept_ref, wanted):
+    genes = kept_ref.shape[0]
+    size = piece(genes, wanted)
+    for at in range(0, genes, size):
+        yield at, kept_ref[at : at + size]
+
+
+def first_kernel(kept_ref, cells_ref, gene_ref, part_ref, rows_ref):
     rank, genes = gene_ref.shape
     width = cells_ref.shape[1]
-    done = head_ref.shape[0]
-    copies = start_copies(counts_ref, landed, sems, done)
     factor_rows = jnp.concatenate(split(cells_ref[...]), axis=0)
     gsum = jnp.zeros((rank, 1), jnp.float32)
     total = jnp.zeros((rank, width), jnp.float32)
-    for at in range(0, genes, COPY_COLUMNS):
-        hf = gene_ref[:, at : at + COPY_COLUMNS]
+    for at, counts in runs_of(kept_ref, 1024):
+        end = at + counts.shape[0]
+        hf = gene_ref[:, at:end]
         wide = hf.astype(jnp.float32)
         gsum += jnp.sum(wide, axis=1, keepdims=True)
         rows = jnp.concatenate([wide, wide], axis=0).T.astype(jnp.bfloat16)
-        rows_ref[at : at + COPY_COLUMNS] = rows
-        if at < done:
-            counts = head_ref[at : at + COPY_COLUMNS]
-        else:
-            copies[(at - done) // COPY_COLUMNS].wait()
-            counts = turned(landed, at - done)
-            tail_ref[at - done : at - done + COPY_COLUMNS] = counts
+        rows_ref[at:end] = rows
         ratio = ratio_of(counts, rows, factor_rows)
         total += jnp.dot(hf, ratio, preferred_element_type=jnp.float32)
     part_ref[:, :width] = total
@@ -168,24 +165,15 @@
     return cells, flags
 
 
-def runs_of(head_ref, tail_ref, wanted):
-    start = 0
-    for ref in (head_ref, tail_ref):
-        size = piece(ref.shape[0], wanted)
-        for at in range(0, ref.shape[0], size):
-            yield start + at, ref[at : at + size]
-        start += ref.shape[0]
-
-
 def next_kernel(
-    updated_ref, tissue_ref, first_ref, second_ref, pick_ref, head_ref, tail_ref,
+    updated_ref, tissue_ref, first_ref, second_ref, pick_ref, kept_ref,
     gene_ref, rows_ref, cells_ref, numer_ref,
 ):
     cells, _ = smoothed(updated_ref, tissue_ref, first_ref, second_ref, pick_ref)
     cells_ref[...] = cells
     factor_rows = jnp.concatenate(split(cells), axis=0)
     total = jnp.zeros(cells.shape, jnp.float32)
-    for at, counts in runs_of(head_ref, tail_ref, 1024):
+    for at, counts in runs_of(kept_ref, 1024):
         end = at + counts.shape[0]
         ratio = ratio_of(counts, rows_ref[at:end], factor_rows)
         total += jnp.dot(gene_ref[:, at:end], ratio, preferred_element_type=jnp.float32)
@@ -197,7 +185,7 @@
 
 
 def coded_kernel(
-    updated_ref, tissue_ref, first_ref, second_ref, pick_ref, head_ref, tail_ref,
+    updated_ref, tissue_ref, first_ref, second_ref, pick_ref, kept_ref,
     rows_ref, cells_ref, sent_ref, totals_ref,
 ):
     rank, genes = totals_ref.shape
@@ -209,6 +197,7 @@
     masked = jnp.where(flags, cells, 0.0)
     factor_rows = jnp.concatenate(split(cells), axis=0)
     masked_parts = jnp.concatenate(split(masked), axis=0)
+    masked_columns = masked_parts.astype(jnp.float32).T.astype(jnp.bfloat16)
     hden = jnp.sum(masked, axis=1, keepdims=True)
     power = exponent(hden)
     scaled = hden * jnp.exp2(-power) * FULL
@@ -217,12 +206,10 @@
     stats = jnp.zeros((rank, LANES), jnp.float32)
     for at, value in enumerate((power, high, jnp.floor((scaled - high) * FULL))):
         stats = jnp.where(lane == at + 1, value, stats)
-    for at, counts in runs_of(head_ref, tail_ref, 512):
+    for at, counts in runs_of(kept_ref, 1024):
         end = at + counts.shape[0]
         ratio = ratio_of(counts, rows_ref[at:end], factor_rows)
-        both = lax.dot_general(
-            masked_parts, ratio, (((1,), (1,)), ((), ())), preferred_element_type=jnp.float32
-        )
+        both = jnp.dot(ratio, masked_columns, preferred_element_type=jnp.float32).T
         totals_ref[:, at:end] = both[:rank] + both[rank:]
     blank = jnp.zeros((ROWS, LANES), jnp.int32)
     for column in range(genes // columns):
@@ -295,8 +282,9 @@
     for low in range(offset, tiles - 1, 2):
         paired |= {low, low + 1}
         for gene in range(halves):
-            pairs.append((low * halves + gene, (low + 1) * halves + gene))
-            pairs.append(((low + 1) * halves + gene, low * halves + gene))
+            other = (gene + 1) % halves
+            pairs.append((low * halves + gene, (low + 1) * halves + other))
+            pairs.append(((low + 1) * halves + gene, low * halves + other))
     for tile in range(tiles):
         if tile not in paired:
             for gene in range(halves):
@@ -314,30 +302,20 @@
     edge = shape((rank + ROWS, LANES), jnp.float32)
     gene_rows = shape((genes, 2 * rank), jnp.bfloat16)
     far = pl.BlockSpec(memory_space=pl.ANY)
-    near = pl.BlockSpec(memory_space=pltpu.VMEM)
-
-    def landing(columns):
-        return [
-            pltpu.VMEM((width, columns), counts.dtype),
-            pltpu.SemaphoreType.DMA((columns // COPY_COLUMNS,)),
-        ]
-
-    head = genes // 4
-    kept_head = call(
-        head_kernel, shape((head, width), jnp.bfloat16), landing(head), [far],
-        HEAD_VMEM_BYTES,
+
+    kept = call(
+        turn_kernel,
+        shape((genes, width), jnp.bfloat16),
+        [
+            pltpu.VMEM(counts.shape, counts.dtype),
+            pltpu.SemaphoreType.DMA((genes // COPY_COLUMNS,)),
+        ],
+        [far],
+        COUNTS_VMEM_BYTES,
     )(counts)
-    part, kept_tail, rows = call(
-        first_kernel,
-        (
-            shape((rank, width + LANES), jnp.float32),
-            shape((genes - head, width), jnp.bfloat16),
-            gene_rows,
-        ),
-        landing(genes - head),
-        [far] + [near] * 3,
-        FIRST_VMEM_BYTES,
-    )(counts, kept_head, cell_factor, gene_factor)
+    part, rows = call(
+        first_kernel, (shape((rank, width + LANES), jnp.float32), gene_rows)
+    )(kept, cell_factor, gene_factor)
     pick = call(pick_kernel, shape((width + LANES, width), jnp.bfloat16))(neighbours)
 
     def swapped(part):
@@ -350,7 +328,7 @@
             lax.ppermute(edges, ("tile", "gene"), beside(tiles, halves, offset))
             for offset in (0, 1)
         ]
-        return updated, flag_row, *sides, pick, kept_head, kept_tail
+        return updated, flag_row, *sides, pick, kept
 
     updated, edges, gsum = call(
         first_update_kernel, (factor, edge, shape((rank, LANES), jnp.float32))

time: 50.1 us -> 48.9 us (0.976)
  blocking collectives: 25.9 us -> 27.2 us
  Pallas kernels: 8.9 us -> 7.61 us
  waiting for transfers between devices: 5.28 us -> 4.57 us
    pallas_call x8, Pallas kernels: 8.9 us -> 7.61 us  [call(): pl.pallas_call(kernel, out_shape=outs, in_specs=specs or [whole] * len(ar...]
    all_to_all x1, blocking collectives: 14.7 us -> 15.7 us  [on_device(): got = lax.all_to_all(sent, 'tile', 0, 0)]
    ppermute x4, starting transfers between devices: 7.8 us -> 7.2 us  [around(): lax.ppermute(edges, ('tile', 'gene'), beside(tiles, halves, offset))]
    ppermute x4, waiting for transfers between devices: 3.18 us -> 2.63 us  [around(): lax.ppermute(edges, ('tile', 'gene'), beside(tiles, halves, offset))]
where the time goes in v5:
time: 48.9 us; the launch traced here: 48.7 us
  blocking collectives  27.2 us (56%)
  starting transfers between devices  7.82 us (16%)
  Pallas kernels  7.61 us (16%)
  waiting for transfers between devices  4.57 us (9%)
  local copies, waits for them, and re-layouts  0.72 us (1%)
  between operations  0.72 us (1%)
    all_to_all x1, blocking collectives, on_device(): got = lax.all_to_all(sent, 'tile', 0, 0)  15.7 us
    all_to_all x1, blocking collectives, on_device(): every = lax.all_to_all(fresh, 'tile', 0, 0)  11.5 us
    pallas_call x8, Pallas kernels, call(): pl.pallas_call(kernel, out_shape=outs, in_specs=specs or [whole] * len(ar...  7.61 us
    ppermute x4, starting transfers between devices, around(): lax.ppermute(edges, ('tile', 'gene'), beside(tiles, halves, offset))  7.2 us
    ppermute x4, waiting for transfers between devices, around(): lax.ppermute(edges, ('tile', 'gene'), beside(tiles, halves, offset))  2.63 us
    ppermute x2, waiting for transfers between devices, swapped(): return lax.ppermute(part, 'gene', [(0, 1), (1, 0)])  1.94 us
  transfers between devices with their start and end apart: 6, of which 4 were waited for; matrix products, arithmetic and copies ran while one was open for 0% of the time, Pallas kernels for 1%

profile of v5, /device:TPU:0, one launch (start us, length us, event | category | flops | bytes accessed | tf_op | source)
XLA Modules:
  0.0 48.7 jit_solution(17010138712436507911)
XLA Ops:
  0.6 0.0 copy-start
  0.6 0.0 copy-start.1
  0.7 0.0 copy-start.2
  0.7 0.0 copy-start.3
  0.7 2.4 %shard_map.68.kept_ref = bf16[4096,256]{1,0:T(8,128)(2,1)S(1)} custom-call(s32[256,4096]{1,0:T(8,128)} %counts_ref.1), custom_call_target="tpu_custom_call" | custom-call | tf_op jit(solution)/shard_map/pallas_call | solution.py:269
  3.1 0.0 copy-done
  3.1 0.0 copy-done.1
  3.1 1.2 %shard_map.69 = (f32[32,384]{1,0:T(8,128)S(1)}, bf16[4096,64]{1,0:T(8,128)(2,1)S(1)}) custom-call(bf16[4096,256]{1,0:T(8,128)(2,1)S(1)} %shard_map.68.kept_ref, f32[32,256]{1,0:T(8,128)S(1)} %copy-done.1, bf16[32,4096]{1,0:T(8,128)(2,1)S(1)} %copy-done), custom_call_target="tpu_custom_call" | custom-call | tf_op jit(solution)/shard_map/pallas_call | solution.py:269
  4.3 0.5 collective-permute-start
  4.8 0.9 %collective-permute-done.other_ref = f32[32,384]{1,0:T(8,128)S(1)} collective-permute-done((f32[32,384]{1,0:T(8,128)S(1)}, f32[32,384]{1,0:T(8,128)S(1)}, u32[]{:S(2)}, u32[]{:S(2)}) %collective-permute-start) | collective-permute-done | bytes 49184 | tf_op jit(solution)/shard_map/ppermute | solution.py:323
  5.7 0.0 copy-done.2
  5.7 0.2 shard_map.70
  5.8 0.4 collective-permute-start.2
  6.2 3.8 %collective-permute-start.1 = (f32[40,128]{1,0:T(8,128)S(1)}, f32[40,128]{1,0:T(8,128)S(1)}, u32[]{:S(2)}, u32[]{:S(2)}) collective-permute-start(f32[40,128]{1,0:T(8,128)S(1)} %get-tuple-element.15), channel_id=1, source_target_pairs={{0,3},{2,1},{1,2},{3,0},{4,7},{6,5},{5,6},{7,4},{8,11},{10,9},{9,1... | collective-permute-start | bytes 61448 | tf_op jit(solution)/shard_map/ppermute | solution.py:328
  9.9 0.0 copy-done.3
  9.9 0.3 shard_map.71.pick_ref
  10.3 0.0 collective-permute-done.2.second_ref
  10.3 1.1 %collective-permute-done.1.first_ref = f32[40,128]{1,0:T(8,128)S(1)} collective-permute-done((f32[40,128]{1,0:T(8,128)S(1)}, f32[40,128]{1,0:T(8,128)S(1)}, u32[]{:S(2)}, u32[]{:S(2)}) %collective-permute-start.1) | collective-permute-done | bytes 20512 | tf_op jit(solution)/shard_map/ppermute | solution.py:328
  11.4 1.3 %shard_map.72 = (f32[32,256]{1,0:T(8,128)S(1)}, f32[32,256]{1,0:T(8,128)S(1)}) custom-call(f32[32,256]{1,0:T(8,128)S(1)} %get-tuple-element.14.updated_ref, s32[1,256]{1,0:T(1,128)S(1)} %bitcast.7, f32[40,128]{1,0:T(8,128)S(1)} %collective-permute-done.1.first_ref, f32[40,128]{1,0:T(8,128)S(1)} %collective-permute-done.2.second_ref, ...), custom_call_target="tpu_custom_call" | custom-call | tf_op jit(solution)/shard_map/pallas_call | solution.py:269
  12.7 0.2 collective-permute-start.3
  12.8 1.1 %collective-permute-done.3.other_ref = f32[32,256]{1,0:T(8,128)S(1)} collective-permute-done((f32[32,256]{1,0:T(8,128)S(1)}, f32[32,256]{1,0:T(8,128)S(1)}, u32[]{:S(2)}, u32[]{:S(2)}) %collective-permute-start.3) | collective-permute-done | bytes 32800 | tf_op jit(solution)/shard_map/ppermute | solution.py:323
  13.9 0.1 shard_map.73
  14.1 0.2 collective-permute-start.5
  14.2 2.9 %collective-permute-start.4 = (f32[40,128]{1,0:T(8,128)S(1)}, f32[40,128]{1,0:T(8,128)S(1)}, u32[]{:S(2)}, u32[]{:S(2)}) collective-permute-start(f32[40,128]{1,0:T(8,128)S(1)} %get-tuple-element.21), channel_id=1, source_target_pairs={{0,3},{2,1},{1,2},{3,0},{4,7},{6,5},{5,6},{7,4},{8,11},{10,9},{9,1... | collective-permute-start | bytes 61448 | tf_op jit(solution)/shard_map/ppermute | solution.py:328
  17.1 0.0 collective-permute-done.5.second_ref
  17.1 1.5 %collective-permute-done.4.first_ref = f32[40,128]{1,0:T(8,128)S(1)} collective-permute-done((f32[40,128]{1,0:T(8,128)S(1)}, f32[40,128]{1,0:T(8,128)S(1)}, u32[]{:S(2)}, u32[]{:S(2)}) %collective-permute-start.4) | collective-permute-done | bytes 20512 | tf_op jit(solution)/shard_map/ppermute | solution.py:328
  18.6 1.9 %shard_map.74 = (f32[32,256]{1,0:T(8,128)}, s16[8,144,128]{2,1,0:T(8,128)(2,1)S(1)}) custom-call(f32[32,256]{1,0:T(8,128)S(1)} %get-tuple-element.20.updated_ref, s32[1,256]{1,0:T(1,128)S(1)} %bitcast.9, f32[40,128]{1,0:T(8,128)S(1)} %collective-permute-done.4.first_ref, f32[40,128]{1,0:T(8,128)S(1)} %collective-permute-done.5.second_ref, ...), custom_call_target="tpu_custom_call" | custom-call | tf_op jit(solution)/shard_map/pallas_call | solution.py:269
  20.5 15.7 %all_to_all.10.got_ref = s16[8,144,128]{2,1,0:T(8,128)(2,1)S(1)} all-to-all(s16[8,144,128]{2,1,0:T(8,128)(2,1)S(1)} %get-tuple-element.23), channel_id=1, replica_groups=mesh['grp'=2,'tile'=8,'gene'=2] {'tile'}, dimensions={0} | all-to-all | bytes 589824 | tf_op jit(solution)/shard_map/all_to_all | solution.py:351
  36.3 0.2 shard_map.75
  36.5 11.5 %all_to_all.11 = bf16[8,8,2048]{2,1,0:T(8,128)(2,1)S(1)} all-to-all(bf16[8,8,2048]{2,1,0:T(8,128)(2,1)S(1)} %shard_map.75), channel_id=1, replica_groups=mesh['grp'=2,'tile'=8,'gene'=2] {'tile'}, dimensions={0} | all-to-all | bytes 524288 | tf_op jit(solution)/shard_map/all_to_all | solution.py:353
  48.0 0.7 %copy.8 = bf16[32,4096]{1,0:T(8,128)(2,1)} copy(bf16[32,4096]{1,0:T(8,128)(2,1)S(1)} %bitcast.10) | data formatting | bytes 524288
Async XLA Ops:
  0.6 2.5 %copy-start = (bf16[32,4096]{1,0:T(8,128)(2,1)S(1)}, bf16[32,4096]{1,0:T(8,128)(2,1)}, u32[]{:S(2)}) copy-start(bf16[32,4096]{1,0:T(8,128)(2,1)} %gene_ref.5) | copy-start | bytes 786436
  0.6 2.5 %copy-start.1 = (f32[32,256]{1,0:T(8,128)S(1)}, f32[32,256]{1,0:T(8,128)}, u32[]{:S(2)}) copy-start(f32[32,256]{1,0:T(8,128)} %cells_ref.3) | copy-start | bytes 98308
  0.7 5.0 %copy-start.2 = (s32[256]{0:T(256)S(1)}, s32[256]{0:T(256)}, u32[]{:S(2)}) copy-start(s32[256]{0:T(256)} %param.8) | copy-start | bytes 3076
  0.7 9.3 %copy-start.3 = (s32[8,256]{1,0:T(8,128)S(1)}, s32[8,256]{1,0:T(8,128)}, u32[]{:S(2)}) copy-start(s32[8,256]{1,0:T(8,128)} %neigh_ref.1) | copy-start | bytes 24580
  4.3 1.3 %collective-permute-start = (f32[32,384]{1,0:T(8,128)S(1)}, f32[32,384]{1,0:T(8,128)S(1)}, u32[]{:S(2)}, u32[]{:S(2)}) collective-permute-start(f32[32,384]{1,0:T(8,128)S(1)} %get-tuple-element.13.part_ref), channel_id=1, source_target_pairs={{0,1},{1,0},{2,3},{3,2},{4,5},{5,4},{6,7},{7,6},{8,9},{9,8},{10,11... | collective-permute-start | bytes 147464 | tf_op jit(solution)/shard_map/ppermute | solution.py:323
  5.8 4.4 %collective-permute-start.2 = (f32[40,128]{1,0:T(8,128)S(1)}, f32[40,128]{1,0:T(8,128)S(1)}, u32[]{:S(2)}, u32[]{:S(2)}) collective-permute-start(f32[40,128]{1,0:T(8,128)S(1)} %get-tuple-element.15), channel_id=1, source_target_pairs={{2,5},{4,3},{3,4},{5,2},{6,9},{8,7},{7,8},{9,6},{10,13},{12,11},{1... | collective-permute-start | bytes 61448 | tf_op jit(solution)/shard_map/ppermute | solution.py:328
  6.2 5.2 %collective-permute-start.1 = (f32[40,128]{1,0:T(8,128)S(1)}, f32[40,128]{1,0:T(8,128)S(1)}, u32[]{:S(2)}, u32[]{:S(2)}) collective-permute-start(f32[40,128]{1,0:T(8,128)S(1)} %get-tuple-element.15), channel_id=1, source_target_pairs={{0,3},{2,1},{1,2},{3,0},{4,7},{6,5},{5,6},{7,4},{8,11},{10,9},{9,1... | collective-permute-start | bytes 61448 | tf_op jit(solution)/shard_map/ppermute | solution.py:328
  12.7 1.2 %collective-permute-start.3 = (f32[32,256]{1,0:T(8,128)S(1)}, f32[32,256]{1,0:T(8,128)S(1)}, u32[]{:S(2)}, u32[]{:S(2)}) collective-permute-start(f32[32,256]{1,0:T(8,128)S(1)} %get-tuple-element.17.numer_ref), channel_id=1, source_target_pairs={{0,1},{1,0},{2,3},{3,2},{4,5},{5,4},{6,7},{7,6},{8,9},{9,8},{10,11... | collective-permute-start | bytes 98312 | tf_op jit(solution)/shard_map/ppermute | solution.py:323
  14.1 3.1 %collective-permute-start.5 = (f32[40,128]{1,0:T(8,128)S(1)}, f32[40,128]{1,0:T(8,128)S(1)}, u32[]{:S(2)}, u32[]{:S(2)}) collective-permute-start(f32[40,128]{1,0:T(8,128)S(1)} %get-tuple-element.21), channel_id=1, source_target_pairs={{2,5},{4,3},{3,4},{5,2},{6,9},{8,7},{7,8},{9,6},{10,13},{12,11},{1... | collective-permute-start | bytes 61448 | tf_op jit(solution)/shard_map/ppermute | solution.py:328
  14.2 4.4 %collective-permute-start.4 = (f32[40,128]{1,0:T(8,128)S(1)}, f32[40,128]{1,0:T(8,128)S(1)}, u32[]{:S(2)}, u32[]{:S(2)}) collective-permute-start(f32[40,128]{1,0:T(8,128)S(1)} %get-tuple-element.21), channel_id=1, source_target_pairs={{0,3},{2,1},{1,2},{3,0},{4,7},{6,5},{5,6},{7,4},{8,11},{10,9},{9,1... | collective-permute-start | bytes 61448 | tf_op jit(solution)/shard_map/ppermute | solution.py:328

commit v6 on v5

--- a/solution.py
+++ b/solution.py
@@ -1,3 +1,5 @@
+import functools
+
 import jax
 import jax.numpy as jnp
 from jax import lax
@@ -184,84 +186,169 @@
     return jnp.ceil(jnp.log2(jnp.maximum(values, 1e-30)))
 
 
-def coded_kernel(
-    updated_ref, tissue_ref, first_ref, second_ref, pick_ref, kept_ref,
-    rows_ref, cells_ref, sent_ref, totals_ref,
+def share_height(columns):
+    blocks = columns // LANES
+    return (blocks + blocks % 2) * ROWS + STAT_ROWS
+
+
+def encode(values, hden, target):
+    power = exponent(jnp.max(values, axis=1, keepdims=True))
+    coded = (values * (jnp.exp2(-power) * FULL) + 0.5).astype(jnp.int32)
+    hden_power = exponent(hden)
+    scaled = hden * jnp.exp2(-hden_power) * FULL
+    high = jnp.floor(scaled)
+    low = jnp.floor((scaled - high) * FULL)
+    lane = lax.broadcasted_iota(jnp.int32, (ROWS, LANES), 1)
+    marks = jnp.zeros((ROWS, LANES), jnp.float32)
+    for at, value in enumerate((power, hden_power, high, low)):
+        marks = jnp.where(lane == at, value, marks)
+    blank = jnp.zeros((ROWS, LANES), jnp.int32)
+    blocks = [coded[:, at : at + LANES] for at in range(0, values.shape[1], LANES)]
+    blocks += [blank] * (len(blocks) % 2) + [marks.astype(jnp.int32), blank]
+    for i in range(0, len(blocks), 2):
+        target[i * ROWS : (i + 2) * ROWS] = jnp.concatenate(
+            blocks[i : i + 2], axis=0
+        ).astype(jnp.int16)
+
+
+def decode(source, columns):
+    def number(start):
+        return source[start : start + 2 * ROWS].astype(jnp.int32).astype(jnp.float32)
+
+    height = source.shape[0]
+    marks = number(height - STAT_ROWS)[:ROWS]
+    scale = jnp.exp2(marks[:, :1]) / FULL
+    hden = (marks[:, 2:3] + marks[:, 3:4] / FULL) * (jnp.exp2(marks[:, 1:2]) / FULL)
+    blocks = []
+    for start in range(0, height - STAT_ROWS, 2 * ROWS):
+        both = number(start)
+        blocks += [both[:ROWS] * scale, both[ROWS:] * scale]
+    return jnp.concatenate(blocks[: columns // LANES], axis=1), hden
+
+
+def last_pass(
+    updated_ref, tissue_ref, first_ref, second_ref, pick_ref, kept_ref, rows_ref,
+    cells_ref, totals_ref,
 ):
-    rank, genes = totals_ref.shape
-    tiles = sent_ref.shape[0]
-    groups = rank // ROWS
-    columns = genes * groups // tiles
+    rank, genes = totals_ref.shape[0], kept_ref.shape[0]
     cells, flags = smoothed(updated_ref, tissue_ref, first_ref, second_ref, pick_ref)
     cells_ref[...] = cells
     masked = jnp.where(flags, cells, 0.0)
     factor_rows = jnp.concatenate(split(cells), axis=0)
-    masked_parts = jnp.concatenate(split(masked), axis=0)
-    masked_columns = masked_parts.astype(jnp.float32).T.astype(jnp.bfloat16)
+    masked_rows = jnp.concatenate(split(masked), axis=0)
+    masked_columns = masked_rows.astype(jnp.float32).T.astype(jnp.bfloat16)
     hden = jnp.sum(masked, axis=1, keepdims=True)
-    power = exponent(hden)
-    scaled = hden * jnp.exp2(-power) * FULL
-    high = jnp.floor(scaled)
-    lane = lax.broadcasted_iota(jnp.int32, (rank, LANES), 1)
-    stats = jnp.zeros((rank, LANES), jnp.float32)
-    for at, value in enumerate((power, high, jnp.floor((scaled - high) * FULL))):
-        stats = jnp.where(lane == at + 1, value, stats)
+    totals_ref[:, genes:] = jnp.broadcast_to(hden, (rank, LANES))
     for at, counts in runs_of(kept_ref, 1024):
         end = at + counts.shape[0]
         ratio = ratio_of(counts, rows_ref[at:end], factor_rows)
         both = jnp.dot(ratio, masked_columns, preferred_element_type=jnp.float32).T
         totals_ref[:, at:end] = both[:rank] + both[rank:]
-    blank = jnp.zeros((ROWS, LANES), jnp.int32)
-    for column in range(genes // columns):
-        totals = totals_ref[:, column * columns : (column + 1) * columns]
-        power = exponent(jnp.max(totals, axis=1, keepdims=True))
-        coded = (totals * (jnp.exp2(-power) * FULL) + 0.5).astype(jnp.int32)
-        marks = jnp.where(lane == 0, power, stats).astype(jnp.int32)
-        for group in range(groups):
-            tile = group * (genes // columns) + column
-            ranks = slice(group * ROWS, (group + 1) * ROWS)
-            blocks = [coded[ranks, at : at + LANES] for at in range(0, columns, LANES)]
-            blocks += [blank] * (len(blocks) % 2) + [marks[ranks], blank]
-            for i in range(0, len(blocks), 2):
-                sent_ref[tile, i * ROWS : (i + 2) * ROWS] = jnp.concatenate(
-                    blocks[i : i + 2], axis=0
-                ).astype(jnp.int16)
-
-
-def fresh_kernel(got_ref, gene_ref, fresh_ref):
-    tiles, height, _ = got_ref.shape
-    columns = fresh_ref.shape[2]
-    groups = gene_ref.shape[0] // ROWS
+
+
+def shares_kernel(*refs):
+    *passed, sent_ref, totals_ref = refs
+    last_pass(*passed, totals_ref)
+    rank = totals_ref.shape[0]
+    genes = totals_ref.shape[1] - LANES
+    across = sent_ref.shape[0] * ROWS // rank
+    columns = genes // across
+    for tile in range(sent_ref.shape[0]):
+        ranks = pl.ds(tile // across * ROWS, ROWS)
+        start = tile % across * columns
+        encode(
+            totals_ref[ranks, start : start + columns],
+            totals_ref[ranks, genes : genes + 1],
+            sent_ref.at[tile],
+        )
+
+
+def distance_kernel(*refs):
+    passed, (*sent_refs, own_ref, totals_ref, coded_ref) = refs[:8], refs[8:]
+    last_pass(*passed, totals_ref)
+    tiles, height, _ = coded_ref.shape
+    genes = totals_ref.shape[1] - LANES
+    columns = genes // 2
+    for tile in range(tiles):
+        ranks = slice(tile // 2 * ROWS, (tile // 2 + 1) * ROWS)
+        start = tile % 2 * columns
+        encode(
+            totals_ref[ranks, start : start + columns],
+            totals_ref[ranks, genes : genes + 1],
+            coded_ref.at[tile],
+        )
+    tile = lax.axis_index("tile")
+    for distance in range(tiles // 2):
+        there = tile ^ (2 * distance)
+        own_ref[distance * height : (distance + 1) * height] = coded_ref[there]
+        place = sent_refs[(distance or tiles // 2 - 1) - 1]
+        start = 0 if distance else height
+        place[start : start + height] = coded_ref[there ^ 1]
+
+
+def column_kernel(distance, columns, got_ref, own_ref, sent_ref):
+    height = sent_ref.shape[0]
+    start = 0 if distance else height
+    values, hden = decode(got_ref.at[start : start + height], columns)
+    start = height * distance
+    more, more_hden = decode(own_ref.at[start : start + height], columns)
+    encode(values + more, hden + more_hden, sent_ref)
+
+
+def fresh_of(hnum, hden, gene_ref, across):
+    columns = hnum.shape[1]
     here = lax.axis_index("tile")
-    across = tiles // groups
-
-    def number(coded):
-        return coded.astype(jnp.int32).astype(jnp.float32)
-
-    def twice(values):
-        return jnp.concatenate([values, values], axis=0)
-
-    hden = jnp.zeros((ROWS, 1), jnp.float32)
-    scales = []
-    for tile in range(tiles):
-        marks = number(got_ref[tile, height - STAT_ROWS :])[:ROWS]
-        scales.append(twice(jnp.exp2(marks[:, :1]) / FULL))
-        hden += (marks[:, 2:3] + marks[:, 3:4] / FULL) * (jnp.exp2(marks[:, 1:2]) / FULL)
-    totals = []
-    for at in range(0, height - STAT_ROWS, 2 * ROWS):
-        total = jnp.zeros((2 * ROWS, LANES), jnp.float32)
-        for tile in range(tiles):
-            total += number(got_ref[tile, at : at + 2 * ROWS]) * scales[tile]
-        totals += [total[:ROWS], total[ROWS:]]
-    hnum = jnp.concatenate(totals[: columns // LANES], axis=1)
     place = pl.multiple_of(lax.rem(here, across) * columns, LANES)
     every = gene_ref[:, pl.ds(place, columns)].astype(jnp.float32)
     hf = every[:ROWS]
-    for group in range(1, groups):
+    for group in range(1, gene_ref.shape[0] // ROWS):
         hf = jnp.where(here // across == group, every[group * ROWS : (group + 1) * ROWS], hf)
-    fresh = (hf * hnum / hden).astype(jnp.bfloat16)
+    return (hf * hnum / hden).astype(jnp.bfloat16)
+
+
+def all_shares_kernel(got_ref, gene_ref, fresh_ref):
+    tiles, _, columns = fresh_ref.shape
+    hnum, hden = decode(got_ref.at[0], columns)
+    for tile in range(1, tiles):
+        more, more_hden = decode(got_ref.at[tile], columns)
+        hnum += more
+        hden += more_hden
+    fresh = fresh_of(hnum, hden, gene_ref, tiles * ROWS // gene_ref.shape[0])
     for tile in range(tiles):
         fresh_ref[tile] = fresh
+
+
+def fresh_kernel(*refs):
+    *got_refs, gene_ref, fresh_ref = refs
+    hnum, hden = 0.0, 0.0
+    for ref in got_refs:
+        more, more_hden = decode(ref, fresh_ref.shape[1])
+        hnum += more
+        hden += more_hden
+    fresh_ref[...] = fresh_of(hnum, hden, gene_ref, 2)
+
+
+def spread_kernel(*refs):
+    *share_refs, out_ref = refs
+    groups = len(share_refs) // 2
+    columns = share_refs[0].shape[1]
+    tile = lax.axis_index("tile")
+    here, side = tile // 2, lax.rem(tile, 2)
+    shares = [ref[...].astype(jnp.float32) for ref in share_refs]
+    for column in range(2):
+        own = side == column
+        picked = []
+        for group in range(groups):
+            distance = here ^ group
+            share = jnp.where(own, shares[0], shares[groups])
+            for at in range(1, groups):
+                either = jnp.where(own, shares[at], shares[groups + at])
+                share = jnp.where(distance == at, either, share)
+            picked.append(share)
+        for group in range(0, groups, 2):
+            out_ref[
+                group * ROWS : (group + 2) * ROWS, column * columns : (column + 1) * columns
+            ] = jnp.concatenate(picked[group : group + 2], axis=0).astype(jnp.bfloat16)
 
 
 def call(kernel, outs, scratch=(), specs=None, limit=VMEM_BYTES):
@@ -340,19 +427,58 @@
         numer, swapped(numer), gsum, cells, flag_row
     )
     across = tiles * ROWS // rank
+    groups = rank // ROWS
     columns = genes // across
-    blocks = columns // LANES
-    height = (blocks + blocks % 2) * ROWS + STAT_ROWS
-    cells, sent = call(
-        coded_kernel,
-        (factor, shape((tiles, height, LANES), jnp.int16)),
-        [pltpu.VMEM((rank, genes), jnp.float32)],
-    )(*around(updated, edges), rows)
-    got = lax.all_to_all(sent, "tile", 0, 0)
-    fresh = call(fresh_kernel, shape((tiles, ROWS, columns), jnp.bfloat16))(got, gene_factor)
-    every = lax.all_to_all(fresh, "tile", 0, 0)
-    every = every.reshape(rank // ROWS, across, ROWS, columns)
-    return cells, every.transpose(0, 2, 1, 3).reshape(rank, genes)
+    height = share_height(columns)
+    last = (*around(updated, edges), rows)
+    totals = [pltpu.VMEM((rank, genes + LANES), jnp.float32)]
+    if across != 2 or groups != 4 or halves != 2:
+        cells, sent = call(
+            shares_kernel, (factor, shape((tiles, height, LANES), jnp.int16)), totals
+        )(*last)
+        got = lax.all_to_all(sent, "tile", 0, 0)
+        fresh = call(all_shares_kernel, shape((tiles, ROWS, columns), jnp.bfloat16))(
+            got, gene_factor
+        )
+        every = lax.all_to_all(fresh, "tile", 0, 0).reshape(groups, across, ROWS, columns)
+        return cells, every.transpose(0, 2, 1, 3).reshape(rank, genes)
+
+    def moved(array, step, cross):
+        pairs = [
+            (tile * halves + gene, (tile ^ step) * halves + (gene ^ cross))
+            for tile in range(tiles)
+            for gene in range(halves)
+        ]
+        return lax.ppermute(array, ("tile", "gene"), pairs)
+
+    one = shape((height, LANES), jnp.int16)
+    cells, *sent, own = call(
+        distance_kernel,
+        (
+            factor,
+            *[one] * (groups - 2),
+            shape((2 * height, LANES), jnp.int16),
+            shape((groups * height, LANES), jnp.int16),
+        ),
+        totals + [pltpu.VMEM((tiles, height, LANES), jnp.int16)],
+    )(*last)
+    distances = range(groups - 1, 0, -1)
+    own = moved(own, 0, 1)
+    got = {distance: moved(sent[distance - 1], 1, 1) for distance in distances}
+    got[0] = got[groups - 1]
+    summed = []
+    for distance in (*distances, 0):
+        both = call(functools.partial(column_kernel, distance, columns), one)(
+            got[distance], own
+        )
+        summed.append(moved(both, 2 * distance, 1))
+    fresh = call(fresh_kernel, shape((ROWS, columns), jnp.bfloat16))(*summed, gene_factor)
+    shares, others = [fresh], [moved(fresh, 1, 0)]
+    passing = {distance: moved(fresh, 2 * distance, 1) for distance in distances}
+    for distance in range(1, groups):
+        shares.append(moved(passing[distance], 0, 1))
+        others.append(moved(passing[distance], 1, 1))
+    return cells, call(spread_kernel, shape((rank, genes), jnp.bfloat16))(*shares, *others)
 
 
 def solution(mesh):

time: 48.9 us -> 47.5 us (0.971)
  blocking collectives: 27.2 us -> 0 us
  starting transfers between devices: 7.82 us -> 25 us
  waiting for transfers between devices: 4.57 us -> 12.1 us
  Pallas kernels: 7.61 us -> 9.5 us
  local copies, waits for them, and re-layouts: 0.72 us -> 0.02 us
    all_to_all x2 -> x0, blocking collectives: 27.2 us -> none  [the longest x1 15.7 us: on_device(): got = lax.all_to_all(sent, 'tile', 0, 0)]
    ppermute x0 -> x18, starting transfers between devices: none -> 17.2 us  [moved(): return lax.ppermute(array, ('tile', 'gene'), pairs)]
    ppermute x0 -> x18, waiting for transfers between devices: none -> 7.52 us  [moved(): return lax.ppermute(array, ('tile', 'gene'), pairs)]
    pallas_call x8 -> x13, Pallas kernels: 7.61 us -> 9.5 us  [call(): pl.pallas_call(kernel, out_shape=outs, in_specs=specs or [whole] * len(ar...]
    unnamed x9 -> x8, local copies, waits for them, and re-layouts: 0.72 us -> 0.02 us
  transfers between devices with their start and end apart: 6 -> 24, of which waited for: 4 -> 11; matrix products, arithmetic and copies ran while one was open for 0% -> 0% of each run, Pallas kernels for 1% -> 2%
where the time goes in v6:
time: 47.5 us; the launch traced here: 47.4 us
  starting transfers between devices  25 us (53%)
  waiting for transfers between devices  12.1 us (25%)
  Pallas kernels  9.5 us (20%)
  between operations  0.79 us (2%)
    ppermute x18, starting transfers between devices, moved(): return lax.ppermute(array, ('tile', 'gene'), pairs)  17.2 us
    pallas_call x13, Pallas kernels, call(): pl.pallas_call(kernel, out_shape=outs, in_specs=specs or [whole] * len(ar...  9.5 us
    ppermute x18, waiting for transfers between devices, moved(): return lax.ppermute(array, ('tile', 'gene'), pairs)  7.52 us
    ppermute x4, starting transfers between devices, around(): lax.ppermute(edges, ('tile', 'gene'), beside(tiles, halves, offset))  7.2 us
    ppermute x4, waiting for transfers between devices, around(): lax.ppermute(edges, ('tile', 'gene'), beside(tiles, halves, offset))  2.63 us
    ppermute x2, waiting for transfers between devices, swapped(): return lax.ppermute(part, 'gene', [(0, 1), (1, 0)])  1.94 us
  transfers between devices with their start and end apart: 24, of which 11 were waited for; matrix products, arithmetic and copies ran while one was open for 0% of the time, Pallas kernels for 2%

profile of v6, /device:TPU:0, one launch (start us, length us, event | category | flops | bytes accessed | tf_op | source)
XLA Modules:
  0.0 47.4 jit_solution(4684493353401836756)
XLA Ops:
  0.6 0.0 copy-start
  0.7 2.4 %shard_map.68.kept_ref.refs_5_ = bf16[4096,256]{1,0:T(8,128)(2,1)S(1)} custom-call(s32[256,4096]{1,0:T(8,128)} %counts_ref.1), custom_call_target="tpu_custom_call" | custom-call | tf_op jit(solution)/shard_map/pallas_call | solution.py:356
  3.1 0.0 copy-done
  3.1 0.0 copy-done.1
  3.1 1.2 %shard_map.69 = (f32[32,384]{1,0:T(8,128)S(1)}, bf16[4096,64]{1,0:T(8,128)(2,1)S(1)}) custom-call(bf16[4096,256]{1,0:T(8,128)(2,1)S(1)} %shard_map.68.kept_ref.refs_5_, f32[32,256]{1,0:T(8,128)S(1)} %copy-done.1, bf16[32,4096]{1,0:T(8,128)(2,1)S(1)} %copy-done), custom_call_target="tpu_custom_call" | custom-call | tf_op jit(solution)/shard_map/pallas_call | solution.py:356
  4.3 0.5 collective-permute-start
  4.8 0.9 %collective-permute-done.other_ref = f32[32,384]{1,0:T(8,128)S(1)} collective-permute-done((f32[32,384]{1,0:T(8,128)S(1)}, f32[32,384]{1,0:T(8,128)S(1)}, u32[]{:S(2)}, u32[]{:S(2)}) %collective-permute-start) | collective-permute-done | bytes 49184 | tf_op jit(solution)/shard_map/ppermute | solution.py:410
  5.7 0.2 shard_map.70
  5.8 0.4 collective-permute-start.2
  6.2 3.8 %collective-permute-start.1 = (f32[40,128]{1,0:T(8,128)S(1)}, f32[40,128]{1,0:T(8,128)S(1)}, u32[]{:S(2)}, u32[]{:S(2)}) collective-permute-start(f32[40,128]{1,0:T(8,128)S(1)} %get-tuple-element.18), channel_id=1, source_target_pairs={{0,3},{2,1},{1,2},{3,0},{4,7},{6,5},{5,6},{7,4},{8,11},{10,9},{9,1... | collective-permute-start | bytes 61448 | tf_op jit(solution)/shard_map/ppermute | solution.py:415
  9.9 0.3 shard_map.71.pick_ref.refs_4_
  10.3 0.0 collective-permute-done.2.second_ref
  10.3 1.1 %collective-permute-done.1.first_ref = f32[40,128]{1,0:T(8,128)S(1)} collective-permute-done((f32[40,128]{1,0:T(8,128)S(1)}, f32[40,128]{1,0:T(8,128)S(1)}, u32[]{:S(2)}, u32[]{:S(2)}) %collective-permute-start.1) | collective-permute-done | bytes 20512 | tf_op jit(solution)/shard_map/ppermute | solution.py:415
  11.4 1.3 %shard_map.72 = (f32[32,256]{1,0:T(8,128)S(1)}, f32[32,256]{1,0:T(8,128)S(1)}) custom-call(f32[32,256]{1,0:T(8,128)S(1)} %get-tuple-element.17.updated_ref, s32[1,256]{1,0:T(1,128)S(1)} %bitcast.2, f32[40,128]{1,0:T(8,128)S(1)} %collective-permute-done.1.first_ref, f32[40,128]{1,0:T(8,128)S(1)} %collective-permute-done.2.second_ref, ...), custom_call_target="tpu_custom_call" | custom-call | tf_op jit(solution)/shard_map/pallas_call | solution.py:356
  12.7 0.2 collective-permute-start.3
  12.8 1.1 %collective-permute-done.3.other_ref = f32[32,256]{1,0:T(8,128)S(1)} collective-permute-done((f32[32,256]{1,0:T(8,128)S(1)}, f32[32,256]{1,0:T(8,128)S(1)}, u32[]{:S(2)}, u32[]{:S(2)}) %collective-permute-start.3) | collective-permute-done | bytes 32800 | tf_op jit(solution)/shard_map/ppermute | solution.py:410
  13.9 0.1 shard_map.73
  14.1 0.2 collective-permute-start.5
  14.2 2.9 %collective-permute-start.4 = (f32[40,128]{1,0:T(8,128)S(1)}, f32[40,128]{1,0:T(8,128)S(1)}, u32[]{:S(2)}, u32[]{:S(2)}) collective-permute-start(f32[40,128]{1,0:T(8,128)S(1)} %get-tuple-element.24), channel_id=1, source_target_pairs={{0,3},{2,1},{1,2},{3,0},{4,7},{6,5},{5,6},{7,4},{8,11},{10,9},{9,1... | collective-permute-start | bytes 61448 | tf_op jit(solution)/shard_map/ppermute | solution.py:415
  17.1 0.0 collective-permute-done.5.refs_3_
  17.1 1.5 %collective-permute-done.4.refs_2_ = f32[40,128]{1,0:T(8,128)S(1)} collective-permute-done((f32[40,128]{1,0:T(8,128)S(1)}, f32[40,128]{1,0:T(8,128)S(1)}, u32[]{:S(2)}, u32[]{:S(2)}) %collective-permute-start.4) | collective-permute-done | bytes 20512 | tf_op jit(solution)/shard_map/ppermute | solution.py:415
  18.6 2.2 %shard_map.74 = (f32[32,256]{1,0:T(8,128)}, s16[144,128]{1,0:T(8,128)(2,1)S(1)}, s16[144,128]{1,0:T(8,128)(2,1)S(1)}, s16[288,128]{1,0:T(8,128)(2,1)S(1)}, s16[576,128]{1,0:T(8,128)(2,1)S(1)}) custom-call(f32[32,256]{1,0:T(8,128)S(1)} %get-tuple-element.23.refs_0_, s32[1,256]{1,0:T(1,128)S(1)} %bitcast.4, f32[40,128]{1,0:T(8,128)S(1)} %collective-permute-done.4.refs_2_, ...), custom_call_target="tpu_custom_call" | custom-call | tf_op jit(solution)/shard_map/pallas_call | solution.py:356
  20.8 0.1 collective-permute-start.7
  21.0 2.0 %collective-permute-start.6 = (s16[288,128]{1,0:T(8,128)(2,1)S(1)}, s16[288,128]{1,0:T(8,128)(2,1)S(1)}, u32[]{:S(2)}, u32[]{:S(2)}) collective-permute-start(s16[288,128]{1,0:T(8,128)(2,1)S(1)} %get-tuple-element.26), channel_id=1, source_target_pairs={{0,3},{1,2},{2,1},{3,0},{4,7},{5,6},{6,5},{7,4},{8,11},{9,10},{10,... | collective-permute-start | bytes 221192 | tf_op jit(solution)/shard_map/ppermute | solution.py:452
  22.9 0.0 collective-permute-start.9
  23.0 1.7 %collective-permute-start.11 = (s16[144,128]{1,0:T(8,128)(2,1)S(1)}, s16[144,128]{1,0:T(8,128)(2,1)S(1)}, u32[]{:S(2)}, u32[]{:S(2)}) collective-permute-start(s16[144,128]{1,0:T(8,128)(2,1)S(1)} %get-tuple-element.29), channel_id=1, source_target_pairs={{0,3},{1,2},{2,1},{3,0},{4,7},{5,6},{6,5},{7,4},{8,11},{9,10},{10,... | collective-permute-start | bytes 110600 | tf_op jit(solution)/shard_map/ppermute | solution.py:452
  24.7 0.8 %collective-permute-done.6.got_ref = s16[288,128]{1,0:T(8,128)(2,1)S(1)} collective-permute-done((s16[288,128]{1,0:T(8,128)(2,1)S(1)}, s16[288,128]{1,0:T(8,128)(2,1)S(1)}, u32[]{:S(2)}, u32[]{:S(2)}) %collective-permute-start.6) | collective-permute-done | bytes 73760 | tf_op jit(solution)/shard_map/ppermute | solution.py:452
  25.5 0.0 collective-permute-done.7.own_ref
  25.5 0.2 shard_map.75
  25.7 4.3 %collective-permute-start.8 = (s16[144,128]{1,0:T(8,128)(2,1)S(1)}, s16[144,128]{1,0:T(8,128)(2,1)S(1)}, u32[]{:S(2)}, u32[]{:S(2)}) collective-permute-start(s16[144,128]{1,0:T(8,128)(2,1)S(1)} %shard_map.75), channel_id=1, source_target_pairs={{0,13},{1,12},{2,15},{3,14},{4,9},{5,8},{6,11},{7,10},{8,5},{9,4},... | collective-permute-start | bytes 110600 | tf_op jit(solution)/shard_map/ppermute | solution.py:452
  30.0 0.2 shard_map.78
  30.2 0.1 collective-permute-start.13
  30.3 0.0 collective-permute-done.9.got_ref
  30.3 0.2 shard_map.76
  30.5 0.1 collective-permute-start.10
  30.6 0.0 collective-permute-done.11.got_ref
  30.6 0.2 shard_map.77
  30.8 0.7 %collective-permute-start.12 = (s16[144,128]{1,0:T(8,128)(2,1)S(1)}, s16[144,128]{1,0:T(8,128)(2,1)S(1)}, u32[]{:S(2)}, u32[]{:S(2)}) collective-permute-start(s16[144,128]{1,0:T(8,128)(2,1)S(1)} %shard_map.77), channel_id=1, source_target_pairs={{0,5},{1,4},{2,7},{3,6},{4,1},{5,0},{6,3},{7,2},{8,13},{9,12},{10,... | collective-permute-start | bytes 110600 | tf_op jit(solution)/shard_map/ppermute | solution.py:452
  31.5 0.2 collective-permute-done.8.refs_0_
  31.8 0.0 collective-permute-done.13.refs_3_
  31.8 3.1 %collective-permute-done.10.refs_1_ = s16[144,128]{1,0:T(8,128)(2,1)S(1)} collective-permute-done((s16[144,128]{1,0:T(8,128)(2,1)S(1)}, s16[144,128]{1,0:T(8,128)(2,1)S(1)}, u32[]{:S(2)}, u32[]{:S(2)}) %collective-permute-start.10) | collective-permute-done | bytes 36896 | tf_op jit(solution)/shard_map/ppermute | solution.py:452
  34.9 0.0 collective-permute-done.12.refs_2_
  34.9 0.2 shard_map.79.refs_0_
  35.1 1.9 %collective-permute-start.18 = (bf16[8,2048]{1,0:T(8,128)(2,1)S(1)}, bf16[8,2048]{1,0:T(8,128)(2,1)S(1)}, u32[]{:S(2)}, u32[]{:S(2)}) collective-permute-start(bf16[8,2048]{1,0:T(8,128)(2,1)S(1)} %shard_map.79.refs_0_), channel_id=1, source_target_pairs={{0,13},{1,12},{2,15},{3,14},{4,9},{5,8},{6,11},{7,10},{8,5},{9,4},... | collective-permute-start | bytes 98312 | tf_op jit(solution)/shard_map/ppermute | solution.py:452
  37.0 0.5 %collective-permute-start.16 = (bf16[8,2048]{1,0:T(8,128)(2,1)S(1)}, bf16[8,2048]{1,0:T(8,128)(2,1)S(1)}, u32[]{:S(2)}, u32[]{:S(2)}) collective-permute-start(bf16[8,2048]{1,0:T(8,128)(2,1)S(1)} %shard_map.79.refs_0_), channel_id=1, source_target_pairs={{0,9},{1,8},{2,11},{3,10},{4,13},{5,12},{6,15},{7,14},{8,1},{9,0},... | collective-permute-start | bytes 98312 | tf_op jit(solution)/shard_map/ppermute | solution.py:452
  37.5 0.9 %collective-permute-start.20 = (bf16[8,2048]{1,0:T(8,128)(2,1)S(1)}, bf16[8,2048]{1,0:T(8,128)(2,1)S(1)}, u32[]{:S(2)}, u32[]{:S(2)}) collective-permute-start(bf16[8,2048]{1,0:T(8,128)(2,1)S(1)} %shard_map.79.refs_0_), channel_id=1, source_target_pairs={{0,2},{1,3},{2,0},{3,1},{4,6},{5,7},{6,4},{7,5},{8,10},{9,11},{10,... | collective-permute-start | bytes 98312 | tf_op jit(solution)/shard_map/ppermute | solution.py:452
  38.4 1.3 %collective-permute-start.14 = (bf16[8,2048]{1,0:T(8,128)(2,1)S(1)}, bf16[8,2048]{1,0:T(8,128)(2,1)S(1)}, u32[]{:S(2)}, u32[]{:S(2)}) collective-permute-start(bf16[8,2048]{1,0:T(8,128)(2,1)S(1)} %shard_map.79.refs_0_), channel_id=1, source_target_pairs={{0,5},{1,4},{2,7},{3,6},{4,1},{5,0},{6,3},{7,2},{8,13},{9,12},{10,... | collective-permute-start | bytes 98312 | tf_op jit(solution)/shard_map/ppermute | solution.py:452
  39.8 0.5 %collective-permute-done.18 = bf16[8,2048]{1,0:T(8,128)(2,1)S(1)} collective-permute-done((bf16[8,2048]{1,0:T(8,128)(2,1)S(1)}, bf16[8,2048]{1,0:T(8,128)(2,1)S(1)}, u32[]{:S(2)}, u32[]{:S(2)}) %collective-permute-start.18) | collective-permute-done | bytes 32800 | tf_op jit(solution)/shard_map/ppermute | solution.py:452
  40.3 1.1 %collective-permute-start.23 = (bf16[8,2048]{1,0:T(8,128)(2,1)S(1)}, bf16[8,2048]{1,0:T(8,128)(2,1)S(1)}, u32[]{:S(2)}, u32[]{:S(2)}) collective-permute-start(bf16[8,2048]{1,0:T(8,128)(2,1)S(1)} %collective-permute-done.18), channel_id=1, source_target_pairs={{0,3},{1,2},{2,1},{3,0},{4,7},{5,6},{6,5},{7,4},{8,11},{9,10},{10,... | collective-permute-start | bytes 98312 | tf_op jit(solution)/shard_map/ppermute | solution.py:452
  41.4 0.1 collective-permute-start.19
  41.5 0.9 %collective-permute-done.16 = bf16[8,2048]{1,0:T(8,128)(2,1)S(1)} collective-permute-done((bf16[8,2048]{1,0:T(8,128)(2,1)S(1)}, bf16[8,2048]{1,0:T(8,128)(2,1)S(1)}, u32[]{:S(2)}, u32[]{:S(2)}) %collective-permute-start.16) | collective-permute-done | bytes 32800 | tf_op jit(solution)/shard_map/ppermute | solution.py:452
  42.4 0.3 collective-permute-start.22
  42.8 0.0 collective-permute-done.20.refs_4_
  42.8 0.1 collective-permute-start.17
  42.9 0.0 collective-permute-done.14
  42.9 1.4 %collective-permute-start.21 = (bf16[8,2048]{1,0:T(8,128)(2,1)S(1)}, bf16[8,2048]{1,0:T(8,128)(2,1)S(1)}, u32[]{:S(2)}, u32[]{:S(2)}) collective-permute-start(bf16[8,2048]{1,0:T(8,128)(2,1)S(1)} %collective-permute-done.14), channel_id=1, source_target_pairs={{0,3},{1,2},{2,1},{3,0},{4,7},{5,6},{6,5},{7,4},{8,11},{9,10},{10,... | collective-permute-start | bytes 98312 | tf_op jit(solution)/shard_map/ppermute | solution.py:452
  44.3 0.0 collective-permute-done.23.refs_7_
  44.3 0.4 collective-permute-start.15
  44.7 0.0 collective-permute-done.19.refs_3_
  44.7 1.1 %collective-permute-done.22.refs_6_ = bf16[8,2048]{1,0:T(8,128)(2,1)S(1)} collective-permute-done((bf16[8,2048]{1,0:T(8,128)(2,1)S(1)}, bf16[8,2048]{1,0:T(8,128)(2,1)S(1)}, u32[]{:S(2)}, u32[]{:S(2)}) %collective-permute-start.22) | collective-permute-done | bytes 32800 | tf_op jit(solution)/shard_map/ppermute | solution.py:452
  45.9 0.0 collective-permute-done.17.refs_2_
  45.9 0.7 %collective-permute-done.21.refs_5_ = bf16[8,2048]{1,0:T(8,128)(2,1)S(1)} collective-permute-done((bf16[8,2048]{1,0:T(8,128)(2,1)S(1)}, bf16[8,2048]{1,0:T(8,128)(2,1)S(1)}, u32[]{:S(2)}, u32[]{:S(2)}) %collective-permute-start.21) | collective-permute-done | bytes 32800 | tf_op jit(solution)/shard_map/ppermute | solution.py:452
  46.5 0.0 collective-permute-done.15.refs_1_
  46.5 0.8 %shard_map.80 = bf16[32,4096]{1,0:T(8,128)(2,1)} custom-call(bf16[8,2048]{1,0:T(8,128)(2,1)S(1)} %shard_map.79.refs_0_, bf16[8,2048]{1,0:T(8,128)(2,1)S(1)} %collective-permute-done.15.refs_1_, bf16[8,2048]{1,0:T(8,128)(2,1)S(1)} %collective-permute-done.17.refs_2_, bf16[8,2048]{1,0:T(8,128)(2,1)S(1)} %collective-permute-done.19.refs_3_, ...), custom_call_target="tpu_custom_call" | custom-call | tf_op jit(solution)/shard_map/pallas_call | solution.py:356
  (5 shorter events, 0.0 us)
Async XLA Ops:
  0.6 2.5 %copy-start = (bf16[32,4096]{1,0:T(8,128)(2,1)S(1)}, bf16[32,4096]{1,0:T(8,128)(2,1)}, u32[]{:S(2)}) copy-start(bf16[32,4096]{1,0:T(8,128)(2,1)} %refs_4_.1) | copy-start | bytes 786436
  0.6 2.5 %copy-start.1 = (f32[32,256]{1,0:T(8,128)S(1)}, f32[32,256]{1,0:T(8,128)}, u32[]{:S(2)}) copy-start(f32[32,256]{1,0:T(8,128)} %cells_ref.3) | copy-start | bytes 98308
  0.7 5.0 %copy-start.2 = (s32[256]{0:T(256)S(1)}, s32[256]{0:T(256)}, u32[]{:S(2)}) copy-start(s32[256]{0:T(256)} %param.8) | copy-start | bytes 3076
  0.7 9.3 %copy-start.3 = (s32[8,256]{1,0:T(8,128)S(1)}, s32[8,256]{1,0:T(8,128)}, u32[]{:S(2)}) copy-start(s32[8,256]{1,0:T(8,128)} %neigh_ref.1) | copy-start | bytes 24580
  4.3 1.3 %collective-permute-start = (f32[32,384]{1,0:T(8,128)S(1)}, f32[32,384]{1,0:T(8,128)S(1)}, u32[]{:S(2)}, u32[]{:S(2)}) collective-permute-start(f32[32,384]{1,0:T(8,128)S(1)} %get-tuple-element.16.part_ref), channel_id=1, source_target_pairs={{0,1},{1,0},{2,3},{3,2},{4,5},{5,4},{6,7},{7,6},{8,9},{9,8},{10,11... | collective-permute-start | bytes 147464 | tf_op jit(solution)/shard_map/ppermute | solution.py:410
  5.8 4.4 %collective-permute-start.2 = (f32[40,128]{1,0:T(8,128)S(1)}, f32[40,128]{1,0:T(8,128)S(1)}, u32[]{:S(2)}, u32[]{:S(2)}) collective-permute-start(f32[40,128]{1,0:T(8,128)S(1)} %get-tuple-element.18), channel_id=1, source_target_pairs={{2,5},{4,3},{3,4},{5,2},{6,9},{8,7},{7,8},{9,6},{10,13},{12,11},{1... | collective-permute-start | bytes 61448 | tf_op jit(solution)/shard_map/ppermute | solution.py:415
  6.2 5.2 %collective-permute-start.1 = (f32[40,128]{1,0:T(8,128)S(1)}, f32[40,128]{1,0:T(8,128)S(1)}, u32[]{:S(2)}, u32[]{:S(2)}) collective-permute-start(f32[40,128]{1,0:T(8,128)S(1)} %get-tuple-element.18), channel_id=1, source_target_pairs={{0,3},{2,1},{1,2},{3,0},{4,7},{6,5},{5,6},{7,4},{8,11},{10,9},{9,1... | collective-permute-start | bytes 61448 | tf_op jit(solution)/shard_map/ppermute | solution.py:415
  12.7 1.2 %collective-permute-start.3 = (f32[32,256]{1,0:T(8,128)S(1)}, f32[32,256]{1,0:T(8,128)S(1)}, u32[]{:S(2)}, u32[]{:S(2)}) collective-permute-start(f32[32,256]{1,0:T(8,128)S(1)} %get-tuple-element.20.numer_ref), channel_id=1, source_target_pairs={{0,1},{1,0},{2,3},{3,2},{4,5},{5,4},{6,7},{7,6},{8,9},{9,8},{10,11... | collective-permute-start | bytes 98312 | tf_op jit(solution)/shard_map/ppermute | solution.py:410
  14.1 3.1 %collective-permute-start.5 = (f32[40,128]{1,0:T(8,128)S(1)}, f32[40,128]{1,0:T(8,128)S(1)}, u32[]{:S(2)}, u32[]{:S(2)}) collective-permute-start(f32[40,128]{1,0:T(8,128)S(1)} %get-tuple-element.24), channel_id=1, source_target_pairs={{2,5},{4,3},{3,4},{5,2},{6,9},{8,7},{7,8},{9,6},{10,13},{12,11},{1... | collective-permute-start | bytes 61448 | tf_op jit(solution)/shard_map/ppermute | solution.py:415
  14.2 4.4 %collective-permute-start.4 = (f32[40,128]{1,0:T(8,128)S(1)}, f32[40,128]{1,0:T(8,128)S(1)}, u32[]{:S(2)}, u32[]{:S(2)}) collective-permute-start(f32[40,128]{1,0:T(8,128)S(1)} %get-tuple-element.24), channel_id=1, source_target_pairs={{0,3},{2,1},{1,2},{3,0},{4,7},{6,5},{5,6},{7,4},{8,11},{10,9},{9,1... | collective-permute-start | bytes 61448 | tf_op jit(solution)/shard_map/ppermute | solution.py:415
  20.8 4.7 %collective-permute-start.7 = (s16[576,128]{1,0:T(8,128)(2,1)S(1)}, s16[576,128]{1,0:T(8,128)(2,1)S(1)}, u32[]{:S(2)}, u32[]{:S(2)}) collective-permute-start(s16[576,128]{1,0:T(8,128)(2,1)S(1)} %get-tuple-element.27), channel_id=1, source_target_pairs={{0,1},{1,0},{2,3},{3,2},{4,5},{5,4},{6,7},{7,6},{8,9},{9,8},{10,11... | collective-permute-start | bytes 442376 | tf_op jit(solution)/shard_map/ppermute | solution.py:452
  21.0 4.6 %collective-permute-start.6 = (s16[288,128]{1,0:T(8,128)(2,1)S(1)}, s16[288,128]{1,0:T(8,128)(2,1)S(1)}, u32[]{:S(2)}, u32[]{:S(2)}) collective-permute-start(s16[288,128]{1,0:T(8,128)(2,1)S(1)} %get-tuple-element.26), channel_id=1, source_target_pairs={{0,3},{1,2},{2,1},{3,0},{4,7},{5,6},{6,5},{7,4},{8,11},{9,10},{10,... | collective-permute-start | bytes 221192 | tf_op jit(solution)/shard_map/ppermute | solution.py:452
  22.9 7.4 %collective-permute-start.9 = (s16[144,128]{1,0:T(8,128)(2,1)S(1)}, s16[144,128]{1,0:T(8,128)(2,1)S(1)}, u32[]{:S(2)}, u32[]{:S(2)}) collective-permute-start(s16[144,128]{1,0:T(8,128)(2,1)S(1)} %get-tuple-element.28), channel_id=1, source_target_pairs={{0,3},{1,2},{2,1},{3,0},{4,7},{5,6},{6,5},{7,4},{8,11},{9,10},{10,... | collective-permute-start | bytes 110600 | tf_op jit(solution)/shard_map/ppermute | solution.py:452
  23.0 7.6 %collective-permute-start.11 = (s16[144,128]{1,0:T(8,128)(2,1)S(1)}, s16[144,128]{1,0:T(8,128)(2,1)S(1)}, u32[]{:S(2)}, u32[]{:S(2)}) collective-permute-start(s16[144,128]{1,0:T(8,128)(2,1)S(1)} %get-tuple-element.29), channel_id=1, source_target_pairs={{0,3},{1,2},{2,1},{3,0},{4,7},{5,6},{6,5},{7,4},{8,11},{9,10},{10,... | collective-permute-start | bytes 110600 | tf_op jit(solution)/shard_map/ppermute | solution.py:452
  25.7 6.0 %collective-permute-start.8 = (s16[144,128]{1,0:T(8,128)(2,1)S(1)}, s16[144,128]{1,0:T(8,128)(2,1)S(1)}, u32[]{:S(2)}, u32[]{:S(2)}) collective-permute-start(s16[144,128]{1,0:T(8,128)(2,1)S(1)} %shard_map.75), channel_id=1, source_target_pairs={{0,13},{1,12},{2,15},{3,14},{4,9},{5,8},{6,11},{7,10},{8,5},{9,4},... | collective-permute-start | bytes 110600 | tf_op jit(solution)/shard_map/ppermute | solution.py:452
  30.2 1.5 %collective-permute-start.13 = (s16[144,128]{1,0:T(8,128)(2,1)S(1)}, s16[144,128]{1,0:T(8,128)(2,1)S(1)}, u32[]{:S(2)}, u32[]{:S(2)}) collective-permute-start(s16[144,128]{1,0:T(8,128)(2,1)S(1)} %shard_map.78), channel_id=1, source_target_pairs={{0,1},{1,0},{2,3},{3,2},{4,5},{5,4},{6,7},{7,6},{8,9},{9,8},{10,11... | collective-permute-start | bytes 110600 | tf_op jit(solution)/shard_map/ppermute | solution.py:452
  30.5 4.4 %collective-permute-start.10 = (s16[144,128]{1,0:T(8,128)(2,1)S(1)}, s16[144,128]{1,0:T(8,128)(2,1)S(1)}, u32[]{:S(2)}, u32[]{:S(2)}) collective-permute-start(s16[144,128]{1,0:T(8,128)(2,1)S(1)} %shard_map.76), channel_id=1, source_target_pairs={{0,9},{1,8},{2,11},{3,10},{4,13},{5,12},{6,15},{7,14},{8,1},{9,0},... | collective-permute-start | bytes 110600 | tf_op jit(solution)/shard_map/ppermute | solution.py:452
  30.8 4.1 %collective-permute-start.12 = (s16[144,128]{1,0:T(8,128)(2,1)S(1)}, s16[144,128]{1,0:T(8,128)(2,1)S(1)}, u32[]{:S(2)}, u32[]{:S(2)}) collective-permute-start(s16[144,128]{1,0:T(8,128)(2,1)S(1)} %shard_map.77), channel_id=1, source_target_pairs={{0,5},{1,4},{2,7},{3,6},{4,1},{5,0},{6,3},{7,2},{8,13},{9,12},{10,... | collective-permute-start | bytes 110600 | tf_op jit(solution)/shard_map/ppermute | solution.py:452
  35.1 5.2 %collective-permute-start.18 = (bf16[8,2048]{1,0:T(8,128)(2,1)S(1)}, bf16[8,2048]{1,0:T(8,128)(2,1)S(1)}, u32[]{:S(2)}, u32[]{:S(2)}) collective-permute-start(bf16[8,2048]{1,0:T(8,128)(2,1)S(1)} %shard_map.79.refs_0_), channel_id=1, source_target_pairs={{0,13},{1,12},{2,15},{3,14},{4,9},{5,8},{6,11},{7,10},{8,5},{9,4},... | collective-permute-start | bytes 98312 | tf_op jit(solution)/shard_map/ppermute | solution.py:452
  37.0 5.5 %collective-permute-start.16 = (bf16[8,2048]{1,0:T(8,128)(2,1)S(1)}, bf16[8,2048]{1,0:T(8,128)(2,1)S(1)}, u32[]{:S(2)}, u32[]{:S(2)}) collective-permute-start(bf16[8,2048]{1,0:T(8,128)(2,1)S(1)} %shard_map.79.refs_0_), channel_id=1, source_target_pairs={{0,9},{1,8},{2,11},{3,10},{4,13},{5,12},{6,15},{7,14},{8,1},{9,0},... | collective-permute-start | bytes 98312 | tf_op jit(solution)/shard_map/ppermute | solution.py:452
  37.5 5.3 %collective-permute-start.20 = (bf16[8,2048]{1,0:T(8,128)(2,1)S(1)}, bf16[8,2048]{1,0:T(8,128)(2,1)S(1)}, u32[]{:S(2)}, u32[]{:S(2)}) collective-permute-start(bf16[8,2048]{1,0:T(8,128)(2,1)S(1)} %shard_map.79.refs_0_), channel_id=1, source_target_pairs={{0,2},{1,3},{2,0},{3,1},{4,6},{5,7},{6,4},{7,5},{8,10},{9,11},{10,... | collective-permute-start | bytes 98312 | tf_op jit(solution)/shard_map/ppermute | solution.py:452
  38.4 4.5 %collective-permute-start.14 = (bf16[8,2048]{1,0:T(8,128)(2,1)S(1)}, bf16[8,2048]{1,0:T(8,128)(2,1)S(1)}, u32[]{:S(2)}, u32[]{:S(2)}) collective-permute-start(bf16[8,2048]{1,0:T(8,128)(2,1)S(1)} %shard_map.79.refs_0_), channel_id=1, source_target_pairs={{0,5},{1,4},{2,7},{3,6},{4,1},{5,0},{6,3},{7,2},{8,13},{9,12},{10,... | collective-permute-start | bytes 98312 | tf_op jit(solution)/shard_map/ppermute | solution.py:452
  40.3 4.0 %collective-permute-start.23 = (bf16[8,2048]{1,0:T(8,128)(2,1)S(1)}, bf16[8,2048]{1,0:T(8,128)(2,1)S(1)}, u32[]{:S(2)}, u32[]{:S(2)}) collective-permute-start(bf16[8,2048]{1,0:T(8,128)(2,1)S(1)} %collective-permute-done.18), channel_id=1, source_target_pairs={{0,3},{1,2},{2,1},{3,0},{4,7},{5,6},{6,5},{7,4},{8,11},{9,10},{10,... | collective-permute-start | bytes 98312 | tf_op jit(solution)/shard_map/ppermute | solution.py:452
  41.4 3.3 %collective-permute-start.19 = (bf16[8,2048]{1,0:T(8,128)(2,1)S(1)}, bf16[8,2048]{1,0:T(8,128)(2,1)S(1)}, u32[]{:S(2)}, u32[]{:S(2)}) collective-permute-start(bf16[8,2048]{1,0:T(8,128)(2,1)S(1)} %collective-permute-done.18), channel_id=1, source_target_pairs={{0,1},{1,0},{2,3},{3,2},{4,5},{5,4},{6,7},{7,6},{8,9},{9,8},{10,11... | collective-permute-start | bytes 98312 | tf_op jit(solution)/shard_map/ppermute | solution.py:452
  42.4 3.4 %collective-permute-start.22 = (bf16[8,2048]{1,0:T(8,128)(2,1)S(1)}, bf16[8,2048]{1,0:T(8,128)(2,1)S(1)}, u32[]{:S(2)}, u32[]{:S(2)}) collective-permute-start(bf16[8,2048]{1,0:T(8,128)(2,1)S(1)} %collective-permute-done.16), channel_id=1, source_target_pairs={{0,3},{1,2},{2,1},{3,0},{4,7},{5,6},{6,5},{7,4},{8,11},{9,10},{10,... | collective-permute-start | bytes 98312 | tf_op jit(solution)/shard_map/ppermute | solution.py:452
  42.8 3.1 %collective-permute-start.17 = (bf16[8,2048]{1,0:T(8,128)(2,1)S(1)}, bf16[8,2048]{1,0:T(8,128)(2,1)S(1)}, u32[]{:S(2)}, u32[]{:S(2)}) collective-permute-start(bf16[8,2048]{1,0:T(8,128)(2,1)S(1)} %collective-permute-done.16), channel_id=1, source_target_pairs={{0,1},{1,0},{2,3},{3,2},{4,5},{5,4},{6,7},{7,6},{8,9},{9,8},{10,11... | collective-permute-start | bytes 98312 | tf_op jit(solution)/shard_map/ppermute | solution.py:452
  42.9 3.6 %collective-permute-start.21 = (bf16[8,2048]{1,0:T(8,128)(2,1)S(1)}, bf16[8,2048]{1,0:T(8,128)(2,1)S(1)}, u32[]{:S(2)}, u32[]{:S(2)}) collective-permute-start(bf16[8,2048]{1,0:T(8,128)(2,1)S(1)} %collective-permute-done.14), channel_id=1, source_target_pairs={{0,3},{1,2},{2,1},{3,0},{4,7},{5,6},{6,5},{7,4},{8,11},{9,10},{10,... | collective-permute-start | bytes 98312 | tf_op jit(solution)/shard_map/ppermute | solution.py:452
  44.3 2.2 %collective-permute-start.15 = (bf16[8,2048]{1,0:T(8,128)(2,1)S(1)}, bf16[8,2048]{1,0:T(8,128)(2,1)S(1)}, u32[]{:S(2)}, u32[]{:S(2)}) collective-permute-start(bf16[8,2048]{1,0:T(8,128)(2,1)S(1)} %collective-permute-done.14), channel_id=1, source_target_pairs={{0,1},{1,0},{2,3},{3,2},{4,5},{5,4},{6,7},{7,6},{8,9},{9,8},{10,11... | collective-permute-start | bytes 98312 | tf_op jit(solution)/shard_map/ppermute | solution.py:452

commit v7 on v6

--- a/solution.py
+++ b/solution.py
@@ -25,17 +25,45 @@
 
 
 def piece(total, wanted):
-    for size in (1024, 512, 256, 128):
+    for size in (4096, 2048, 1024, 512, 256, 128):
         if size <= wanted and total % size == 0:
             return size
     return total
 
 
-def ratio_of(counts, gene_rows, factor_rows):
+def quarter(width):
+    return width // 4
+
+
+def outer_of(values):
+    side = quarter(values.shape[1])
+    return jnp.concatenate([values[:, :side], values[:, -side:]], axis=1)
+
+
+def inner_of(values):
+    side = quarter(values.shape[1])
+    return values[:, side:-side]
+
+
+def whole_of(outer, inner):
+    side = quarter(2 * outer.shape[1])
+    return jnp.concatenate([outer[:, :side], inner, outer[:, side:]], axis=1)
+
+
+def ratio_of(kept_ref, run, gene_rows, cells):
+    factor_rows = jnp.concatenate(split(cells), axis=0)
     product = jnp.dot(gene_rows, factor_rows, preferred_element_type=jnp.float32)
-    return (counts.astype(jnp.float32) * pl.reciprocal(product, approx=True)).astype(
-        jnp.bfloat16
-    )
+    counts = kept_ref[run].astype(jnp.float32)
+    return (counts * pl.reciprocal(product, approx=True)).astype(jnp.bfloat16)
+
+
+def runs_of(genes, wanted=1024):
+    size = piece(genes, wanted)
+    return [slice(at, at + size) for at in range(0, genes, size)]
+
+
+def numerator(gene_ref, run, ratio):
+    return jnp.dot(gene_ref[:, run], ratio, preferred_element_type=jnp.float32)
 
 
 def partner(tile, tiles, offset):
@@ -48,6 +76,7 @@
     tiles = lax.axis_size("tile")
     here = lax.axis_index("tile")
     neigh = neigh_ref[...] - here * width
+    neigh = jnp.concatenate([outer_of(neigh), inner_of(neigh)], axis=1)
 
     def found(where):
         total = jnp.zeros((LANES, width), jnp.float32)
@@ -66,56 +95,46 @@
     pick_ref[width:] = jnp.where(beside < 0, 0.0, found(where)).astype(jnp.bfloat16)
 
 
-def start_copies(counts_ref, landed, sems):
+def turn_kernel(counts_ref, outer_ref, inner_ref, landed, sems):
+    width, genes = landed.shape
+    side = quarter(width)
     copies = []
-    for i in range(landed.shape[1] // COPY_COLUMNS):
-        at = i * COPY_COLUMNS
+    for i in range(genes // COPY_COLUMNS):
+        columns = pl.ds(i * COPY_COLUMNS, COPY_COLUMNS)
         copies.append(
             pltpu.make_async_copy(
-                counts_ref.at[:, pl.ds(at, COPY_COLUMNS)],
-                landed.at[:, pl.ds(at, COPY_COLUMNS)],
-                sems.at[i],
+                counts_ref.at[:, columns], landed.at[:, columns], sems.at[i]
             )
         )
     for copy in copies:
         copy.start()
-    return copies
-
-
-def turned(landed, at):
-    return landed[:, at : at + COPY_COLUMNS].astype(jnp.float32).T.astype(jnp.bfloat16)
-
-
-def turn_kernel(counts_ref, kept_ref, landed, sems):
-    for i, copy in enumerate(start_copies(counts_ref, landed, sems)):
+    for i, copy in enumerate(copies):
         copy.wait()
-        at = i * COPY_COLUMNS
-        kept_ref[at : at + COPY_COLUMNS] = turned(landed, at)
-
-
-def runs_of(kept_ref, wanted):
-    genes = kept_ref.shape[0]
-    size = piece(genes, wanted)
-    for at in range(0, genes, size):
-        yield at, kept_ref[at : at + size]
-
-
-def first_kernel(kept_ref, cells_ref, gene_ref, part_ref, rows_ref):
+        run = slice(i * COPY_COLUMNS, (i + 1) * COPY_COLUMNS)
+        ends = jnp.concatenate([landed[:side, run], landed[width - side :, run]], axis=0)
+        outer_ref[run] = ends.astype(jnp.float32).T.astype(jnp.bfloat16)
+        middle = landed[side : width - side, run]
+        inner_ref[run] = middle.astype(jnp.float32).T.astype(jnp.bfloat16)
+
+
+def first_kernel(outer_ref, inner_ref, cells_ref, gene_ref, part_ref, rows_ref):
     rank, genes = gene_ref.shape
     width = cells_ref.shape[1]
-    factor_rows = jnp.concatenate(split(cells_ref[...]), axis=0)
+    cells = cells_ref[...]
+    cells = jnp.concatenate([outer_of(cells), inner_of(cells)], axis=1)
+    factor_rows = jnp.concatenate(split(cells), axis=0)
     gsum = jnp.zeros((rank, 1), jnp.float32)
     total = jnp.zeros((rank, width), jnp.float32)
-    for at, counts in runs_of(kept_ref, 1024):
-        end = at + counts.shape[0]
-        hf = gene_ref[:, at:end]
-        wide = hf.astype(jnp.float32)
+    for run in runs_of(genes):
+        wide = gene_ref[:, run].astype(jnp.float32)
         gsum += jnp.sum(wide, axis=1, keepdims=True)
         rows = jnp.concatenate([wide, wide], axis=0).T.astype(jnp.bfloat16)
-        rows_ref[at:end] = rows
-        ratio = ratio_of(counts, rows, factor_rows)
-        total += jnp.dot(hf, ratio, preferred_element_type=jnp.float32)
-    part_ref[:, :width] = total
+        rows_ref[run] = rows
+        product = jnp.dot(rows, factor_rows, preferred_element_type=jnp.float32)
+        counts = jnp.concatenate([outer_ref[run], inner_ref[run]], axis=1)
+        ratio = counts.astype(jnp.float32) * pl.reciprocal(product, approx=True)
+        total += numerator(gene_ref, run, ratio.astype(jnp.bfloat16))
+    part_ref[:, :width] = whole_of(total[:, : width // 2], total[:, width // 2 :])
     part_ref[:, width:] = jnp.broadcast_to(gsum, (rank, LANES))
 
 
@@ -148,38 +167,62 @@
     )
 
 
-def smoothed(updated_ref, tissue_ref, first_ref, second_ref, pick_ref):
-    rank, width = updated_ref.shape
-    updated = updated_ref[...]
-    flags = tissue_ref[...] > 0
-    own = masked_rows(updated, flags)
+def mixed(updated, flags, near):
+    rank = updated.shape[0]
+    mean = near[:rank] / jnp.maximum(near[rank : rank + 1], 1.0)
+    return jnp.where(
+        flags, (1.0 - smooth_weight) * updated + smooth_weight * mean, updated
+    )
+
+
+def picked(values, pick):
+    return sum(
+        jnp.dot(part, pick, preferred_element_type=jnp.float32) for part in split(values)
+    )
+
+
+def smoothed_inner(updated_ref, tissue_ref, pick_ref):
+    updated, tissue = updated_ref[...], tissue_ref[...]
+    width = updated.shape[1]
+    near = picked(masked_rows(updated, tissue > 0), pick_ref[:width, width // 2 :])
+    flags = inner_of(tissue) > 0
+    return mixed(inner_of(updated), flags, near), flags
+
+
+def smoothed_outer(updated_ref, tissue_ref, pick_ref, first_ref, second_ref):
+    updated, tissue = updated_ref[...], tissue_ref[...]
+    width = updated.shape[1]
     sides = jnp.concatenate(
         [first_ref[:, : 2 * BORDER], second_ref[:, : 2 * BORDER]], axis=1
     )
-    near = jnp.zeros(own.shape, jnp.float32)
-    for values, pick in ((own, pick_ref[:width]), (sides, pick_ref[width:])):
-        for part in split(values):
-            near += jnp.dot(part, pick, preferred_element_type=jnp.float32)
-    mean = near[:rank] / jnp.maximum(near[rank : rank + 1], 1.0)
-    cells = jnp.where(
-        flags, (1.0 - smooth_weight) * updated + smooth_weight * mean, updated
-    )
-    return cells, flags
-
-
-def next_kernel(
-    updated_ref, tissue_ref, first_ref, second_ref, pick_ref, kept_ref,
-    gene_ref, rows_ref, cells_ref, numer_ref,
+    near = picked(masked_rows(updated, tissue > 0), pick_ref[:width, : width // 2])
+    near += picked(sides, pick_ref[width:, : width // 2])
+    flags = outer_of(tissue) > 0
+    return mixed(outer_of(updated), flags, near), flags
+
+
+def inner_kernel(
+    updated_ref, tissue_ref, pick_ref, kept_ref, rows_ref, gene_ref, cells_ref, numer_ref
 ):
-    cells, _ = smoothed(updated_ref, tissue_ref, first_ref, second_ref, pick_ref)
+    cells, _ = smoothed_inner(updated_ref, tissue_ref, pick_ref)
     cells_ref[...] = cells
-    factor_rows = jnp.concatenate(split(cells), axis=0)
-    total = jnp.zeros(cells.shape, jnp.float32)
-    for at, counts in runs_of(kept_ref, 1024):
-        end = at + counts.shape[0]
-        ratio = ratio_of(counts, rows_ref[at:end], factor_rows)
-        total += jnp.dot(gene_ref[:, at:end], ratio, preferred_element_type=jnp.float32)
-    numer_ref[...] = total
+    numer_ref[...] = sum(
+        numerator(gene_ref, run, ratio_of(kept_ref, run, rows_ref[run], cells))
+        for run in runs_of(gene_ref.shape[1], 2048)
+    )
+
+
+def outer_kernel(
+    updated_ref, tissue_ref, pick_ref, first_ref, second_ref, kept_ref, rows_ref,
+    gene_ref, inner_cells_ref, inner_numer_ref, cells_ref, numer_ref,
+):
+    cells, _ = smoothed_outer(updated_ref, tissue_ref, pick_ref, first_ref, second_ref)
+    cells_ref[...] = whole_of(cells, inner_cells_ref[...])
+    numer = sum(
+        numerator(gene_ref, run, ratio_of(kept_ref, run, rows_ref[run], cells))
+        for run in runs_of(gene_ref.shape[1], 2048)
+    )
+    numer_ref[...] = whole_of(numer, inner_numer_ref[...])
 
 
 def exponent(values):
@@ -191,24 +234,27 @@
     return (blocks + blocks % 2) * ROWS + STAT_ROWS
 
 
-def encode(values, hden, target):
+def encode(values, hden, targets):
     power = exponent(jnp.max(values, axis=1, keepdims=True))
     coded = (values * (jnp.exp2(-power) * FULL) + 0.5).astype(jnp.int32)
     hden_power = exponent(hden)
     scaled = hden * jnp.exp2(-hden_power) * FULL
     high = jnp.floor(scaled)
     low = jnp.floor((scaled - high) * FULL)
-    lane = lax.broadcasted_iota(jnp.int32, (ROWS, LANES), 1)
-    marks = jnp.zeros((ROWS, LANES), jnp.float32)
+    lane = lax.broadcasted_iota(jnp.int32, (values.shape[0], LANES), 1)
+    marks = jnp.zeros((values.shape[0], LANES), jnp.float32)
     for at, value in enumerate((power, hden_power, high, low)):
         marks = jnp.where(lane == at, value, marks)
+    marks = marks.astype(jnp.int32)
     blank = jnp.zeros((ROWS, LANES), jnp.int32)
-    blocks = [coded[:, at : at + LANES] for at in range(0, values.shape[1], LANES)]
-    blocks += [blank] * (len(blocks) % 2) + [marks.astype(jnp.int32), blank]
-    for i in range(0, len(blocks), 2):
-        target[i * ROWS : (i + 2) * ROWS] = jnp.concatenate(
-            blocks[i : i + 2], axis=0
-        ).astype(jnp.int16)
+    for group, target in enumerate(targets):
+        ranks = slice(group * ROWS, (group + 1) * ROWS)
+        blocks = [coded[ranks, at : at + LANES] for at in range(0, values.shape[1], LANES)]
+        blocks += [blank] * (len(blocks) % 2) + [marks[ranks], blank]
+        for i in range(0, len(blocks), 2):
+            target[i * ROWS : (i + 2) * ROWS] = jnp.concatenate(
+                blocks[i : i + 2], axis=0
+            ).astype(jnp.int16)
 
 
 def decode(source, columns):
@@ -226,57 +272,62 @@
     return jnp.concatenate(blocks[: columns // LANES], axis=1), hden
 
 
-def last_pass(
-    updated_ref, tissue_ref, first_ref, second_ref, pick_ref, kept_ref, rows_ref,
-    cells_ref, totals_ref,
-):
-    rank, genes = totals_ref.shape[0], kept_ref.shape[0]
-    cells, flags = smoothed(updated_ref, tissue_ref, first_ref, second_ref, pick_ref)
-    cells_ref[...] = cells
+def gene_totals(cells, flags, kept_ref, rows_ref, totals_ref):
+    rank = cells.shape[0]
+    genes = totals_ref.shape[1] - LANES
     masked = jnp.where(flags, cells, 0.0)
-    factor_rows = jnp.concatenate(split(cells), axis=0)
-    masked_rows = jnp.concatenate(split(masked), axis=0)
-    masked_columns = masked_rows.astype(jnp.float32).T.astype(jnp.bfloat16)
+    parts = jnp.concatenate(split(masked), axis=0)
+    columns = parts.astype(jnp.float32).T.astype(jnp.bfloat16)
     hden = jnp.sum(masked, axis=1, keepdims=True)
     totals_ref[:, genes:] = jnp.broadcast_to(hden, (rank, LANES))
-    for at, counts in runs_of(kept_ref, 1024):
-        end = at + counts.shape[0]
-        ratio = ratio_of(counts, rows_ref[at:end], factor_rows)
-        both = jnp.dot(ratio, masked_columns, preferred_element_type=jnp.float32).T
-        totals_ref[:, at:end] = both[:rank] + both[rank:]
+    for run in runs_of(genes, 1024):
+        ratio = ratio_of(kept_ref, run, rows_ref[run], cells)
+        total = jnp.dot(ratio, columns, preferred_element_type=jnp.float32).T
+        totals_ref[:, run] = total[:rank] + total[rank:]
+
+
+def inner_totals_kernel(
+    updated_ref, tissue_ref, pick_ref, kept_ref, rows_ref, cells_ref, totals_ref
+):
+    cells, flags = smoothed_inner(updated_ref, tissue_ref, pick_ref)
+    cells_ref[...] = cells
+    gene_totals(cells, flags, kept_ref, rows_ref, totals_ref)
+
+
+def last_pass(
+    updated_ref, tissue_ref, pick_ref, first_ref, second_ref, kept_ref, rows_ref,
+    inner_cells_ref, inner_totals_ref, cells_ref, totals_ref,
+):
+    cells, flags = smoothed_outer(updated_ref, tissue_ref, pick_ref, first_ref, second_ref)
+    cells_ref[...] = whole_of(cells, inner_cells_ref[...])
+    gene_totals(cells, flags, kept_ref, rows_ref, totals_ref)
+    totals_ref[...] += inner_totals_ref[...]
+
+
+def encode_tiles(totals_ref, sent_ref):
+    rank, genes = totals_ref.shape[0], totals_ref.shape[1] - LANES
+    tiles = sent_ref.shape[0]
+    across = tiles * ROWS // rank
+    columns = genes // across
+    for column in range(across):
+        encode(
+            totals_ref[:, column * columns : (column + 1) * columns],
+            totals_ref[:, genes : genes + 1],
+            [sent_ref.at[tile] for tile in range(column, tiles, across)],
+        )
 
 
 def shares_kernel(*refs):
     *passed, sent_ref, totals_ref = refs
     last_pass(*passed, totals_ref)
-    rank = totals_ref.shape[0]
-    genes = totals_ref.shape[1] - LANES
-    across = sent_ref.shape[0] * ROWS // rank
-    columns = genes // across
-    for tile in range(sent_ref.shape[0]):
-        ranks = pl.ds(tile // across * ROWS, ROWS)
-        start = tile % across * columns
-        encode(
-            totals_ref[ranks, start : start + columns],
-            totals_ref[ranks, genes : genes + 1],
-            sent_ref.at[tile],
-        )
+    encode_tiles(totals_ref, sent_ref)
 
 
 def distance_kernel(*refs):
-    passed, (*sent_refs, own_ref, totals_ref, coded_ref) = refs[:8], refs[8:]
+    passed, (*sent_refs, own_ref, totals_ref, coded_ref) = refs[:10], refs[10:]
     last_pass(*passed, totals_ref)
     tiles, height, _ = coded_ref.shape
-    genes = totals_ref.shape[1] - LANES
-    columns = genes // 2
-    for tile in range(tiles):
-        ranks = slice(tile // 2 * ROWS, (tile // 2 + 1) * ROWS)
-        start = tile % 2 * columns
-        encode(
-            totals_ref[ranks, start : start + columns],
-            totals_ref[ranks, genes : genes + 1],
-            coded_ref.at[tile],
-        )
+    encode_tiles(totals_ref, coded_ref)
     tile = lax.axis_index("tile")
     for distance in range(tiles // 2):
         there = tile ^ (2 * distance)
@@ -292,7 +343,7 @@
     values, hden = decode(got_ref.at[start : start + height], columns)
     start = height * distance
     more, more_hden = decode(own_ref.at[start : start + height], columns)
-    encode(values + more, hden + more_hden, sent_ref)
+    encode(values + more, hden + more_hden, [sent_ref])
 
 
 def fresh_of(hnum, hden, gene_ref, across):
@@ -387,12 +438,14 @@
     shape = jax.ShapeDtypeStruct
     factor = shape((rank, width), jnp.float32)
     edge = shape((rank + ROWS, LANES), jnp.float32)
+    half = shape((rank, width // 2), jnp.float32)
+    half_kept = shape((genes, width // 2), jnp.bfloat16)
     gene_rows = shape((genes, 2 * rank), jnp.bfloat16)
     far = pl.BlockSpec(memory_space=pl.ANY)
 
-    kept = call(
+    outer, inner = call(
         turn_kernel,
-        shape((genes, width), jnp.bfloat16),
+        (half_kept, half_kept),
         [
             pltpu.VMEM(counts.shape, counts.dtype),
             pltpu.SemaphoreType.DMA((genes // COPY_COLUMNS,)),
@@ -402,7 +455,7 @@
     )(counts)
     part, rows = call(
         first_kernel, (shape((rank, width + LANES), jnp.float32), gene_rows)
-    )(kept, cell_factor, gene_factor)
+    )(outer, inner, cell_factor, gene_factor)
     pick = call(pick_kernel, shape((width + LANES, width), jnp.bfloat16))(neighbours)
 
     def swapped(part):
@@ -410,18 +463,20 @@
             return lax.ppermute(part, "gene", [(0, 1), (1, 0)])
         return lax.psum(part, "gene") - part
 
-    def around(updated, edges):
-        sides = [
+    def around(edges):
+        return [
             lax.ppermute(edges, ("tile", "gene"), beside(tiles, halves, offset))
             for offset in (0, 1)
         ]
-        return updated, flag_row, *sides, pick, kept
 
     updated, edges, gsum = call(
         first_update_kernel, (factor, edge, shape((rank, LANES), jnp.float32))
     )(part, swapped(part), cell_factor, flag_row)
-    cells, numer = call(next_kernel, (factor, factor))(
-        *around(updated, edges), gene_factor, rows
+    inner_of_both = call(inner_kernel, (half, half))(
+        updated, flag_row, pick, inner, rows, gene_factor
+    )
+    cells, numer = call(outer_kernel, (factor, factor))(
+        updated, flag_row, pick, *around(edges), outer, rows, gene_factor, *inner_of_both
     )
     updated, edges = call(update_kernel, (factor, edge))(
         numer, swapped(numer), gsum, cells, flag_row
@@ -430,7 +485,10 @@
     groups = rank // ROWS
     columns = genes // across
     height = share_height(columns)
-    last = (*around(updated, edges), rows)
+    inner_of_both = call(
+        inner_totals_kernel, (half, shape((rank, genes + LANES), jnp.float32))
+    )(updated, flag_row, pick, inner, rows)
+    last = (updated, flag_row, pick, *around(edges), outer, rows, *inner_of_both)
     totals = [pltpu.VMEM((rank, genes + LANES), jnp.float32)]
     if across != 2 or groups != 4 or halves != 2:
         cells, sent = call(

time: 47.5 us -> 46.8 us (0.985)
  waiting for transfers between devices: 12.1 us -> 9.95 us
  Pallas kernels: 9.5 us -> 10.8 us
    ppermute x4, waiting for transfers between devices: 2.63 us -> 0.5 us  [around(): lax.ppermute(edges, ('tile', 'gene'), beside(tiles, halves, offset))]
    pallas_call x13 -> x15, Pallas kernels: 9.5 us -> 10.8 us  [call(): pl.pallas_call(kernel, out_shape=outs, in_specs=specs or [whole] * len(ar...]
  transfers between devices with their start and end apart: 24 -> 24, of which waited for: 11 -> 11; matrix products, arithmetic and copies ran while one was open for 0% -> 0% of each run, Pallas kernels for 2% -> 7%
where the time goes in v7:
time: 46.8 us; the launch traced here: 46.7 us
  starting transfers between devices  25.1 us (54%)
  Pallas kernels  10.8 us (23%)
  waiting for transfers between devices  9.95 us (21%)
  between operations  0.83 us (2%)
    ppermute x18, starting transfers between devices, moved(): return lax.ppermute(array, ('tile', 'gene'), pairs)  17.2 us
    pallas_call x15, Pallas kernels, call(): pl.pallas_call(kernel, out_shape=outs, in_specs=specs or [whole] * len(ar...  10.8 us
    ppermute x18, waiting for transfers between devices, moved(): return lax.ppermute(array, ('tile', 'gene'), pairs)  7.52 us
    ppermute x4, starting transfers between devices, around(): lax.ppermute(edges, ('tile', 'gene'), beside(tiles, halves, offset))  7.2 us
    ppermute x2, waiting for transfers between devices, swapped(): return lax.ppermute(part, 'gene', [(0, 1), (1, 0)])  1.94 us
  transfers between devices with their start and end apart: 24, of which 11 were waited for; matrix products, arithmetic and copies ran while one was open for 0% of the time, Pallas kernels for 7%

profile of v7, /device:TPU:0, one launch (start us, length us, event | category | flops | bytes accessed | tf_op | source)
XLA Modules:
  0.0 46.7 jit_solution(8421314728996036984)
XLA Ops:
  0.6 0.0 copy-start
  0.7 2.4 %shard_map.68 = (bf16[4096,128]{1,0:T(8,128)(2,1)S(1)}, bf16[4096,128]{1,0:T(8,128)(2,1)S(1)}) custom-call(s32[256,4096]{1,0:T(8,128)} %counts_ref.1), custom_call_target="tpu_custom_call" | custom-call | tf_op jit(solution)/shard_map/pallas_call | solution.py:407
  3.1 1.3 %shard_map.69 = (f32[32,384]{1,0:T(8,128)S(1)}, bf16[4096,64]{1,0:T(8,128)(2,1)S(1)}) custom-call(bf16[4096,128]{1,0:T(8,128)(2,1)S(1)} %get-tuple-element.22.outer_ref.kept_ref.refs_5_, bf16[4096,128]{1,0:T(8,128)(2,1)S(1)} %get-tuple-element.23.inner_ref.kept_ref, f32[32,256]{1,0:T(8,128)S(1)} %copy-done.1, bf16[32,4096]{1,0:T(8,128)(2,1)S(1)} %copy-done), custom_call_target="tpu_custom_call" | custom-call | tf_op jit(solution)/shard_map/pallas_call | solution.py:407
  4.4 0.5 %collective-permute-start = (f32[32,384]{1,0:T(8,128)S(1)}, f32[32,384]{1,0:T(8,128)S(1)}, u32[]{:S(2)}, u32[]{:S(2)}) collective-permute-start(f32[32,384]{1,0:T(8,128)S(1)} %get-tuple-element.24.part_ref), channel_id=1, source_target_pairs={{0,1},{1,0},{2,3},{3,2},{4,5},{5,4},{6,7},{7,6},{8,9},{9,8},{10,11... | collective-permute-start | bytes 147464 | tf_op jit(solution)/shard_map/ppermute | solution.py:463
  4.9 0.9 %collective-permute-done.other_ref = f32[32,384]{1,0:T(8,128)S(1)} collective-permute-done((f32[32,384]{1,0:T(8,128)S(1)}, f32[32,384]{1,0:T(8,128)S(1)}, u32[]{:S(2)}, u32[]{:S(2)}) %collective-permute-start) | collective-permute-done | bytes 49184 | tf_op jit(solution)/shard_map/ppermute | solution.py:463
  5.8 0.2 shard_map.70
  5.9 0.4 collective-permute-start.2
  6.3 3.8 %collective-permute-start.1 = (f32[40,128]{1,0:T(8,128)S(1)}, f32[40,128]{1,0:T(8,128)S(1)}, u32[]{:S(2)}, u32[]{:S(2)}) collective-permute-start(f32[40,128]{1,0:T(8,128)S(1)} %get-tuple-element.26), channel_id=1, source_target_pairs={{0,3},{2,1},{1,2},{3,0},{4,7},{6,5},{5,6},{7,4},{8,11},{10,9},{9,1... | collective-permute-start | bytes 61448 | tf_op jit(solution)/shard_map/ppermute | solution.py:468
  10.0 0.4 shard_map.71.pick_ref.refs_2_
  10.4 0.9 %shard_map.72 = (f32[32,128]{1,0:T(8,128)S(1)}, f32[32,128]{1,0:T(8,128)S(1)}) custom-call(f32[32,256]{1,0:T(8,128)S(1)} %get-tuple-element.25.updated_ref, s32[1,256]{1,0:T(1,128)S(1)} %bitcast.2, bf16[384,256]{1,0:T(8,128)(2,1)S(1)} %shard_map.71.pick_ref.refs_2_, bf16[4096,128]{1,0:T(8,128)(2,1)S(1)} %get-tuple-element.23.inner_ref.kept_ref, ...), custom_call_target="tpu_custom_call" | custom-call | tf_op jit(solution)/shard_map/pallas_call | solution.py:407
  11.3 0.0 collective-permute-done.2.second_ref
  11.3 0.2 collective-permute-done.1.first_ref
  11.5 0.8 %shard_map.73 = (f32[32,256]{1,0:T(8,128)S(1)}, f32[32,256]{1,0:T(8,128)S(1)}) custom-call(f32[32,256]{1,0:T(8,128)S(1)} %get-tuple-element.25.updated_ref, s32[1,256]{1,0:T(1,128)S(1)} %bitcast.3, bf16[384,256]{1,0:T(8,128)(2,1)S(1)} %shard_map.71.pick_ref.refs_2_, f32[40,128]{1,0:T(8,128)S(1)} %collective-permute-done.1.first_ref, ...), custom_call_target="tpu_custom_call" | custom-call | tf_op jit(solution)/shard_map/pallas_call | solution.py:407
  12.3 0.2 collective-permute-start.3
  12.6 1.1 %collective-permute-done.3.other_ref = f32[32,256]{1,0:T(8,128)S(1)} collective-permute-done((f32[32,256]{1,0:T(8,128)S(1)}, f32[32,256]{1,0:T(8,128)S(1)}, u32[]{:S(2)}, u32[]{:S(2)}) %collective-permute-start.3) | collective-permute-done | bytes 32800 | tf_op jit(solution)/shard_map/ppermute | solution.py:463
  13.6 0.1 shard_map.74
  13.8 0.2 collective-permute-start.5
  13.9 2.9 %collective-permute-start.4 = (f32[40,128]{1,0:T(8,128)S(1)}, f32[40,128]{1,0:T(8,128)S(1)}, u32[]{:S(2)}, u32[]{:S(2)}) collective-permute-start(f32[40,128]{1,0:T(8,128)S(1)} %get-tuple-element.34), channel_id=1, source_target_pairs={{0,3},{2,1},{1,2},{3,0},{4,7},{6,5},{5,6},{7,4},{8,11},{10,9},{9,1... | collective-permute-start | bytes 61448 | tf_op jit(solution)/shard_map/ppermute | solution.py:468
  16.9 1.1 %shard_map.75 = (f32[32,128]{1,0:T(8,128)S(1)}, f32[32,4224]{1,0:T(8,128)S(1)}) custom-call(f32[32,256]{1,0:T(8,128)S(1)} %get-tuple-element.33.updated_ref.refs_0_, s32[1,256]{1,0:T(1,128)S(1)} %bitcast.5, bf16[384,256]{1,0:T(8,128)(2,1)S(1)} %shard_map.71.pick_ref.refs_2_, bf16[4096,128]{1,0:T(8,128)(2,1)S(1)} %get-tuple-element.23.inner_ref.kept_ref, ...), custom_call_target="tpu_custom_call" | custom-call | tf_op jit(solution)/shard_map/pallas_call | solution.py:407
  18.0 0.0 collective-permute-done.5.refs_4_
  18.0 0.3 collective-permute-done.4.refs_3_
  18.3 1.8 %shard_map.76 = (f32[32,256]{1,0:T(8,128)}, s16[144,128]{1,0:T(8,128)(2,1)S(1)}, s16[144,128]{1,0:T(8,128)(2,1)S(1)}, s16[288,128]{1,0:T(8,128)(2,1)S(1)}, s16[576,128]{1,0:T(8,128)(2,1)S(1)}) custom-call(f32[32,256]{1,0:T(8,128)S(1)} %get-tuple-element.33.updated_ref.refs_0_, s32[1,256]{1,0:T(1,128)S(1)} %bitcast.6, ...), custom_call_target="tpu_custom_call" | custom-call | tf_op jit(solution)/shard_map/pallas_call | solution.py:407
  20.1 0.1 collective-permute-start.7
  20.3 2.0 %collective-permute-start.6 = (s16[288,128]{1,0:T(8,128)(2,1)S(1)}, s16[288,128]{1,0:T(8,128)(2,1)S(1)}, u32[]{:S(2)}, u32[]{:S(2)}) collective-permute-start(s16[288,128]{1,0:T(8,128)(2,1)S(1)} %get-tuple-element.38), channel_id=1, source_target_pairs={{0,3},{1,2},{2,1},{3,0},{4,7},{5,6},{6,5},{7,4},{8,11},{9,10},{10,... | collective-permute-start | bytes 221192 | tf_op jit(solution)/shard_map/ppermute | solution.py:510
  22.2 0.0 collective-permute-start.9
  22.3 1.7 %collective-permute-start.11 = (s16[144,128]{1,0:T(8,128)(2,1)S(1)}, s16[144,128]{1,0:T(8,128)(2,1)S(1)}, u32[]{:S(2)}, u32[]{:S(2)}) collective-permute-start(s16[144,128]{1,0:T(8,128)(2,1)S(1)} %get-tuple-element.41), channel_id=1, source_target_pairs={{0,3},{1,2},{2,1},{3,0},{4,7},{5,6},{6,5},{7,4},{8,11},{9,10},{10,... | collective-permute-start | bytes 110600 | tf_op jit(solution)/shard_map/ppermute | solution.py:510
  24.0 0.8 %collective-permute-done.6.got_ref = s16[288,128]{1,0:T(8,128)(2,1)S(1)} collective-permute-done((s16[288,128]{1,0:T(8,128)(2,1)S(1)}, s16[288,128]{1,0:T(8,128)(2,1)S(1)}, u32[]{:S(2)}, u32[]{:S(2)}) %collective-permute-start.6) | collective-permute-done | bytes 73760 | tf_op jit(solution)/shard_map/ppermute | solution.py:510
  24.8 0.0 collective-permute-done.7.own_ref
  24.8 0.2 shard_map.77
  25.0 4.3 %collective-permute-start.8 = (s16[144,128]{1,0:T(8,128)(2,1)S(1)}, s16[144,128]{1,0:T(8,128)(2,1)S(1)}, u32[]{:S(2)}, u32[]{:S(2)}) collective-permute-start(s16[144,128]{1,0:T(8,128)(2,1)S(1)} %shard_map.77), channel_id=1, source_target_pairs={{0,13},{1,12},{2,15},{3,14},{4,9},{5,8},{6,11},{7,10},{8,5},{9,4},... | collective-permute-start | bytes 110600 | tf_op jit(solution)/shard_map/ppermute | solution.py:510
  29.4 0.2 shard_map.80
  29.6 0.1 collective-permute-start.13
  29.6 0.0 collective-permute-done.9.got_ref
  29.6 0.2 shard_map.78
  29.8 0.1 collective-permute-start.10
  29.9 0.0 collective-permute-done.11.got_ref
  29.9 0.2 shard_map.79
  30.1 0.7 %collective-permute-start.12 = (s16[144,128]{1,0:T(8,128)(2,1)S(1)}, s16[144,128]{1,0:T(8,128)(2,1)S(1)}, u32[]{:S(2)}, u32[]{:S(2)}) collective-permute-start(s16[144,128]{1,0:T(8,128)(2,1)S(1)} %shard_map.79), channel_id=1, source_target_pairs={{0,5},{1,4},{2,7},{3,6},{4,1},{5,0},{6,3},{7,2},{8,13},{9,12},{10,... | collective-permute-start | bytes 110600 | tf_op jit(solution)/shard_map/ppermute | solution.py:510
  30.8 0.2 collective-permute-done.8.refs_0_
  31.1 0.0 collective-permute-done.13.refs_3_
  31.1 3.1 %collective-permute-done.10.refs_1_ = s16[144,128]{1,0:T(8,128)(2,1)S(1)} collective-permute-done((s16[144,128]{1,0:T(8,128)(2,1)S(1)}, s16[144,128]{1,0:T(8,128)(2,1)S(1)}, u32[]{:S(2)}, u32[]{:S(2)}) %collective-permute-start.10) | collective-permute-done | bytes 36896 | tf_op jit(solution)/shard_map/ppermute | solution.py:510
  34.2 0.0 collective-permute-done.12.refs_2_
  34.2 0.2 shard_map.81.refs_0_
  34.4 1.9 %collective-permute-start.18 = (bf16[8,2048]{1,0:T(8,128)(2,1)S(1)}, bf16[8,2048]{1,0:T(8,128)(2,1)S(1)}, u32[]{:S(2)}, u32[]{:S(2)}) collective-permute-start(bf16[8,2048]{1,0:T(8,128)(2,1)S(1)} %shard_map.81.refs_0_), channel_id=1, source_target_pairs={{0,13},{1,12},{2,15},{3,14},{4,9},{5,8},{6,11},{7,10},{8,5},{9,4},... | collective-permute-start | bytes 98312 | tf_op jit(solution)/shard_map/ppermute | solution.py:510
  36.3 0.5 %collective-permute-start.16 = (bf16[8,2048]{1,0:T(8,128)(2,1)S(1)}, bf16[8,2048]{1,0:T(8,128)(2,1)S(1)}, u32[]{:S(2)}, u32[]{:S(2)}) collective-permute-start(bf16[8,2048]{1,0:T(8,128)(2,1)S(1)} %shard_map.81.refs_0_), channel_id=1, source_target_pairs={{0,9},{1,8},{2,11},{3,10},{4,13},{5,12},{6,15},{7,14},{8,1},{9,0},... | collective-permute-start | bytes 98312 | tf_op jit(solution)/shard_map/ppermute | solution.py:510
  36.8 1.0 %collective-permute-start.20 = (bf16[8,2048]{1,0:T(8,128)(2,1)S(1)}, bf16[8,2048]{1,0:T(8,128)(2,1)S(1)}, u32[]{:S(2)}, u32[]{:S(2)}) collective-permute-start(bf16[8,2048]{1,0:T(8,128)(2,1)S(1)} %shard_map.81.refs_0_), channel_id=1, source_target_pairs={{0,2},{1,3},{2,0},{3,1},{4,6},{5,7},{6,4},{7,5},{8,10},{9,11},{10,... | collective-permute-start | bytes 98312 | tf_op jit(solution)/shard_map/ppermute | solution.py:510
  37.8 1.3 %collective-permute-start.14 = (bf16[8,2048]{1,0:T(8,128)(2,1)S(1)}, bf16[8,2048]{1,0:T(8,128)(2,1)S(1)}, u32[]{:S(2)}, u32[]{:S(2)}) collective-permute-start(bf16[8,2048]{1,0:T(8,128)(2,1)S(1)} %shard_map.81.refs_0_), channel_id=1, source_target_pairs={{0,5},{1,4},{2,7},{3,6},{4,1},{5,0},{6,3},{7,2},{8,13},{9,12},{10,... | collective-permute-start | bytes 98312 | tf_op jit(solution)/shard_map/ppermute | solution.py:510
  39.1 0.5 %collective-permute-done.18 = bf16[8,2048]{1,0:T(8,128)(2,1)S(1)} collective-permute-done((bf16[8,2048]{1,0:T(8,128)(2,1)S(1)}, bf16[8,2048]{1,0:T(8,128)(2,1)S(1)}, u32[]{:S(2)}, u32[]{:S(2)}) %collective-permute-start.18) | collective-permute-done | bytes 32800 | tf_op jit(solution)/shard_map/ppermute | solution.py:510
  39.6 1.1 %collective-permute-start.23 = (bf16[8,2048]{1,0:T(8,128)(2,1)S(1)}, bf16[8,2048]{1,0:T(8,128)(2,1)S(1)}, u32[]{:S(2)}, u32[]{:S(2)}) collective-permute-start(bf16[8,2048]{1,0:T(8,128)(2,1)S(1)} %collective-permute-done.18), channel_id=1, source_target_pairs={{0,3},{1,2},{2,1},{3,0},{4,7},{5,6},{6,5},{7,4},{8,11},{9,10},{10,... | collective-permute-start | bytes 98312 | tf_op jit(solution)/shard_map/ppermute | solution.py:510
  40.7 0.1 collective-permute-start.19
  40.8 0.9 %collective-permute-done.16 = bf16[8,2048]{1,0:T(8,128)(2,1)S(1)} collective-permute-done((bf16[8,2048]{1,0:T(8,128)(2,1)S(1)}, bf16[8,2048]{1,0:T(8,128)(2,1)S(1)}, u32[]{:S(2)}, u32[]{:S(2)}) %collective-permute-start.16) | collective-permute-done | bytes 32800 | tf_op jit(solution)/shard_map/ppermute | solution.py:510
  41.8 0.3 collective-permute-start.22
  42.1 0.0 collective-permute-done.20.refs_4_
  42.1 0.1 collective-permute-start.17
  42.2 0.0 collective-permute-done.14
  42.2 1.4 %collective-permute-start.21 = (bf16[8,2048]{1,0:T(8,128)(2,1)S(1)}, bf16[8,2048]{1,0:T(8,128)(2,1)S(1)}, u32[]{:S(2)}, u32[]{:S(2)}) collective-permute-start(bf16[8,2048]{1,0:T(8,128)(2,1)S(1)} %collective-permute-done.14), channel_id=1, source_target_pairs={{0,3},{1,2},{2,1},{3,0},{4,7},{5,6},{6,5},{7,4},{8,11},{9,10},{10,... | collective-permute-start | bytes 98312 | tf_op jit(solution)/shard_map/ppermute | solution.py:510
  43.6 0.0 collective-permute-done.23.refs_7_
  43.6 0.4 collective-permute-start.15
  44.0 0.0 collective-permute-done.19.refs_3_
  44.0 1.1 %collective-permute-done.22.refs_6_ = bf16[8,2048]{1,0:T(8,128)(2,1)S(1)} collective-permute-done((bf16[8,2048]{1,0:T(8,128)(2,1)S(1)}, bf16[8,2048]{1,0:T(8,128)(2,1)S(1)}, u32[]{:S(2)}, u32[]{:S(2)}) %collective-permute-start.22) | collective-permute-done | bytes 32800 | tf_op jit(solution)/shard_map/ppermute | solution.py:510
  45.2 0.0 collective-permute-done.17.refs_2_
  45.2 0.7 %collective-permute-done.21.refs_5_ = bf16[8,2048]{1,0:T(8,128)(2,1)S(1)} collective-permute-done((bf16[8,2048]{1,0:T(8,128)(2,1)S(1)}, bf16[8,2048]{1,0:T(8,128)(2,1)S(1)}, u32[]{:S(2)}, u32[]{:S(2)}) %collective-permute-start.21) | collective-permute-done | bytes 32800 | tf_op jit(solution)/shard_map/ppermute | solution.py:510
  45.8 0.0 collective-permute-done.15.refs_1_
  45.8 0.8 %shard_map.82 = bf16[32,4096]{1,0:T(8,128)(2,1)} custom-call(bf16[8,2048]{1,0:T(8,128)(2,1)S(1)} %shard_map.81.refs_0_, bf16[8,2048]{1,0:T(8,128)(2,1)S(1)} %collective-permute-done.15.refs_1_, bf16[8,2048]{1,0:T(8,128)(2,1)S(1)} %collective-permute-done.17.refs_2_, bf16[8,2048]{1,0:T(8,128)(2,1)S(1)} %collective-permute-done.19.refs_3_, ...), custom_call_target="tpu_custom_call" | custom-call | tf_op jit(solution)/shard_map/pallas_call | solution.py:407
  (7 shorter events, 0.0 us)
Async XLA Ops:
  0.6 2.5 %copy-start = (bf16[32,4096]{1,0:T(8,128)(2,1)S(1)}, bf16[32,4096]{1,0:T(8,128)(2,1)}, u32[]{:S(2)}) copy-start(bf16[32,4096]{1,0:T(8,128)(2,1)} %refs_4_.1) | copy-start | bytes 786436
  0.6 2.5 %copy-start.1 = (f32[32,256]{1,0:T(8,128)S(1)}, f32[32,256]{1,0:T(8,128)}, u32[]{:S(2)}) copy-start(f32[32,256]{1,0:T(8,128)} %cells_ref.3) | copy-start | bytes 98308
  0.7 5.1 %copy-start.2 = (s32[256]{0:T(256)S(1)}, s32[256]{0:T(256)}, u32[]{:S(2)}) copy-start(s32[256]{0:T(256)} %param.8) | copy-start | bytes 3076
  0.7 9.4 %copy-start.3 = (s32[8,256]{1,0:T(8,128)S(1)}, s32[8,256]{1,0:T(8,128)}, u32[]{:S(2)}) copy-start(s32[8,256]{1,0:T(8,128)} %neigh_ref.1) | copy-start | bytes 24580
  4.4 1.4 %collective-permute-start = (f32[32,384]{1,0:T(8,128)S(1)}, f32[32,384]{1,0:T(8,128)S(1)}, u32[]{:S(2)}, u32[]{:S(2)}) collective-permute-start(f32[32,384]{1,0:T(8,128)S(1)} %get-tuple-element.24.part_ref), channel_id=1, source_target_pairs={{0,1},{1,0},{2,3},{3,2},{4,5},{5,4},{6,7},{7,6},{8,9},{9,8},{10,11... | collective-permute-start | bytes 147464 | tf_op jit(solution)/shard_map/ppermute | solution.py:463
  5.9 5.4 %collective-permute-start.2 = (f32[40,128]{1,0:T(8,128)S(1)}, f32[40,128]{1,0:T(8,128)S(1)}, u32[]{:S(2)}, u32[]{:S(2)}) collective-permute-start(f32[40,128]{1,0:T(8,128)S(1)} %get-tuple-element.26), channel_id=1, source_target_pairs={{2,5},{4,3},{3,4},{5,2},{6,9},{8,7},{7,8},{9,6},{10,13},{12,11},{1... | collective-permute-start | bytes 61448 | tf_op jit(solution)/shard_map/ppermute | solution.py:468
  6.3 5.2 %collective-permute-start.1 = (f32[40,128]{1,0:T(8,128)S(1)}, f32[40,128]{1,0:T(8,128)S(1)}, u32[]{:S(2)}, u32[]{:S(2)}) collective-permute-start(f32[40,128]{1,0:T(8,128)S(1)} %get-tuple-element.26), channel_id=1, source_target_pairs={{0,3},{2,1},{1,2},{3,0},{4,7},{6,5},{5,6},{7,4},{8,11},{10,9},{9,1... | collective-permute-start | bytes 61448 | tf_op jit(solution)/shard_map/ppermute | solution.py:468
  12.3 1.3 %collective-permute-start.3 = (f32[32,256]{1,0:T(8,128)S(1)}, f32[32,256]{1,0:T(8,128)S(1)}, u32[]{:S(2)}, u32[]{:S(2)}) collective-permute-start(f32[32,256]{1,0:T(8,128)S(1)} %get-tuple-element.30.numer_ref), channel_id=1, source_target_pairs={{0,1},{1,0},{2,3},{3,2},{4,5},{5,4},{6,7},{7,6},{8,9},{9,8},{10,11... | collective-permute-start | bytes 98312 | tf_op jit(solution)/shard_map/ppermute | solution.py:463
  13.8 4.2 %collective-permute-start.5 = (f32[40,128]{1,0:T(8,128)S(1)}, f32[40,128]{1,0:T(8,128)S(1)}, u32[]{:S(2)}, u32[]{:S(2)}) collective-permute-start(f32[40,128]{1,0:T(8,128)S(1)} %get-tuple-element.34), channel_id=1, source_target_pairs={{2,5},{4,3},{3,4},{5,2},{6,9},{8,7},{7,8},{9,6},{10,13},{12,11},{1... | collective-permute-start | bytes 61448 | tf_op jit(solution)/shard_map/ppermute | solution.py:468
  13.9 4.4 %collective-permute-start.4 = (f32[40,128]{1,0:T(8,128)S(1)}, f32[40,128]{1,0:T(8,128)S(1)}, u32[]{:S(2)}, u32[]{:S(2)}) collective-permute-start(f32[40,128]{1,0:T(8,128)S(1)} %get-tuple-element.34), channel_id=1, source_target_pairs={{0,3},{2,1},{1,2},{3,0},{4,7},{6,5},{5,6},{7,4},{8,11},{10,9},{9,1... | collective-permute-start | bytes 61448 | tf_op jit(solution)/shard_map/ppermute | solution.py:468
  20.1 4.7 %collective-permute-start.7 = (s16[576,128]{1,0:T(8,128)(2,1)S(1)}, s16[576,128]{1,0:T(8,128)(2,1)S(1)}, u32[]{:S(2)}, u32[]{:S(2)}) collective-permute-start(s16[576,128]{1,0:T(8,128)(2,1)S(1)} %get-tuple-element.39), channel_id=1, source_target_pairs={{0,1},{1,0},{2,3},{3,2},{4,5},{5,4},{6,7},{7,6},{8,9},{9,8},{10,11... | collective-permute-start | bytes 442376 | tf_op jit(solution)/shard_map/ppermute | solution.py:510
  20.3 4.6 %collective-permute-start.6 = (s16[288,128]{1,0:T(8,128)(2,1)S(1)}, s16[288,128]{1,0:T(8,128)(2,1)S(1)}, u32[]{:S(2)}, u32[]{:S(2)}) collective-permute-start(s16[288,128]{1,0:T(8,128)(2,1)S(1)} %get-tuple-element.38), channel_id=1, source_target_pairs={{0,3},{1,2},{2,1},{3,0},{4,7},{5,6},{6,5},{7,4},{8,11},{9,10},{10,... | collective-permute-start | bytes 221192 | tf_op jit(solution)/shard_map/ppermute | solution.py:510
  22.2 7.4 %collective-permute-start.9 = (s16[144,128]{1,0:T(8,128)(2,1)S(1)}, s16[144,128]{1,0:T(8,128)(2,1)S(1)}, u32[]{:S(2)}, u32[]{:S(2)}) collective-permute-start(s16[144,128]{1,0:T(8,128)(2,1)S(1)} %get-tuple-element.40), channel_id=1, source_target_pairs={{0,3},{1,2},{2,1},{3,0},{4,7},{5,6},{6,5},{7,4},{8,11},{9,10},{10,... | collective-permute-start | bytes 110600 | tf_op jit(solution)/shard_map/ppermute | solution.py:510
  22.3 7.6 %collective-permute-start.11 = (s16[144,128]{1,0:T(8,128)(2,1)S(1)}, s16[144,128]{1,0:T(8,128)(2,1)S(1)}, u32[]{:S(2)}, u32[]{:S(2)}) collective-permute-start(s16[144,128]{1,0:T(8,128)(2,1)S(1)} %get-tuple-element.41), channel_id=1, source_target_pairs={{0,3},{1,2},{2,1},{3,0},{4,7},{5,6},{6,5},{7,4},{8,11},{9,10},{10,... | collective-permute-start | bytes 110600 | tf_op jit(solution)/shard_map/ppermute | solution.py:510
  25.0 6.1 %collective-permute-start.8 = (s16[144,128]{1,0:T(8,128)(2,1)S(1)}, s16[144,128]{1,0:T(8,128)(2,1)S(1)}, u32[]{:S(2)}, u32[]{:S(2)}) collective-permute-start(s16[144,128]{1,0:T(8,128)(2,1)S(1)} %shard_map.77), channel_id=1, source_target_pairs={{0,13},{1,12},{2,15},{3,14},{4,9},{5,8},{6,11},{7,10},{8,5},{9,4},... | collective-permute-start | bytes 110600 | tf_op jit(solution)/shard_map/ppermute | solution.py:510
  29.6 1.5 %collective-permute-start.13 = (s16[144,128]{1,0:T(8,128)(2,1)S(1)}, s16[144,128]{1,0:T(8,128)(2,1)S(1)}, u32[]{:S(2)}, u32[]{:S(2)}) collective-permute-start(s16[144,128]{1,0:T(8,128)(2,1)S(1)} %shard_map.80), channel_id=1, source_target_pairs={{0,1},{1,0},{2,3},{3,2},{4,5},{5,4},{6,7},{7,6},{8,9},{9,8},{10,11... | collective-permute-start | bytes 110600 | tf_op jit(solution)/shard_map/ppermute | solution.py:510
  29.8 4.4 %collective-permute-start.10 = (s16[144,128]{1,0:T(8,128)(2,1)S(1)}, s16[144,128]{1,0:T(8,128)(2,1)S(1)}, u32[]{:S(2)}, u32[]{:S(2)}) collective-permute-start(s16[144,128]{1,0:T(8,128)(2,1)S(1)} %shard_map.78), channel_id=1, source_target_pairs={{0,9},{1,8},{2,11},{3,10},{4,13},{5,12},{6,15},{7,14},{8,1},{9,0},... | collective-permute-start | bytes 110600 | tf_op jit(solution)/shard_map/ppermute | solution.py:510
  30.1 4.1 %collective-permute-start.12 = (s16[144,128]{1,0:T(8,128)(2,1)S(1)}, s16[144,128]{1,0:T(8,128)(2,1)S(1)}, u32[]{:S(2)}, u32[]{:S(2)}) collective-permute-start(s16[144,128]{1,0:T(8,128)(2,1)S(1)} %shard_map.79), channel_id=1, source_target_pairs={{0,5},{1,4},{2,7},{3,6},{4,1},{5,0},{6,3},{7,2},{8,13},{9,12},{10,... | collective-permute-start | bytes 110600 | tf_op jit(solution)/shard_map/ppermute | solution.py:510
  34.4 5.2 %collective-permute-start.18 = (bf16[8,2048]{1,0:T(8,128)(2,1)S(1)}, bf16[8,2048]{1,0:T(8,128)(2,1)S(1)}, u32[]{:S(2)}, u32[]{:S(2)}) collective-permute-start(bf16[8,2048]{1,0:T(8,128)(2,1)S(1)} %shard_map.81.refs_0_), channel_id=1, source_target_pairs={{0,13},{1,12},{2,15},{3,14},{4,9},{5,8},{6,11},{7,10},{8,5},{9,4},... | collective-permute-start | bytes 98312 | tf_op jit(solution)/shard_map/ppermute | solution.py:510
  36.3 5.5 %collective-permute-start.16 = (bf16[8,2048]{1,0:T(8,128)(2,1)S(1)}, bf16[8,2048]{1,0:T(8,128)(2,1)S(1)}, u32[]{:S(2)}, u32[]{:S(2)}) collective-permute-start(bf16[8,2048]{1,0:T(8,128)(2,1)S(1)} %shard_map.81.refs_0_), channel_id=1, source_target_pairs={{0,9},{1,8},{2,11},{3,10},{4,13},{5,12},{6,15},{7,14},{8,1},{9,0},... | collective-permute-start | bytes 98312 | tf_op jit(solution)/shard_map/ppermute | solution.py:510
  36.8 5.3 %collective-permute-start.20 = (bf16[8,2048]{1,0:T(8,128)(2,1)S(1)}, bf16[8,2048]{1,0:T(8,128)(2,1)S(1)}, u32[]{:S(2)}, u32[]{:S(2)}) collective-permute-start(bf16[8,2048]{1,0:T(8,128)(2,1)S(1)} %shard_map.81.refs_0_), channel_id=1, source_target_pairs={{0,2},{1,3},{2,0},{3,1},{4,6},{5,7},{6,4},{7,5},{8,10},{9,11},{10,... | collective-permute-start | bytes 98312 | tf_op jit(solution)/shard_map/ppermute | solution.py:510
  37.8 4.5 %collective-permute-start.14 = (bf16[8,2048]{1,0:T(8,128)(2,1)S(1)}, bf16[8,2048]{1,0:T(8,128)(2,1)S(1)}, u32[]{:S(2)}, u32[]{:S(2)}) collective-permute-start(bf16[8,2048]{1,0:T(8,128)(2,1)S(1)} %shard_map.81.refs_0_), channel_id=1, source_target_pairs={{0,5},{1,4},{2,7},{3,6},{4,1},{5,0},{6,3},{7,2},{8,13},{9,12},{10,... | collective-permute-start | bytes 98312 | tf_op jit(solution)/shard_map/ppermute | solution.py:510
  39.6 4.0 %collective-permute-start.23 = (bf16[8,2048]{1,0:T(8,128)(2,1)S(1)}, bf16[8,2048]{1,0:T(8,128)(2,1)S(1)}, u32[]{:S(2)}, u32[]{:S(2)}) collective-permute-start(bf16[8,2048]{1,0:T(8,128)(2,1)S(1)} %collective-permute-done.18), channel_id=1, source_target_pairs={{0,3},{1,2},{2,1},{3,0},{4,7},{5,6},{6,5},{7,4},{8,11},{9,10},{10,... | collective-permute-start | bytes 98312 | tf_op jit(solution)/shard_map/ppermute | solution.py:510
  40.7 3.3 %collective-permute-start.19 = (bf16[8,2048]{1,0:T(8,128)(2,1)S(1)}, bf16[8,2048]{1,0:T(8,128)(2,1)S(1)}, u32[]{:S(2)}, u32[]{:S(2)}) collective-permute-start(bf16[8,2048]{1,0:T(8,128)(2,1)S(1)} %collective-permute-done.18), channel_id=1, source_target_pairs={{0,1},{1,0},{2,3},{3,2},{4,5},{5,4},{6,7},{7,6},{8,9},{9,8},{10,11... | collective-permute-start | bytes 98312 | tf_op jit(solution)/shard_map/ppermute | solution.py:510
  41.8 3.4 %collective-permute-start.22 = (bf16[8,2048]{1,0:T(8,128)(2,1)S(1)}, bf16[8,2048]{1,0:T(8,128)(2,1)S(1)}, u32[]{:S(2)}, u32[]{:S(2)}) collective-permute-start(bf16[8,2048]{1,0:T(8,128)(2,1)S(1)} %collective-permute-done.16), channel_id=1, source_target_pairs={{0,3},{1,2},{2,1},{3,0},{4,7},{5,6},{6,5},{7,4},{8,11},{9,10},{10,... | collective-permute-start | bytes 98312 | tf_op jit(solution)/shard_map/ppermute | solution.py:510
  42.1 3.1 %collective-permute-start.17 = (bf16[8,2048]{1,0:T(8,128)(2,1)S(1)}, bf16[8,2048]{1,0:T(8,128)(2,1)S(1)}, u32[]{:S(2)}, u32[]{:S(2)}) collective-permute-start(bf16[8,2048]{1,0:T(8,128)(2,1)S(1)} %collective-permute-done.16), channel_id=1, source_target_pairs={{0,1},{1,0},{2,3},{3,2},{4,5},{5,4},{6,7},{7,6},{8,9},{9,8},{10,11... | collective-permute-start | bytes 98312 | tf_op jit(solution)/shard_map/ppermute | solution.py:510
  42.2 3.6 %collective-permute-start.21 = (bf16[8,2048]{1,0:T(8,128)(2,1)S(1)}, bf16[8,2048]{1,0:T(8,128)(2,1)S(1)}, u32[]{:S(2)}, u32[]{:S(2)}) collective-permute-start(bf16[8,2048]{1,0:T(8,128)(2,1)S(1)} %collective-permute-done.14), channel_id=1, source_target_pairs={{0,3},{1,2},{2,1},{3,0},{4,7},{5,6},{6,5},{7,4},{8,11},{9,10},{10,... | collective-permute-start | bytes 98312 | tf_op jit(solution)/shard_map/ppermute | solution.py:510
  43.6 2.2 %collective-permute-start.15 = (bf16[8,2048]{1,0:T(8,128)(2,1)S(1)}, bf16[8,2048]{1,0:T(8,128)(2,1)S(1)}, u32[]{:S(2)}, u32[]{:S(2)}) collective-permute-start(bf16[8,2048]{1,0:T(8,128)(2,1)S(1)} %collective-permute-done.14), channel_id=1, source_target_pairs={{0,1},{1,0},{2,3},{3,2},{4,5},{5,4},{6,7},{7,6},{8,9},{9,8},{10,11... | collective-permute-start | bytes 98312 | tf_op jit(solution)/shard_map/ppermute | solution.py:510

commit v8 on v7

--- a/solution.py
+++ b/solution.py
@@ -157,7 +157,7 @@
 
 
 def first_update_kernel(
-    part_ref, other_ref, cells_ref, tissue_ref, updated_ref, edges_ref, gsum_ref
+    part_ref, other_ref, cells_ref, tissue_ref, _, updated_ref, edges_ref, gsum_ref
 ):
     width = cells_ref.shape[1]
     gsum_ref[...] = part_ref[:, width:] + other_ref[:, width:]
@@ -272,18 +272,23 @@
     return jnp.concatenate(blocks[: columns // LANES], axis=1), hden
 
 
-def gene_totals(cells, flags, kept_ref, rows_ref, totals_ref):
+def gene_totals(cells, flags, kept_ref, rows_ref, totals_ref, others_ref=None):
+    def put(columns, values):
+        if others_ref is not None:
+            values += others_ref[:, columns]
+        totals_ref[:, columns] = values
+
     rank = cells.shape[0]
     genes = totals_ref.shape[1] - LANES
     masked = jnp.where(flags, cells, 0.0)
     parts = jnp.concatenate(split(masked), axis=0)
     columns = parts.astype(jnp.float32).T.astype(jnp.bfloat16)
     hden = jnp.sum(masked, axis=1, keepdims=True)
-    totals_ref[:, genes:] = jnp.broadcast_to(hden, (rank, LANES))
+    put(slice(genes, genes + LANES), jnp.broadcast_to(hden, (rank, LANES)))
     for run in runs_of(genes, 1024):
         ratio = ratio_of(kept_ref, run, rows_ref[run], cells)
         total = jnp.dot(ratio, columns, preferred_element_type=jnp.float32).T
-        totals_ref[:, run] = total[:rank] + total[rank:]
+        put(run, total[:rank] + total[rank:])
 
 
 def inner_totals_kernel(
@@ -300,8 +305,7 @@
 ):
     cells, flags = smoothed_outer(updated_ref, tissue_ref, pick_ref, first_ref, second_ref)
     cells_ref[...] = whole_of(cells, inner_cells_ref[...])
-    gene_totals(cells, flags, kept_ref, rows_ref, totals_ref)
-    totals_ref[...] += inner_totals_ref[...]
+    gene_totals(cells, flags, kept_ref, rows_ref, totals_ref, inner_totals_ref)
 
 
 def encode_tiles(totals_ref, sent_ref):
@@ -337,7 +341,8 @@
         place[start : start + height] = coded_ref[there ^ 1]
 
 
-def column_kernel(distance, columns, got_ref, own_ref, sent_ref):
+def column_kernel(distance, columns, got_ref, own_ref, *refs):
+    sent_ref = refs[-1]
     height = sent_ref.shape[0]
     start = 0 if distance else height
     values, hden = decode(got_ref.at[start : start + height], columns)
@@ -442,6 +447,7 @@
     half_kept = shape((genes, width // 2), jnp.bfloat16)
     gene_rows = shape((genes, 2 * rank), jnp.bfloat16)
     far = pl.BlockSpec(memory_space=pl.ANY)
+    near = pl.BlockSpec(memory_space=pltpu.VMEM)
 
     outer, inner = call(
         turn_kernel,
@@ -470,8 +476,10 @@
         ]
 
     updated, edges, gsum = call(
-        first_update_kernel, (factor, edge, shape((rank, LANES), jnp.float32))
-    )(part, swapped(part), cell_factor, flag_row)
+        first_update_kernel,
+        (factor, edge, shape((rank, LANES), jnp.float32)),
+        specs=[near] * 4 + [far],
+    )(part, swapped(part), cell_factor, flag_row, pick)
     inner_of_both = call(inner_kernel, (half, half))(
         updated, flag_row, pick, inner, rows, gene_factor
     )
@@ -526,9 +534,11 @@
     got[0] = got[groups - 1]
     summed = []
     for distance in (*distances, 0):
-        both = call(functools.partial(column_kernel, distance, columns), one)(
-            got[distance], own
-        )
+        after = () if distance else summed[:1]
+        both = call(
+            functools.partial(column_kernel, distance, columns), one,
+            specs=[near] * 2 + [far] * len(after),
+        )(got[distance], own, *after)
         summed.append(moved(both, 2 * distance, 1))
     fresh = call(fresh_kernel, shape((ROWS, columns), jnp.bfloat16))(*summed, gene_factor)
     shares, others = [fresh], [moved(fresh, 1, 0)]

time: 46.8 us -> 46.4 us (level)
  starting transfers between devices: 25.1 us -> 23 us
  waiting for transfers between devices: 9.95 us -> 11.6 us
    ppermute x18, starting transfers between devices: 17.2 us -> 15 us  [moved(): return lax.ppermute(array, ('tile', 'gene'), pairs)]
    ppermute x18, waiting for transfers between devices: 7.52 us -> 9.18 us  [moved(): return lax.ppermute(array, ('tile', 'gene'), pairs)]
  transfers between devices with their start and end apart: 24 -> 24, of which waited for: 11 -> 13; matrix products, arithmetic and copies ran while one was open for 0% -> 0% of each run, Pallas kernels for 7% -> 7%
where the time goes in v8:
time: 46.4 us; the launch traced here: 46.2 us
  starting transfers between devices  23 us (50%)
  waiting for transfers between devices  11.6 us (25%)
  Pallas kernels  10.8 us (23%)
  between operations  0.83 us (2%)
    ppermute x18, starting transfers between devices, moved(): return lax.ppermute(array, ('tile', 'gene'), pairs)  15 us
    pallas_call x15, Pallas kernels, call(): pl.pallas_call(kernel, out_shape=outs, in_specs=specs or [whole] * len(ar...  10.8 us
    ppermute x18, waiting for transfers between devices, moved(): return lax.ppermute(array, ('tile', 'gene'), pairs)  9.18 us
    ppermute x4, starting transfers between devices, around(): lax.ppermute(edges, ('tile', 'gene'), beside(tiles, halves, offset))  7.2 us
    ppermute x2, waiting for transfers between devices, swapped(): return lax.ppermute(part, 'gene', [(0, 1), (1, 0)])  1.55 us
  transfers between devices with their start and end apart: 24, of which 13 were waited for; matrix products, arithmetic and copies ran while one was open for 0% of the time, Pallas kernels for 7%

profile of v8, /device:TPU:0, one launch (start us, length us, event | category | flops | bytes accessed | tf_op | source)
XLA Modules:
  0.0 46.2 jit_solution(15650780938521287419)
XLA Ops:
  0.7 2.4 %shard_map.68 = (bf16[4096,128]{1,0:T(8,128)(2,1)S(1)}, bf16[4096,128]{1,0:T(8,128)(2,1)S(1)}) custom-call(s32[256,4096]{1,0:T(8,128)} %counts_ref.1), custom_call_target="tpu_custom_call" | custom-call | tf_op jit(solution)/shard_map/pallas_call | solution.py:412
  3.1 0.0 copy-done
  3.1 1.3 %shard_map.69 = (f32[32,384]{1,0:T(8,128)S(1)}, bf16[4096,64]{1,0:T(8,128)(2,1)S(1)}) custom-call(bf16[4096,128]{1,0:T(8,128)(2,1)S(1)} %get-tuple-element.22.outer_ref.kept_ref.refs_5_, bf16[4096,128]{1,0:T(8,128)(2,1)S(1)} %get-tuple-element.23.inner_ref.kept_ref, f32[32,256]{1,0:T(8,128)S(1)} %copy-done.1, bf16[32,4096]{1,0:T(8,128)(2,1)S(1)} %copy-done), custom_call_target="tpu_custom_call" | custom-call | tf_op jit(solution)/shard_map/pallas_call | solution.py:412
  4.4 0.5 %collective-permute-start = (f32[32,384]{1,0:T(8,128)S(1)}, f32[32,384]{1,0:T(8,128)S(1)}, u32[]{:S(2)}, u32[]{:S(2)}) collective-permute-start(f32[32,384]{1,0:T(8,128)S(1)} %get-tuple-element.24.part_ref), channel_id=1, source_target_pairs={{0,1},{1,0},{2,3},{3,2},{4,5},{5,4},{6,7},{7,6},{8,9},{9,8},{10,11... | collective-permute-start | bytes 147464 | tf_op jit(solution)/shard_map/ppermute | solution.py:469
  4.9 0.4 shard_map.70._.pick_ref.refs_2_
  5.3 0.5 %collective-permute-done.other_ref = f32[32,384]{1,0:T(8,128)S(1)} collective-permute-done((f32[32,384]{1,0:T(8,128)S(1)}, f32[32,384]{1,0:T(8,128)S(1)}, u32[]{:S(2)}, u32[]{:S(2)}) %collective-permute-start) | collective-permute-done | bytes 49184 | tf_op jit(solution)/shard_map/ppermute | solution.py:469
  5.8 0.2 shard_map.71
  5.9 0.4 collective-permute-start.2
  6.3 3.8 %collective-permute-start.1 = (f32[40,128]{1,0:T(8,128)S(1)}, f32[40,128]{1,0:T(8,128)S(1)}, u32[]{:S(2)}, u32[]{:S(2)}) collective-permute-start(f32[40,128]{1,0:T(8,128)S(1)} %get-tuple-element.26), channel_id=1, source_target_pairs={{0,3},{2,1},{1,2},{3,0},{4,7},{6,5},{5,6},{7,4},{8,11},{10,9},{9,1... | collective-permute-start | bytes 61448 | tf_op jit(solution)/shard_map/ppermute | solution.py:474
  10.0 0.9 %shard_map.72 = (f32[32,128]{1,0:T(8,128)S(1)}, f32[32,128]{1,0:T(8,128)S(1)}) custom-call(f32[32,256]{1,0:T(8,128)S(1)} %get-tuple-element.25.updated_ref, s32[1,256]{1,0:T(1,128)S(1)} %bitcast.2, bf16[384,256]{1,0:T(8,128)(2,1)S(1)} %shard_map.70._.pick_ref.refs_2_, bf16[4096,128]{1,0:T(8,128)(2,1)S(1)} %get-tuple-element.23.inner_ref.kept_ref, ...), custom_call_target="tpu_custom_call" | custom-call | tf_op jit(solution)/shard_map/pallas_call | solution.py:412
  10.9 0.0 collective-permute-done.2.second_ref
  11.0 0.6 %collective-permute-done.1.first_ref = f32[40,128]{1,0:T(8,128)S(1)} collective-permute-done((f32[40,128]{1,0:T(8,128)S(1)}, f32[40,128]{1,0:T(8,128)S(1)}, u32[]{:S(2)}, u32[]{:S(2)}) %collective-permute-start.1) | collective-permute-done | bytes 20512 | tf_op jit(solution)/shard_map/ppermute | solution.py:474
  11.5 0.8 %shard_map.73 = (f32[32,256]{1,0:T(8,128)S(1)}, f32[32,256]{1,0:T(8,128)S(1)}) custom-call(f32[32,256]{1,0:T(8,128)S(1)} %get-tuple-element.25.updated_ref, s32[1,256]{1,0:T(1,128)S(1)} %bitcast.3, bf16[384,256]{1,0:T(8,128)(2,1)S(1)} %shard_map.70._.pick_ref.refs_2_, f32[40,128]{1,0:T(8,128)S(1)} %collective-permute-done.1.first_ref, ...), custom_call_target="tpu_custom_call" | custom-call | tf_op jit(solution)/shard_map/pallas_call | solution.py:412
  12.3 0.2 collective-permute-start.3
  12.6 1.1 %collective-permute-done.3.other_ref = f32[32,256]{1,0:T(8,128)S(1)} collective-permute-done((f32[32,256]{1,0:T(8,128)S(1)}, f32[32,256]{1,0:T(8,128)S(1)}, u32[]{:S(2)}, u32[]{:S(2)}) %collective-permute-start.3) | collective-permute-done | bytes 32800 | tf_op jit(solution)/shard_map/ppermute | solution.py:469
  13.6 0.1 shard_map.74
  13.8 0.2 collective-permute-start.5
  13.9 2.9 %collective-permute-start.4 = (f32[40,128]{1,0:T(8,128)S(1)}, f32[40,128]{1,0:T(8,128)S(1)}, u32[]{:S(2)}, u32[]{:S(2)}) collective-permute-start(f32[40,128]{1,0:T(8,128)S(1)} %get-tuple-element.34), channel_id=1, source_target_pairs={{0,3},{2,1},{1,2},{3,0},{4,7},{6,5},{5,6},{7,4},{8,11},{10,9},{9,1... | collective-permute-start | bytes 61448 | tf_op jit(solution)/shard_map/ppermute | solution.py:474
  16.9 1.1 %shard_map.75 = (f32[32,128]{1,0:T(8,128)S(1)}, f32[32,4224]{1,0:T(8,128)S(1)}) custom-call(f32[32,256]{1,0:T(8,128)S(1)} %get-tuple-element.33.updated_ref.refs_0_, s32[1,256]{1,0:T(1,128)S(1)} %bitcast.5, bf16[384,256]{1,0:T(8,128)(2,1)S(1)} %shard_map.70._.pick_ref.refs_2_, bf16[4096,128]{1,0:T(8,128)(2,1)S(1)} %get-tuple-element.23.inner_ref.kept_ref, ...), custom_call_target="tpu_custom_call" | custom-call | tf_op jit(solution)/shard_map/pallas_call | solution.py:412
  18.0 0.0 collective-permute-done.5.refs_4_
  18.0 0.3 collective-permute-done.4.refs_3_
  18.3 1.8 %shard_map.76 = (f32[32,256]{1,0:T(8,128)}, s16[144,128]{1,0:T(8,128)(2,1)S(1)}, s16[144,128]{1,0:T(8,128)(2,1)S(1)}, s16[288,128]{1,0:T(8,128)(2,1)S(1)}, s16[576,128]{1,0:T(8,128)(2,1)S(1)}) custom-call(f32[32,256]{1,0:T(8,128)S(1)} %get-tuple-element.33.updated_ref.refs_0_, s32[1,256]{1,0:T(1,128)S(1)} %bitcast.6, ...), custom_call_target="tpu_custom_call" | custom-call | tf_op jit(solution)/shard_map/pallas_call | solution.py:412
  20.1 0.1 collective-permute-start.7
  20.3 2.0 %collective-permute-start.6 = (s16[288,128]{1,0:T(8,128)(2,1)S(1)}, s16[288,128]{1,0:T(8,128)(2,1)S(1)}, u32[]{:S(2)}, u32[]{:S(2)}) collective-permute-start(s16[288,128]{1,0:T(8,128)(2,1)S(1)} %get-tuple-element.38), channel_id=1, source_target_pairs={{0,3},{1,2},{2,1},{3,0},{4,7},{5,6},{6,5},{7,4},{8,11},{9,10},{10,... | collective-permute-start | bytes 221192 | tf_op jit(solution)/shard_map/ppermute | solution.py:518
  22.2 0.0 collective-permute-start.9
  22.3 1.7 %collective-permute-start.11 = (s16[144,128]{1,0:T(8,128)(2,1)S(1)}, s16[144,128]{1,0:T(8,128)(2,1)S(1)}, u32[]{:S(2)}, u32[]{:S(2)}) collective-permute-start(s16[144,128]{1,0:T(8,128)(2,1)S(1)} %get-tuple-element.41), channel_id=1, source_target_pairs={{0,3},{1,2},{2,1},{3,0},{4,7},{5,6},{6,5},{7,4},{8,11},{9,10},{10,... | collective-permute-start | bytes 110600 | tf_op jit(solution)/shard_map/ppermute | solution.py:518
  24.0 0.8 %collective-permute-done.6.got_ref = s16[288,128]{1,0:T(8,128)(2,1)S(1)} collective-permute-done((s16[288,128]{1,0:T(8,128)(2,1)S(1)}, s16[288,128]{1,0:T(8,128)(2,1)S(1)}, u32[]{:S(2)}, u32[]{:S(2)}) %collective-permute-start.6) | collective-permute-done | bytes 73760 | tf_op jit(solution)/shard_map/ppermute | solution.py:518
  24.8 0.0 collective-permute-done.7.own_ref
  24.8 0.2 shard_map.77
  25.0 4.3 %collective-permute-start.8 = (s16[144,128]{1,0:T(8,128)(2,1)S(1)}, s16[144,128]{1,0:T(8,128)(2,1)S(1)}, u32[]{:S(2)}, u32[]{:S(2)}) collective-permute-start(s16[144,128]{1,0:T(8,128)(2,1)S(1)} %shard_map.77), channel_id=1, source_target_pairs={{0,13},{1,12},{2,15},{3,14},{4,9},{5,8},{6,11},{7,10},{8,5},{9,4},... | collective-permute-start | bytes 110600 | tf_op jit(solution)/shard_map/ppermute | solution.py:518
  29.4 0.0 collective-permute-done.9.got_ref
  29.4 0.2 shard_map.78
  29.6 0.1 collective-permute-start.10
  29.6 0.0 collective-permute-done.11.got_ref
  29.6 0.2 shard_map.79
  29.8 0.2 collective-permute-start.12
  30.1 1.0 %collective-permute-done.8.refs_0_ = s16[144,128]{1,0:T(8,128)(2,1)S(1)} collective-permute-done((s16[144,128]{1,0:T(8,128)(2,1)S(1)}, s16[144,128]{1,0:T(8,128)(2,1)S(1)}, u32[]{:S(2)}, u32[]{:S(2)}) %collective-permute-start.8) | collective-permute-done | bytes 36896 | tf_op jit(solution)/shard_map/ppermute | solution.py:518
  31.1 0.2 shard_map.80
  31.3 0.1 collective-permute-start.13
  31.4 2.7 %collective-permute-done.10.refs_1_ = s16[144,128]{1,0:T(8,128)(2,1)S(1)} collective-permute-done((s16[144,128]{1,0:T(8,128)(2,1)S(1)}, s16[144,128]{1,0:T(8,128)(2,1)S(1)}, u32[]{:S(2)}, u32[]{:S(2)}) %collective-permute-start.10) | collective-permute-done | bytes 36896 | tf_op jit(solution)/shard_map/ppermute | solution.py:518
  34.1 0.1 collective-permute-done.12.refs_2_
  34.1 0.0 collective-permute-done.13.refs_3_
  34.2 0.2 shard_map.81.refs_0_
  34.3 1.9 %collective-permute-start.18 = (bf16[8,2048]{1,0:T(8,128)(2,1)S(1)}, bf16[8,2048]{1,0:T(8,128)(2,1)S(1)}, u32[]{:S(2)}, u32[]{:S(2)}) collective-permute-start(bf16[8,2048]{1,0:T(8,128)(2,1)S(1)} %shard_map.81.refs_0_), channel_id=1, source_target_pairs={{0,13},{1,12},{2,15},{3,14},{4,9},{5,8},{6,11},{7,10},{8,5},{9,4},... | collective-permute-start | bytes 98312 | tf_op jit(solution)/shard_map/ppermute | solution.py:518
  36.3 0.0 collective-permute-start.16
  36.3 0.5 %collective-permute-start.20 = (bf16[8,2048]{1,0:T(8,128)(2,1)S(1)}, bf16[8,2048]{1,0:T(8,128)(2,1)S(1)}, u32[]{:S(2)}, u32[]{:S(2)}) collective-permute-start(bf16[8,2048]{1,0:T(8,128)(2,1)S(1)} %shard_map.81.refs_0_), channel_id=1, source_target_pairs={{0,2},{1,3},{2,0},{3,1},{4,6},{5,7},{6,4},{7,5},{8,10},{9,11},{10,... | collective-permute-start | bytes 98312 | tf_op jit(solution)/shard_map/ppermute | solution.py:518
  36.8 1.5 %collective-permute-start.14 = (bf16[8,2048]{1,0:T(8,128)(2,1)S(1)}, bf16[8,2048]{1,0:T(8,128)(2,1)S(1)}, u32[]{:S(2)}, u32[]{:S(2)}) collective-permute-start(bf16[8,2048]{1,0:T(8,128)(2,1)S(1)} %shard_map.81.refs_0_), channel_id=1, source_target_pairs={{0,5},{1,4},{2,7},{3,6},{4,1},{5,0},{6,3},{7,2},{8,13},{9,12},{10,... | collective-permute-start | bytes 98312 | tf_op jit(solution)/shard_map/ppermute | solution.py:518
  38.3 1.3 %collective-permute-done.18 = bf16[8,2048]{1,0:T(8,128)(2,1)S(1)} collective-permute-done((bf16[8,2048]{1,0:T(8,128)(2,1)S(1)}, bf16[8,2048]{1,0:T(8,128)(2,1)S(1)}, u32[]{:S(2)}, u32[]{:S(2)}) %collective-permute-start.18) | collective-permute-done | bytes 32800 | tf_op jit(solution)/shard_map/ppermute | solution.py:518
  39.7 0.6 %collective-permute-start.23 = (bf16[8,2048]{1,0:T(8,128)(2,1)S(1)}, bf16[8,2048]{1,0:T(8,128)(2,1)S(1)}, u32[]{:S(2)}, u32[]{:S(2)}) collective-permute-start(bf16[8,2048]{1,0:T(8,128)(2,1)S(1)} %collective-permute-done.18), channel_id=1, source_target_pairs={{0,3},{1,2},{2,1},{3,0},{4,7},{5,6},{6,5},{7,4},{8,11},{9,10},{10,... | collective-permute-start | bytes 98312 | tf_op jit(solution)/shard_map/ppermute | solution.py:518
  40.3 0.0 collective-permute-start.19
  40.3 0.8 %collective-permute-done.16 = bf16[8,2048]{1,0:T(8,128)(2,1)S(1)} collective-permute-done((bf16[8,2048]{1,0:T(8,128)(2,1)S(1)}, bf16[8,2048]{1,0:T(8,128)(2,1)S(1)}, u32[]{:S(2)}, u32[]{:S(2)}) %collective-permute-start.16) | collective-permute-done | bytes 32800 | tf_op jit(solution)/shard_map/ppermute | solution.py:518
  41.1 0.4 collective-permute-start.22
  41.4 0.0 collective-permute-done.20.refs_4_
  41.4 0.5 %collective-permute-start.17 = (bf16[8,2048]{1,0:T(8,128)(2,1)S(1)}, bf16[8,2048]{1,0:T(8,128)(2,1)S(1)}, u32[]{:S(2)}, u32[]{:S(2)}) collective-permute-start(bf16[8,2048]{1,0:T(8,128)(2,1)S(1)} %collective-permute-done.16), channel_id=1, source_target_pairs={{0,1},{1,0},{2,3},{3,2},{4,5},{5,4},{6,7},{7,6},{8,9},{9,8},{10,11... | collective-permute-start | bytes 98312 | tf_op jit(solution)/shard_map/ppermute | solution.py:518
  41.9 0.0 collective-permute-done.14
  41.9 0.9 %collective-permute-start.21 = (bf16[8,2048]{1,0:T(8,128)(2,1)S(1)}, bf16[8,2048]{1,0:T(8,128)(2,1)S(1)}, u32[]{:S(2)}, u32[]{:S(2)}) collective-permute-start(bf16[8,2048]{1,0:T(8,128)(2,1)S(1)} %collective-permute-done.14), channel_id=1, source_target_pairs={{0,3},{1,2},{2,1},{3,0},{4,7},{5,6},{6,5},{7,4},{8,11},{9,10},{10,... | collective-permute-start | bytes 98312 | tf_op jit(solution)/shard_map/ppermute | solution.py:518
  42.9 0.4 collective-permute-done.23.refs_7_
  43.3 0.1 collective-permute-start.15
  43.4 0.0 collective-permute-done.19.refs_3_
  43.4 1.2 %collective-permute-done.22.refs_6_ = bf16[8,2048]{1,0:T(8,128)(2,1)S(1)} collective-permute-done((bf16[8,2048]{1,0:T(8,128)(2,1)S(1)}, bf16[8,2048]{1,0:T(8,128)(2,1)S(1)}, u32[]{:S(2)}, u32[]{:S(2)}) %collective-permute-start.22) | collective-permute-done | bytes 32800 | tf_op jit(solution)/shard_map/ppermute | solution.py:518
  44.6 0.0 collective-permute-done.17.refs_2_
  44.6 0.8 %collective-permute-done.21.refs_5_ = bf16[8,2048]{1,0:T(8,128)(2,1)S(1)} collective-permute-done((bf16[8,2048]{1,0:T(8,128)(2,1)S(1)}, bf16[8,2048]{1,0:T(8,128)(2,1)S(1)}, u32[]{:S(2)}, u32[]{:S(2)}) %collective-permute-start.21) | collective-permute-done | bytes 32800 | tf_op jit(solution)/shard_map/ppermute | solution.py:518
  45.4 0.0 collective-permute-done.15.refs_1_
  45.4 0.8 %shard_map.82 = bf16[32,4096]{1,0:T(8,128)(2,1)} custom-call(bf16[8,2048]{1,0:T(8,128)(2,1)S(1)} %shard_map.81.refs_0_, bf16[8,2048]{1,0:T(8,128)(2,1)S(1)} %collective-permute-done.15.refs_1_, bf16[8,2048]{1,0:T(8,128)(2,1)S(1)} %collective-permute-done.17.refs_2_, bf16[8,2048]{1,0:T(8,128)(2,1)S(1)} %collective-permute-done.19.refs_3_, ...), custom_call_target="tpu_custom_call" | custom-call | tf_op jit(solution)/shard_map/pallas_call | solution.py:412
  (7 shorter events, 0.0 us)
Async XLA Ops:
  0.6 2.5 %copy-start = (bf16[32,4096]{1,0:T(8,128)(2,1)S(1)}, bf16[32,4096]{1,0:T(8,128)(2,1)}, u32[]{:S(2)}) copy-start(bf16[32,4096]{1,0:T(8,128)(2,1)} %refs_4_.1) | copy-start | bytes 786436
  0.6 2.5 %copy-start.1 = (f32[32,256]{1,0:T(8,128)S(1)}, f32[32,256]{1,0:T(8,128)}, u32[]{:S(2)}) copy-start(f32[32,256]{1,0:T(8,128)} %cells_ref.3) | copy-start | bytes 98308
  0.7 4.2 %copy-start.3 = (s32[8,256]{1,0:T(8,128)S(1)}, s32[8,256]{1,0:T(8,128)}, u32[]{:S(2)}) copy-start(s32[8,256]{1,0:T(8,128)} %neigh_ref.1) | copy-start | bytes 24580
  0.7 5.1 %copy-start.2 = (s32[256]{0:T(256)S(1)}, s32[256]{0:T(256)}, u32[]{:S(2)}) copy-start(s32[256]{0:T(256)} %param.8) | copy-start | bytes 3076
  4.4 1.4 %collective-permute-start = (f32[32,384]{1,0:T(8,128)S(1)}, f32[32,384]{1,0:T(8,128)S(1)}, u32[]{:S(2)}, u32[]{:S(2)}) collective-permute-start(f32[32,384]{1,0:T(8,128)S(1)} %get-tuple-element.24.part_ref), channel_id=1, source_target_pairs={{0,1},{1,0},{2,3},{3,2},{4,5},{5,4},{6,7},{7,6},{8,9},{9,8},{10,11... | collective-permute-start | bytes 147464 | tf_op jit(solution)/shard_map/ppermute | solution.py:469
  5.9 5.0 %collective-permute-start.2 = (f32[40,128]{1,0:T(8,128)S(1)}, f32[40,128]{1,0:T(8,128)S(1)}, u32[]{:S(2)}, u32[]{:S(2)}) collective-permute-start(f32[40,128]{1,0:T(8,128)S(1)} %get-tuple-element.26), channel_id=1, source_target_pairs={{2,5},{4,3},{3,4},{5,2},{6,9},{8,7},{7,8},{9,6},{10,13},{12,11},{1... | collective-permute-start | bytes 61448 | tf_op jit(solution)/shard_map/ppermute | solution.py:474
  6.3 5.2 %collective-permute-start.1 = (f32[40,128]{1,0:T(8,128)S(1)}, f32[40,128]{1,0:T(8,128)S(1)}, u32[]{:S(2)}, u32[]{:S(2)}) collective-permute-start(f32[40,128]{1,0:T(8,128)S(1)} %get-tuple-element.26), channel_id=1, source_target_pairs={{0,3},{2,1},{1,2},{3,0},{4,7},{6,5},{5,6},{7,4},{8,11},{10,9},{9,1... | collective-permute-start | bytes 61448 | tf_op jit(solution)/shard_map/ppermute | solution.py:474
  12.3 1.3 %collective-permute-start.3 = (f32[32,256]{1,0:T(8,128)S(1)}, f32[32,256]{1,0:T(8,128)S(1)}, u32[]{:S(2)}, u32[]{:S(2)}) collective-permute-start(f32[32,256]{1,0:T(8,128)S(1)} %get-tuple-element.30.numer_ref), channel_id=1, source_target_pairs={{0,1},{1,0},{2,3},{3,2},{4,5},{5,4},{6,7},{7,6},{8,9},{9,8},{10,11... | collective-permute-start | bytes 98312 | tf_op jit(solution)/shard_map/ppermute | solution.py:469
  13.8 4.2 %collective-permute-start.5 = (f32[40,128]{1,0:T(8,128)S(1)}, f32[40,128]{1,0:T(8,128)S(1)}, u32[]{:S(2)}, u32[]{:S(2)}) collective-permute-start(f32[40,128]{1,0:T(8,128)S(1)} %get-tuple-element.34), channel_id=1, source_target_pairs={{2,5},{4,3},{3,4},{5,2},{6,9},{8,7},{7,8},{9,6},{10,13},{12,11},{1... | collective-permute-start | bytes 61448 | tf_op jit(solution)/shard_map/ppermute | solution.py:474
  13.9 4.4 %collective-permute-start.4 = (f32[40,128]{1,0:T(8,128)S(1)}, f32[40,128]{1,0:T(8,128)S(1)}, u32[]{:S(2)}, u32[]{:S(2)}) collective-permute-start(f32[40,128]{1,0:T(8,128)S(1)} %get-tuple-element.34), channel_id=1, source_target_pairs={{0,3},{2,1},{1,2},{3,0},{4,7},{6,5},{5,6},{7,4},{8,11},{10,9},{9,1... | collective-permute-start | bytes 61448 | tf_op jit(solution)/shard_map/ppermute | solution.py:474
  20.1 4.7 %collective-permute-start.7 = (s16[576,128]{1,0:T(8,128)(2,1)S(1)}, s16[576,128]{1,0:T(8,128)(2,1)S(1)}, u32[]{:S(2)}, u32[]{:S(2)}) collective-permute-start(s16[576,128]{1,0:T(8,128)(2,1)S(1)} %get-tuple-element.39), channel_id=1, source_target_pairs={{0,1},{1,0},{2,3},{3,2},{4,5},{5,4},{6,7},{7,6},{8,9},{9,8},{10,11... | collective-permute-start | bytes 442376 | tf_op jit(solution)/shard_map/ppermute | solution.py:518
  20.3 4.6 %collective-permute-start.6 = (s16[288,128]{1,0:T(8,128)(2,1)S(1)}, s16[288,128]{1,0:T(8,128)(2,1)S(1)}, u32[]{:S(2)}, u32[]{:S(2)}) collective-permute-start(s16[288,128]{1,0:T(8,128)(2,1)S(1)} %get-tuple-element.38), channel_id=1, source_target_pairs={{0,3},{1,2},{2,1},{3,0},{4,7},{5,6},{6,5},{7,4},{8,11},{9,10},{10,... | collective-permute-start | bytes 221192 | tf_op jit(solution)/shard_map/ppermute | solution.py:518
  22.2 7.1 %collective-permute-start.9 = (s16[144,128]{1,0:T(8,128)(2,1)S(1)}, s16[144,128]{1,0:T(8,128)(2,1)S(1)}, u32[]{:S(2)}, u32[]{:S(2)}) collective-permute-start(s16[144,128]{1,0:T(8,128)(2,1)S(1)} %get-tuple-element.40), channel_id=1, source_target_pairs={{0,3},{1,2},{2,1},{3,0},{4,7},{5,6},{6,5},{7,4},{8,11},{9,10},{10,... | collective-permute-start | bytes 110600 | tf_op jit(solution)/shard_map/ppermute | solution.py:518
  22.3 7.4 %collective-permute-start.11 = (s16[144,128]{1,0:T(8,128)(2,1)S(1)}, s16[144,128]{1,0:T(8,128)(2,1)S(1)}, u32[]{:S(2)}, u32[]{:S(2)}) collective-permute-start(s16[144,128]{1,0:T(8,128)(2,1)S(1)} %get-tuple-element.41), channel_id=1, source_target_pairs={{0,3},{1,2},{2,1},{3,0},{4,7},{5,6},{6,5},{7,4},{8,11},{9,10},{10,... | collective-permute-start | bytes 110600 | tf_op jit(solution)/shard_map/ppermute | solution.py:518
  25.0 6.1 %collective-permute-start.8 = (s16[144,128]{1,0:T(8,128)(2,1)S(1)}, s16[144,128]{1,0:T(8,128)(2,1)S(1)}, u32[]{:S(2)}, u32[]{:S(2)}) collective-permute-start(s16[144,128]{1,0:T(8,128)(2,1)S(1)} %shard_map.77), channel_id=1, source_target_pairs={{0,13},{1,12},{2,15},{3,14},{4,9},{5,8},{6,11},{7,10},{8,5},{9,4},... | collective-permute-start | bytes 110600 | tf_op jit(solution)/shard_map/ppermute | solution.py:518
  29.6 4.5 %collective-permute-start.10 = (s16[144,128]{1,0:T(8,128)(2,1)S(1)}, s16[144,128]{1,0:T(8,128)(2,1)S(1)}, u32[]{:S(2)}, u32[]{:S(2)}) collective-permute-start(s16[144,128]{1,0:T(8,128)(2,1)S(1)} %shard_map.78), channel_id=1, source_target_pairs={{0,9},{1,8},{2,11},{3,10},{4,13},{5,12},{6,15},{7,14},{8,1},{9,0},... | collective-permute-start | bytes 110600 | tf_op jit(solution)/shard_map/ppermute | solution.py:518
  29.8 4.3 %collective-permute-start.12 = (s16[144,128]{1,0:T(8,128)(2,1)S(1)}, s16[144,128]{1,0:T(8,128)(2,1)S(1)}, u32[]{:S(2)}, u32[]{:S(2)}) collective-permute-start(s16[144,128]{1,0:T(8,128)(2,1)S(1)} %shard_map.79), channel_id=1, source_target_pairs={{0,5},{1,4},{2,7},{3,6},{4,1},{5,0},{6,3},{7,2},{8,13},{9,12},{10,... | collective-permute-start | bytes 110600 | tf_op jit(solution)/shard_map/ppermute | solution.py:518
  31.3 2.9 %collective-permute-start.13 = (s16[144,128]{1,0:T(8,128)(2,1)S(1)}, s16[144,128]{1,0:T(8,128)(2,1)S(1)}, u32[]{:S(2)}, u32[]{:S(2)}) collective-permute-start(s16[144,128]{1,0:T(8,128)(2,1)S(1)} %shard_map.80), channel_id=1, source_target_pairs={{0,1},{1,0},{2,3},{3,2},{4,5},{5,4},{6,7},{7,6},{8,9},{9,8},{10,11... | collective-permute-start | bytes 110600 | tf_op jit(solution)/shard_map/ppermute | solution.py:518
  34.3 5.3 %collective-permute-start.18 = (bf16[8,2048]{1,0:T(8,128)(2,1)S(1)}, bf16[8,2048]{1,0:T(8,128)(2,1)S(1)}, u32[]{:S(2)}, u32[]{:S(2)}) collective-permute-start(bf16[8,2048]{1,0:T(8,128)(2,1)S(1)} %shard_map.81.refs_0_), channel_id=1, source_target_pairs={{0,13},{1,12},{2,15},{3,14},{4,9},{5,8},{6,11},{7,10},{8,5},{9,4},... | collective-permute-start | bytes 98312 | tf_op jit(solution)/shard_map/ppermute | solution.py:518
  36.3 4.8 %collective-permute-start.16 = (bf16[8,2048]{1,0:T(8,128)(2,1)S(1)}, bf16[8,2048]{1,0:T(8,128)(2,1)S(1)}, u32[]{:S(2)}, u32[]{:S(2)}) collective-permute-start(bf16[8,2048]{1,0:T(8,128)(2,1)S(1)} %shard_map.81.refs_0_), channel_id=1, source_target_pairs={{0,9},{1,8},{2,11},{3,10},{4,13},{5,12},{6,15},{7,14},{8,1},{9,0},... | collective-permute-start | bytes 98312 | tf_op jit(solution)/shard_map/ppermute | solution.py:518
  36.3 5.1 %collective-permute-start.20 = (bf16[8,2048]{1,0:T(8,128)(2,1)S(1)}, bf16[8,2048]{1,0:T(8,128)(2,1)S(1)}, u32[]{:S(2)}, u32[]{:S(2)}) collective-permute-start(bf16[8,2048]{1,0:T(8,128)(2,1)S(1)} %shard_map.81.refs_0_), channel_id=1, source_target_pairs={{0,2},{1,3},{2,0},{3,1},{4,6},{5,7},{6,4},{7,5},{8,10},{9,11},{10,... | collective-permute-start | bytes 98312 | tf_op jit(solution)/shard_map/ppermute | solution.py:518
  36.8 5.1 %collective-permute-start.14 = (bf16[8,2048]{1,0:T(8,128)(2,1)S(1)}, bf16[8,2048]{1,0:T(8,128)(2,1)S(1)}, u32[]{:S(2)}, u32[]{:S(2)}) collective-permute-start(bf16[8,2048]{1,0:T(8,128)(2,1)S(1)} %shard_map.81.refs_0_), channel_id=1, source_target_pairs={{0,5},{1,4},{2,7},{3,6},{4,1},{5,0},{6,3},{7,2},{8,13},{9,12},{10,... | collective-permute-start | bytes 98312 | tf_op jit(solution)/shard_map/ppermute | solution.py:518
  39.7 3.6 %collective-permute-start.23 = (bf16[8,2048]{1,0:T(8,128)(2,1)S(1)}, bf16[8,2048]{1,0:T(8,128)(2,1)S(1)}, u32[]{:S(2)}, u32[]{:S(2)}) collective-permute-start(bf16[8,2048]{1,0:T(8,128)(2,1)S(1)} %collective-permute-done.18), channel_id=1, source_target_pairs={{0,3},{1,2},{2,1},{3,0},{4,7},{5,6},{6,5},{7,4},{8,11},{9,10},{10,... | collective-permute-start | bytes 98312 | tf_op jit(solution)/shard_map/ppermute | solution.py:518
  40.3 3.1 %collective-permute-start.19 = (bf16[8,2048]{1,0:T(8,128)(2,1)S(1)}, bf16[8,2048]{1,0:T(8,128)(2,1)S(1)}, u32[]{:S(2)}, u32[]{:S(2)}) collective-permute-start(bf16[8,2048]{1,0:T(8,128)(2,1)S(1)} %collective-permute-done.18), channel_id=1, source_target_pairs={{0,1},{1,0},{2,3},{3,2},{4,5},{5,4},{6,7},{7,6},{8,9},{9,8},{10,11... | collective-permute-start | bytes 98312 | tf_op jit(solution)/shard_map/ppermute | solution.py:518
  41.1 3.5 %collective-permute-start.22 = (bf16[8,2048]{1,0:T(8,128)(2,1)S(1)}, bf16[8,2048]{1,0:T(8,128)(2,1)S(1)}, u32[]{:S(2)}, u32[]{:S(2)}) collective-permute-start(bf16[8,2048]{1,0:T(8,128)(2,1)S(1)} %collective-permute-done.16), channel_id=1, source_target_pairs={{0,3},{1,2},{2,1},{3,0},{4,7},{5,6},{6,5},{7,4},{8,11},{9,10},{10,... | collective-permute-start | bytes 98312 | tf_op jit(solution)/shard_map/ppermute | solution.py:518
  41.4 3.1 %collective-permute-start.17 = (bf16[8,2048]{1,0:T(8,128)(2,1)S(1)}, bf16[8,2048]{1,0:T(8,128)(2,1)S(1)}, u32[]{:S(2)}, u32[]{:S(2)}) collective-permute-start(bf16[8,2048]{1,0:T(8,128)(2,1)S(1)} %collective-permute-done.16), channel_id=1, source_target_pairs={{0,1},{1,0},{2,3},{3,2},{4,5},{5,4},{6,7},{7,6},{8,9},{9,8},{10,11... | collective-permute-start | bytes 98312 | tf_op jit(solution)/shard_map/ppermute | solution.py:518
  41.9 3.4 %collective-permute-start.21 = (bf16[8,2048]{1,0:T(8,128)(2,1)S(1)}, bf16[8,2048]{1,0:T(8,128)(2,1)S(1)}, u32[]{:S(2)}, u32[]{:S(2)}) collective-permute-start(bf16[8,2048]{1,0:T(8,128)(2,1)S(1)} %collective-permute-done.14), channel_id=1, source_target_pairs={{0,3},{1,2},{2,1},{3,0},{4,7},{5,6},{6,5},{7,4},{8,11},{9,10},{10,... | collective-permute-start | bytes 98312 | tf_op jit(solution)/shard_map/ppermute | solution.py:518
  43.3 2.1 %collective-permute-start.15 = (bf16[8,2048]{1,0:T(8,128)(2,1)S(1)}, bf16[8,2048]{1,0:T(8,128)(2,1)S(1)}, u32[]{:S(2)}, u32[]{:S(2)}) collective-permute-start(bf16[8,2048]{1,0:T(8,128)(2,1)S(1)} %collective-permute-done.14), channel_id=1, source_target_pairs={{0,1},{1,0},{2,3},{3,2},{4,5},{5,4},{6,7},{7,6},{8,9},{9,8},{10,11... | collective-permute-start | bytes 98312 | tf_op jit(solution)/shard_map/ppermute | solution.py:518

commit v9 on v8

--- a/solution.py
+++ b/solution.py
@@ -336,16 +336,13 @@
     for distance in range(tiles // 2):
         there = tile ^ (2 * distance)
         own_ref[distance * height : (distance + 1) * height] = coded_ref[there]
-        place = sent_refs[(distance or tiles // 2 - 1) - 1]
-        start = 0 if distance else height
-        place[start : start + height] = coded_ref[there ^ 1]
+        sent_refs[distance][...] = coded_ref[there ^ 1]
 
 
 def column_kernel(distance, columns, got_ref, own_ref, *refs):
     sent_ref = refs[-1]
     height = sent_ref.shape[0]
-    start = 0 if distance else height
-    values, hden = decode(got_ref.at[start : start + height], columns)
+    values, hden = decode(got_ref, columns)
     start = height * distance
     more, more_hden = decode(own_ref.at[start : start + height], columns)
     encode(values + more, hden + more_hden, [sent_ref])
@@ -522,16 +519,14 @@
         distance_kernel,
         (
             factor,
-            *[one] * (groups - 2),
-            shape((2 * height, LANES), jnp.int16),
+            *[one] * groups,
             shape((groups * height, LANES), jnp.int16),
         ),
         totals + [pltpu.VMEM((tiles, height, LANES), jnp.int16)],
     )(*last)
     distances = range(groups - 1, 0, -1)
     own = moved(own, 0, 1)
-    got = {distance: moved(sent[distance - 1], 1, 1) for distance in distances}
-    got[0] = got[groups - 1]
+    got = [moved(share, 1, 1) for share in sent]
     summed = []
     for distance in (*distances, 0):
         after = () if distance else summed[:1]

time: 46.4 us -> 45.8 us (0.987)
  waiting for transfers between devices: 11.6 us -> 10.8 us
    ppermute x18 -> x19, waiting for transfers between devices: 9.18 us -> 8.38 us  [moved(): return lax.ppermute(array, ('tile', 'gene'), pairs)]
    ppermute x18 -> x19, starting transfers between devices: 15 us -> 15.3 us  [moved(): return lax.ppermute(array, ('tile', 'gene'), pairs)]
  transfers between devices with their start and end apart: 24 -> 25, of which waited for: 13 -> 11; matrix products, arithmetic and copies ran while one was open for 0% -> 0% of each run, Pallas kernels for 7% -> 7%
where the time goes in v9:
time: 45.8 us; the launch traced here: 45.7 us
  starting transfers between devices  23.3 us (51%)
  Pallas kernels  10.8 us (24%)
  waiting for transfers between devices  10.8 us (24%)
  between operations  0.8 us (2%)
    ppermute x19, starting transfers between devices, moved(): return lax.ppermute(array, ('tile', 'gene'), pairs)  15.3 us
    pallas_call x15, Pallas kernels, call(): pl.pallas_call(kernel, out_shape=outs, in_specs=specs or [whole] * len(ar...  10.8 us
    ppermute x19, waiting for transfers between devices, moved(): return lax.ppermute(array, ('tile', 'gene'), pairs)  8.38 us
    ppermute x4, starting transfers between devices, around(): lax.ppermute(edges, ('tile', 'gene'), beside(tiles, halves, offset))  7.2 us
    ppermute x2, waiting for transfers between devices, swapped(): return lax.ppermute(part, 'gene', [(0, 1), (1, 0)])  1.55 us
  transfers between devices with their start and end apart: 25, of which 11 were waited for; matrix products, arithmetic and copies ran while one was open for 0% of the time, Pallas kernels for 7%

profile of v9, /device:TPU:0, one launch (start us, length us, event | category | flops | bytes accessed | tf_op | source)
XLA Modules:
  0.0 45.7 jit_solution(3990415826502965494)
XLA Ops:
  0.7 2.4 %shard_map.68 = (bf16[4096,128]{1,0:T(8,128)(2,1)S(1)}, bf16[4096,128]{1,0:T(8,128)(2,1)S(1)}) custom-call(s32[256,4096]{1,0:T(8,128)} %counts_ref.1), custom_call_target="tpu_custom_call" | custom-call | tf_op jit(solution)/shard_map/pallas_call | solution.py:409
  3.1 1.3 %shard_map.69 = (f32[32,384]{1,0:T(8,128)S(1)}, bf16[4096,64]{1,0:T(8,128)(2,1)S(1)}) custom-call(bf16[4096,128]{1,0:T(8,128)(2,1)S(1)} %get-tuple-element.23.outer_ref.kept_ref.refs_5_, bf16[4096,128]{1,0:T(8,128)(2,1)S(1)} %get-tuple-element.24.inner_ref.kept_ref, f32[32,256]{1,0:T(8,128)S(1)} %copy-done.1, bf16[32,4096]{1,0:T(8,128)(2,1)S(1)} %copy-done), custom_call_target="tpu_custom_call" | custom-call | tf_op jit(solution)/shard_map/pallas_call | solution.py:409
  4.4 0.5 %collective-permute-start = (f32[32,384]{1,0:T(8,128)S(1)}, f32[32,384]{1,0:T(8,128)S(1)}, u32[]{:S(2)}, u32[]{:S(2)}) collective-permute-start(f32[32,384]{1,0:T(8,128)S(1)} %get-tuple-element.25.part_ref), channel_id=1, source_target_pairs={{0,1},{1,0},{2,3},{3,2},{4,5},{5,4},{6,7},{7,6},{8,9},{9,8},{10,11... | collective-permute-start | bytes 147464 | tf_op jit(solution)/shard_map/ppermute | solution.py:466
  4.9 0.4 shard_map.70._.pick_ref.refs_2_
  5.3 0.5 %collective-permute-done.other_ref = f32[32,384]{1,0:T(8,128)S(1)} collective-permute-done((f32[32,384]{1,0:T(8,128)S(1)}, f32[32,384]{1,0:T(8,128)S(1)}, u32[]{:S(2)}, u32[]{:S(2)}) %collective-permute-start) | collective-permute-done | bytes 49184 | tf_op jit(solution)/shard_map/ppermute | solution.py:466
  5.8 0.2 shard_map.71
  5.9 0.4 collective-permute-start.2
  6.3 3.8 %collective-permute-start.1 = (f32[40,128]{1,0:T(8,128)S(1)}, f32[40,128]{1,0:T(8,128)S(1)}, u32[]{:S(2)}, u32[]{:S(2)}) collective-permute-start(f32[40,128]{1,0:T(8,128)S(1)} %get-tuple-element.27), channel_id=1, source_target_pairs={{0,3},{2,1},{1,2},{3,0},{4,7},{6,5},{5,6},{7,4},{8,11},{10,9},{9,1... | collective-permute-start | bytes 61448 | tf_op jit(solution)/shard_map/ppermute | solution.py:471
  10.0 0.9 %shard_map.72 = (f32[32,128]{1,0:T(8,128)S(1)}, f32[32,128]{1,0:T(8,128)S(1)}) custom-call(f32[32,256]{1,0:T(8,128)S(1)} %get-tuple-element.26.updated_ref, s32[1,256]{1,0:T(1,128)S(1)} %bitcast.2, bf16[384,256]{1,0:T(8,128)(2,1)S(1)} %shard_map.70._.pick_ref.refs_2_, bf16[4096,128]{1,0:T(8,128)(2,1)S(1)} %get-tuple-element.24.inner_ref.kept_ref, ...), custom_call_target="tpu_custom_call" | custom-call | tf_op jit(solution)/shard_map/pallas_call | solution.py:409
  10.9 0.0 collective-permute-done.2.second_ref
  11.0 0.6 %collective-permute-done.1.first_ref = f32[40,128]{1,0:T(8,128)S(1)} collective-permute-done((f32[40,128]{1,0:T(8,128)S(1)}, f32[40,128]{1,0:T(8,128)S(1)}, u32[]{:S(2)}, u32[]{:S(2)}) %collective-permute-start.1) | collective-permute-done | bytes 20512 | tf_op jit(solution)/shard_map/ppermute | solution.py:471
  11.5 0.8 %shard_map.73 = (f32[32,256]{1,0:T(8,128)S(1)}, f32[32,256]{1,0:T(8,128)S(1)}) custom-call(f32[32,256]{1,0:T(8,128)S(1)} %get-tuple-element.26.updated_ref, s32[1,256]{1,0:T(1,128)S(1)} %bitcast.3, bf16[384,256]{1,0:T(8,128)(2,1)S(1)} %shard_map.70._.pick_ref.refs_2_, f32[40,128]{1,0:T(8,128)S(1)} %collective-permute-done.1.first_ref, ...), custom_call_target="tpu_custom_call" | custom-call | tf_op jit(solution)/shard_map/pallas_call | solution.py:409
  12.3 0.2 collective-permute-start.3
  12.6 1.1 %collective-permute-done.3.other_ref = f32[32,256]{1,0:T(8,128)S(1)} collective-permute-done((f32[32,256]{1,0:T(8,128)S(1)}, f32[32,256]{1,0:T(8,128)S(1)}, u32[]{:S(2)}, u32[]{:S(2)}) %collective-permute-start.3) | collective-permute-done | bytes 32800 | tf_op jit(solution)/shard_map/ppermute | solution.py:466
  13.6 0.1 shard_map.74
  13.8 0.2 collective-permute-start.5
  13.9 2.9 %collective-permute-start.4 = (f32[40,128]{1,0:T(8,128)S(1)}, f32[40,128]{1,0:T(8,128)S(1)}, u32[]{:S(2)}, u32[]{:S(2)}) collective-permute-start(f32[40,128]{1,0:T(8,128)S(1)} %get-tuple-element.35), channel_id=1, source_target_pairs={{0,3},{2,1},{1,2},{3,0},{4,7},{6,5},{5,6},{7,4},{8,11},{10,9},{9,1... | collective-permute-start | bytes 61448 | tf_op jit(solution)/shard_map/ppermute | solution.py:471
  16.9 1.1 %shard_map.75 = (f32[32,128]{1,0:T(8,128)S(1)}, f32[32,4224]{1,0:T(8,128)S(1)}) custom-call(f32[32,256]{1,0:T(8,128)S(1)} %get-tuple-element.34.updated_ref.refs_0_, s32[1,256]{1,0:T(1,128)S(1)} %bitcast.5, bf16[384,256]{1,0:T(8,128)(2,1)S(1)} %shard_map.70._.pick_ref.refs_2_, bf16[4096,128]{1,0:T(8,128)(2,1)S(1)} %get-tuple-element.24.inner_ref.kept_ref, ...), custom_call_target="tpu_custom_call" | custom-call | tf_op jit(solution)/shard_map/pallas_call | solution.py:409
  18.0 0.0 collective-permute-done.5.refs_4_
  18.0 0.3 collective-permute-done.4.refs_3_
  18.3 1.8 %shard_map.76 = (f32[32,256]{1,0:T(8,128)}, s16[144,128]{1,0:T(8,128)(2,1)S(1)}, s16[144,128]{1,0:T(8,128)(2,1)S(1)}, s16[144,128]{1,0:T(8,128)(2,1)S(1)}, s16[1...) custom-call(f32[32,256]{1,0:T(8,128)S(1)} %get-tuple-element.34.updated_ref.refs_0_, s32[1,256]{1,0:T(1,128)S(1)} %bitcast.6, ...), custom_call_target="tpu_custom_call" | custom-call | tf_op jit(solution)/shard_map/pallas_call | solution.py:409
  20.1 0.1 collective-permute-start.7
  20.3 2.0 %collective-permute-start.6 = (s16[144,128]{1,0:T(8,128)(2,1)S(1)}, s16[144,128]{1,0:T(8,128)(2,1)S(1)}, u32[]{:S(2)}, u32[]{:S(2)}) collective-permute-start(s16[144,128]{1,0:T(8,128)(2,1)S(1)} %get-tuple-element.39), channel_id=1, source_target_pairs={{0,3},{1,2},{2,1},{3,0},{4,7},{5,6},{6,5},{7,4},{8,11},{9,10},{10,... | collective-permute-start | bytes 110600 | tf_op jit(solution)/shard_map/ppermute | solution.py:515
  22.2 0.0 collective-permute-start.9
  22.3 1.7 %collective-permute-start.11 = (s16[144,128]{1,0:T(8,128)(2,1)S(1)}, s16[144,128]{1,0:T(8,128)(2,1)S(1)}, u32[]{:S(2)}, u32[]{:S(2)}) collective-permute-start(s16[144,128]{1,0:T(8,128)(2,1)S(1)} %get-tuple-element.42), channel_id=1, source_target_pairs={{0,3},{1,2},{2,1},{3,0},{4,7},{5,6},{6,5},{7,4},{8,11},{9,10},{10,... | collective-permute-start | bytes 110600 | tf_op jit(solution)/shard_map/ppermute | solution.py:515
  24.0 0.0 collective-permute-start.13
  24.0 0.0 collective-permute-done.6.got_ref
  24.0 0.0 collective-permute-done.7.own_ref
  24.1 0.2 shard_map.77
  24.3 4.2 %collective-permute-start.8 = (s16[144,128]{1,0:T(8,128)(2,1)S(1)}, s16[144,128]{1,0:T(8,128)(2,1)S(1)}, u32[]{:S(2)}, u32[]{:S(2)}) collective-permute-start(s16[144,128]{1,0:T(8,128)(2,1)S(1)} %shard_map.77), channel_id=1, source_target_pairs={{0,13},{1,12},{2,15},{3,14},{4,9},{5,8},{6,11},{7,10},{8,5},{9,4},... | collective-permute-start | bytes 110600 | tf_op jit(solution)/shard_map/ppermute | solution.py:515
  28.4 0.0 collective-permute-done.9.got_ref
  28.5 0.2 shard_map.78
  28.7 0.3 collective-permute-start.10
  28.9 0.0 collective-permute-done.11.got_ref
  28.9 0.2 shard_map.79
  29.1 0.1 collective-permute-start.12
  29.3 0.0 collective-permute-done.13.got_ref
  29.3 1.2 %collective-permute-done.8.refs_0_ = s16[144,128]{1,0:T(8,128)(2,1)S(1)} collective-permute-done((s16[144,128]{1,0:T(8,128)(2,1)S(1)}, s16[144,128]{1,0:T(8,128)(2,1)S(1)}, u32[]{:S(2)}, u32[]{:S(2)}) %collective-permute-start.8) | collective-permute-done | bytes 36896 | tf_op jit(solution)/shard_map/ppermute | solution.py:515
  30.5 0.2 shard_map.80
  30.7 0.2 collective-permute-start.14
  30.8 2.7 %collective-permute-done.10.refs_1_ = s16[144,128]{1,0:T(8,128)(2,1)S(1)} collective-permute-done((s16[144,128]{1,0:T(8,128)(2,1)S(1)}, s16[144,128]{1,0:T(8,128)(2,1)S(1)}, u32[]{:S(2)}, u32[]{:S(2)}) %collective-permute-start.10) | collective-permute-done | bytes 36896 | tf_op jit(solution)/shard_map/ppermute | solution.py:515
  33.5 0.2 collective-permute-done.12.refs_2_
  33.7 0.0 collective-permute-done.14.refs_3_
  33.7 0.2 shard_map.81.refs_0_
  33.9 1.5 %collective-permute-start.19 = (bf16[8,2048]{1,0:T(8,128)(2,1)S(1)}, bf16[8,2048]{1,0:T(8,128)(2,1)S(1)}, u32[]{:S(2)}, u32[]{:S(2)}) collective-permute-start(bf16[8,2048]{1,0:T(8,128)(2,1)S(1)} %shard_map.81.refs_0_), channel_id=1, source_target_pairs={{0,13},{1,12},{2,15},{3,14},{4,9},{5,8},{6,11},{7,10},{8,5},{9,4},... | collective-permute-start | bytes 98312 | tf_op jit(solution)/shard_map/ppermute | solution.py:515
  35.4 0.0 collective-permute-start.17
  35.4 0.7 %collective-permute-start.21 = (bf16[8,2048]{1,0:T(8,128)(2,1)S(1)}, bf16[8,2048]{1,0:T(8,128)(2,1)S(1)}, u32[]{:S(2)}, u32[]{:S(2)}) collective-permute-start(bf16[8,2048]{1,0:T(8,128)(2,1)S(1)} %shard_map.81.refs_0_), channel_id=1, source_target_pairs={{0,2},{1,3},{2,0},{3,1},{4,6},{5,7},{6,4},{7,5},{8,10},{9,11},{10,... | collective-permute-start | bytes 98312 | tf_op jit(solution)/shard_map/ppermute | solution.py:515
  36.0 1.7 %collective-permute-start.15 = (bf16[8,2048]{1,0:T(8,128)(2,1)S(1)}, bf16[8,2048]{1,0:T(8,128)(2,1)S(1)}, u32[]{:S(2)}, u32[]{:S(2)}) collective-permute-start(bf16[8,2048]{1,0:T(8,128)(2,1)S(1)} %shard_map.81.refs_0_), channel_id=1, source_target_pairs={{0,5},{1,4},{2,7},{3,6},{4,1},{5,0},{6,3},{7,2},{8,13},{9,12},{10,... | collective-permute-start | bytes 98312 | tf_op jit(solution)/shard_map/ppermute | solution.py:515
  37.7 1.5 %collective-permute-done.19 = bf16[8,2048]{1,0:T(8,128)(2,1)S(1)} collective-permute-done((bf16[8,2048]{1,0:T(8,128)(2,1)S(1)}, bf16[8,2048]{1,0:T(8,128)(2,1)S(1)}, u32[]{:S(2)}, u32[]{:S(2)}) %collective-permute-start.19) | collective-permute-done | bytes 32800 | tf_op jit(solution)/shard_map/ppermute | solution.py:515
  39.2 0.6 %collective-permute-start.24 = (bf16[8,2048]{1,0:T(8,128)(2,1)S(1)}, bf16[8,2048]{1,0:T(8,128)(2,1)S(1)}, u32[]{:S(2)}, u32[]{:S(2)}) collective-permute-start(bf16[8,2048]{1,0:T(8,128)(2,1)S(1)} %collective-permute-done.19), channel_id=1, source_target_pairs={{0,3},{1,2},{2,1},{3,0},{4,7},{5,6},{6,5},{7,4},{8,11},{9,10},{10,... | collective-permute-start | bytes 98312 | tf_op jit(solution)/shard_map/ppermute | solution.py:515
  39.8 0.0 collective-permute-start.20
  39.8 1.0 %collective-permute-done.17 = bf16[8,2048]{1,0:T(8,128)(2,1)S(1)} collective-permute-done((bf16[8,2048]{1,0:T(8,128)(2,1)S(1)}, bf16[8,2048]{1,0:T(8,128)(2,1)S(1)}, u32[]{:S(2)}, u32[]{:S(2)}) %collective-permute-start.17) | collective-permute-done | bytes 32800 | tf_op jit(solution)/shard_map/ppermute | solution.py:515
  40.8 0.5 %collective-permute-start.23 = (bf16[8,2048]{1,0:T(8,128)(2,1)S(1)}, bf16[8,2048]{1,0:T(8,128)(2,1)S(1)}, u32[]{:S(2)}, u32[]{:S(2)}) collective-permute-start(bf16[8,2048]{1,0:T(8,128)(2,1)S(1)} %collective-permute-done.17), channel_id=1, source_target_pairs={{0,3},{1,2},{2,1},{3,0},{4,7},{5,6},{6,5},{7,4},{8,11},{9,10},{10,... | collective-permute-start | bytes 98312 | tf_op jit(solution)/shard_map/ppermute | solution.py:515
  41.2 0.0 collective-permute-done.21.refs_4_
  41.2 0.2 collective-permute-start.18
  41.5 0.0 collective-permute-done.15
  41.5 1.1 %collective-permute-start.22 = (bf16[8,2048]{1,0:T(8,128)(2,1)S(1)}, bf16[8,2048]{1,0:T(8,128)(2,1)S(1)}, u32[]{:S(2)}, u32[]{:S(2)}) collective-permute-start(bf16[8,2048]{1,0:T(8,128)(2,1)S(1)} %collective-permute-done.15), channel_id=1, source_target_pairs={{0,3},{1,2},{2,1},{3,0},{4,7},{5,6},{6,5},{7,4},{8,11},{9,10},{10,... | collective-permute-start | bytes 98312 | tf_op jit(solution)/shard_map/ppermute | solution.py:515
  42.6 0.0 collective-permute-done.24.refs_7_
  42.6 0.4 collective-permute-start.16
  43.0 0.0 collective-permute-done.20.refs_3_
  43.0 1.1 %collective-permute-done.23.refs_6_ = bf16[8,2048]{1,0:T(8,128)(2,1)S(1)} collective-permute-done((bf16[8,2048]{1,0:T(8,128)(2,1)S(1)}, bf16[8,2048]{1,0:T(8,128)(2,1)S(1)}, u32[]{:S(2)}, u32[]{:S(2)}) %collective-permute-start.23) | collective-permute-done | bytes 32800 | tf_op jit(solution)/shard_map/ppermute | solution.py:515
  44.2 0.0 collective-permute-done.18.refs_2_
  44.2 0.7 %collective-permute-done.22.refs_5_ = bf16[8,2048]{1,0:T(8,128)(2,1)S(1)} collective-permute-done((bf16[8,2048]{1,0:T(8,128)(2,1)S(1)}, bf16[8,2048]{1,0:T(8,128)(2,1)S(1)}, u32[]{:S(2)}, u32[]{:S(2)}) %collective-permute-start.22) | collective-permute-done | bytes 32800 | tf_op jit(solution)/shard_map/ppermute | solution.py:515
  44.8 0.8 %shard_map.82 = bf16[32,4096]{1,0:T(8,128)(2,1)} custom-call(bf16[8,2048]{1,0:T(8,128)(2,1)S(1)} %shard_map.81.refs_0_, bf16[8,2048]{1,0:T(8,128)(2,1)S(1)} %collective-permute-done.16.refs_1_, bf16[8,2048]{1,0:T(8,128)(2,1)S(1)} %collective-permute-done.18.refs_2_, bf16[8,2048]{1,0:T(8,128)(2,1)S(1)} %collective-permute-done.20.refs_3_, ...), custom_call_target="tpu_custom_call" | custom-call | tf_op jit(solution)/shard_map/pallas_call | solution.py:409
  (9 shorter events, 0.0 us)
Async XLA Ops:
  0.6 2.5 %copy-start = (bf16[32,4096]{1,0:T(8,128)(2,1)S(1)}, bf16[32,4096]{1,0:T(8,128)(2,1)}, u32[]{:S(2)}) copy-start(bf16[32,4096]{1,0:T(8,128)(2,1)} %refs_4_.1) | copy-start | bytes 786436
  0.6 2.5 %copy-start.1 = (f32[32,256]{1,0:T(8,128)S(1)}, f32[32,256]{1,0:T(8,128)}, u32[]{:S(2)}) copy-start(f32[32,256]{1,0:T(8,128)} %cells_ref.3) | copy-start | bytes 98308
  0.7 4.2 %copy-start.3 = (s32[8,256]{1,0:T(8,128)S(1)}, s32[8,256]{1,0:T(8,128)}, u32[]{:S(2)}) copy-start(s32[8,256]{1,0:T(8,128)} %neigh_ref.1) | copy-start | bytes 24580
  0.7 5.1 %copy-start.2 = (s32[256]{0:T(256)S(1)}, s32[256]{0:T(256)}, u32[]{:S(2)}) copy-start(s32[256]{0:T(256)} %param.8) | copy-start | bytes 3076
  4.4 1.4 %collective-permute-start = (f32[32,384]{1,0:T(8,128)S(1)}, f32[32,384]{1,0:T(8,128)S(1)}, u32[]{:S(2)}, u32[]{:S(2)}) collective-permute-start(f32[32,384]{1,0:T(8,128)S(1)} %get-tuple-element.25.part_ref), channel_id=1, source_target_pairs={{0,1},{1,0},{2,3},{3,2},{4,5},{5,4},{6,7},{7,6},{8,9},{9,8},{10,11... | collective-permute-start | bytes 147464 | tf_op jit(solution)/shard_map/ppermute | solution.py:466
  5.9 5.0 %collective-permute-start.2 = (f32[40,128]{1,0:T(8,128)S(1)}, f32[40,128]{1,0:T(8,128)S(1)}, u32[]{:S(2)}, u32[]{:S(2)}) collective-permute-start(f32[40,128]{1,0:T(8,128)S(1)} %get-tuple-element.27), channel_id=1, source_target_pairs={{2,5},{4,3},{3,4},{5,2},{6,9},{8,7},{7,8},{9,6},{10,13},{12,11},{1... | collective-permute-start | bytes 61448 | tf_op jit(solution)/shard_map/ppermute | solution.py:471
  6.3 5.2 %collective-permute-start.1 = (f32[40,128]{1,0:T(8,128)S(1)}, f32[40,128]{1,0:T(8,128)S(1)}, u32[]{:S(2)}, u32[]{:S(2)}) collective-permute-start(f32[40,128]{1,0:T(8,128)S(1)} %get-tuple-element.27), channel_id=1, source_target_pairs={{0,3},{2,1},{1,2},{3,0},{4,7},{6,5},{5,6},{7,4},{8,11},{10,9},{9,1... | collective-permute-start | bytes 61448 | tf_op jit(solution)/shard_map/ppermute | solution.py:471
  12.3 1.3 %collective-permute-start.3 = (f32[32,256]{1,0:T(8,128)S(1)}, f32[32,256]{1,0:T(8,128)S(1)}, u32[]{:S(2)}, u32[]{:S(2)}) collective-permute-start(f32[32,256]{1,0:T(8,128)S(1)} %get-tuple-element.31.numer_ref), channel_id=1, source_target_pairs={{0,1},{1,0},{2,3},{3,2},{4,5},{5,4},{6,7},{7,6},{8,9},{9,8},{10,11... | collective-permute-start | bytes 98312 | tf_op jit(solution)/shard_map/ppermute | solution.py:466
  13.8 4.2 %collective-permute-start.5 = (f32[40,128]{1,0:T(8,128)S(1)}, f32[40,128]{1,0:T(8,128)S(1)}, u32[]{:S(2)}, u32[]{:S(2)}) collective-permute-start(f32[40,128]{1,0:T(8,128)S(1)} %get-tuple-element.35), channel_id=1, source_target_pairs={{2,5},{4,3},{3,4},{5,2},{6,9},{8,7},{7,8},{9,6},{10,13},{12,11},{1... | collective-permute-start | bytes 61448 | tf_op jit(solution)/shard_map/ppermute | solution.py:471
  13.9 4.4 %collective-permute-start.4 = (f32[40,128]{1,0:T(8,128)S(1)}, f32[40,128]{1,0:T(8,128)S(1)}, u32[]{:S(2)}, u32[]{:S(2)}) collective-permute-start(f32[40,128]{1,0:T(8,128)S(1)} %get-tuple-element.35), channel_id=1, source_target_pairs={{0,3},{2,1},{1,2},{3,0},{4,7},{6,5},{5,6},{7,4},{8,11},{10,9},{9,1... | collective-permute-start | bytes 61448 | tf_op jit(solution)/shard_map/ppermute | solution.py:471
  20.1 3.9 %collective-permute-start.7 = (s16[576,128]{1,0:T(8,128)(2,1)S(1)}, s16[576,128]{1,0:T(8,128)(2,1)S(1)}, u32[]{:S(2)}, u32[]{:S(2)}) collective-permute-start(s16[576,128]{1,0:T(8,128)(2,1)S(1)} %get-tuple-element.40), channel_id=1, source_target_pairs={{0,1},{1,0},{2,3},{3,2},{4,5},{5,4},{6,7},{7,6},{8,9},{9,8},{10,11... | collective-permute-start | bytes 442376 | tf_op jit(solution)/shard_map/ppermute | solution.py:515
  20.3 3.8 %collective-permute-start.6 = (s16[144,128]{1,0:T(8,128)(2,1)S(1)}, s16[144,128]{1,0:T(8,128)(2,1)S(1)}, u32[]{:S(2)}, u32[]{:S(2)}) collective-permute-start(s16[144,128]{1,0:T(8,128)(2,1)S(1)} %get-tuple-element.39), channel_id=1, source_target_pairs={{0,3},{1,2},{2,1},{3,0},{4,7},{5,6},{6,5},{7,4},{8,11},{9,10},{10,... | collective-permute-start | bytes 110600 | tf_op jit(solution)/shard_map/ppermute | solution.py:515
  22.2 6.2 %collective-permute-start.9 = (s16[144,128]{1,0:T(8,128)(2,1)S(1)}, s16[144,128]{1,0:T(8,128)(2,1)S(1)}, u32[]{:S(2)}, u32[]{:S(2)}) collective-permute-start(s16[144,128]{1,0:T(8,128)(2,1)S(1)} %get-tuple-element.41), channel_id=1, source_target_pairs={{0,3},{1,2},{2,1},{3,0},{4,7},{5,6},{6,5},{7,4},{8,11},{9,10},{10,... | collective-permute-start | bytes 110600 | tf_op jit(solution)/shard_map/ppermute | solution.py:515
  22.3 6.7 %collective-permute-start.11 = (s16[144,128]{1,0:T(8,128)(2,1)S(1)}, s16[144,128]{1,0:T(8,128)(2,1)S(1)}, u32[]{:S(2)}, u32[]{:S(2)}) collective-permute-start(s16[144,128]{1,0:T(8,128)(2,1)S(1)} %get-tuple-element.42), channel_id=1, source_target_pairs={{0,3},{1,2},{2,1},{3,0},{4,7},{5,6},{6,5},{7,4},{8,11},{9,10},{10,... | collective-permute-start | bytes 110600 | tf_op jit(solution)/shard_map/ppermute | solution.py:515
  24.0 5.3 %collective-permute-start.13 = (s16[144,128]{1,0:T(8,128)(2,1)S(1)}, s16[144,128]{1,0:T(8,128)(2,1)S(1)}, u32[]{:S(2)}, u32[]{:S(2)}) collective-permute-start(s16[144,128]{1,0:T(8,128)(2,1)S(1)} %get-tuple-element.43), channel_id=1, source_target_pairs={{0,3},{1,2},{2,1},{3,0},{4,7},{5,6},{6,5},{7,4},{8,11},{9,10},{10,... | collective-permute-start | bytes 110600 | tf_op jit(solution)/shard_map/ppermute | solution.py:515
  24.3 6.2 %collective-permute-start.8 = (s16[144,128]{1,0:T(8,128)(2,1)S(1)}, s16[144,128]{1,0:T(8,128)(2,1)S(1)}, u32[]{:S(2)}, u32[]{:S(2)}) collective-permute-start(s16[144,128]{1,0:T(8,128)(2,1)S(1)} %shard_map.77), channel_id=1, source_target_pairs={{0,13},{1,12},{2,15},{3,14},{4,9},{5,8},{6,11},{7,10},{8,5},{9,4},... | collective-permute-start | bytes 110600 | tf_op jit(solution)/shard_map/ppermute | solution.py:515
  28.7 4.8 %collective-permute-start.10 = (s16[144,128]{1,0:T(8,128)(2,1)S(1)}, s16[144,128]{1,0:T(8,128)(2,1)S(1)}, u32[]{:S(2)}, u32[]{:S(2)}) collective-permute-start(s16[144,128]{1,0:T(8,128)(2,1)S(1)} %shard_map.78), channel_id=1, source_target_pairs={{0,9},{1,8},{2,11},{3,10},{4,13},{5,12},{6,15},{7,14},{8,1},{9,0},... | collective-permute-start | bytes 110600 | tf_op jit(solution)/shard_map/ppermute | solution.py:515
  29.1 4.6 %collective-permute-start.12 = (s16[144,128]{1,0:T(8,128)(2,1)S(1)}, s16[144,128]{1,0:T(8,128)(2,1)S(1)}, u32[]{:S(2)}, u32[]{:S(2)}) collective-permute-start(s16[144,128]{1,0:T(8,128)(2,1)S(1)} %shard_map.79), channel_id=1, source_target_pairs={{0,5},{1,4},{2,7},{3,6},{4,1},{5,0},{6,3},{7,2},{8,13},{9,12},{10,... | collective-permute-start | bytes 110600 | tf_op jit(solution)/shard_map/ppermute | solution.py:515
  30.7 3.0 %collective-permute-start.14 = (s16[144,128]{1,0:T(8,128)(2,1)S(1)}, s16[144,128]{1,0:T(8,128)(2,1)S(1)}, u32[]{:S(2)}, u32[]{:S(2)}) collective-permute-start(s16[144,128]{1,0:T(8,128)(2,1)S(1)} %shard_map.80), channel_id=1, source_target_pairs={{0,1},{1,0},{2,3},{3,2},{4,5},{5,4},{6,7},{7,6},{8,9},{9,8},{10,11... | collective-permute-start | bytes 110600 | tf_op jit(solution)/shard_map/ppermute | solution.py:515
  33.9 5.4 %collective-permute-start.19 = (bf16[8,2048]{1,0:T(8,128)(2,1)S(1)}, bf16[8,2048]{1,0:T(8,128)(2,1)S(1)}, u32[]{:S(2)}, u32[]{:S(2)}) collective-permute-start(bf16[8,2048]{1,0:T(8,128)(2,1)S(1)} %shard_map.81.refs_0_), channel_id=1, source_target_pairs={{0,13},{1,12},{2,15},{3,14},{4,9},{5,8},{6,11},{7,10},{8,5},{9,4},... | collective-permute-start | bytes 98312 | tf_op jit(solution)/shard_map/ppermute | solution.py:515
  35.4 5.4 %collective-permute-start.17 = (bf16[8,2048]{1,0:T(8,128)(2,1)S(1)}, bf16[8,2048]{1,0:T(8,128)(2,1)S(1)}, u32[]{:S(2)}, u32[]{:S(2)}) collective-permute-start(bf16[8,2048]{1,0:T(8,128)(2,1)S(1)} %shard_map.81.refs_0_), channel_id=1, source_target_pairs={{0,9},{1,8},{2,11},{3,10},{4,13},{5,12},{6,15},{7,14},{8,1},{9,0},... | collective-permute-start | bytes 98312 | tf_op jit(solution)/shard_map/ppermute | solution.py:515
  35.4 5.9 %collective-permute-start.21 = (bf16[8,2048]{1,0:T(8,128)(2,1)S(1)}, bf16[8,2048]{1,0:T(8,128)(2,1)S(1)}, u32[]{:S(2)}, u32[]{:S(2)}) collective-permute-start(bf16[8,2048]{1,0:T(8,128)(2,1)S(1)} %shard_map.81.refs_0_), channel_id=1, source_target_pairs={{0,2},{1,3},{2,0},{3,1},{4,6},{5,7},{6,4},{7,5},{8,10},{9,11},{10,... | collective-permute-start | bytes 98312 | tf_op jit(solution)/shard_map/ppermute | solution.py:515
  36.0 5.5 %collective-permute-start.15 = (bf16[8,2048]{1,0:T(8,128)(2,1)S(1)}, bf16[8,2048]{1,0:T(8,128)(2,1)S(1)}, u32[]{:S(2)}, u32[]{:S(2)}) collective-permute-start(bf16[8,2048]{1,0:T(8,128)(2,1)S(1)} %shard_map.81.refs_0_), channel_id=1, source_target_pairs={{0,5},{1,4},{2,7},{3,6},{4,1},{5,0},{6,3},{7,2},{8,13},{9,12},{10,... | collective-permute-start | bytes 98312 | tf_op jit(solution)/shard_map/ppermute | solution.py:515
  39.2 3.4 %collective-permute-start.24 = (bf16[8,2048]{1,0:T(8,128)(2,1)S(1)}, bf16[8,2048]{1,0:T(8,128)(2,1)S(1)}, u32[]{:S(2)}, u32[]{:S(2)}) collective-permute-start(bf16[8,2048]{1,0:T(8,128)(2,1)S(1)} %collective-permute-done.19), channel_id=1, source_target_pairs={{0,3},{1,2},{2,1},{3,0},{4,7},{5,6},{6,5},{7,4},{8,11},{9,10},{10,... | collective-permute-start | bytes 98312 | tf_op jit(solution)/shard_map/ppermute | solution.py:515
  39.8 3.2 %collective-permute-start.20 = (bf16[8,2048]{1,0:T(8,128)(2,1)S(1)}, bf16[8,2048]{1,0:T(8,128)(2,1)S(1)}, u32[]{:S(2)}, u32[]{:S(2)}) collective-permute-start(bf16[8,2048]{1,0:T(8,128)(2,1)S(1)} %collective-permute-done.19), channel_id=1, source_target_pairs={{0,1},{1,0},{2,3},{3,2},{4,5},{5,4},{6,7},{7,6},{8,9},{9,8},{10,11... | collective-permute-start | bytes 98312 | tf_op jit(solution)/shard_map/ppermute | solution.py:515
  40.8 3.4 %collective-permute-start.23 = (bf16[8,2048]{1,0:T(8,128)(2,1)S(1)}, bf16[8,2048]{1,0:T(8,128)(2,1)S(1)}, u32[]{:S(2)}, u32[]{:S(2)}) collective-permute-start(bf16[8,2048]{1,0:T(8,128)(2,1)S(1)} %collective-permute-done.17), channel_id=1, source_target_pairs={{0,3},{1,2},{2,1},{3,0},{4,7},{5,6},{6,5},{7,4},{8,11},{9,10},{10,... | collective-permute-start | bytes 98312 | tf_op jit(solution)/shard_map/ppermute | solution.py:515
  41.2 2.9 %collective-permute-start.18 = (bf16[8,2048]{1,0:T(8,128)(2,1)S(1)}, bf16[8,2048]{1,0:T(8,128)(2,1)S(1)}, u32[]{:S(2)}, u32[]{:S(2)}) collective-permute-start(bf16[8,2048]{1,0:T(8,128)(2,1)S(1)} %collective-permute-done.17), channel_id=1, source_target_pairs={{0,1},{1,0},{2,3},{3,2},{4,5},{5,4},{6,7},{7,6},{8,9},{9,8},{10,11... | collective-permute-start | bytes 98312 | tf_op jit(solution)/shard_map/ppermute | solution.py:515
  41.5 3.3 %collective-permute-start.22 = (bf16[8,2048]{1,0:T(8,128)(2,1)S(1)}, bf16[8,2048]{1,0:T(8,128)(2,1)S(1)}, u32[]{:S(2)}, u32[]{:S(2)}) collective-permute-start(bf16[8,2048]{1,0:T(8,128)(2,1)S(1)} %collective-permute-done.15), channel_id=1, source_target_pairs={{0,3},{1,2},{2,1},{3,0},{4,7},{5,6},{6,5},{7,4},{8,11},{9,10},{10,... | collective-permute-start | bytes 98312 | tf_op jit(solution)/shard_map/ppermute | solution.py:515
  42.6 2.2 %collective-permute-start.16 = (bf16[8,2048]{1,0:T(8,128)(2,1)S(1)}, bf16[8,2048]{1,0:T(8,128)(2,1)S(1)}, u32[]{:S(2)}, u32[]{:S(2)}) collective-permute-start(bf16[8,2048]{1,0:T(8,128)(2,1)S(1)} %collective-permute-done.15), channel_id=1, source_target_pairs={{0,1},{1,0},{2,3},{3,2},{4,5},{5,4},{6,7},{7,6},{8,9},{9,8},{10,11... | collective-permute-start | bytes 98312 | tf_op jit(solution)/shard_map/ppermute | solution.py:515

commit v10 on v9

--- a/solution.py
+++ b/solution.py
@@ -382,7 +382,8 @@
 
 
 def spread_kernel(*refs):
-    *share_refs, out_ref = refs
+    *share_refs, cells_ref, new_cells_ref, out_ref = refs
+    new_cells_ref[...] = cells_ref[...]
     groups = len(share_refs) // 2
     columns = share_refs[0].shape[1]
     tile = lax.axis_index("tile")
@@ -541,7 +542,9 @@
     for distance in range(1, groups):
         shares.append(moved(passing[distance], 0, 1))
         others.append(moved(passing[distance], 1, 1))
-    return cells, call(spread_kernel, shape((rank, genes), jnp.bfloat16))(*shares, *others)
+    return call(spread_kernel, (factor, shape((rank, genes), jnp.bfloat16)))(
+        *shares, *others, cells
+    )
 
 
 def solution(mesh):

time: 45.8 us -> 45.5 us (level)
  Pallas kernels: 10.8 us -> 10.3 us
where the time goes in v10:
time: 45.5 us; the launch traced here: 45.3 us
  starting transfers between devices  23.3 us (51%)
  waiting for transfers between devices  10.8 us (24%)
  Pallas kernels  10.3 us (23%)
  between operations  0.81 us (2%)
    ppermute x19, starting transfers between devices, moved(): return lax.ppermute(array, ('tile', 'gene'), pairs)  15.4 us
    pallas_call x15, Pallas kernels, call(): pl.pallas_call(kernel, out_shape=outs, in_specs=specs or [whole] * len(ar...  10.3 us
    ppermute x19, waiting for transfers between devices, moved(): return lax.ppermute(array, ('tile', 'gene'), pairs)  8.38 us
    ppermute x4, starting transfers between devices, around(): lax.ppermute(edges, ('tile', 'gene'), beside(tiles, halves, offset))  7.2 us
    ppermute x2, waiting for transfers between devices, swapped(): return lax.ppermute(part, 'gene', [(0, 1), (1, 0)])  1.55 us
  transfers between devices with their start and end apart: 25, of which 11 were waited for; matrix products, arithmetic and copies ran while one was open for 0% of the time, Pallas kernels for 7%

profile of v10, /device:TPU:0, one launch (start us, length us, event | category | flops | bytes accessed | tf_op | source)
XLA Modules:
  0.0 45.3 jit_solution(33974925436163300)
XLA Ops:
  0.7 2.4 %shard_map.68 = (bf16[4096,128]{1,0:T(8,128)(2,1)S(1)}, bf16[4096,128]{1,0:T(8,128)(2,1)S(1)}) custom-call(s32[256,4096]{1,0:T(8,128)} %counts_ref.1), custom_call_target="tpu_custom_call" | custom-call | tf_op jit(solution)/shard_map/pallas_call | solution.py:410
  3.1 1.3 %shard_map.69 = (f32[32,384]{1,0:T(8,128)S(1)}, bf16[4096,64]{1,0:T(8,128)(2,1)S(1)}) custom-call(bf16[4096,128]{1,0:T(8,128)(2,1)S(1)} %get-tuple-element.23.outer_ref.kept_ref.refs_5_, bf16[4096,128]{1,0:T(8,128)(2,1)S(1)} %get-tuple-element.24.inner_ref.kept_ref, f32[32,256]{1,0:T(8,128)S(1)} %copy-done.1, bf16[32,4096]{1,0:T(8,128)(2,1)S(1)} %copy-done), custom_call_target="tpu_custom_call" | custom-call | tf_op jit(solution)/shard_map/pallas_call | solution.py:410
  4.4 0.5 %collective-permute-start = (f32[32,384]{1,0:T(8,128)S(1)}, f32[32,384]{1,0:T(8,128)S(1)}, u32[]{:S(2)}, u32[]{:S(2)}) collective-permute-start(f32[32,384]{1,0:T(8,128)S(1)} %get-tuple-element.25.part_ref), channel_id=1, source_target_pairs={{0,1},{1,0},{2,3},{3,2},{4,5},{5,4},{6,7},{7,6},{8,9},{9,8},{10,11... | collective-permute-start | bytes 147464 | tf_op jit(solution)/shard_map/ppermute | solution.py:467
  4.9 0.4 shard_map.70._.pick_ref.refs_2_
  5.3 0.5 %collective-permute-done.other_ref = f32[32,384]{1,0:T(8,128)S(1)} collective-permute-done((f32[32,384]{1,0:T(8,128)S(1)}, f32[32,384]{1,0:T(8,128)S(1)}, u32[]{:S(2)}, u32[]{:S(2)}) %collective-permute-start) | collective-permute-done | bytes 49184 | tf_op jit(solution)/shard_map/ppermute | solution.py:467
  5.8 0.2 shard_map.71
  5.9 0.4 collective-permute-start.2
  6.3 3.8 %collective-permute-start.1 = (f32[40,128]{1,0:T(8,128)S(1)}, f32[40,128]{1,0:T(8,128)S(1)}, u32[]{:S(2)}, u32[]{:S(2)}) collective-permute-start(f32[40,128]{1,0:T(8,128)S(1)} %get-tuple-element.27), channel_id=1, source_target_pairs={{0,3},{2,1},{1,2},{3,0},{4,7},{6,5},{5,6},{7,4},{8,11},{10,9},{9,1... | collective-permute-start | bytes 61448 | tf_op jit(solution)/shard_map/ppermute | solution.py:472
  10.0 0.9 %shard_map.72 = (f32[32,128]{1,0:T(8,128)S(1)}, f32[32,128]{1,0:T(8,128)S(1)}) custom-call(f32[32,256]{1,0:T(8,128)S(1)} %get-tuple-element.26.updated_ref, s32[1,256]{1,0:T(1,128)S(1)} %bitcast.2, bf16[384,256]{1,0:T(8,128)(2,1)S(1)} %shard_map.70._.pick_ref.refs_2_, bf16[4096,128]{1,0:T(8,128)(2,1)S(1)} %get-tuple-element.24.inner_ref.kept_ref, ...), custom_call_target="tpu_custom_call" | custom-call | tf_op jit(solution)/shard_map/pallas_call | solution.py:410
  10.9 0.0 collective-permute-done.2.second_ref
  11.0 0.6 %collective-permute-done.1.first_ref = f32[40,128]{1,0:T(8,128)S(1)} collective-permute-done((f32[40,128]{1,0:T(8,128)S(1)}, f32[40,128]{1,0:T(8,128)S(1)}, u32[]{:S(2)}, u32[]{:S(2)}) %collective-permute-start.1) | collective-permute-done | bytes 20512 | tf_op jit(solution)/shard_map/ppermute | solution.py:472
  11.5 0.8 %shard_map.73 = (f32[32,256]{1,0:T(8,128)S(1)}, f32[32,256]{1,0:T(8,128)S(1)}) custom-call(f32[32,256]{1,0:T(8,128)S(1)} %get-tuple-element.26.updated_ref, s32[1,256]{1,0:T(1,128)S(1)} %bitcast.3, bf16[384,256]{1,0:T(8,128)(2,1)S(1)} %shard_map.70._.pick_ref.refs_2_, f32[40,128]{1,0:T(8,128)S(1)} %collective-permute-done.1.first_ref, ...), custom_call_target="tpu_custom_call" | custom-call | tf_op jit(solution)/shard_map/pallas_call | solution.py:410
  12.3 0.2 collective-permute-start.3
  12.6 1.1 %collective-permute-done.3.other_ref = f32[32,256]{1,0:T(8,128)S(1)} collective-permute-done((f32[32,256]{1,0:T(8,128)S(1)}, f32[32,256]{1,0:T(8,128)S(1)}, u32[]{:S(2)}, u32[]{:S(2)}) %collective-permute-start.3) | collective-permute-done | bytes 32800 | tf_op jit(solution)/shard_map/ppermute | solution.py:467
  13.6 0.1 shard_map.74
  13.8 0.2 collective-permute-start.5
  13.9 2.9 %collective-permute-start.4 = (f32[40,128]{1,0:T(8,128)S(1)}, f32[40,128]{1,0:T(8,128)S(1)}, u32[]{:S(2)}, u32[]{:S(2)}) collective-permute-start(f32[40,128]{1,0:T(8,128)S(1)} %get-tuple-element.35), channel_id=1, source_target_pairs={{0,3},{2,1},{1,2},{3,0},{4,7},{6,5},{5,6},{7,4},{8,11},{10,9},{9,1... | collective-permute-start | bytes 61448 | tf_op jit(solution)/shard_map/ppermute | solution.py:472
  16.9 1.1 %shard_map.75 = (f32[32,128]{1,0:T(8,128)S(1)}, f32[32,4224]{1,0:T(8,128)S(1)}) custom-call(f32[32,256]{1,0:T(8,128)S(1)} %get-tuple-element.34.updated_ref.refs_0_, s32[1,256]{1,0:T(1,128)S(1)} %bitcast.5, bf16[384,256]{1,0:T(8,128)(2,1)S(1)} %shard_map.70._.pick_ref.refs_2_, bf16[4096,128]{1,0:T(8,128)(2,1)S(1)} %get-tuple-element.24.inner_ref.kept_ref, ...), custom_call_target="tpu_custom_call" | custom-call | tf_op jit(solution)/shard_map/pallas_call | solution.py:410
  18.0 0.0 collective-permute-done.5.refs_4_
  18.0 0.3 collective-permute-done.4.refs_3_
  18.3 1.3 %shard_map.76 = (f32[32,256]{1,0:T(8,128)S(1)}, s16[144,128]{1,0:T(8,128)(2,1)S(1)}, s16[144,128]{1,0:T(8,128)(2,1)S(1)}, s16[144,128]{1,0:T(8,128)(2,1)S(1)}, s...) custom-call(f32[32,256]{1,0:T(8,128)S(1)} %get-tuple-element.34.updated_ref.refs_0_, s32[1,256]{1,0:T(1,128)S(1)} %bitcast.6, ...), custom_call_target="tpu_custom_call" | custom-call | tf_op jit(solution)/shard_map/pallas_call | solution.py:410
  19.7 0.2 collective-permute-start.7
  19.9 2.0 %collective-permute-start.6 = (s16[144,128]{1,0:T(8,128)(2,1)S(1)}, s16[144,128]{1,0:T(8,128)(2,1)S(1)}, u32[]{:S(2)}, u32[]{:S(2)}) collective-permute-start(s16[144,128]{1,0:T(8,128)(2,1)S(1)} %get-tuple-element.38), channel_id=1, source_target_pairs={{0,3},{1,2},{2,1},{3,0},{4,7},{5,6},{6,5},{7,4},{8,11},{9,10},{10,... | collective-permute-start | bytes 110600 | tf_op jit(solution)/shard_map/ppermute | solution.py:516
  21.9 0.0 collective-permute-start.9
  21.9 1.7 %collective-permute-start.11 = (s16[144,128]{1,0:T(8,128)(2,1)S(1)}, s16[144,128]{1,0:T(8,128)(2,1)S(1)}, u32[]{:S(2)}, u32[]{:S(2)}) collective-permute-start(s16[144,128]{1,0:T(8,128)(2,1)S(1)} %get-tuple-element.41), channel_id=1, source_target_pairs={{0,3},{1,2},{2,1},{3,0},{4,7},{5,6},{6,5},{7,4},{8,11},{9,10},{10,... | collective-permute-start | bytes 110600 | tf_op jit(solution)/shard_map/ppermute | solution.py:516
  23.6 0.0 collective-permute-start.13
  23.7 0.0 collective-permute-done.6.got_ref
  23.7 0.0 collective-permute-done.7.own_ref
  23.7 0.2 shard_map.77
  23.9 4.2 %collective-permute-start.8 = (s16[144,128]{1,0:T(8,128)(2,1)S(1)}, s16[144,128]{1,0:T(8,128)(2,1)S(1)}, u32[]{:S(2)}, u32[]{:S(2)}) collective-permute-start(s16[144,128]{1,0:T(8,128)(2,1)S(1)} %shard_map.77), channel_id=1, source_target_pairs={{0,13},{1,12},{2,15},{3,14},{4,9},{5,8},{6,11},{7,10},{8,5},{9,4},... | collective-permute-start | bytes 110600 | tf_op jit(solution)/shard_map/ppermute | solution.py:516
  28.1 0.0 collective-permute-done.9.got_ref
  28.1 0.2 shard_map.78
  28.3 0.3 collective-permute-start.10
  28.6 0.0 collective-permute-done.11.got_ref
  28.6 0.2 shard_map.79
  28.8 0.1 collective-permute-start.12
  28.9 0.0 collective-permute-done.13.got_ref
  28.9 1.2 %collective-permute-done.8.refs_0_ = s16[144,128]{1,0:T(8,128)(2,1)S(1)} collective-permute-done((s16[144,128]{1,0:T(8,128)(2,1)S(1)}, s16[144,128]{1,0:T(8,128)(2,1)S(1)}, u32[]{:S(2)}, u32[]{:S(2)}) %collective-permute-start.8) | collective-permute-done | bytes 36896 | tf_op jit(solution)/shard_map/ppermute | solution.py:516
  30.1 0.2 shard_map.80
  30.3 0.2 collective-permute-start.14
  30.5 2.6 %collective-permute-done.10.refs_1_ = s16[144,128]{1,0:T(8,128)(2,1)S(1)} collective-permute-done((s16[144,128]{1,0:T(8,128)(2,1)S(1)}, s16[144,128]{1,0:T(8,128)(2,1)S(1)}, u32[]{:S(2)}, u32[]{:S(2)}) %collective-permute-start.10) | collective-permute-done | bytes 36896 | tf_op jit(solution)/shard_map/ppermute | solution.py:516
  33.1 0.2 collective-permute-done.12.refs_2_
  33.3 0.0 collective-permute-done.14.refs_3_
  33.3 0.2 shard_map.81.refs_0_
  33.5 1.5 %collective-permute-start.19 = (bf16[8,2048]{1,0:T(8,128)(2,1)S(1)}, bf16[8,2048]{1,0:T(8,128)(2,1)S(1)}, u32[]{:S(2)}, u32[]{:S(2)}) collective-permute-start(bf16[8,2048]{1,0:T(8,128)(2,1)S(1)} %shard_map.81.refs_0_), channel_id=1, source_target_pairs={{0,13},{1,12},{2,15},{3,14},{4,9},{5,8},{6,11},{7,10},{8,5},{9,4},... | collective-permute-start | bytes 98312 | tf_op jit(solution)/shard_map/ppermute | solution.py:516
  35.0 0.0 collective-permute-start.17
  35.0 0.7 %collective-permute-start.21 = (bf16[8,2048]{1,0:T(8,128)(2,1)S(1)}, bf16[8,2048]{1,0:T(8,128)(2,1)S(1)}, u32[]{:S(2)}, u32[]{:S(2)}) collective-permute-start(bf16[8,2048]{1,0:T(8,128)(2,1)S(1)} %shard_map.81.refs_0_), channel_id=1, source_target_pairs={{0,2},{1,3},{2,0},{3,1},{4,6},{5,7},{6,4},{7,5},{8,10},{9,11},{10,... | collective-permute-start | bytes 98312 | tf_op jit(solution)/shard_map/ppermute | solution.py:516
  35.6 1.7 %collective-permute-start.15 = (bf16[8,2048]{1,0:T(8,128)(2,1)S(1)}, bf16[8,2048]{1,0:T(8,128)(2,1)S(1)}, u32[]{:S(2)}, u32[]{:S(2)}) collective-permute-start(bf16[8,2048]{1,0:T(8,128)(2,1)S(1)} %shard_map.81.refs_0_), channel_id=1, source_target_pairs={{0,5},{1,4},{2,7},{3,6},{4,1},{5,0},{6,3},{7,2},{8,13},{9,12},{10,... | collective-permute-start | bytes 98312 | tf_op jit(solution)/shard_map/ppermute | solution.py:516
  37.3 1.5 %collective-permute-done.19 = bf16[8,2048]{1,0:T(8,128)(2,1)S(1)} collective-permute-done((bf16[8,2048]{1,0:T(8,128)(2,1)S(1)}, bf16[8,2048]{1,0:T(8,128)(2,1)S(1)}, u32[]{:S(2)}, u32[]{:S(2)}) %collective-permute-start.19) | collective-permute-done | bytes 32800 | tf_op jit(solution)/shard_map/ppermute | solution.py:516
  38.8 0.6 %collective-permute-start.24 = (bf16[8,2048]{1,0:T(8,128)(2,1)S(1)}, bf16[8,2048]{1,0:T(8,128)(2,1)S(1)}, u32[]{:S(2)}, u32[]{:S(2)}) collective-permute-start(bf16[8,2048]{1,0:T(8,128)(2,1)S(1)} %collective-permute-done.19), channel_id=1, source_target_pairs={{0,3},{1,2},{2,1},{3,0},{4,7},{5,6},{6,5},{7,4},{8,11},{9,10},{10,... | collective-permute-start | bytes 98312 | tf_op jit(solution)/shard_map/ppermute | solution.py:516
  39.4 0.0 collective-permute-start.20
  39.4 1.0 %collective-permute-done.17 = bf16[8,2048]{1,0:T(8,128)(2,1)S(1)} collective-permute-done((bf16[8,2048]{1,0:T(8,128)(2,1)S(1)}, bf16[8,2048]{1,0:T(8,128)(2,1)S(1)}, u32[]{:S(2)}, u32[]{:S(2)}) %collective-permute-start.17) | collective-permute-done | bytes 32800 | tf_op jit(solution)/shard_map/ppermute | solution.py:516
  40.4 0.5 %collective-permute-start.23 = (bf16[8,2048]{1,0:T(8,128)(2,1)S(1)}, bf16[8,2048]{1,0:T(8,128)(2,1)S(1)}, u32[]{:S(2)}, u32[]{:S(2)}) collective-permute-start(bf16[8,2048]{1,0:T(8,128)(2,1)S(1)} %collective-permute-done.17), channel_id=1, source_target_pairs={{0,3},{1,2},{2,1},{3,0},{4,7},{5,6},{6,5},{7,4},{8,11},{9,10},{10,... | collective-permute-start | bytes 98312 | tf_op jit(solution)/shard_map/ppermute | solution.py:516
  40.9 0.0 collective-permute-done.21.refs_4_
  40.9 0.2 collective-permute-start.18
  41.1 0.0 collective-permute-done.15
  41.1 1.1 %collective-permute-start.22 = (bf16[8,2048]{1,0:T(8,128)(2,1)S(1)}, bf16[8,2048]{1,0:T(8,128)(2,1)S(1)}, u32[]{:S(2)}, u32[]{:S(2)}) collective-permute-start(bf16[8,2048]{1,0:T(8,128)(2,1)S(1)} %collective-permute-done.15), channel_id=1, source_target_pairs={{0,3},{1,2},{2,1},{3,0},{4,7},{5,6},{6,5},{7,4},{8,11},{9,10},{10,... | collective-permute-start | bytes 98312 | tf_op jit(solution)/shard_map/ppermute | solution.py:516
  42.3 0.0 collective-permute-done.24.refs_7_
  42.3 0.4 collective-permute-start.16
  42.7 0.0 collective-permute-done.20.refs_3_
  42.7 1.1 %collective-permute-done.23.refs_6_ = bf16[8,2048]{1,0:T(8,128)(2,1)S(1)} collective-permute-done((bf16[8,2048]{1,0:T(8,128)(2,1)S(1)}, bf16[8,2048]{1,0:T(8,128)(2,1)S(1)}, u32[]{:S(2)}, u32[]{:S(2)}) %collective-permute-start.23) | collective-permute-done | bytes 32800 | tf_op jit(solution)/shard_map/ppermute | solution.py:516
  43.8 0.0 collective-permute-done.18.refs_2_
  43.8 0.7 %collective-permute-done.22.refs_5_ = bf16[8,2048]{1,0:T(8,128)(2,1)S(1)} collective-permute-done((bf16[8,2048]{1,0:T(8,128)(2,1)S(1)}, bf16[8,2048]{1,0:T(8,128)(2,1)S(1)}, u32[]{:S(2)}, u32[]{:S(2)}) %collective-permute-start.22) | collective-permute-done | bytes 32800 | tf_op jit(solution)/shard_map/ppermute | solution.py:516
  44.5 0.8 %shard_map.82 = (f32[32,256]{1,0:T(8,128)}, bf16[32,4096]{1,0:T(8,128)(2,1)}) custom-call(bf16[8,2048]{1,0:T(8,128)(2,1)S(1)} %shard_map.81.refs_0_, bf16[8,2048]{1,0:T(8,128)(2,1)S(1)} %collective-permute-done.16.refs_1_, bf16[8,2048]{1,0:T(8,128)(2,1)S(1)} %collective-permute-done.18.refs_2_, bf16[8,2048]{1,0:T(8,128)(2,1)S(1)} %collective-permute-done.20.refs_3_, ...), custom_call_target="tpu_custom_call" | custom-call | tf_op jit(solution)/shard_map/pallas_call | solution.py:410
  (9 shorter events, 0.0 us)
Async XLA Ops:
  0.6 2.5 %copy-start = (bf16[32,4096]{1,0:T(8,128)(2,1)S(1)}, bf16[32,4096]{1,0:T(8,128)(2,1)}, u32[]{:S(2)}) copy-start(bf16[32,4096]{1,0:T(8,128)(2,1)} %refs_4_.1) | copy-start | bytes 786436
  0.6 2.5 %copy-start.1 = (f32[32,256]{1,0:T(8,128)S(1)}, f32[32,256]{1,0:T(8,128)}, u32[]{:S(2)}) copy-start(f32[32,256]{1,0:T(8,128)} %cells_ref.3) | copy-start | bytes 98308
  0.7 4.2 %copy-start.3 = (s32[8,256]{1,0:T(8,128)S(1)}, s32[8,256]{1,0:T(8,128)}, u32[]{:S(2)}) copy-start(s32[8,256]{1,0:T(8,128)} %neigh_ref.1) | copy-start | bytes 24580
  0.7 5.1 %copy-start.2 = (s32[256]{0:T(256)S(1)}, s32[256]{0:T(256)}, u32[]{:S(2)}) copy-start(s32[256]{0:T(256)} %param.8) | copy-start | bytes 3076
  4.4 1.4 %collective-permute-start = (f32[32,384]{1,0:T(8,128)S(1)}, f32[32,384]{1,0:T(8,128)S(1)}, u32[]{:S(2)}, u32[]{:S(2)}) collective-permute-start(f32[32,384]{1,0:T(8,128)S(1)} %get-tuple-element.25.part_ref), channel_id=1, source_target_pairs={{0,1},{1,0},{2,3},{3,2},{4,5},{5,4},{6,7},{7,6},{8,9},{9,8},{10,11... | collective-permute-start | bytes 147464 | tf_op jit(solution)/shard_map/ppermute | solution.py:467
  5.9 5.0 %collective-permute-start.2 = (f32[40,128]{1,0:T(8,128)S(1)}, f32[40,128]{1,0:T(8,128)S(1)}, u32[]{:S(2)}, u32[]{:S(2)}) collective-permute-start(f32[40,128]{1,0:T(8,128)S(1)} %get-tuple-element.27), channel_id=1, source_target_pairs={{2,5},{4,3},{3,4},{5,2},{6,9},{8,7},{7,8},{9,6},{10,13},{12,11},{1... | collective-permute-start | bytes 61448 | tf_op jit(solution)/shard_map/ppermute | solution.py:472
  6.3 5.2 %collective-permute-start.1 = (f32[40,128]{1,0:T(8,128)S(1)}, f32[40,128]{1,0:T(8,128)S(1)}, u32[]{:S(2)}, u32[]{:S(2)}) collective-permute-start(f32[40,128]{1,0:T(8,128)S(1)} %get-tuple-element.27), channel_id=1, source_target_pairs={{0,3},{2,1},{1,2},{3,0},{4,7},{6,5},{5,6},{7,4},{8,11},{10,9},{9,1... | collective-permute-start | bytes 61448 | tf_op jit(solution)/shard_map/ppermute | solution.py:472
  12.3 1.3 %collective-permute-start.3 = (f32[32,256]{1,0:T(8,128)S(1)}, f32[32,256]{1,0:T(8,128)S(1)}, u32[]{:S(2)}, u32[]{:S(2)}) collective-permute-start(f32[32,256]{1,0:T(8,128)S(1)} %get-tuple-element.31.numer_ref), channel_id=1, source_target_pairs={{0,1},{1,0},{2,3},{3,2},{4,5},{5,4},{6,7},{7,6},{8,9},{9,8},{10,11... | collective-permute-start | bytes 98312 | tf_op jit(solution)/shard_map/ppermute | solution.py:467
  13.8 4.2 %collective-permute-start.5 = (f32[40,128]{1,0:T(8,128)S(1)}, f32[40,128]{1,0:T(8,128)S(1)}, u32[]{:S(2)}, u32[]{:S(2)}) collective-permute-start(f32[40,128]{1,0:T(8,128)S(1)} %get-tuple-element.35), channel_id=1, source_target_pairs={{2,5},{4,3},{3,4},{5,2},{6,9},{8,7},{7,8},{9,6},{10,13},{12,11},{1... | collective-permute-start | bytes 61448 | tf_op jit(solution)/shard_map/ppermute | solution.py:472
  13.9 4.4 %collective-permute-start.4 = (f32[40,128]{1,0:T(8,128)S(1)}, f32[40,128]{1,0:T(8,128)S(1)}, u32[]{:S(2)}, u32[]{:S(2)}) collective-permute-start(f32[40,128]{1,0:T(8,128)S(1)} %get-tuple-element.35), channel_id=1, source_target_pairs={{0,3},{2,1},{1,2},{3,0},{4,7},{6,5},{5,6},{7,4},{8,11},{10,9},{9,1... | collective-permute-start | bytes 61448 | tf_op jit(solution)/shard_map/ppermute | solution.py:472
  19.7 4.0 %collective-permute-start.7 = (s16[576,128]{1,0:T(8,128)(2,1)S(1)}, s16[576,128]{1,0:T(8,128)(2,1)S(1)}, u32[]{:S(2)}, u32[]{:S(2)}) collective-permute-start(s16[576,128]{1,0:T(8,128)(2,1)S(1)} %get-tuple-element.39), channel_id=1, source_target_pairs={{0,1},{1,0},{2,3},{3,2},{4,5},{5,4},{6,7},{7,6},{8,9},{9,8},{10,11... | collective-permute-start | bytes 442376 | tf_op jit(solution)/shard_map/ppermute | solution.py:516
  19.9 3.8 %collective-permute-start.6 = (s16[144,128]{1,0:T(8,128)(2,1)S(1)}, s16[144,128]{1,0:T(8,128)(2,1)S(1)}, u32[]{:S(2)}, u32[]{:S(2)}) collective-permute-start(s16[144,128]{1,0:T(8,128)(2,1)S(1)} %get-tuple-element.38), channel_id=1, source_target_pairs={{0,3},{1,2},{2,1},{3,0},{4,7},{5,6},{6,5},{7,4},{8,11},{9,10},{10,... | collective-permute-start | bytes 110600 | tf_op jit(solution)/shard_map/ppermute | solution.py:516
  21.9 6.2 %collective-permute-start.9 = (s16[144,128]{1,0:T(8,128)(2,1)S(1)}, s16[144,128]{1,0:T(8,128)(2,1)S(1)}, u32[]{:S(2)}, u32[]{:S(2)}) collective-permute-start(s16[144,128]{1,0:T(8,128)(2,1)S(1)} %get-tuple-element.40), channel_id=1, source_target_pairs={{0,3},{1,2},{2,1},{3,0},{4,7},{5,6},{6,5},{7,4},{8,11},{9,10},{10,... | collective-permute-start | bytes 110600 | tf_op jit(solution)/shard_map/ppermute | solution.py:516
  21.9 6.7 %collective-permute-start.11 = (s16[144,128]{1,0:T(8,128)(2,1)S(1)}, s16[144,128]{1,0:T(8,128)(2,1)S(1)}, u32[]{:S(2)}, u32[]{:S(2)}) collective-permute-start(s16[144,128]{1,0:T(8,128)(2,1)S(1)} %get-tuple-element.41), channel_id=1, source_target_pairs={{0,3},{1,2},{2,1},{3,0},{4,7},{5,6},{6,5},{7,4},{8,11},{9,10},{10,... | collective-permute-start | bytes 110600 | tf_op jit(solution)/shard_map/ppermute | solution.py:516
  23.6 5.3 %collective-permute-start.13 = (s16[144,128]{1,0:T(8,128)(2,1)S(1)}, s16[144,128]{1,0:T(8,128)(2,1)S(1)}, u32[]{:S(2)}, u32[]{:S(2)}) collective-permute-start(s16[144,128]{1,0:T(8,128)(2,1)S(1)} %get-tuple-element.42), channel_id=1, source_target_pairs={{0,3},{1,2},{2,1},{3,0},{4,7},{5,6},{6,5},{7,4},{8,11},{9,10},{10,... | collective-permute-start | bytes 110600 | tf_op jit(solution)/shard_map/ppermute | solution.py:516
  23.9 6.2 %collective-permute-start.8 = (s16[144,128]{1,0:T(8,128)(2,1)S(1)}, s16[144,128]{1,0:T(8,128)(2,1)S(1)}, u32[]{:S(2)}, u32[]{:S(2)}) collective-permute-start(s16[144,128]{1,0:T(8,128)(2,1)S(1)} %shard_map.77), channel_id=1, source_target_pairs={{0,13},{1,12},{2,15},{3,14},{4,9},{5,8},{6,11},{7,10},{8,5},{9,4},... | collective-permute-start | bytes 110600 | tf_op jit(solution)/shard_map/ppermute | solution.py:516
  28.3 4.8 %collective-permute-start.10 = (s16[144,128]{1,0:T(8,128)(2,1)S(1)}, s16[144,128]{1,0:T(8,128)(2,1)S(1)}, u32[]{:S(2)}, u32[]{:S(2)}) collective-permute-start(s16[144,128]{1,0:T(8,128)(2,1)S(1)} %shard_map.78), channel_id=1, source_target_pairs={{0,9},{1,8},{2,11},{3,10},{4,13},{5,12},{6,15},{7,14},{8,1},{9,0},... | collective-permute-start | bytes 110600 | tf_op jit(solution)/shard_map/ppermute | solution.py:516
  28.8 4.6 %collective-permute-start.12 = (s16[144,128]{1,0:T(8,128)(2,1)S(1)}, s16[144,128]{1,0:T(8,128)(2,1)S(1)}, u32[]{:S(2)}, u32[]{:S(2)}) collective-permute-start(s16[144,128]{1,0:T(8,128)(2,1)S(1)} %shard_map.79), channel_id=1, source_target_pairs={{0,5},{1,4},{2,7},{3,6},{4,1},{5,0},{6,3},{7,2},{8,13},{9,12},{10,... | collective-permute-start | bytes 110600 | tf_op jit(solution)/shard_map/ppermute | solution.py:516
  30.3 3.0 %collective-permute-start.14 = (s16[144,128]{1,0:T(8,128)(2,1)S(1)}, s16[144,128]{1,0:T(8,128)(2,1)S(1)}, u32[]{:S(2)}, u32[]{:S(2)}) collective-permute-start(s16[144,128]{1,0:T(8,128)(2,1)S(1)} %shard_map.80), channel_id=1, source_target_pairs={{0,1},{1,0},{2,3},{3,2},{4,5},{5,4},{6,7},{7,6},{8,9},{9,8},{10,11... | collective-permute-start | bytes 110600 | tf_op jit(solution)/shard_map/ppermute | solution.py:516
  33.5 5.4 %collective-permute-start.19 = (bf16[8,2048]{1,0:T(8,128)(2,1)S(1)}, bf16[8,2048]{1,0:T(8,128)(2,1)S(1)}, u32[]{:S(2)}, u32[]{:S(2)}) collective-permute-start(bf16[8,2048]{1,0:T(8,128)(2,1)S(1)} %shard_map.81.refs_0_), channel_id=1, source_target_pairs={{0,13},{1,12},{2,15},{3,14},{4,9},{5,8},{6,11},{7,10},{8,5},{9,4},... | collective-permute-start | bytes 98312 | tf_op jit(solution)/shard_map/ppermute | solution.py:516
  35.0 5.4 %collective-permute-start.17 = (bf16[8,2048]{1,0:T(8,128)(2,1)S(1)}, bf16[8,2048]{1,0:T(8,128)(2,1)S(1)}, u32[]{:S(2)}, u32[]{:S(2)}) collective-permute-start(bf16[8,2048]{1,0:T(8,128)(2,1)S(1)} %shard_map.81.refs_0_), channel_id=1, source_target_pairs={{0,9},{1,8},{2,11},{3,10},{4,13},{5,12},{6,15},{7,14},{8,1},{9,0},... | collective-permute-start | bytes 98312 | tf_op jit(solution)/shard_map/ppermute | solution.py:516
  35.0 5.9 %collective-permute-start.21 = (bf16[8,2048]{1,0:T(8,128)(2,1)S(1)}, bf16[8,2048]{1,0:T(8,128)(2,1)S(1)}, u32[]{:S(2)}, u32[]{:S(2)}) collective-permute-start(bf16[8,2048]{1,0:T(8,128)(2,1)S(1)} %shard_map.81.refs_0_), channel_id=1, source_target_pairs={{0,2},{1,3},{2,0},{3,1},{4,6},{5,7},{6,4},{7,5},{8,10},{9,11},{10,... | collective-permute-start | bytes 98312 | tf_op jit(solution)/shard_map/ppermute | solution.py:516
  35.6 5.5 %collective-permute-start.15 = (bf16[8,2048]{1,0:T(8,128)(2,1)S(1)}, bf16[8,2048]{1,0:T(8,128)(2,1)S(1)}, u32[]{:S(2)}, u32[]{:S(2)}) collective-permute-start(bf16[8,2048]{1,0:T(8,128)(2,1)S(1)} %shard_map.81.refs_0_), channel_id=1, source_target_pairs={{0,5},{1,4},{2,7},{3,6},{4,1},{5,0},{6,3},{7,2},{8,13},{9,12},{10,... | collective-permute-start | bytes 98312 | tf_op jit(solution)/shard_map/ppermute | solution.py:516
  38.8 3.4 %collective-permute-start.24 = (bf16[8,2048]{1,0:T(8,128)(2,1)S(1)}, bf16[8,2048]{1,0:T(8,128)(2,1)S(1)}, u32[]{:S(2)}, u32[]{:S(2)}) collective-permute-start(bf16[8,2048]{1,0:T(8,128)(2,1)S(1)} %collective-permute-done.19), channel_id=1, source_target_pairs={{0,3},{1,2},{2,1},{3,0},{4,7},{5,6},{6,5},{7,4},{8,11},{9,10},{10,... | collective-permute-start | bytes 98312 | tf_op jit(solution)/shard_map/ppermute | solution.py:516
  39.4 3.2 %collective-permute-start.20 = (bf16[8,2048]{1,0:T(8,128)(2,1)S(1)}, bf16[8,2048]{1,0:T(8,128)(2,1)S(1)}, u32[]{:S(2)}, u32[]{:S(2)}) collective-permute-start(bf16[8,2048]{1,0:T(8,128)(2,1)S(1)} %collective-permute-done.19), channel_id=1, source_target_pairs={{0,1},{1,0},{2,3},{3,2},{4,5},{5,4},{6,7},{7,6},{8,9},{9,8},{10,11... | collective-permute-start | bytes 98312 | tf_op jit(solution)/shard_map/ppermute | solution.py:516
  40.4 3.4 %collective-permute-start.23 = (bf16[8,2048]{1,0:T(8,128)(2,1)S(1)}, bf16[8,2048]{1,0:T(8,128)(2,1)S(1)}, u32[]{:S(2)}, u32[]{:S(2)}) collective-permute-start(bf16[8,2048]{1,0:T(8,128)(2,1)S(1)} %collective-permute-done.17), channel_id=1, source_target_pairs={{0,3},{1,2},{2,1},{3,0},{4,7},{5,6},{6,5},{7,4},{8,11},{9,10},{10,... | collective-permute-start | bytes 98312 | tf_op jit(solution)/shard_map/ppermute | solution.py:516
  40.9 2.9 %collective-permute-start.18 = (bf16[8,2048]{1,0:T(8,128)(2,1)S(1)}, bf16[8,2048]{1,0:T(8,128)(2,1)S(1)}, u32[]{:S(2)}, u32[]{:S(2)}) collective-permute-start(bf16[8,2048]{1,0:T(8,128)(2,1)S(1)} %collective-permute-done.17), channel_id=1, source_target_pairs={{0,1},{1,0},{2,3},{3,2},{4,5},{5,4},{6,7},{7,6},{8,9},{9,8},{10,11... | collective-permute-start | bytes 98312 | tf_op jit(solution)/shard_map/ppermute | solution.py:516
  41.1 3.3 %collective-permute-start.22 = (bf16[8,2048]{1,0:T(8,128)(2,1)S(1)}, bf16[8,2048]{1,0:T(8,128)(2,1)S(1)}, u32[]{:S(2)}, u32[]{:S(2)}) collective-permute-start(bf16[8,2048]{1,0:T(8,128)(2,1)S(1)} %collective-permute-done.15), channel_id=1, source_target_pairs={{0,3},{1,2},{2,1},{3,0},{4,7},{5,6},{6,5},{7,4},{8,11},{9,10},{10,... | collective-permute-start | bytes 98312 | tf_op jit(solution)/shard_map/ppermute | solution.py:516
  42.3 2.2 %collective-permute-start.16 = (bf16[8,2048]{1,0:T(8,128)(2,1)S(1)}, bf16[8,2048]{1,0:T(8,128)(2,1)S(1)}, u32[]{:S(2)}, u32[]{:S(2)}) collective-permute-start(bf16[8,2048]{1,0:T(8,128)(2,1)S(1)} %collective-permute-done.15), channel_id=1, source_target_pairs={{0,1},{1,0},{2,3},{3,2},{4,5},{5,4},{6,7},{7,6},{8,9},{9,8},{10,11... | collective-permute-start | bytes 98312 | tf_op jit(solution)/shard_map/ppermute | solution.py:516

commit v11 on v10

--- a/solution.py
+++ b/solution.py
@@ -389,20 +389,18 @@
     tile = lax.axis_index("tile")
     here, side = tile // 2, lax.rem(tile, 2)
     shares = [ref[...].astype(jnp.float32) for ref in share_refs]
-    for column in range(2):
-        own = side == column
+    for some, column in ((shares[:groups], side), (shares[groups:], 1 - side)):
         picked = []
         for group in range(groups):
-            distance = here ^ group
-            share = jnp.where(own, shares[0], shares[groups])
+            share = some[0]
             for at in range(1, groups):
-                either = jnp.where(own, shares[at], shares[groups + at])
-                share = jnp.where(distance == at, either, share)
+                share = jnp.where(here ^ group == at, some[at], share)
             picked.append(share)
+        place = pl.ds(pl.multiple_of(column * columns, LANES), columns)
         for group in range(0, groups, 2):
-            out_ref[
-                group * ROWS : (group + 2) * ROWS, column * columns : (column + 1) * columns
-            ] = jnp.concatenate(picked[group : group + 2], axis=0).astype(jnp.bfloat16)
+            out_ref[group * ROWS : (group + 2) * ROWS, place] = jnp.concatenate(
+                picked[group : group + 2], axis=0
+            ).astype(jnp.bfloat16)
 
 
 def call(kernel, outs, scratch=(), specs=None, limit=VMEM_BYTES):

time: 45.5 us -> 45.4 us (level)
  no operation moved by 1% of the time
where the time goes in v11:
time: 45.4 us; the launch traced here: 45.3 us
  starting transfers between devices  23.3 us (51%)
  waiting for transfers between devices  10.8 us (24%)
  Pallas kernels  10.3 us (23%)
  between operations  0.81 us (2%)
    ppermute x19, starting transfers between devices, moved(): return lax.ppermute(array, ('tile', 'gene'), pairs)  15.4 us
    pallas_call x15, Pallas kernels, call(): pl.pallas_call(kernel, out_shape=outs, in_specs=specs or [whole] * len(ar...  10.3 us
    ppermute x19, waiting for transfers between devices, moved(): return lax.ppermute(array, ('tile', 'gene'), pairs)  8.38 us
    ppermute x4, starting transfers between devices, around(): lax.ppermute(edges, ('tile', 'gene'), beside(tiles, halves, offset))  7.2 us
    ppermute x2, waiting for transfers between devices, swapped(): return lax.ppermute(part, 'gene', [(0, 1), (1, 0)])  1.55 us
  transfers between devices with their start and end apart: 25, of which 11 were waited for; matrix products, arithmetic and copies ran while one was open for 0% of the time, Pallas kernels for 7%

profile of v11, /device:TPU:0, one launch (start us, length us, event | category | flops | bytes accessed | tf_op | source)
XLA Modules:
  0.0 45.3 jit_solution(9447547016454656624)
XLA Ops:
  0.7 2.4 %shard_map.68 = (bf16[4096,128]{1,0:T(8,128)(2,1)S(1)}, bf16[4096,128]{1,0:T(8,128)(2,1)S(1)}) custom-call(s32[256,4096]{1,0:T(8,128)} %counts_ref.1), custom_call_target="tpu_custom_call" | custom-call | tf_op jit(solution)/shard_map/pallas_call | solution.py:408
  3.1 1.3 %shard_map.69 = (f32[32,384]{1,0:T(8,128)S(1)}, bf16[4096,64]{1,0:T(8,128)(2,1)S(1)}) custom-call(bf16[4096,128]{1,0:T(8,128)(2,1)S(1)} %get-tuple-element.23.outer_ref.kept_ref.refs_5_, bf16[4096,128]{1,0:T(8,128)(2,1)S(1)} %get-tuple-element.24.inner_ref.kept_ref, f32[32,256]{1,0:T(8,128)S(1)} %copy-done.1, bf16[32,4096]{1,0:T(8,128)(2,1)S(1)} %copy-done), custom_call_target="tpu_custom_call" | custom-call | tf_op jit(solution)/shard_map/pallas_call | solution.py:408
  4.4 0.5 %collective-permute-start = (f32[32,384]{1,0:T(8,128)S(1)}, f32[32,384]{1,0:T(8,128)S(1)}, u32[]{:S(2)}, u32[]{:S(2)}) collective-permute-start(f32[32,384]{1,0:T(8,128)S(1)} %get-tuple-element.25.part_ref), channel_id=1, source_target_pairs={{0,1},{1,0},{2,3},{3,2},{4,5},{5,4},{6,7},{7,6},{8,9},{9,8},{10,11... | collective-permute-start | bytes 147464 | tf_op jit(solution)/shard_map/ppermute | solution.py:465
  4.9 0.4 shard_map.70._.pick_ref.refs_2_
  5.3 0.5 %collective-permute-done.other_ref = f32[32,384]{1,0:T(8,128)S(1)} collective-permute-done((f32[32,384]{1,0:T(8,128)S(1)}, f32[32,384]{1,0:T(8,128)S(1)}, u32[]{:S(2)}, u32[]{:S(2)}) %collective-permute-start) | collective-permute-done | bytes 49184 | tf_op jit(solution)/shard_map/ppermute | solution.py:465
  5.8 0.2 shard_map.71
  5.9 0.4 collective-permute-start.2
  6.3 3.8 %collective-permute-start.1 = (f32[40,128]{1,0:T(8,128)S(1)}, f32[40,128]{1,0:T(8,128)S(1)}, u32[]{:S(2)}, u32[]{:S(2)}) collective-permute-start(f32[40,128]{1,0:T(8,128)S(1)} %get-tuple-element.27), channel_id=1, source_target_pairs={{0,3},{2,1},{1,2},{3,0},{4,7},{6,5},{5,6},{7,4},{8,11},{10,9},{9,1... | collective-permute-start | bytes 61448 | tf_op jit(solution)/shard_map/ppermute | solution.py:470
  10.0 0.9 %shard_map.72 = (f32[32,128]{1,0:T(8,128)S(1)}, f32[32,128]{1,0:T(8,128)S(1)}) custom-call(f32[32,256]{1,0:T(8,128)S(1)} %get-tuple-element.26.updated_ref, s32[1,256]{1,0:T(1,128)S(1)} %bitcast.2, bf16[384,256]{1,0:T(8,128)(2,1)S(1)} %shard_map.70._.pick_ref.refs_2_, bf16[4096,128]{1,0:T(8,128)(2,1)S(1)} %get-tuple-element.24.inner_ref.kept_ref, ...), custom_call_target="tpu_custom_call" | custom-call | tf_op jit(solution)/shard_map/pallas_call | solution.py:408
  10.9 0.0 collective-permute-done.2.second_ref
  11.0 0.6 %collective-permute-done.1.first_ref = f32[40,128]{1,0:T(8,128)S(1)} collective-permute-done((f32[40,128]{1,0:T(8,128)S(1)}, f32[40,128]{1,0:T(8,128)S(1)}, u32[]{:S(2)}, u32[]{:S(2)}) %collective-permute-start.1) | collective-permute-done | bytes 20512 | tf_op jit(solution)/shard_map/ppermute | solution.py:470
  11.5 0.8 %shard_map.73 = (f32[32,256]{1,0:T(8,128)S(1)}, f32[32,256]{1,0:T(8,128)S(1)}) custom-call(f32[32,256]{1,0:T(8,128)S(1)} %get-tuple-element.26.updated_ref, s32[1,256]{1,0:T(1,128)S(1)} %bitcast.3, bf16[384,256]{1,0:T(8,128)(2,1)S(1)} %shard_map.70._.pick_ref.refs_2_, f32[40,128]{1,0:T(8,128)S(1)} %collective-permute-done.1.first_ref, ...), custom_call_target="tpu_custom_call" | custom-call | tf_op jit(solution)/shard_map/pallas_call | solution.py:408
  12.3 0.2 collective-permute-start.3
  12.6 1.1 %collective-permute-done.3.other_ref = f32[32,256]{1,0:T(8,128)S(1)} collective-permute-done((f32[32,256]{1,0:T(8,128)S(1)}, f32[32,256]{1,0:T(8,128)S(1)}, u32[]{:S(2)}, u32[]{:S(2)}) %collective-permute-start.3) | collective-permute-done | bytes 32800 | tf_op jit(solution)/shard_map/ppermute | solution.py:465
  13.6 0.1 shard_map.74
  13.8 0.2 collective-permute-start.5
  13.9 2.9 %collective-permute-start.4 = (f32[40,128]{1,0:T(8,128)S(1)}, f32[40,128]{1,0:T(8,128)S(1)}, u32[]{:S(2)}, u32[]{:S(2)}) collective-permute-start(f32[40,128]{1,0:T(8,128)S(1)} %get-tuple-element.35), channel_id=1, source_target_pairs={{0,3},{2,1},{1,2},{3,0},{4,7},{6,5},{5,6},{7,4},{8,11},{10,9},{9,1... | collective-permute-start | bytes 61448 | tf_op jit(solution)/shard_map/ppermute | solution.py:470
  16.9 1.1 %shard_map.75 = (f32[32,128]{1,0:T(8,128)S(1)}, f32[32,4224]{1,0:T(8,128)S(1)}) custom-call(f32[32,256]{1,0:T(8,128)S(1)} %get-tuple-element.34.updated_ref.refs_0_, s32[1,256]{1,0:T(1,128)S(1)} %bitcast.5, bf16[384,256]{1,0:T(8,128)(2,1)S(1)} %shard_map.70._.pick_ref.refs_2_, bf16[4096,128]{1,0:T(8,128)(2,1)S(1)} %get-tuple-element.24.inner_ref.kept_ref, ...), custom_call_target="tpu_custom_call" | custom-call | tf_op jit(solution)/shard_map/pallas_call | solution.py:408
  18.0 0.0 collective-permute-done.5.refs_4_
  18.0 0.3 collective-permute-done.4.refs_3_
  18.3 1.3 %shard_map.76 = (f32[32,256]{1,0:T(8,128)S(1)}, s16[144,128]{1,0:T(8,128)(2,1)S(1)}, s16[144,128]{1,0:T(8,128)(2,1)S(1)}, s16[144,128]{1,0:T(8,128)(2,1)S(1)}, s...) custom-call(f32[32,256]{1,0:T(8,128)S(1)} %get-tuple-element.34.updated_ref.refs_0_, s32[1,256]{1,0:T(1,128)S(1)} %bitcast.6, ...), custom_call_target="tpu_custom_call" | custom-call | tf_op jit(solution)/shard_map/pallas_call | solution.py:408
  19.7 0.2 collective-permute-start.7
  19.9 2.0 %collective-permute-start.6 = (s16[144,128]{1,0:T(8,128)(2,1)S(1)}, s16[144,128]{1,0:T(8,128)(2,1)S(1)}, u32[]{:S(2)}, u32[]{:S(2)}) collective-permute-start(s16[144,128]{1,0:T(8,128)(2,1)S(1)} %get-tuple-element.38), channel_id=1, source_target_pairs={{0,3},{1,2},{2,1},{3,0},{4,7},{5,6},{6,5},{7,4},{8,11},{9,10},{10,... | collective-permute-start | bytes 110600 | tf_op jit(solution)/shard_map/ppermute | solution.py:514
  21.9 0.0 collective-permute-start.9
  21.9 1.7 %collective-permute-start.11 = (s16[144,128]{1,0:T(8,128)(2,1)S(1)}, s16[144,128]{1,0:T(8,128)(2,1)S(1)}, u32[]{:S(2)}, u32[]{:S(2)}) collective-permute-start(s16[144,128]{1,0:T(8,128)(2,1)S(1)} %get-tuple-element.41), channel_id=1, source_target_pairs={{0,3},{1,2},{2,1},{3,0},{4,7},{5,6},{6,5},{7,4},{8,11},{9,10},{10,... | collective-permute-start | bytes 110600 | tf_op jit(solution)/shard_map/ppermute | solution.py:514
  23.6 0.0 collective-permute-start.13
  23.7 0.0 collective-permute-done.6.got_ref
  23.7 0.0 collective-permute-done.7.own_ref
  23.7 0.2 shard_map.77
  23.9 4.2 %collective-permute-start.8 = (s16[144,128]{1,0:T(8,128)(2,1)S(1)}, s16[144,128]{1,0:T(8,128)(2,1)S(1)}, u32[]{:S(2)}, u32[]{:S(2)}) collective-permute-start(s16[144,128]{1,0:T(8,128)(2,1)S(1)} %shard_map.77), channel_id=1, source_target_pairs={{0,13},{1,12},{2,15},{3,14},{4,9},{5,8},{6,11},{7,10},{8,5},{9,4},... | collective-permute-start | bytes 110600 | tf_op jit(solution)/shard_map/ppermute | solution.py:514
  28.1 0.0 collective-permute-done.9.got_ref
  28.1 0.2 shard_map.78
  28.3 0.3 collective-permute-start.10
  28.6 0.0 collective-permute-done.11.got_ref
  28.6 0.2 shard_map.79
  28.8 0.1 collective-permute-start.12
  28.9 0.0 collective-permute-done.13.got_ref
  28.9 1.2 %collective-permute-done.8.refs_0_ = s16[144,128]{1,0:T(8,128)(2,1)S(1)} collective-permute-done((s16[144,128]{1,0:T(8,128)(2,1)S(1)}, s16[144,128]{1,0:T(8,128)(2,1)S(1)}, u32[]{:S(2)}, u32[]{:S(2)}) %collective-permute-start.8) | collective-permute-done | bytes 36896 | tf_op jit(solution)/shard_map/ppermute | solution.py:514
  30.1 0.2 shard_map.80
  30.3 0.2 collective-permute-start.14
  30.5 2.6 %collective-permute-done.10.refs_1_ = s16[144,128]{1,0:T(8,128)(2,1)S(1)} collective-permute-done((s16[144,128]{1,0:T(8,128)(2,1)S(1)}, s16[144,128]{1,0:T(8,128)(2,1)S(1)}, u32[]{:S(2)}, u32[]{:S(2)}) %collective-permute-start.10) | collective-permute-done | bytes 36896 | tf_op jit(solution)/shard_map/ppermute | solution.py:514
  33.1 0.2 collective-permute-done.12.refs_2_
  33.3 0.0 collective-permute-done.14.refs_3_
  33.3 0.2 shard_map.81.refs_0_
  33.5 1.5 %collective-permute-start.19 = (bf16[8,2048]{1,0:T(8,128)(2,1)S(1)}, bf16[8,2048]{1,0:T(8,128)(2,1)S(1)}, u32[]{:S(2)}, u32[]{:S(2)}) collective-permute-start(bf16[8,2048]{1,0:T(8,128)(2,1)S(1)} %shard_map.81.refs_0_), channel_id=1, source_target_pairs={{0,13},{1,12},{2,15},{3,14},{4,9},{5,8},{6,11},{7,10},{8,5},{9,4},... | collective-permute-start | bytes 98312 | tf_op jit(solution)/shard_map/ppermute | solution.py:514
  35.0 0.0 collective-permute-start.17
  35.0 0.7 %collective-permute-start.21 = (bf16[8,2048]{1,0:T(8,128)(2,1)S(1)}, bf16[8,2048]{1,0:T(8,128)(2,1)S(1)}, u32[]{:S(2)}, u32[]{:S(2)}) collective-permute-start(bf16[8,2048]{1,0:T(8,128)(2,1)S(1)} %shard_map.81.refs_0_), channel_id=1, source_target_pairs={{0,2},{1,3},{2,0},{3,1},{4,6},{5,7},{6,4},{7,5},{8,10},{9,11},{10,... | collective-permute-start | bytes 98312 | tf_op jit(solution)/shard_map/ppermute | solution.py:514
  35.6 1.7 %collective-permute-start.15 = (bf16[8,2048]{1,0:T(8,128)(2,1)S(1)}, bf16[8,2048]{1,0:T(8,128)(2,1)S(1)}, u32[]{:S(2)}, u32[]{:S(2)}) collective-permute-start(bf16[8,2048]{1,0:T(8,128)(2,1)S(1)} %shard_map.81.refs_0_), channel_id=1, source_target_pairs={{0,5},{1,4},{2,7},{3,6},{4,1},{5,0},{6,3},{7,2},{8,13},{9,12},{10,... | collective-permute-start | bytes 98312 | tf_op jit(solution)/shard_map/ppermute | solution.py:514
  37.3 1.5 %collective-permute-done.19 = bf16[8,2048]{1,0:T(8,128)(2,1)S(1)} collective-permute-done((bf16[8,2048]{1,0:T(8,128)(2,1)S(1)}, bf16[8,2048]{1,0:T(8,128)(2,1)S(1)}, u32[]{:S(2)}, u32[]{:S(2)}) %collective-permute-start.19) | collective-permute-done | bytes 32800 | tf_op jit(solution)/shard_map/ppermute | solution.py:514
  38.8 0.6 %collective-permute-start.24 = (bf16[8,2048]{1,0:T(8,128)(2,1)S(1)}, bf16[8,2048]{1,0:T(8,128)(2,1)S(1)}, u32[]{:S(2)}, u32[]{:S(2)}) collective-permute-start(bf16[8,2048]{1,0:T(8,128)(2,1)S(1)} %collective-permute-done.19), channel_id=1, source_target_pairs={{0,3},{1,2},{2,1},{3,0},{4,7},{5,6},{6,5},{7,4},{8,11},{9,10},{10,... | collective-permute-start | bytes 98312 | tf_op jit(solution)/shard_map/ppermute | solution.py:514
  39.4 0.0 collective-permute-start.20
  39.4 1.0 %collective-permute-done.17 = bf16[8,2048]{1,0:T(8,128)(2,1)S(1)} collective-permute-done((bf16[8,2048]{1,0:T(8,128)(2,1)S(1)}, bf16[8,2048]{1,0:T(8,128)(2,1)S(1)}, u32[]{:S(2)}, u32[]{:S(2)}) %collective-permute-start.17) | collective-permute-done | bytes 32800 | tf_op jit(solution)/shard_map/ppermute | solution.py:514
  40.4 0.5 %collective-permute-start.23 = (bf16[8,2048]{1,0:T(8,128)(2,1)S(1)}, bf16[8,2048]{1,0:T(8,128)(2,1)S(1)}, u32[]{:S(2)}, u32[]{:S(2)}) collective-permute-start(bf16[8,2048]{1,0:T(8,128)(2,1)S(1)} %collective-permute-done.17), channel_id=1, source_target_pairs={{0,3},{1,2},{2,1},{3,0},{4,7},{5,6},{6,5},{7,4},{8,11},{9,10},{10,... | collective-permute-start | bytes 98312 | tf_op jit(solution)/shard_map/ppermute | solution.py:514
  40.9 0.0 collective-permute-done.21.refs_4_
  40.9 0.2 collective-permute-start.18
  41.1 0.0 collective-permute-done.15
  41.1 1.1 %collective-permute-start.22 = (bf16[8,2048]{1,0:T(8,128)(2,1)S(1)}, bf16[8,2048]{1,0:T(8,128)(2,1)S(1)}, u32[]{:S(2)}, u32[]{:S(2)}) collective-permute-start(bf16[8,2048]{1,0:T(8,128)(2,1)S(1)} %collective-permute-done.15), channel_id=1, source_target_pairs={{0,3},{1,2},{2,1},{3,0},{4,7},{5,6},{6,5},{7,4},{8,11},{9,10},{10,... | collective-permute-start | bytes 98312 | tf_op jit(solution)/shard_map/ppermute | solution.py:514
  42.3 0.0 collective-permute-done.24.refs_7_
  42.3 0.4 collective-permute-start.16
  42.7 0.0 collective-permute-done.20.refs_3_
  42.7 1.1 %collective-permute-done.23.refs_6_ = bf16[8,2048]{1,0:T(8,128)(2,1)S(1)} collective-permute-done((bf16[8,2048]{1,0:T(8,128)(2,1)S(1)}, bf16[8,2048]{1,0:T(8,128)(2,1)S(1)}, u32[]{:S(2)}, u32[]{:S(2)}) %collective-permute-start.23) | collective-permute-done | bytes 32800 | tf_op jit(solution)/shard_map/ppermute | solution.py:514
  43.8 0.0 collective-permute-done.18.refs_2_
  43.8 0.7 %collective-permute-done.22.refs_5_ = bf16[8,2048]{1,0:T(8,128)(2,1)S(1)} collective-permute-done((bf16[8,2048]{1,0:T(8,128)(2,1)S(1)}, bf16[8,2048]{1,0:T(8,128)(2,1)S(1)}, u32[]{:S(2)}, u32[]{:S(2)}) %collective-permute-start.22) | collective-permute-done | bytes 32800 | tf_op jit(solution)/shard_map/ppermute | solution.py:514
  44.5 0.8 %shard_map.82 = (f32[32,256]{1,0:T(8,128)}, bf16[32,4096]{1,0:T(8,128)(2,1)}) custom-call(bf16[8,2048]{1,0:T(8,128)(2,1)S(1)} %shard_map.81.refs_0_, bf16[8,2048]{1,0:T(8,128)(2,1)S(1)} %collective-permute-done.16.refs_1_, bf16[8,2048]{1,0:T(8,128)(2,1)S(1)} %collective-permute-done.18.refs_2_, bf16[8,2048]{1,0:T(8,128)(2,1)S(1)} %collective-permute-done.20.refs_3_, ...), custom_call_target="tpu_custom_call" | custom-call | tf_op jit(solution)/shard_map/pallas_call | solution.py:408
  (9 shorter events, 0.0 us)
Async XLA Ops:
  0.6 2.5 %copy-start = (bf16[32,4096]{1,0:T(8,128)(2,1)S(1)}, bf16[32,4096]{1,0:T(8,128)(2,1)}, u32[]{:S(2)}) copy-start(bf16[32,4096]{1,0:T(8,128)(2,1)} %refs_4_.1) | copy-start | bytes 786436
  0.6 2.5 %copy-start.1 = (f32[32,256]{1,0:T(8,128)S(1)}, f32[32,256]{1,0:T(8,128)}, u32[]{:S(2)}) copy-start(f32[32,256]{1,0:T(8,128)} %cells_ref.3) | copy-start | bytes 98308
  0.7 4.2 %copy-start.3 = (s32[8,256]{1,0:T(8,128)S(1)}, s32[8,256]{1,0:T(8,128)}, u32[]{:S(2)}) copy-start(s32[8,256]{1,0:T(8,128)} %neigh_ref.1) | copy-start | bytes 24580
  0.7 5.1 %copy-start.2 = (s32[256]{0:T(256)S(1)}, s32[256]{0:T(256)}, u32[]{:S(2)}) copy-start(s32[256]{0:T(256)} %param.8) | copy-start | bytes 3076
  4.4 1.4 %collective-permute-start = (f32[32,384]{1,0:T(8,128)S(1)}, f32[32,384]{1,0:T(8,128)S(1)}, u32[]{:S(2)}, u32[]{:S(2)}) collective-permute-start(f32[32,384]{1,0:T(8,128)S(1)} %get-tuple-element.25.part_ref), channel_id=1, source_target_pairs={{0,1},{1,0},{2,3},{3,2},{4,5},{5,4},{6,7},{7,6},{8,9},{9,8},{10,11... | collective-permute-start | bytes 147464 | tf_op jit(solution)/shard_map/ppermute | solution.py:465
  5.9 5.0 %collective-permute-start.2 = (f32[40,128]{1,0:T(8,128)S(1)}, f32[40,128]{1,0:T(8,128)S(1)}, u32[]{:S(2)}, u32[]{:S(2)}) collective-permute-start(f32[40,128]{1,0:T(8,128)S(1)} %get-tuple-element.27), channel_id=1, source_target_pairs={{2,5},{4,3},{3,4},{5,2},{6,9},{8,7},{7,8},{9,6},{10,13},{12,11},{1... | collective-permute-start | bytes 61448 | tf_op jit(solution)/shard_map/ppermute | solution.py:470
  6.3 5.2 %collective-permute-start.1 = (f32[40,128]{1,0:T(8,128)S(1)}, f32[40,128]{1,0:T(8,128)S(1)}, u32[]{:S(2)}, u32[]{:S(2)}) collective-permute-start(f32[40,128]{1,0:T(8,128)S(1)} %get-tuple-element.27), channel_id=1, source_target_pairs={{0,3},{2,1},{1,2},{3,0},{4,7},{6,5},{5,6},{7,4},{8,11},{10,9},{9,1... | collective-permute-start | bytes 61448 | tf_op jit(solution)/shard_map/ppermute | solution.py:470
  12.3 1.3 %collective-permute-start.3 = (f32[32,256]{1,0:T(8,128)S(1)}, f32[32,256]{1,0:T(8,128)S(1)}, u32[]{:S(2)}, u32[]{:S(2)}) collective-permute-start(f32[32,256]{1,0:T(8,128)S(1)} %get-tuple-element.31.numer_ref), channel_id=1, source_target_pairs={{0,1},{1,0},{2,3},{3,2},{4,5},{5,4},{6,7},{7,6},{8,9},{9,8},{10,11... | collective-permute-start | bytes 98312 | tf_op jit(solution)/shard_map/ppermute | solution.py:465
  13.8 4.2 %collective-permute-start.5 = (f32[40,128]{1,0:T(8,128)S(1)}, f32[40,128]{1,0:T(8,128)S(1)}, u32[]{:S(2)}, u32[]{:S(2)}) collective-permute-start(f32[40,128]{1,0:T(8,128)S(1)} %get-tuple-element.35), channel_id=1, source_target_pairs={{2,5},{4,3},{3,4},{5,2},{6,9},{8,7},{7,8},{9,6},{10,13},{12,11},{1... | collective-permute-start | bytes 61448 | tf_op jit(solution)/shard_map/ppermute | solution.py:470
  13.9 4.4 %collective-permute-start.4 = (f32[40,128]{1,0:T(8,128)S(1)}, f32[40,128]{1,0:T(8,128)S(1)}, u32[]{:S(2)}, u32[]{:S(2)}) collective-permute-start(f32[40,128]{1,0:T(8,128)S(1)} %get-tuple-element.35), channel_id=1, source_target_pairs={{0,3},{2,1},{1,2},{3,0},{4,7},{6,5},{5,6},{7,4},{8,11},{10,9},{9,1... | collective-permute-start | bytes 61448 | tf_op jit(solution)/shard_map/ppermute | solution.py:470
  19.7 4.0 %collective-permute-start.7 = (s16[576,128]{1,0:T(8,128)(2,1)S(1)}, s16[576,128]{1,0:T(8,128)(2,1)S(1)}, u32[]{:S(2)}, u32[]{:S(2)}) collective-permute-start(s16[576,128]{1,0:T(8,128)(2,1)S(1)} %get-tuple-element.39), channel_id=1, source_target_pairs={{0,1},{1,0},{2,3},{3,2},{4,5},{5,4},{6,7},{7,6},{8,9},{9,8},{10,11... | collective-permute-start | bytes 442376 | tf_op jit(solution)/shard_map/ppermute | solution.py:514
  19.9 3.8 %collective-permute-start.6 = (s16[144,128]{1,0:T(8,128)(2,1)S(1)}, s16[144,128]{1,0:T(8,128)(2,1)S(1)}, u32[]{:S(2)}, u32[]{:S(2)}) collective-permute-start(s16[144,128]{1,0:T(8,128)(2,1)S(1)} %get-tuple-element.38), channel_id=1, source_target_pairs={{0,3},{1,2},{2,1},{3,0},{4,7},{5,6},{6,5},{7,4},{8,11},{9,10},{10,... | collective-permute-start | bytes 110600 | tf_op jit(solution)/shard_map/ppermute | solution.py:514
  21.9 6.2 %collective-permute-start.9 = (s16[144,128]{1,0:T(8,128)(2,1)S(1)}, s16[144,128]{1,0:T(8,128)(2,1)S(1)}, u32[]{:S(2)}, u32[]{:S(2)}) collective-permute-start(s16[144,128]{1,0:T(8,128)(2,1)S(1)} %get-tuple-element.40), channel_id=1, source_target_pairs={{0,3},{1,2},{2,1},{3,0},{4,7},{5,6},{6,5},{7,4},{8,11},{9,10},{10,... | collective-permute-start | bytes 110600 | tf_op jit(solution)/shard_map/ppermute | solution.py:514
  21.9 6.7 %collective-permute-start.11 = (s16[144,128]{1,0:T(8,128)(2,1)S(1)}, s16[144,128]{1,0:T(8,128)(2,1)S(1)}, u32[]{:S(2)}, u32[]{:S(2)}) collective-permute-start(s16[144,128]{1,0:T(8,128)(2,1)S(1)} %get-tuple-element.41), channel_id=1, source_target_pairs={{0,3},{1,2},{2,1},{3,0},{4,7},{5,6},{6,5},{7,4},{8,11},{9,10},{10,... | collective-permute-start | bytes 110600 | tf_op jit(solution)/shard_map/ppermute | solution.py:514
  23.6 5.3 %collective-permute-start.13 = (s16[144,128]{1,0:T(8,128)(2,1)S(1)}, s16[144,128]{1,0:T(8,128)(2,1)S(1)}, u32[]{:S(2)}, u32[]{:S(2)}) collective-permute-start(s16[144,128]{1,0:T(8,128)(2,1)S(1)} %get-tuple-element.42), channel_id=1, source_target_pairs={{0,3},{1,2},{2,1},{3,0},{4,7},{5,6},{6,5},{7,4},{8,11},{9,10},{10,... | collective-permute-start | bytes 110600 | tf_op jit(solution)/shard_map/ppermute | solution.py:514
  23.9 6.2 %collective-permute-start.8 = (s16[144,128]{1,0:T(8,128)(2,1)S(1)}, s16[144,128]{1,0:T(8,128)(2,1)S(1)}, u32[]{:S(2)}, u32[]{:S(2)}) collective-permute-start(s16[144,128]{1,0:T(8,128)(2,1)S(1)} %shard_map.77), channel_id=1, source_target_pairs={{0,13},{1,12},{2,15},{3,14},{4,9},{5,8},{6,11},{7,10},{8,5},{9,4},... | collective-permute-start | bytes 110600 | tf_op jit(solution)/shard_map/ppermute | solution.py:514
  28.3 4.8 %collective-permute-start.10 = (s16[144,128]{1,0:T(8,128)(2,1)S(1)}, s16[144,128]{1,0:T(8,128)(2,1)S(1)}, u32[]{:S(2)}, u32[]{:S(2)}) collective-permute-start(s16[144,128]{1,0:T(8,128)(2,1)S(1)} %shard_map.78), channel_id=1, source_target_pairs={{0,9},{1,8},{2,11},{3,10},{4,13},{5,12},{6,15},{7,14},{8,1},{9,0},... | collective-permute-start | bytes 110600 | tf_op jit(solution)/shard_map/ppermute | solution.py:514
  28.8 4.6 %collective-permute-start.12 = (s16[144,128]{1,0:T(8,128)(2,1)S(1)}, s16[144,128]{1,0:T(8,128)(2,1)S(1)}, u32[]{:S(2)}, u32[]{:S(2)}) collective-permute-start(s16[144,128]{1,0:T(8,128)(2,1)S(1)} %shard_map.79), channel_id=1, source_target_pairs={{0,5},{1,4},{2,7},{3,6},{4,1},{5,0},{6,3},{7,2},{8,13},{9,12},{10,... | collective-permute-start | bytes 110600 | tf_op jit(solution)/shard_map/ppermute | solution.py:514
  30.3 3.0 %collective-permute-start.14 = (s16[144,128]{1,0:T(8,128)(2,1)S(1)}, s16[144,128]{1,0:T(8,128)(2,1)S(1)}, u32[]{:S(2)}, u32[]{:S(2)}) collective-permute-start(s16[144,128]{1,0:T(8,128)(2,1)S(1)} %shard_map.80), channel_id=1, source_target_pairs={{0,1},{1,0},{2,3},{3,2},{4,5},{5,4},{6,7},{7,6},{8,9},{9,8},{10,11... | collective-permute-start | bytes 110600 | tf_op jit(solution)/shard_map/ppermute | solution.py:514
  33.5 5.4 %collective-permute-start.19 = (bf16[8,2048]{1,0:T(8,128)(2,1)S(1)}, bf16[8,2048]{1,0:T(8,128)(2,1)S(1)}, u32[]{:S(2)}, u32[]{:S(2)}) collective-permute-start(bf16[8,2048]{1,0:T(8,128)(2,1)S(1)} %shard_map.81.refs_0_), channel_id=1, source_target_pairs={{0,13},{1,12},{2,15},{3,14},{4,9},{5,8},{6,11},{7,10},{8,5},{9,4},... | collective-permute-start | bytes 98312 | tf_op jit(solution)/shard_map/ppermute | solution.py:514
  35.0 5.4 %collective-permute-start.17 = (bf16[8,2048]{1,0:T(8,128)(2,1)S(1)}, bf16[8,2048]{1,0:T(8,128)(2,1)S(1)}, u32[]{:S(2)}, u32[]{:S(2)}) collective-permute-start(bf16[8,2048]{1,0:T(8,128)(2,1)S(1)} %shard_map.81.refs_0_), channel_id=1, source_target_pairs={{0,9},{1,8},{2,11},{3,10},{4,13},{5,12},{6,15},{7,14},{8,1},{9,0},... | collective-permute-start | bytes 98312 | tf_op jit(solution)/shard_map/ppermute | solution.py:514
  35.0 5.9 %collective-permute-start.21 = (bf16[8,2048]{1,0:T(8,128)(2,1)S(1)}, bf16[8,2048]{1,0:T(8,128)(2,1)S(1)}, u32[]{:S(2)}, u32[]{:S(2)}) collective-permute-start(bf16[8,2048]{1,0:T(8,128)(2,1)S(1)} %shard_map.81.refs_0_), channel_id=1, source_target_pairs={{0,2},{1,3},{2,0},{3,1},{4,6},{5,7},{6,4},{7,5},{8,10},{9,11},{10,... | collective-permute-start | bytes 98312 | tf_op jit(solution)/shard_map/ppermute | solution.py:514
  35.6 5.5 %collective-permute-start.15 = (bf16[8,2048]{1,0:T(8,128)(2,1)S(1)}, bf16[8,2048]{1,0:T(8,128)(2,1)S(1)}, u32[]{:S(2)}, u32[]{:S(2)}) collective-permute-start(bf16[8,2048]{1,0:T(8,128)(2,1)S(1)} %shard_map.81.refs_0_), channel_id=1, source_target_pairs={{0,5},{1,4},{2,7},{3,6},{4,1},{5,0},{6,3},{7,2},{8,13},{9,12},{10,... | collective-permute-start | bytes 98312 | tf_op jit(solution)/shard_map/ppermute | solution.py:514
  38.8 3.4 %collective-permute-start.24 = (bf16[8,2048]{1,0:T(8,128)(2,1)S(1)}, bf16[8,2048]{1,0:T(8,128)(2,1)S(1)}, u32[]{:S(2)}, u32[]{:S(2)}) collective-permute-start(bf16[8,2048]{1,0:T(8,128)(2,1)S(1)} %collective-permute-done.19), channel_id=1, source_target_pairs={{0,3},{1,2},{2,1},{3,0},{4,7},{5,6},{6,5},{7,4},{8,11},{9,10},{10,... | collective-permute-start | bytes 98312 | tf_op jit(solution)/shard_map/ppermute | solution.py:514
  39.4 3.2 %collective-permute-start.20 = (bf16[8,2048]{1,0:T(8,128)(2,1)S(1)}, bf16[8,2048]{1,0:T(8,128)(2,1)S(1)}, u32[]{:S(2)}, u32[]{:S(2)}) collective-permute-start(bf16[8,2048]{1,0:T(8,128)(2,1)S(1)} %collective-permute-done.19), channel_id=1, source_target_pairs={{0,1},{1,0},{2,3},{3,2},{4,5},{5,4},{6,7},{7,6},{8,9},{9,8},{10,11... | collective-permute-start | bytes 98312 | tf_op jit(solution)/shard_map/ppermute | solution.py:514
  40.4 3.4 %collective-permute-start.23 = (bf16[8,2048]{1,0:T(8,128)(2,1)S(1)}, bf16[8,2048]{1,0:T(8,128)(2,1)S(1)}, u32[]{:S(2)}, u32[]{:S(2)}) collective-permute-start(bf16[8,2048]{1,0:T(8,128)(2,1)S(1)} %collective-permute-done.17), channel_id=1, source_target_pairs={{0,3},{1,2},{2,1},{3,0},{4,7},{5,6},{6,5},{7,4},{8,11},{9,10},{10,... | collective-permute-start | bytes 98312 | tf_op jit(solution)/shard_map/ppermute | solution.py:514
  40.9 2.9 %collective-permute-start.18 = (bf16[8,2048]{1,0:T(8,128)(2,1)S(1)}, bf16[8,2048]{1,0:T(8,128)(2,1)S(1)}, u32[]{:S(2)}, u32[]{:S(2)}) collective-permute-start(bf16[8,2048]{1,0:T(8,128)(2,1)S(1)} %collective-permute-done.17), channel_id=1, source_target_pairs={{0,1},{1,0},{2,3},{3,2},{4,5},{5,4},{6,7},{7,6},{8,9},{9,8},{10,11... | collective-permute-start | bytes 98312 | tf_op jit(solution)/shard_map/ppermute | solution.py:514
  41.1 3.3 %collective-permute-start.22 = (bf16[8,2048]{1,0:T(8,128)(2,1)S(1)}, bf16[8,2048]{1,0:T(8,128)(2,1)S(1)}, u32[]{:S(2)}, u32[]{:S(2)}) collective-permute-start(bf16[8,2048]{1,0:T(8,128)(2,1)S(1)} %collective-permute-done.15), channel_id=1, source_target_pairs={{0,3},{1,2},{2,1},{3,0},{4,7},{5,6},{6,5},{7,4},{8,11},{9,10},{10,... | collective-permute-start | bytes 98312 | tf_op jit(solution)/shard_map/ppermute | solution.py:514
  42.3 2.2 %collective-permute-start.16 = (bf16[8,2048]{1,0:T(8,128)(2,1)S(1)}, bf16[8,2048]{1,0:T(8,128)(2,1)S(1)}, u32[]{:S(2)}, u32[]{:S(2)}) collective-permute-start(bf16[8,2048]{1,0:T(8,128)(2,1)S(1)} %collective-permute-done.15), channel_id=1, source_target_pairs={{0,1},{1,0},{2,3},{3,2},{4,5},{5,4},{6,7},{7,6},{8,9},{9,8},{10,11... | collective-permute-start | bytes 98312 | tf_op jit(solution)/shard_map/ppermute | solution.py:514
